TPU v7x, 32 devices: a whole 2x2x4 slice. The times are simulated.
32 devices in a mesh: gx: 2 (over core), gy: 4 (over y, x), gz: 4 (over z).
Axes of the slice: x: 2, y: 2, z: 4, core: 2. Of those that a mesh axis runs over, the one named last changes fastest.
Arguments:
- features: float32 [4, 8, 4, 128, 128], P('gx', 'gy', 'gz'), may hold values from -6 to 6
- positions: float32 [4, 8, 4, 3, 128], P('gx', 'gy', 'gz'), may hold values from 0 to 1
- counts: int32 [4, 8, 4], P('gx', 'gy', 'gz'), may hold values from 64 to 128, as said below
- waves: int32 [3, 2048], replicated, may hold values from -8 to 8
- filter_table: float32 [2048, 128], replicated, may hold values from -6 to 6
- w_value: float32 [128, 128], replicated, may hold values from -0.5 to 0.5
- w_charge: float32 [128, 128], replicated, may hold values from -0.5 to 0.5
- radial_mix: float32 [8, 128], replicated, may hold values from -2 to 2
- w_hidden: float32 [128, 256], replicated, may hold values from -0.5 to 0.5
- w_out: float32 [256, 128], replicated, may hold values from -0.375 to 0.375
Outputs:
- updated: float32 [4, 8, 4, 128, 128], P('gx', 'gy', 'gz')
Inputs may be any that keep to these rules, and one draw needn't show every extreme that they name: `counts`: slots below a cell's count hold atoms, the others are padding.
All inputs are finite; a program needn't handle non-finite values.
Results may differ from a plain program's by a relative error of at most 0.0001.
Values sent between devices are 32-bit elements; how exact they have to be, the bound alone decides.
No kernel may reach another device: no remote copies, remote signals or barrier semaphores. Data moves between devices by JAX's collectives and lax.ppermute only.
A program may use at most 64 MiB of HBM per device.

v0:
```python
import math

import jax
import jax.numpy as jnp
from jax import lax
from jax.sharding import PartitionSpec as P

K = 2048
B = 8
A = 128


highest = lax.Precision.HIGHEST
cut_radius = 1.0
message_scale = 0.125


def with_halo(block, sides, width):
    for axis, dim in sides:
        count = lax.axis_size(axis)
        forward = [(i, i + 1) for i in range(count - 1)]
        forward.append((count - 1, 0))
        backward = [(target, source) for source, target in forward]
        low = lax.ppermute(
            lax.slice_in_dim(block, block.shape[dim] - width, None, axis=dim), axis, forward
        )
        high = lax.ppermute(lax.slice_in_dim(block, 0, width, axis=dim), axis, backward)
        block = jnp.concatenate([low, block, high], axis=dim)
    return block


def radial_kernel(own_pos, nearby_pos, shift, self_pair):
    offsets = shift[:, None, None] + nearby_pos[..., :, None, :] - own_pos[..., :, :, None]
    squared = jnp.sum(offsets * offsets, axis=-3)
    distance = jnp.sqrt(squared)
    envelope = jnp.square(jnp.maximum(1.0 - squared / (cut_radius * cut_radius), 0.0))
    envelope = envelope * (1.0 - self_pair * jnp.eye(A, dtype=jnp.float32))
    centres = jnp.arange(B, dtype=jnp.float32) * (cut_radius / (B - 1))
    scaled = (distance[..., None, :, :] - centres[:, None, None]) * ((B - 1) / cut_radius)
    return jnp.exp(-scaled * scaled) * envelope[..., None, :, :]


def pair_term(own_pos, nearby, shift, self_pair, radial_mix):
    channels = nearby.shape[-2] - 3
    kernel = radial_kernel(own_pos, nearby[..., channels:, :], shift, self_pair)
    weighted = radial_mix[:, :, None] * nearby[..., None, :channels, :]
    return jnp.einsum("...bij,...bcj->...ci", kernel, weighted, precision=highest)


def plane_waves(frac_x, frac_y, frac_z, waves):
    expand = (waves.shape[1],) + (1,) * frac_x.ndim
    wave_float = waves.astype(jnp.float32)
    angle = (
        wave_float[0].reshape(expand) * frac_x
        + wave_float[1].reshape(expand) * frac_y
        + wave_float[2].reshape(expand) * frac_z
    )
    angle = angle * (2.0 * math.pi)
    return (jnp.cos(angle), jnp.sin(angle))


def shards(
    features, positions, counts, waves, filter_table, w_value, w_charge, radial_mix, w_hidden, w_out
):
    cells_x, cells_y, cells_z = counts.shape
    slot_ids = lax.broadcasted_iota(jnp.int32, (cells_x, cells_y, cells_z, A), 3)
    present = (slot_ids < counts[..., None]).astype(jnp.float32)[..., None, :]
    values = jnp.einsum("dc,xyzda->xyzca", w_value, features, precision=highest) * present
    charges = jnp.einsum("dc,xyzda->xyzca", w_charge, features, precision=highest) * present
    packed = jnp.concatenate([values, positions], axis=3)
    padded = with_halo(packed, (("gx", 0), ("gy", 1), ("gz", 2)), 1)

    def add_offset(step, summed):
        shift_x = step // 9 - 1
        shift_y = step // 3 % 3 - 1
        shift_z = step % 3 - 1
        nearby = lax.dynamic_slice(
            padded, (shift_x + 1, shift_y + 1, shift_z + 1, 0, 0), packed.shape
        )
        shift = jnp.stack([shift_x, shift_y, shift_z]).astype(jnp.float32)
        self_pair = (step == 13).astype(jnp.float32)
        return summed + pair_term(positions, nearby, shift, self_pair, radial_mix)

    messages = lax.fori_loop(0, 27, add_offset, jnp.zeros_like(values))
    grid_x = cells_x * lax.axis_size("gx")
    grid_y = cells_y * lax.axis_size("gy")
    grid_z = cells_z * lax.axis_size("gz")
    cell_x = (lax.axis_index("gx") * cells_x).astype(jnp.float32) + lax.broadcasted_iota(
        jnp.float32, (cells_x, 1, 1, 1), 0
    )
    cell_y = (lax.axis_index("gy") * cells_y).astype(jnp.float32) + lax.broadcasted_iota(
        jnp.float32, (1, cells_y, 1, 1), 1
    )
    cell_z = (lax.axis_index("gz") * cells_z).astype(jnp.float32) + lax.broadcasted_iota(
        jnp.float32, (1, 1, cells_z, 1), 2
    )
    frac_x = (cell_x + positions[:, :, :, 0, :]) / grid_x
    frac_y = (cell_y + positions[:, :, :, 1, :]) / grid_y
    frac_z = (cell_z + positions[:, :, :, 2, :]) / grid_z
    cosine, sine = plane_waves(frac_x, frac_y, frac_z, waves)
    real_part = jnp.einsum("kxyza,xyzca->kc", cosine, charges, precision=highest)
    imag_part = jnp.einsum("kxyza,xyzca->kc", sine, charges, precision=highest)
    partial_factors = jnp.stack([real_part, imag_part])
    normalizer = 1.0 / math.sqrt(grid_x * grid_y * grid_z * A)
    owned_share = lax.psum_scatter(partial_factors, "gz", scatter_dimension=1, tiled=True)
    owned_share = lax.psum(owned_share, ("gx", "gy"))
    block_size = owned_share.shape[1]
    own_filter = lax.dynamic_slice_in_dim(
        filter_table, lax.axis_index("gz") * block_size, block_size, 0
    )
    filtered_share = owned_share * normalizer * own_filter[None]
    filtered = lax.all_gather(filtered_share, "gz", axis=1, tiled=True)
    first = jnp.einsum("kc,kxyza->xyzca", filtered[0], cosine, precision=highest)
    second = jnp.einsum("kc,kxyza->xyzca", filtered[1], sine, precision=highest)
    potentials = (first + second) * (1.0 / math.sqrt(K))
    mixed = features + message_scale * messages + potentials
    hidden = jax.nn.silu(jnp.einsum("cf,xyzca->xyzfa", w_hidden, mixed, precision=highest))
    return (mixed + jnp.einsum("fc,xyzfa->xyzca", w_out, hidden, precision=highest)) * present


def solution(mesh):
    placed = (
        P("gx", "gy", "gz", None, None),
        P("gx", "gy", "gz", None, None),
        P("gx", "gy", "gz"),
        P(),
        P(),
        P(),
        P(),
        P(),
        P(),
        P(),
    )
    return jax.shard_map(
        shards,
        mesh=mesh,
        in_specs=placed,
        out_specs=P("gx", "gy", "gz", None, None),
        check_vma=False,
    )
```

profile of v0, /device:TPU:0, one launch (start us, length us, event | category | flops | bytes accessed | tf_op | source)
XLA Modules:
  0.0 502.2 jit_solution(1007538361044815148)
XLA Ops:
  10.3 21.2 %fusion.38 = f32[1,2048,128]{2,1,0:T(8,128)S(1)} fusion(f32[2,2,128,128]{3,2,1,0:T(8,128)S(1)} %fusion.72, f32[2,2,128]{2,1,0:T(2,128)S(1)} %bitcast.145, f32[2048]{0:T(1024)S(1)} %bitcast.137, f32[2,2,128]{2,1,0:T(2,128)S(1)} %get-tuple-element.283, f32[2048]{0:T(1024)S(1)} %bitcast.141, f32[2,2,128]{2,1,0:T(2,128)S(1)} %get-tuple-element.284, ...), kind=kOutput, calls=%fused_computation.34 | convolution fusion | flops 1616904192 | bytes 1341440 | tf_op jit(solution)/shard_map/kxyza,xyzca->kc/dot_general | solution.py:101
  31.5 21.5 %fusion.35 = f32[1,2048,128]{2,1,0:T(8,128)S(1)} fusion(f32[2,2,128,128]{3,2,1,0:T(8,128)S(1)} %fusion.72, f32[2,2,128]{2,1,0:T(2,128)S(1)} %bitcast.146, f32[2048]{0:T(1024)S(1)} %bitcast.138, f32[2,2,128]{2,1,0:T(2,128)S(1)} %get-tuple-element.283, f32[2048]{0:T(1024)S(1)} %bitcast.142, f32[2,2,128]{2,1,0:T(2,128)S(1)} %get-tuple-element.284, ...), kind=kOutput, calls=%fused_computation.33 | convolution fusion | flops 1616904192 | bytes 1341440 | tf_op jit(solution)/shard_map/kxyza,xyzca->kc/dot_general | solution.py:102
  57.0 2.7 collective-permute-start.2
  60.7 7.4 %collective-permute-done.2 = f32[4,1,1,131,128]{4,3,1,0,2:T(8,128)S(1)} collective-permute-done((f32[4,1,1,131,128]{4,3,1,0,2:T(8,128)S(1)}, f32[4,1,1,131,128]{4,3,1,0,2:T(8,128)S(1)}, u32[]{:S(2)}, u32[]{:S(2)}) %collective-permute-start.2) | collective-permute-done | bytes 268320 | tf_op jit(solution)/shard_map/ppermute | solution.py:24
  68.1 5.9 %collective-permute-done.3 = f32[4,1,1,131,128]{4,3,1,0,2:T(8,128)S(1)} collective-permute-done((f32[4,1,1,131,128]{4,3,1,0,2:T(8,128)S(1)}, f32[4,1,1,131,128]{4,3,1,0,2:T(8,128)S(1)}, u32[]{:S(2)}, u32[]{:S(2)}) %collective-permute-start.3) | collective-permute-done | bytes 268320 | tf_op jit(solution)/shard_map/ppermute | solution.py:27
  76.7 2.2 collective-permute-start.5
  81.5 43.0 %collective-permute-done.4 = f32[4,4,1,131,128]{4,1,3,2,0:T(4,128)} collective-permute-done((f32[4,4,1,131,128]{4,1,3,2,0:T(4,128)S(1)}, f32[4,4,1,131,128]{4,1,3,2,0:T(4,128)}, u32[]{:S(2)}, u32[]{:S(2)}) %collective-permute-start.4) | collective-permute-done | bytes 1073184 | tf_op jit(solution)/shard_map/ppermute | solution.py:24
  124.5 2.4 copy.51
  126.9 18.1 %collective-permute-done.5 = f32[4,4,1,131,128]{4,1,3,2,0:T(4,128)S(1)} collective-permute-done((f32[4,4,1,131,128]{4,1,3,2,0:T(4,128)S(1)}, f32[4,4,1,131,128]{4,1,3,2,0:T(4,128)S(1)}, u32[]{:S(2)}, u32[]{:S(2)}) %collective-permute-start.5) | collective-permute-done | bytes 1073184 | tf_op jit(solution)/shard_map/ppermute | solution.py:27
  146.2 2.2 pad_maximum_fusion
  148.4 52.6 %all-reduce.2.cloned.1.call-done = f32[2,512,128]{2,1,0:T(8,128)} async-done(((f32[2,512,128]{2,1,0:T(8,128)}), f32[2,512,128]{2,1,0:T(8,128)}) %all-reduce.2.cloned.1.call-update) | async-done | bytes 524304 | tf_op jit(solution)/shard_map/psum | solution.py:106
  201.0 1.9 broadcast_multiply_fusion
  203.0 251.8 %while.19 = (s32[]{:T(128)}, f32[2,2,1,128,128]{4,3,1,0,2:T(8,128)}, f32[8,128]{1,0:T(8,128)S(1)}, f32[4,4,3,131,128]{4,3,1,0,2:T(8,128)S(1)}, f32[2,2,1,3,128]{...) while((s32[]{:T(128)}, ...), condition=%wide.region_2.3_spmd.clone, body=%wide.region_0.2_spmd.clone.sunk | while | flops 809420352 | bytes 28811984 | solution.py:84
  205.9 1.8 dynamic-slice_bitcast_fusion.3
  207.8 4.5 fusion.122
  217.0 4.5 fusion.122
  224.5 1.8 dynamic-slice_bitcast_fusion.3
  226.4 4.5 fusion.122
  233.9 1.8 dynamic-slice_bitcast_fusion.3
  235.7 4.5 fusion.122
  243.2 1.8 dynamic-slice_bitcast_fusion.3
  245.0 4.5 fusion.122
  252.5 1.8 dynamic-slice_bitcast_fusion.3
  254.3 4.5 fusion.122
  261.8 1.8 dynamic-slice_bitcast_fusion.3
  263.7 4.5 fusion.122
  271.1 1.8 dynamic-slice_bitcast_fusion.3
  273.0 4.5 fusion.122
  280.5 1.8 dynamic-slice_bitcast_fusion.3
  282.3 4.5 fusion.122
  289.8 1.8 dynamic-slice_bitcast_fusion.3
  291.6 4.5 fusion.122
  299.1 1.8 dynamic-slice_bitcast_fusion.3
  300.9 4.5 fusion.122
  308.4 1.8 dynamic-slice_bitcast_fusion.3
  310.3 4.5 fusion.122
  317.7 1.8 dynamic-slice_bitcast_fusion.3
  319.6 4.5 fusion.122
  327.1 1.8 dynamic-slice_bitcast_fusion.3
  328.9 4.5 fusion.122
  336.4 1.8 dynamic-slice_bitcast_fusion.3
  338.2 4.5 fusion.122
  347.5 4.5 fusion.122
  355.0 1.8 dynamic-slice_bitcast_fusion.3
  356.9 4.5 fusion.122
  364.3 1.8 dynamic-slice_bitcast_fusion.3
  366.2 4.5 fusion.122
  375.5 4.5 fusion.122
  384.8 4.5 fusion.122
  392.3 1.8 dynamic-slice_bitcast_fusion.3
  394.1 4.5 fusion.122
  401.6 1.8 dynamic-slice_bitcast_fusion.3
  403.5 4.5 fusion.122
  412.8 4.5 fusion.122
  420.3 1.8 dynamic-slice_bitcast_fusion.3
  422.1 4.5 fusion.122
  429.6 1.8 dynamic-slice_bitcast_fusion.3
  431.4 4.5 fusion.122
  438.9 1.8 dynamic-slice_bitcast_fusion.3
  440.7 4.5 fusion.122
  448.2 1.8 dynamic-slice_bitcast_fusion.3
  450.1 4.5 fusion.122
  455.9 19.2 %fusion.27 = f32[2,2,128,128]{3,2,1,0:T(8,128)S(1)} fusion(f32[2,2,128]{2,1,0:T(2,128)S(1)} %bitcast.147, f32[2048]{0:T(1024)S(1)} %bitcast.139, f32[2,2,128]{2,1,0:T(2,128)S(1)} %get-tuple-element.283, f32[2048]{0:T(1024)S(1)} %bitcast.143, f32[2,2,128]{2,1,0:T(2,128)S(1)} %get-tuple-element.284, f32[2048]{0:T(1024)S(1)} %bitcast.135, ...), kind=kOutput, calls=%fused_computation.28 | convolution fusion | flops 1616904192 | bytes 1341440 | tf_op jit(solution)/shard_map/kc,kxyza->xyzca/dot_general | solution.py:113
  475.1 18.3 %fusion.82 = f32[2,2,1,128,128]{3,4,1,0,2:T(8,128)S(1)} fusion(f32[2,2,128,128]{3,2,1,0:T(8,128)S(1)} %fusion.27, f32[2,2,128]{2,1,0:T(2,128)S(1)} %bitcast.148, f32[2048]{0:T(1024)S(1)} %bitcast.140, f32[2,2,128]{2,1,0:T(2,128)S(1)} %get-tuple-element.283, f32[2048]{0:T(1024)S(1)} %bitcast.144, f32[2,2,128]{2,1,0:T(2,128)S(1)} %get-tuple-element.284, ...), kind=kOutput, calls=%fused_computation.75 | convolution fusion | flops 1617231872 | bytes 2127872 | tf_op jit(solution)/shard_map/kc,kxyza->xyzca/dot_general | solution.py:114
  (367 shorter events, 106.5 us)
Async XLA Ops:
  6.5 486.8 %copy-start = (f32[128,256]{1,0:T(8,128)S(1)}, f32[128,256]{1,0:T(8,128)}, u32[]{:S(2)}) copy-start(f32[128,256]{1,0:T(8,128)} %param.20) | copy-start | bytes 393220
  6.5 139.6 %reduce-scatter.2.cloned.1.call-start = ((), (), s32[]{:S(2)}) async-start(), calls=%async_computation.1 | async-start | bytes 2621440 | tf_op jit(solution)/shard_map/reduce_scatter | solution.py:105
  54.5 146.5 %all-reduce.2.cloned.1.call-start = ((), (), s32[]{:S(2)}) async-start(), calls=%async_computation.2 | async-start | bytes 1048576 | tf_op jit(solution)/shard_map/psum | solution.py:106
  55.0 19.1 %copy-start.3 = (f32[2,2,1,128,128]{4,3,1,0,2:T(8,128)}, f32[2,2,1,128,128]{4,3,1,0,2:T(8,128)S(1)}, u32[]{:S(2)}) copy-start(f32[2,2,1,128,128]{4,3,1,0,2:T(8,128)S(1)} %fusion.70) | copy-start | bytes 786436
  55.0 1.5 collective-permute-start
  55.5 1.4 collective-permute-start.1
  56.5 17.5 %copy-start.5 = (f32[1,2,1,131,128]{4,3,1,0,2:T(8,128)}, f32[1,2,1,131,128]{4,3,1,0,2:T(8,128)S(1)}, u32[]{:S(2)}) copy-start(f32[1,2,1,131,128]{4,3,1,0,2:T(8,128)S(1)} %collective-permute-done) | copy-start | bytes 402436
  56.9 17.1 %copy-start.6 = (f32[1,2,1,131,128]{4,3,1,0,2:T(8,128)}, f32[1,2,1,131,128]{4,3,1,0,2:T(8,128)S(1)}, u32[]{:S(2)}) copy-start(f32[1,2,1,131,128]{4,3,1,0,2:T(8,128)S(1)} %collective-permute-done.1) | copy-start | bytes 402436
  57.0 11.1 %collective-permute-start.2 = (f32[4,1,1,131,128]{4,3,1,0,2:T(8,128)S(1)}, f32[4,1,1,131,128]{4,3,1,0,2:T(8,128)S(1)}, u32[]{:S(2)}, u32[]{:S(2)}) collective-permute-start(f32[4,1,1,131,128]{4,3,1,0,2:T(8,128)S(1)} %get-tuple-element.273), channel_id=1, source_target_pairs={{0,4},{4,8},{8,12},{12,0},{1,5},{5,9},{9,13},{13,1},{2,6},{6,10},{... | collective-permute-start | bytes 804872 | tf_op jit(solution)/shard_map/ppermute | solution.py:24
  59.7 14.3 %collective-permute-start.3 = (f32[4,1,1,131,128]{4,3,1,0,2:T(8,128)S(1)}, f32[4,1,1,131,128]{4,3,1,0,2:T(8,128)S(1)}, u32[]{:S(2)}, u32[]{:S(2)}) collective-permute-start(f32[4,1,1,131,128]{4,3,1,0,2:T(8,128)S(1)} %get-tuple-element.274), channel_id=1, source_target_pairs={{4,0},{8,4},{12,8},{0,12},{5,1},{9,5},{13,9},{1,13},{6,2},{10,6},{... | collective-permute-start | bytes 804872 | tf_op jit(solution)/shard_map/ppermute | solution.py:27
  68.1 5.9 %copy-start.7 = (f32[4,1,1,131,128]{4,3,1,0,2:T(8,128)}, f32[4,1,1,131,128]{4,3,1,0,2:T(8,128)S(1)}, u32[]{:S(2)}) copy-start(f32[4,1,1,131,128]{4,3,1,0,2:T(8,128)S(1)} %collective-permute-done.2) | copy-start | bytes 804868
  75.1 49.4 %collective-permute-start.4 = (f32[4,4,1,131,128]{4,1,3,2,0:T(4,128)S(1)}, f32[4,4,1,131,128]{4,1,3,2,0:T(4,128)}, u32[]{:S(2)}, u32[]{:S(2)}) collective-permute-start(f32[4,4,1,131,128]{4,1,3,2,0:T(4,128)S(1)} %copy.49), channel_id=1, source_target_pairs={{0,1},{1,2},{2,3},{3,0},{4,5},{5,6},{6,7},{7,4},{8,9},{9,10},{10,1... | collective-permute-start | bytes 3219464 | tf_op jit(solution)/shard_map/ppermute | solution.py:24
  76.7 68.2 %collective-permute-start.5 = (f32[4,4,1,131,128]{4,1,3,2,0:T(4,128)S(1)}, f32[4,4,1,131,128]{4,1,3,2,0:T(4,128)S(1)}, u32[]{:S(2)}, u32[]{:S(2)}) collective-permute-start(f32[4,4,1,131,128]{4,1,3,2,0:T(4,128)S(1)} %copy.49), channel_id=1, source_target_pairs={{1,0},{2,1},{3,2},{0,3},{5,4},{6,5},{7,6},{4,7},{9,8},{10,9},{11,1... | collective-permute-start | bytes 3219464 | tf_op jit(solution)/shard_map/ppermute | solution.py:27
  146.1 56.8 %copy-start.14 = (f32[8,128]{1,0:T(8,128)S(1)}, f32[8,128]{1,0:T(8,128)}, u32[]{:S(2)}) copy-start(f32[8,128]{1,0:T(8,128)} %param.19) | copy-start | bytes 12292
  146.1 309.7 %all-gather.2.cloned.1.call-start = ((), (), s32[]{:S(2)}) async-start(), calls=%async_computation.3 | async-start | bytes 2621440 | tf_op jit(solution)/shard_map/all_gather | solution.py:112
  203.0 1.8 copy-start.1
  205.9 6.3 %copy-start.2 = (f32[4,4,3,131,128]{4,3,1,0,2:T(8,128)S(1)}, f32[4,4,3,131,128]{4,3,1,0,2:T(8,128)}, u32[]{:S(2)}) copy-start(f32[4,4,3,131,128]{4,3,1,0,2:T(8,128)} %copy-done.1) | copy-start | bytes 9658372 | tf_op jit(solution)/shard_map/while
  212.3 1.8 copy-start.1
  215.2 6.4 %copy-start.2 = (f32[4,4,3,131,128]{4,3,1,0,2:T(8,128)S(1)}, f32[4,4,3,131,128]{4,3,1,0,2:T(8,128)}, u32[]{:S(2)}) copy-start(f32[4,4,3,131,128]{4,3,1,0,2:T(8,128)} %copy-done.1) | copy-start | bytes 9658372 | tf_op jit(solution)/shard_map/while
  221.6 1.8 copy-start.1
  224.5 6.4 %copy-start.2 = (f32[4,4,3,131,128]{4,3,1,0,2:T(8,128)S(1)}, f32[4,4,3,131,128]{4,3,1,0,2:T(8,128)}, u32[]{:S(2)}) copy-start(f32[4,4,3,131,128]{4,3,1,0,2:T(8,128)} %copy-done.1) | copy-start | bytes 9658372 | tf_op jit(solution)/shard_map/while
  230.9 1.8 copy-start.1
  233.9 6.4 %copy-start.2 = (f32[4,4,3,131,128]{4,3,1,0,2:T(8,128)S(1)}, f32[4,4,3,131,128]{4,3,1,0,2:T(8,128)}, u32[]{:S(2)}) copy-start(f32[4,4,3,131,128]{4,3,1,0,2:T(8,128)} %copy-done.1) | copy-start | bytes 9658372 | tf_op jit(solution)/shard_map/while
  240.2 1.8 copy-start.1
  243.2 6.4 %copy-start.2 = (f32[4,4,3,131,128]{4,3,1,0,2:T(8,128)S(1)}, f32[4,4,3,131,128]{4,3,1,0,2:T(8,128)}, u32[]{:S(2)}) copy-start(f32[4,4,3,131,128]{4,3,1,0,2:T(8,128)} %copy-done.1) | copy-start | bytes 9658372 | tf_op jit(solution)/shard_map/while
  249.5 1.8 copy-start.1
  252.5 6.4 %copy-start.2 = (f32[4,4,3,131,128]{4,3,1,0,2:T(8,128)S(1)}, f32[4,4,3,131,128]{4,3,1,0,2:T(8,128)}, u32[]{:S(2)}) copy-start(f32[4,4,3,131,128]{4,3,1,0,2:T(8,128)} %copy-done.1) | copy-start | bytes 9658372 | tf_op jit(solution)/shard_map/while
  258.9 1.8 copy-start.1
  261.8 6.4 %copy-start.2 = (f32[4,4,3,131,128]{4,3,1,0,2:T(8,128)S(1)}, f32[4,4,3,131,128]{4,3,1,0,2:T(8,128)}, u32[]{:S(2)}) copy-start(f32[4,4,3,131,128]{4,3,1,0,2:T(8,128)} %copy-done.1) | copy-start | bytes 9658372 | tf_op jit(solution)/shard_map/while
  268.2 1.8 copy-start.1
  271.1 6.4 %copy-start.2 = (f32[4,4,3,131,128]{4,3,1,0,2:T(8,128)S(1)}, f32[4,4,3,131,128]{4,3,1,0,2:T(8,128)}, u32[]{:S(2)}) copy-start(f32[4,4,3,131,128]{4,3,1,0,2:T(8,128)} %copy-done.1) | copy-start | bytes 9658372 | tf_op jit(solution)/shard_map/while
  277.5 1.8 copy-start.1
  280.5 6.4 %copy-start.2 = (f32[4,4,3,131,128]{4,3,1,0,2:T(8,128)S(1)}, f32[4,4,3,131,128]{4,3,1,0,2:T(8,128)}, u32[]{:S(2)}) copy-start(f32[4,4,3,131,128]{4,3,1,0,2:T(8,128)} %copy-done.1) | copy-start | bytes 9658372 | tf_op jit(solution)/shard_map/while
  286.8 1.8 copy-start.1
  289.8 6.4 %copy-start.2 = (f32[4,4,3,131,128]{4,3,1,0,2:T(8,128)S(1)}, f32[4,4,3,131,128]{4,3,1,0,2:T(8,128)}, u32[]{:S(2)}) copy-start(f32[4,4,3,131,128]{4,3,1,0,2:T(8,128)} %copy-done.1) | copy-start | bytes 9658372 | tf_op jit(solution)/shard_map/while
  296.1 1.8 copy-start.1
  299.1 6.4 %copy-start.2 = (f32[4,4,3,131,128]{4,3,1,0,2:T(8,128)S(1)}, f32[4,4,3,131,128]{4,3,1,0,2:T(8,128)}, u32[]{:S(2)}) copy-start(f32[4,4,3,131,128]{4,3,1,0,2:T(8,128)} %copy-done.1) | copy-start | bytes 9658372 | tf_op jit(solution)/shard_map/while
  305.5 1.8 copy-start.1
  308.4 6.4 %copy-start.2 = (f32[4,4,3,131,128]{4,3,1,0,2:T(8,128)S(1)}, f32[4,4,3,131,128]{4,3,1,0,2:T(8,128)}, u32[]{:S(2)}) copy-start(f32[4,4,3,131,128]{4,3,1,0,2:T(8,128)} %copy-done.1) | copy-start | bytes 9658372 | tf_op jit(solution)/shard_map/while
  314.8 1.8 copy-start.1
  317.7 6.4 %copy-start.2 = (f32[4,4,3,131,128]{4,3,1,0,2:T(8,128)S(1)}, f32[4,4,3,131,128]{4,3,1,0,2:T(8,128)}, u32[]{:S(2)}) copy-start(f32[4,4,3,131,128]{4,3,1,0,2:T(8,128)} %copy-done.1) | copy-start | bytes 9658372 | tf_op jit(solution)/shard_map/while
  324.1 1.8 copy-start.1
  327.1 6.4 %copy-start.2 = (f32[4,4,3,131,128]{4,3,1,0,2:T(8,128)S(1)}, f32[4,4,3,131,128]{4,3,1,0,2:T(8,128)}, u32[]{:S(2)}) copy-start(f32[4,4,3,131,128]{4,3,1,0,2:T(8,128)} %copy-done.1) | copy-start | bytes 9658372 | tf_op jit(solution)/shard_map/while
  333.4 1.8 copy-start.1
  336.4 6.4 %copy-start.2 = (f32[4,4,3,131,128]{4,3,1,0,2:T(8,128)S(1)}, f32[4,4,3,131,128]{4,3,1,0,2:T(8,128)}, u32[]{:S(2)}) copy-start(f32[4,4,3,131,128]{4,3,1,0,2:T(8,128)} %copy-done.1) | copy-start | bytes 9658372 | tf_op jit(solution)/shard_map/while
  342.8 1.8 copy-start.1
  345.7 6.4 %copy-start.2 = (f32[4,4,3,131,128]{4,3,1,0,2:T(8,128)S(1)}, f32[4,4,3,131,128]{4,3,1,0,2:T(8,128)}, u32[]{:S(2)}) copy-start(f32[4,4,3,131,128]{4,3,1,0,2:T(8,128)} %copy-done.1) | copy-start | bytes 9658372 | tf_op jit(solution)/shard_map/while
  352.1 1.8 copy-start.1
  355.0 6.4 %copy-start.2 = (f32[4,4,3,131,128]{4,3,1,0,2:T(8,128)S(1)}, f32[4,4,3,131,128]{4,3,1,0,2:T(8,128)}, u32[]{:S(2)}) copy-start(f32[4,4,3,131,128]{4,3,1,0,2:T(8,128)} %copy-done.1) | copy-start | bytes 9658372 | tf_op jit(solution)/shard_map/while
  361.4 1.8 copy-start.1
  364.3 6.4 %copy-start.2 = (f32[4,4,3,131,128]{4,3,1,0,2:T(8,128)S(1)}, f32[4,4,3,131,128]{4,3,1,0,2:T(8,128)}, u32[]{:S(2)}) copy-start(f32[4,4,3,131,128]{4,3,1,0,2:T(8,128)} %copy-done.1) | copy-start | bytes 9658372 | tf_op jit(solution)/shard_map/while
  370.7 1.8 copy-start.1
  373.7 6.4 %copy-start.2 = (f32[4,4,3,131,128]{4,3,1,0,2:T(8,128)S(1)}, f32[4,4,3,131,128]{4,3,1,0,2:T(8,128)}, u32[]{:S(2)}) copy-start(f32[4,4,3,131,128]{4,3,1,0,2:T(8,128)} %copy-done.1) | copy-start | bytes 9658372 | tf_op jit(solution)/shard_map/while
  383.0 6.4 %copy-start.2 = (f32[4,4,3,131,128]{4,3,1,0,2:T(8,128)S(1)}, f32[4,4,3,131,128]{4,3,1,0,2:T(8,128)}, u32[]{:S(2)}) copy-start(f32[4,4,3,131,128]{4,3,1,0,2:T(8,128)} %copy-done.1) | copy-start | bytes 9658372 | tf_op jit(solution)/shard_map/while
  392.3 6.4 %copy-start.2 = (f32[4,4,3,131,128]{4,3,1,0,2:T(8,128)S(1)}, f32[4,4,3,131,128]{4,3,1,0,2:T(8,128)}, u32[]{:S(2)}) copy-start(f32[4,4,3,131,128]{4,3,1,0,2:T(8,128)} %copy-done.1) | copy-start | bytes 9658372 | tf_op jit(solution)/shard_map/while
  401.6 6.4 %copy-start.2 = (f32[4,4,3,131,128]{4,3,1,0,2:T(8,128)S(1)}, f32[4,4,3,131,128]{4,3,1,0,2:T(8,128)}, u32[]{:S(2)}) copy-start(f32[4,4,3,131,128]{4,3,1,0,2:T(8,128)} %copy-done.1) | copy-start | bytes 9658372 | tf_op jit(solution)/shard_map/while
  410.9 6.4 %copy-start.2 = (f32[4,4,3,131,128]{4,3,1,0,2:T(8,128)S(1)}, f32[4,4,3,131,128]{4,3,1,0,2:T(8,128)}, u32[]{:S(2)}) copy-start(f32[4,4,3,131,128]{4,3,1,0,2:T(8,128)} %copy-done.1) | copy-start | bytes 9658372 | tf_op jit(solution)/shard_map/while
  420.3 6.4 %copy-start.2 = (f32[4,4,3,131,128]{4,3,1,0,2:T(8,128)S(1)}, f32[4,4,3,131,128]{4,3,1,0,2:T(8,128)}, u32[]{:S(2)}) copy-start(f32[4,4,3,131,128]{4,3,1,0,2:T(8,128)} %copy-done.1) | copy-start | bytes 9658372 | tf_op jit(solution)/shard_map/while
  429.6 6.4 %copy-start.2 = (f32[4,4,3,131,128]{4,3,1,0,2:T(8,128)S(1)}, f32[4,4,3,131,128]{4,3,1,0,2:T(8,128)}, u32[]{:S(2)}) copy-start(f32[4,4,3,131,128]{4,3,1,0,2:T(8,128)} %copy-done.1) | copy-start | bytes 9658372 | tf_op jit(solution)/shard_map/while
  438.9 6.4 %copy-start.2 = (f32[4,4,3,131,128]{4,3,1,0,2:T(8,128)S(1)}, f32[4,4,3,131,128]{4,3,1,0,2:T(8,128)}, u32[]{:S(2)}) copy-start(f32[4,4,3,131,128]{4,3,1,0,2:T(8,128)} %copy-done.1) | copy-start | bytes 9658372 | tf_op jit(solution)/shard_map/while
  448.2 6.4 %copy-start.2 = (f32[4,4,3,131,128]{4,3,1,0,2:T(8,128)S(1)}, f32[4,4,3,131,128]{4,3,1,0,2:T(8,128)}, u32[]{:S(2)}) copy-start(f32[4,4,3,131,128]{4,3,1,0,2:T(8,128)} %copy-done.1) | copy-start | bytes 9658372 | tf_op jit(solution)/shard_map/while
  455.8 19.2 %copy-start.9 = (f32[2,2,1,128,128]{3,4,1,0,2:T(8,128)S(1)}, f32[2,2,1,128,128]{3,4,1,0,2:T(8,128)}, u32[]{:S(2)}) copy-start(f32[2,2,1,128,128]{3,4,1,0,2:T(8,128)} %copy.55) | copy-start | bytes 786436
  455.9 19.2 %copy-start.12 = (f32[2,2048,128]{2,1,0:T(8,128)S(1)}, f32[2,2048,128]{2,1,0:T(8,128)}, u32[]{:S(2)}) copy-start(f32[2,2048,128]{2,1,0:T(8,128)} %all-gather.2.cloned.1.call-done) | copy-start | bytes 6291460
  475.1 18.9 %copy-start.13 = (f32[256,128]{1,0:T(8,128)S(1)}, f32[256,128]{1,0:T(8,128)}, u32[]{:S(2)}) copy-start(f32[256,128]{1,0:T(8,128)} %param.21) | copy-start | bytes 393220
  (12 other events, 19.4 us)
Sparse Core Ops, SparseCore 0:
  54.6 77.7 reduce-scatter.1
  146.2 54.6 all-reduce.1
  203.1 45.2 all-gather.1
where the time goes:
time: 512 us; the launch traced here: 502 us
  matrix products  205 us (40%)
  waiting for transfers between devices  128 us (25%)
  local copies, waits for them, and re-layouts  100 us (20%)
  other arithmetic  45.6 us (9%)
  between operations  13.6 us (3%)
  starting transfers between devices  8.31 us (2%)
    dot_general x27, matrix products, pair_term(): jnp.einsum('...bij,...bcj->...ci', kernel, weighted, precision=highest)  122 us
    psum x1, waiting for transfers between devices, shards(): owned_share = lax.psum(owned_share, ('gx', 'gy'))  52.6 us
    ppermute x3, waiting for transfers between devices, with_halo(): lax.ppermute(lax.slice_in_dim(block, block.shape[dim] - width, None, axis...  51.3 us
    mul x27, local copies, waits for them, and re-layouts, pair_term(): weighted = radial_mix[:, :, None] * nearby[..., None, :channels, :]  49.5 us
    while x108, local copies, waits for them, and re-layouts  43.2 us
    ppermute x3, waiting for transfers between devices, with_halo(): lax.ppermute(lax.slice_in_dim(block, 0, width, axis=dim), axis, backward)  24.4 us
    sqrt x27, other arithmetic, radial_kernel(): distance = jnp.sqrt(squared)  23.9 us
    dot_general x1, matrix products, shards(): imag_part = jnp.einsum('kxyza,xyzca->kc', sine, charges, precision=highest)  21.5 us
  transfers between devices with their start and end apart: 9, of which 7 were waited for; matrix products, arithmetic and copies ran while one was open for 43% of the time, Pallas kernels for 0%

commit v1 on v0

v1 whole, which is shorter than its diff:
```python
import functools
import math

import numpy as np

import jax
import jax.numpy as jnp
from jax import lax
from jax.experimental import pallas as pl
from jax.experimental.pallas import tpu as pltpu
from jax.sharding import PartitionSpec as P


HIGH = lax.Precision.HIGH
message_scale = 0.125
bf16 = jnp.bfloat16
f32 = jnp.float32
VMEM_LIMIT = 56 * 1024 * 1024


def ring(block, axis, step):
    count = lax.axis_size(axis)
    step = step % count
    if step == 0:
        return block
    return lax.ppermute(block, axis, [(i, (i + step) % count) for i in range(count)])


def split(x):
    high = x.astype(bf16)
    low = (x - high.astype(f32)).astype(bf16)
    return high, low


def whole():
    return pl.BlockSpec(memory_space=pltpu.VMEM)


def params():
    return pltpu.CompilerParams(vmem_limit_bytes=VMEM_LIMIT)


SIN = [math.pi ** (2 * n + 1) * (-1) ** n / math.factorial(2 * n + 1) for n in range(7)]
COS = [math.pi ** (2 * n) * (-1) ** n / math.factorial(2 * n) for n in range(7)]


def poly(coefficients, t):
    acc = jnp.full_like(t, coefficients[-1])
    for c in coefficients[-2::-1]:
        acc = acc * t + c
    return acc


def turns(u):
    u = u - jnp.round(u)
    t = u * u
    twice_sine = poly([2.0 * c for c in SIN], t) * u
    cosine = poly(COS, t)
    return 1.0 - 0.5 * twice_sine * twice_sine, twice_sine * cosine


def factor_kernel(count, rows_of, *refs):
    waves_ref = refs[0]
    blocks = refs[1 : 1 + count]
    factor_ref, high_ref, low_ref, weight_ref = refs[1 + count :]
    cells, _, slots = blocks[0].shape
    channels = factor_ref.shape[-1]
    waves_here = waves_ref.shape[0]

    @pl.when(pl.program_id(0) == 0)
    def _():
        for n, block in enumerate(blocks):
            for cell in range(cells):
                at = (n * cells + cell) * slots
                high, low = split(block[cell, :channels, :].T)
                weight_ref[at : at + slots, :channels] = high
                weight_ref[at : at + slots, channels:] = low

    wave_x = waves_ref[:, 0:1]
    wave_y = waves_ref[:, 1:2]
    wave_z = waves_ref[:, 2:3]
    for n, block in enumerate(blocks):
        for cell in range(cells):
            at = (n * cells + cell) * slots
            frac = block[cell, rows_of : rows_of + 3, :]
            u = wave_x * frac[0:1] + wave_y * frac[1:2] + wave_z * frac[2:3]
            cosine, sine = turns(u)
            high, low = split(cosine)
            high_ref[:waves_here, at : at + slots] = high
            low_ref[:waves_here, at : at + slots] = low
            high, low = split(sine)
            high_ref[waves_here:, at : at + slots] = high
            low_ref[waves_here:, at : at + slots] = low
    both = jnp.dot(high_ref[...], weight_ref[...], preferred_element_type=f32)
    both = both + jnp.dot(low_ref[...], weight_ref[...], preferred_element_type=f32)
    factor_ref[...] = both[:, :channels] + both[:, channels:]


def partial_factors(waves, blocks, channels, frac_row):
    total = waves.shape[0]
    chunk = math.gcd(total, 128)
    cells, rows, slots = blocks[0].shape
    atoms = len(blocks) * cells * slots
    return pl.pallas_call(
        functools.partial(factor_kernel, len(blocks), frac_row),
        grid=(total // chunk,),
        in_specs=[pl.BlockSpec((chunk, 3), lambda j: (j, 0))] + [whole()] * len(blocks),
        out_specs=[
            pl.BlockSpec((2 * chunk, channels), lambda j: (j, 0)),
            pl.BlockSpec((2 * chunk, atoms), lambda j: (j, 0)),
            pl.BlockSpec((2 * chunk, atoms), lambda j: (j, 0)),
        ],
        out_shape=[
            jax.ShapeDtypeStruct((2 * total, channels), f32),
            jax.ShapeDtypeStruct((2 * total, atoms), bf16),
            jax.ShapeDtypeStruct((2 * total, atoms), bf16),
        ],
        scratch_shapes=[pltpu.VMEM((atoms, 2 * channels), bf16)],
        compiler_params=params(),
        cost_estimate=pl.CostEstimate(
            flops=60 * total * atoms, bytes_accessed=8 * total * atoms, transcendentals=0
        ),
        name="factors",
    )(waves, *blocks)


def filter_kernel(*refs):
    parts, (weight_ref, table_ref, out_ref) = refs[:-3], refs[-3:]
    summed = parts[0][...]
    for part in parts[1:]:
        summed = summed + part[...]
    projected = jnp.dot(summed, weight_ref[...], precision=HIGH, preferred_element_type=f32)
    out_ref[...] = projected * table_ref[...]


def filtered_piece(parts, w_charge, table):
    return pl.pallas_call(
        filter_kernel,
        in_specs=[whole()] * (len(parts) + 2),
        out_specs=whole(),
        out_shape=jax.ShapeDtypeStruct(table.shape, f32),
        compiler_params=params(),
        name="filter",
    )(*parts, w_charge, table)


def potential_kernel(groups, pieces, index_ref, *refs):
    held = refs[:groups]
    high_ref, low_ref = refs[groups : groups + 2]
    outs = refs[groups + 2 : -2]
    ordered_ref, turned_ref = refs[-2:]
    step = pl.program_id(0)
    channels = ordered_ref.shape[-1]
    piece = held[0].shape[0] // pieces

    @pl.when(step == 0)
    def _():
        for group in range(groups):
            for n in range(pieces):
                at = pl.multiple_of(index_ref[group * pieces + n] * piece, piece)
                ordered_ref[pl.ds(at, piece), :] = held[group][n * piece : (n + 1) * piece, :]
        high, low = split(ordered_ref[...].T)
        turned_ref[:channels, :] = high
        turned_ref[channels:, :] = low

    both = jnp.dot(turned_ref[...], high_ref[...], preferred_element_type=f32)
    third = jnp.dot(turned_ref[:channels, :], low_ref[...], preferred_element_type=f32)
    potential = both[:channels] + both[channels:] + third
    for n, out in enumerate(outs):

        @pl.when(step == n)
        def _(out=out):
            cells, _, slots = out.shape
            for cell in range(cells):
                out[cell] = potential[:, cell * slots : (cell + 1) * slots]


def potentials_of(index, held, pieces, high, low, cells, slots):
    rows, atoms = high.shape
    channels = held[0].shape[-1]
    count = atoms // (cells * slots)
    span = cells * slots
    return pl.pallas_call(
        functools.partial(potential_kernel, len(held), pieces),
        grid_spec=pltpu.PrefetchScalarGridSpec(
            num_scalar_prefetch=1,
            grid=(count,),
            in_specs=[pl.BlockSpec(h.shape, lambda j, index: (0, 0)) for h in held]
            + [pl.BlockSpec((rows, span), lambda j, index: (0, j))] * 2,
            out_specs=[pl.BlockSpec((cells, channels, slots), lambda j, index: (0, 0, 0))] * count,
            scratch_shapes=[
                pltpu.VMEM((rows, channels), f32),
                pltpu.VMEM((2 * channels, rows), bf16),
            ],
        ),
        out_shape=[jax.ShapeDtypeStruct((cells, channels, slots), f32)] * count,
        compiler_params=params(),
        cost_estimate=pl.CostEstimate(
            flops=6 * rows * atoms * channels, bytes_accessed=4 * rows * atoms, transcendentals=0
        ),
        name="potentials",
    )(index, *held, high, low)


def message_kernel(
    basis, own_z, step_ref, own_ref, ext_ref, mix_ref, value_ref, out_ref,
    cell_ref, own_col_ref, left_ref, right_ref,
):
    step = pl.program_id(0)
    across, along, planes, _, slots = ext_ref.shape
    channels = value_ref.shape[0]
    place_x = step_ref[0, step]
    place_y = step_ref[1, step]
    plane = step_ref[2, step]
    shift_z = step_ref[3, step].astype(f32)
    own = step_ref[4, step]
    first = step_ref[5, step]

    @pl.when(step == 0)
    def _():
        def turn(n, carry):
            x = n // (along * planes)
            y = (n // planes) % along
            z = n % planes
            high, low = split(ext_ref[x, y, z, :channels, :].T)
            cell_ref[n, :, :channels] = high
            cell_ref[n, :, channels:] = low
            return carry

        lax.fori_loop(0, across * along * planes, turn, 0)

    for axis in range(3):
        row = own_ref[own, channels + axis : channels + axis + 1, :]
        own_col_ref[axis] = jnp.broadcast_to(row, (slots, slots)).T

    near = []
    for n in range(9):
        move_x, move_y = n // 3 - 1, n % 3 - 1
        x = place_x + 1 + move_x
        y = place_y + 1 + move_y
        row = (x * along + y) * planes + plane
        cell = cell_ref[row]
        right_ref[n * slots : (n + 1) * slots, :] = cell
        right_ref[(9 + n) * slots : (10 + n) * slots, :] = cell
        at = ext_ref[x, y, plane, channels : channels + 3, :]
        near.append((at[0:1] + float(move_x), at[1:2] + float(move_y), at[2:3] + shift_z))

    tile = 16

    def rows(m, carry):
        at = pl.multiple_of(m * tile, tile)
        own_x = own_col_ref[0, pl.ds(at, tile), :]
        own_y = own_col_ref[1, pl.ds(at, tile), :]
        own_z_pos = own_col_ref[2, pl.ds(at, tile), :]
        for n in range(9):
            dx = near[n][0] - own_x
            dy = near[n][1] - own_y
            dz = near[n][2] - own_z_pos
            squared = dx * dx + dy * dy + dz * dz
            distance = squared * lax.rsqrt(jnp.maximum(squared, 1e-30))
            envelope = jnp.maximum(1.0 - squared, 0.0)
            term = envelope * envelope * jnp.exp(squared * (-float((basis - 1) ** 2)))
            ratio = jnp.exp(distance * (2.0 * (basis - 1)))
            if own_z and n == 4:
                i = lax.broadcasted_iota(jnp.int32, (tile, slots), 0) + at
                j = lax.broadcasted_iota(jnp.int32, (tile, slots), 1)
                same = jnp.logical_and(i == j, step_ref[3, step] == 0)
                term = jnp.where(same, 0.0, term)
            for b in range(basis):
                if b > 0:
                    term = term * ratio
                high, low = split(term)
                left_ref[pl.ds(b * slots + at, tile), n * slots : (n + 1) * slots] = high
                left_ref[pl.ds(b * slots + at, tile), (9 + n) * slots : (10 + n) * slots] = low
        return carry

    lax.fori_loop(0, slots // tile, rows, 0)
    both = jnp.dot(left_ref[...], right_ref[...], preferred_element_type=f32)
    gathered = both[:, :channels] + both[:, channels:]
    projected = jnp.dot(gathered, value_ref[...], precision=HIGH, preferred_element_type=f32)
    message = projected[:slots] * mix_ref[0:1, :]
    for b in range(1, basis):
        message = message + projected[b * slots : (b + 1) * slots] * mix_ref[b : b + 1, :]
    message = message.T

    @pl.when(first == 1)
    def _():
        out_ref[0] = message

    @pl.when(first == 0)
    def _():
        out_ref[0] += message


def pair_messages(steps, own_z, own, ext, mix, w_value):
    cells, _, slots = own.shape
    basis, channels = mix.shape
    across, along, planes = ext.shape[:3]
    count = steps.shape[1]
    return pl.pallas_call(
        functools.partial(message_kernel, basis, own_z),
        grid_spec=pltpu.PrefetchScalarGridSpec(
            num_scalar_prefetch=1,
            grid=(count,),
            in_specs=[whole()] * 4,
            out_specs=pl.BlockSpec((1, channels, slots), lambda s, steps: (steps[4, s], 0, 0)),
            scratch_shapes=[
                pltpu.VMEM((across * along * planes, slots, 2 * channels), bf16),
                pltpu.VMEM((3, slots, slots), f32),
                pltpu.VMEM((basis * slots, 18 * slots), bf16),
                pltpu.VMEM((18 * slots, 2 * channels), bf16),
            ],
        ),
        out_shape=jax.ShapeDtypeStruct((cells, channels, slots), f32),
        compiler_params=params(),
        cost_estimate=pl.CostEstimate(
            flops=count * 8 * basis * slots * 9 * slots * channels, bytes_accessed=1 << 20,
            transcendentals=0,
        ),
        name="messages",
    )(jnp.asarray(steps), own, ext, mix, w_value)


def visits(cells_x, cells_y, cells_z, inside):
    table, seen = [], set()
    for x in range(cells_x):
        for y in range(cells_y):
            for z in range(cells_z):
                own = (x * cells_y + y) * cells_z + z
                for shift in (-1, 0, 1):
                    plane = z + shift
                    here = 0 <= plane < cells_z
                    if here != inside:
                        continue
                    if not here:
                        plane = 0 if plane < 0 else 1
                    table.append((x, y, plane, shift, own, int(own not in seen)))
                    seen.add(own)
    return np.array(table, np.int32).T.copy()


def mlp_kernel(count, *refs):
    counts_ref, feature_ref = refs[:2]
    messages = refs[2:4]
    potentials = refs[4 : 4 + count]
    hidden_ref, back_ref, out_ref = refs[4 + count :]
    cells, channels, slots = feature_ref.shape
    columns = []
    for cell in range(cells):
        mixed = feature_ref[cell] + message_scale * (messages[0][cell] + messages[1][cell])
        for potential in potentials:
            mixed = mixed + potential[cell]
        columns.append(mixed)
    mixed = jnp.concatenate(columns, axis=1)
    inner = jnp.dot(hidden_ref[...].T, mixed, precision=HIGH, preferred_element_type=f32)
    hidden = inner * jax.nn.sigmoid(inner)
    updated = mixed + jnp.dot(back_ref[...].T, hidden, precision=HIGH, preferred_element_type=f32)
    slot = lax.broadcasted_iota(jnp.int32, (channels, slots), 1)
    for cell in range(cells):
        part = updated[:, cell * slots : (cell + 1) * slots]
        out_ref[cell] = jnp.where(slot < counts_ref[cell], part, 0.0)


def atom_mlp(counts, features, messages, potentials, w_hidden, w_out):
    return pl.pallas_call(
        functools.partial(mlp_kernel, len(potentials)),
        in_specs=[pl.BlockSpec(memory_space=pltpu.SMEM)]
        + [whole()] * (5 + len(potentials)),
        out_specs=whole(),
        out_shape=jax.ShapeDtypeStruct(features.shape, f32),
        compiler_params=params(),
        name="atom_mlp",
    )(counts, features, *messages, *potentials, w_hidden, w_out)


def along_y(block, low, high):
    return jnp.concatenate([low, block, high], axis=1)


def with_x(block):
    low = ring(block[-1:], "gx", 1)
    high = ring(block[:1], "gx", -1)
    return jnp.concatenate([low, block, high], axis=0)


def shards(
    features, positions, counts, waves, filter_table, w_value, w_charge, radial_mix, w_hidden, w_out
):
    cells_x, cells_y, cells_z, channels, slots = features.shape
    basis = radial_mix.shape[0]
    total_waves = waves.shape[1]
    size_x, size_y, size_z = (lax.axis_size(a) for a in ("gx", "gy", "gz"))
    at_x, at_y, at_z = (lax.axis_index(a) for a in ("gx", "gy", "gz"))
    grid = (cells_x * size_x, cells_y * size_y, cells_z * size_z)
    cells = cells_x * cells_y * cells_z

    shape = (cells_x, cells_y, cells_z, 1, slots)
    occupied = lax.broadcasted_iota(jnp.int32, shape, 4) < counts[..., None, None]
    fractions = []
    for axis, (at, here) in enumerate(((at_x, cells_x), (at_y, cells_y), (at_z, cells_z))):
        cell = lax.broadcasted_iota(jnp.int32, shape, axis) + at * here
        fractions.append((cell.astype(f32) + positions[..., axis : axis + 1, :]) / grid[axis])
    packed = jnp.concatenate(
        [jnp.where(occupied, features, 0.0), positions] + fractions + [jnp.zeros_like(fractions[0])] * 2,
        axis=3,
    )
    rows = packed.shape[3]

    gathered = [packed] + [ring(packed, "gy", s) for s in range(1, size_y)]
    below_z = ring(packed, "gz", 1)[:, :, -1:]
    above_z = ring(packed, "gz", -1)[:, :, :1]

    share = total_waves // size_y
    own_waves = lax.dynamic_slice_in_dim(waves, at_y * share, share, 1).astype(f32).T
    flat = [block.reshape(cells, rows, slots) for block in gathered]
    factors, high, low = partial_factors(own_waves, flat, channels, channels + 3)

    half = factors.shape[0] // size_x
    summed = lax.dynamic_slice_in_dim(factors, at_x * half, half, 0)
    for s in range(1, size_x):
        other = lax.rem(at_x + s, size_x)
        summed = summed + ring(lax.dynamic_slice_in_dim(factors, other * half, half, 0), "gx", s)
    piece = half // size_z
    parts = [lax.dynamic_slice_in_dim(summed, at_z * piece, piece, 0)]
    for s in range(1, size_z):
        other = lax.rem(at_z + s, size_z)
        parts.append(ring(lax.dynamic_slice_in_dim(summed, other * piece, piece, 0), "gz", s))
    scale = 1.0 / math.sqrt(grid[0] * grid[1] * grid[2] * slots) / math.sqrt(total_waves)
    chunk = math.gcd(share, 128)
    table = lax.dynamic_slice_in_dim(filter_table, at_y * share, share, 0) * scale
    table = jnp.broadcast_to(
        table.reshape(share // chunk, 1, chunk, channels), (share // chunk, 2, chunk, channels)
    ).reshape(2 * share, channels)
    table = lax.dynamic_slice_in_dim(table, at_x * half + at_z * piece, piece, 0)
    filtered = filtered_piece(parts, w_charge, table)

    held_z = jnp.concatenate([filtered] + [ring(filtered, "gz", s) for s in range(1, size_z)], axis=0)
    held = [held_z] + [ring(held_z, "gx", s) for s in range(1, size_x)]
    index = jnp.stack(
        [
            lax.rem(at_x - s + size_x, size_x) * size_z + lax.rem(at_z - t + size_z, size_z)
            for s in range(size_x)
            for t in range(size_z)
        ]
    ).astype(jnp.int32)

    own = packed.reshape(cells, rows, slots)
    plane = with_x(along_y(packed, gathered[1 % size_y][:, -1:], gathered[-1 % size_y][:, :1]))
    sides = jnp.concatenate([below_z, above_z], axis=2)
    sides = along_y(sides, ring(sides[:, -1:], "gy", 1), ring(sides[:, :1], "gy", -1))
    sides = with_x(sides)
    squares = jnp.arange(basis, dtype=f32) ** 2
    mix = radial_mix * jnp.exp(-squares)[:, None]
    near = pair_messages(visits(cells_x, cells_y, cells_z, True), True, own, plane, mix, w_value)
    far = pair_messages(visits(cells_x, cells_y, cells_z, False), False, own, sides, mix, w_value)

    found = potentials_of(index, held, held_z.shape[0] // piece, high, low, cells, slots)
    returned = [found[0]] + [ring(found[s], "gy", -s) for s in range(1, size_y)]

    updated = atom_mlp(
        counts.reshape(cells), features.reshape(cells, channels, slots), [near, far], returned,
        w_hidden, w_out,
    )
    return updated.reshape(features.shape)


def solution(mesh):
    placed = (
        P("gx", "gy", "gz", None, None),
        P("gx", "gy", "gz", None, None),
        P("gx", "gy", "gz"),
        P(),
        P(),
        P(),
        P(),
        P(),
        P(),
        P(),
    )
    return jax.shard_map(
        shards,
        mesh=mesh,
        in_specs=placed,
        out_specs=P("gx", "gy", "gz", None, None),
        check_vma=False,
    )
```

time: 512 us -> 142 us (0.28); the launches traced: 502 us -> 142 us
  matrix products: 205 us -> 0 us
  waiting for transfers between devices: 128 us -> 13.1 us
  local copies, waits for them, and re-layouts: 100 us -> 8.71 us
  Pallas kernels: 0 us -> 81.2 us
  other arithmetic: 45.6 us -> 8.26 us
  starting transfers between devices: 8.31 us -> 30 us
  between operations: 13.6 us -> 0.35 us
    dot_general x35 -> x0, matrix products: 205 us -> none  [the longest x27 122 us: pair_term(): jnp.einsum('...bij,...bcj->...ci', kernel, weighted, precision=highest)]
    pallas_call x0 -> x6, Pallas kernels: none -> 81.2 us  [the longest x2 57.5 us: pair_messages(): pl.pallas_call(functools.partial(message_kernel, basis, own_z), grid_spec...]
    ppermute x6 -> x22, waiting for transfers between devices: 75.7 us -> 13.1 us  [ring(): lax.ppermute(block, axis, [(i, (i + step) % count) for i in range(count)])]
    psum x1 -> x0, waiting for transfers between devices: 52.6 us -> none  [shards(): owned_share = lax.psum(owned_share, ('gx', 'gy'))]
    mul x28 -> x0, local copies, waits for them, and re-layouts: 50.4 us -> none  [the longest x27 49.5 us: pair_term(): weighted = radial_mix[:, :, None] * nearby[..., None, :channels, :]]
    while x109 -> x0, local copies, waits for them, and re-layouts: 44.2 us -> none
    sqrt x27 -> x0, other arithmetic: 23.9 us -> none  [radial_kernel(): distance = jnp.sqrt(squared)]
    ppermute x6 -> x22, starting transfers between devices: 8.23 us -> 30 us  [ring(): lax.ppermute(block, axis, [(i, (i + step) % count) for i in range(count)])]
  transfers between devices with their start and end apart: 9 -> 22, of which waited for: 7 -> 7; matrix products, arithmetic and copies ran while one was open for 43% -> 7% of each run, Pallas kernels for 0% -> 55%
where the time goes in v1:
time: 142 us
  Pallas kernels  81.2 us (57%)
  starting transfers between devices  30 us (21%)
  waiting for transfers between devices  13.1 us (9%)
  local copies, waits for them, and re-layouts  8.71 us (6%)
  other arithmetic  8.26 us (6%)
    pallas_call x2, Pallas kernels, pair_messages(): pl.pallas_call(functools.partial(message_kernel, basis, own_z), grid_spec...  57.5 us
    ppermute x22, starting transfers between devices, ring(): lax.ppermute(block, axis, [(i, (i + step) % count) for i in range(count)])  30 us
    ppermute x22, waiting for transfers between devices, ring(): lax.ppermute(block, axis, [(i, (i + step) % count) for i in range(count)])  13.1 us
    pallas_call x1, Pallas kernels, partial_factors(): pl.pallas_call(functools.partial(factor_kernel, len(blocks), frac_row), g...  11.8 us
    pallas_call x1, Pallas kernels, potentials_of(): pl.pallas_call(functools.partial(potential_kernel, len(held), pieces), gr...  7.15 us
    unnamed x44, local copies, waits for them, and re-layouts  4.78 us
    pallas_call x1, Pallas kernels, atom_mlp(): pl.pallas_call(functools.partial(mlp_kernel, len(potentials)), in_specs=[...  2.95 us
  transfers between devices with their start and end apart: 22, of which 7 were waited for; matrix products, arithmetic and copies ran while one was open for 7% of the time, Pallas kernels for 55%

profile of v1, /device:TPU:0, one launch (start us, length us, event | category | flops | bytes accessed | tf_op | source)
XLA Modules:
  0.0 141.7 jit_solution(981065350291405562)
XLA Ops:
  0.0 0.8 iota_compare_fusion
  0.8 0.7 copy.31
  1.5 1.0 broadcast_select_fusion
  2.5 0.1 iota.25
  2.5 0.1 iota.27
  2.6 0.7 multiply_bitcast_fusion
  3.4 3.0 %collective-permute-start = (f32[2,2,1,136,128]{4,3,2,1,0:T(8,128)S(1)}, f32[2,2,1,136,128]{4,3,2,1,0:T(8,128)S(1)}, u32[]{:S(2)}, u32[]{:S(2)}) collective-permute-start(f32[2,2,1,136,128]{4,3,2,1,0:T(8,128)S(1)} %concatenate.25), channel_id=1, source_target_pairs={{0,4},{4,8},{8,12},{12,0},{1,5},{5,9},{9,13},{13,1},{2,6},{6,10},{... | collective-permute-start | bytes 835592 | tf_op jit(solution)/shard_map/ppermute | solution.py:26
  6.4 1.0 collective-permute-start.1
  7.4 1.9 %collective-permute-start.10 = (f32[2,2,1,136,128]{4,3,2,1,0:T(8,128)S(1)}, f32[2,2,1,136,128]{4,3,2,1,0:T(8,128)S(1)}, u32[]{:S(2)}, u32[]{:S(2)}) collective-permute-start(f32[2,2,1,136,128]{4,3,2,1,0:T(8,128)S(1)} %concatenate.25), channel_id=1, source_target_pairs={{0,8},{4,12},{8,0},{12,4},{1,9},{5,13},{9,1},{13,5},{2,10},{6,14},... | collective-permute-start | bytes 835592 | tf_op jit(solution)/shard_map/ppermute | solution.py:26
  9.4 1.6 %collective-permute-start.4 = (f32[2,2,1,136,128]{4,3,2,1,0:T(8,128)S(1)}, f32[2,2,1,136,128]{4,3,2,1,0:T(8,128)S(1)}, u32[]{:S(2)}, u32[]{:S(2)}) collective-permute-start(f32[2,2,1,136,128]{4,3,2,1,0:T(8,128)S(1)} %concatenate.25), channel_id=1, source_target_pairs={{0,1},{1,2},{2,3},{3,0},{4,5},{5,6},{6,7},{7,4},{8,9},{9,10},{10,1... | collective-permute-start | bytes 835592 | tf_op jit(solution)/shard_map/ppermute | solution.py:26
  10.9 2.2 %collective-permute-start.5 = (f32[2,2,1,136,128]{4,3,2,1,0:T(8,128)S(1)}, f32[2,2,1,136,128]{4,3,2,1,0:T(8,128)S(1)}, u32[]{:S(2)}, u32[]{:S(2)}) collective-permute-start(f32[2,2,1,136,128]{4,3,2,1,0:T(8,128)S(1)} %concatenate.25), channel_id=1, source_target_pairs={{0,3},{1,0},{2,1},{3,2},{4,7},{5,4},{6,5},{7,6},{8,11},{9,8},{10,9... | collective-permute-start | bytes 835592 | tf_op jit(solution)/shard_map/ppermute | solution.py:26
  13.2 0.1 copy.37
  13.4 0.0 copy-start.19
  13.4 0.7 convert_bitcast_fusion.refs_0_
  14.1 0.6 broadcast_multiply_fusion.mix_ref
  14.7 1.0 dynamic-slice_multiply_fusion
  15.8 0.6 constant_dynamic-slice_fusion.refs_5_
  16.4 0.5 broadcast.39
  16.9 0.6 reduce.3
  17.6 0.6 reshape.45.refs_0_
  18.2 0.6 stack.35.index_ref
  18.8 1.5 %collective-permute-done.1 = f32[2,2,1,136,128]{4,3,2,1,0:T(8,128)S(1)} collective-permute-done((f32[2,2,1,136,128]{4,3,2,1,0:T(8,128)S(1)}, f32[2,2,1,136,128]{4,3,2,1,0:T(8,128)S(1)}, u32[]{:S(2)}, u32[]{:S(2)}) %collective-permute-start.1) | collective-permute-done | bytes 278560 | tf_op jit(solution)/shard_map/ppermute | solution.py:26
  20.3 0.7 copy-done.6
  21.0 0.1 copy-done.9
  21.1 11.8 %factors.1 = (f32[1024,128]{1,0:T(8,128)}, bf16[1024,2048]{1,0:T(8,128)(2,1)}, bf16[1024,2048]{1,0:T(8,128)(2,1)}) custom-call(f32[512,3]{1,0:T(8,128)} %convert_bitcast_fusion.refs_0_, f32[4,136,128]{2,1,0:T(8,128)} %bitcast.33, f32[4,136,128]{2,1,0:T(8,128)} %bitcast.39, f32[4,136,128]{2,1,0:T(8,128)} %bitcast.41, f32[4,136,128]{2,1,0:T(8,128)} %bitcast.40), custom_call_target="tpu_custom_call" | custom-call | flops 62914560 | bytes 8388608 | tf_op jit(solution)/shard_map/factors/pallas_call | solution.py:104
  32.9 1.0 constant_dynamic-slice_fusion.5
  33.9 0.1 collective-permute-start.11
  34.1 1.9 %collective-permute-start.6 = (f32[2,1,2,136,128]{4,3,2,1,0:T(8,128)S(1)}, f32[2,1,2,136,128]{4,3,2,1,0:T(8,128)S(1)}, u32[]{:S(2)}, u32[]{:S(2)}) collective-permute-start(f32[2,1,2,136,128]{4,3,2,1,0:T(8,128)S(1)} %get-tuple-element.21), channel_id=1, source_target_pairs={{0,4},{4,8},{8,12},{12,0},{1,5},{5,9},{9,13},{13,1},{2,6},{6,10},{... | collective-permute-start | bytes 835592 | tf_op jit(solution)/shard_map/ppermute | solution.py:26
  36.0 1.1 collective-permute-start.7
  37.3 0.2 collective-permute-start.2
  37.5 0.3 collective-permute-start.3
  37.8 0.4 copy-done.8
  38.2 0.7 constant_dynamic-slice_fusion.1
  38.9 1.6 %collective-permute-start.12 = (f32[128,128]{1,0:T(8,128)S(1)}, f32[128,128]{1,0:T(8,128)S(1)}, u32[]{:S(2)}, u32[]{:S(2)}) collective-permute-start(f32[128,128]{1,0:T(8,128)S(1)} %get-tuple-element.27), channel_id=1, source_target_pairs={{0,1},{1,2},{2,3},{3,0},{4,5},{5,6},{6,7},{7,4},{8,9},{9,10},{10,1... | collective-permute-start | bytes 196616 | tf_op jit(solution)/shard_map/ppermute | solution.py:26
  40.5 4.1 %collective-permute-done.6 = f32[2,1,2,136,128]{4,3,2,1,0:T(8,128)S(1)} collective-permute-done((f32[2,1,2,136,128]{4,3,2,1,0:T(8,128)S(1)}, f32[2,1,2,136,128]{4,3,2,1,0:T(8,128)S(1)}, u32[]{:S(2)}, u32[]{:S(2)}) %collective-permute-start.6) | collective-permute-done | bytes 278560 | tf_op jit(solution)/shard_map/ppermute | solution.py:26
  44.6 2.6 %collective-permute-start.13 = (f32[128,128]{1,0:T(8,128)S(1)}, f32[128,128]{1,0:T(8,128)S(1)}, u32[]{:S(2)}, u32[]{:S(2)}) collective-permute-start(f32[128,128]{1,0:T(8,128)S(1)} %get-tuple-element.26), channel_id=1, source_target_pairs={{0,2},{1,3},{2,0},{3,1},{4,6},{5,7},{6,4},{7,5},{8,10},{9,11},{10,... | collective-permute-start | bytes 196616 | tf_op jit(solution)/shard_map/ppermute | solution.py:26
  47.2 2.7 %collective-permute-done.7 = f32[2,1,2,136,128]{4,3,2,1,0:T(8,128)S(1)} collective-permute-done((f32[2,1,2,136,128]{4,3,2,1,0:T(8,128)S(1)}, f32[2,1,2,136,128]{4,3,2,1,0:T(8,128)S(1)}, u32[]{:S(2)}, u32[]{:S(2)}) %collective-permute-start.7) | collective-permute-done | bytes 278560 | tf_op jit(solution)/shard_map/ppermute | solution.py:26
  50.0 3.6 %collective-permute-start.14 = (f32[128,128]{1,0:T(8,128)S(1)}, f32[128,128]{1,0:T(8,128)S(1)}, u32[]{:S(2)}, u32[]{:S(2)}) collective-permute-start(f32[128,128]{1,0:T(8,128)S(1)} %get-tuple-element.25), channel_id=1, source_target_pairs={{0,3},{1,0},{2,1},{3,2},{4,7},{5,4},{6,5},{7,6},{8,11},{9,8},{10,9... | collective-permute-start | bytes 196616 | tf_op jit(solution)/shard_map/ppermute | solution.py:26
  53.6 0.1 pad_maximum_fusion.2
  53.6 0.1 fusion
  53.7 0.1 collective-permute-start.8
  53.8 0.5 collective-permute-start.9
  54.3 1.1 collective-permute-done.14.refs_3_
  55.5 0.6 copy-done.17
  56.1 1.8 %filter.1 = f32[128,128]{1,0:T(8,128)} custom-call(f32[128,128]{1,0:T(8,128)} %get-tuple-element.28.refs_0_, f32[128,128]{1,0:T(8,128)} %copy-done.15, f32[128,128]{1,0:T(8,128)} %copy-done.16, f32[128,128]{1,0:T(8,128)} %copy-done.17, f32[128,128]{1,0:T(8,128)} %refs_4_.1, f32[128,128]{1,0:T(8,128)} %constant_dynamic-slice_fusion.refs_5_), custom_call_target="tpu_custom_call" | custom-call | tf_op jit(solution)/shard_map/filter/pallas_call | solution.py:137
  57.9 0.3 collective-permute-start.15
  58.2 4.4 %collective-permute-start.16 = (f32[128,128]{1,0:T(8,128)}, f32[128,128]{1,0:T(8,128)S(1)}, u32[]{:S(2)}, u32[]{:S(2)}) collective-permute-start(f32[128,128]{1,0:T(8,128)} %filter.1), channel_id=1, source_target_pairs={{0,2},{1,3},{2,0},{3,1},{4,6},{5,7},{6,4},{7,5},{8,10},{9,11},{10,... | collective-permute-start | bytes 196616 | tf_op jit(solution)/shard_map/ppermute | solution.py:26
  62.6 1.1 pad_maximum_fusion.1.ext_ref
  63.7 1.0 collective-permute-done.15
  64.7 2.0 %collective-permute-done.16 = f32[128,128]{1,0:T(8,128)S(1)} collective-permute-done((f32[128,128]{1,0:T(8,128)}, f32[128,128]{1,0:T(8,128)S(1)}, u32[]{:S(2)}, u32[]{:S(2)}) %collective-permute-start.16) | collective-permute-done | bytes 65568 | tf_op jit(solution)/shard_map/ppermute | solution.py:26
  66.7 0.6 collective-permute-done.17
  67.3 0.0 copy-start.3
  67.3 0.1 collective-permute-start.18
  67.4 20.3 %messages.2.refs_2_ = f32[4,128,128]{2,1,0:T(8,128)} custom-call(s32[6,4]{1,0:T(8,128)} %constant.75.clone.step_ref, f32[4,136,128]{2,1,0:T(8,128)} %bitcast.34, f32[4,4,1,136,128]{4,3,2,1,0:T(8,128)} %pad_maximum_fusion.1.ext_ref, f32[8,128]{1,0:T(8,128)} %broadcast_multiply_fusion.mix_ref, f32[128,128]{1,0:T(8,128)} %value_ref.3), custom_call_target="tpu_custom_call" | custom-call | flops 4831838208 | bytes 1048576 | tf_op jit(solution)/shard_map/messages/pallas_call | solution.py:300
  87.7 0.7 copy-done.13
  88.4 7.1 %potentials.1 = (f32[4,128,128]{2,1,0:T(8,128)}, f32[4,128,128]{2,1,0:T(8,128)}, f32[4,128,128]{2,1,0:T(8,128)}, f32[4,128,128]{2,1,0:T(8,128)}) custom-call(s32[8]{0:T(128)} %stack.35.index_ref, f32[512,128]{1,0:T(8,128)} %copy-done.3, f32[512,128]{1,0:T(8,128)} %copy-done.13, bf16[1024,2048]{1,0:T(8,128)(2,1)} %get-tuple-element.13.refs_2_, ...), custom_call_target="tpu_custom_call" | custom-call | flops 1610612736 | bytes 8388608 | tf_op jit(solution)/shard_map/potentials/pallas_call | solution.py:183
  95.6 2.0 %collective-permute-start.19 = (f32[4,128,128]{2,1,0:T(8,128)}, f32[4,128,128]{2,1,0:T(8,128)S(1)}, u32[]{:S(2)}, u32[]{:S(2)}) collective-permute-start(f32[4,128,128]{2,1,0:T(8,128)} %get-tuple-element.16), channel_id=1, source_target_pairs={{0,12},{4,0},{8,4},{12,8},{1,13},{5,1},{9,5},{13,9},{2,14},{6,2},{... | collective-permute-start | bytes 786440 | tf_op jit(solution)/shard_map/ppermute | solution.py:26
  97.6 1.5 %collective-permute-start.20 = (f32[4,128,128]{2,1,0:T(8,128)}, f32[4,128,128]{2,1,0:T(8,128)S(1)}, u32[]{:S(2)}, u32[]{:S(2)}) collective-permute-start(f32[4,128,128]{2,1,0:T(8,128)} %get-tuple-element.17), channel_id=1, source_target_pairs={{0,8},{4,12},{8,0},{12,4},{1,9},{5,13},{9,1},{13,5},{2,10},{6,14},... | collective-permute-start | bytes 786440 | tf_op jit(solution)/shard_map/ppermute | solution.py:26
  99.1 1.6 %pad_maximum_fusion.ext_ref = f32[4,4,2,136,128]{4,3,2,1,0:T(8,128)} fusion(f32[1,4,2,136,128]{4,3,2,1,0:T(8,128)S(1)} %collective-permute-done.9, f32[2,1,2,136,128]{4,3,2,1,0:T(8,128)S(1)} %collective-permute-done.7, f32[2,2,2,136,128]{4,3,2,1,0:T(8,128)S(1)} %constant_dynamic-update-slice_fusion, f32[2,1,2,136,128]{4,3,2,1,0:T(8,128)S(1)} %collective-permute-done.6, ...), kind=kLoop, calls=%fused_computation | loop fusion | flops 2228224 | bytes 4456448 | tf_op jit(solution)/shard_map/concatenate | solution.py:383
  100.7 37.2 %messages.3.refs_3_ = f32[4,128,128]{2,1,0:T(8,128)} custom-call(s32[6,8]{1,0:T(8,128)} %constant.76.clone.step_ref, f32[4,136,128]{2,1,0:T(8,128)} %bitcast.35, f32[4,4,2,136,128]{4,3,2,1,0:T(8,128)} %pad_maximum_fusion.ext_ref, f32[8,128]{1,0:T(8,128)} %broadcast_multiply_fusion.mix_ref, f32[128,128]{1,0:T(8,128)} %value_ref.3), custom_call_target="tpu_custom_call" | custom-call | flops 9663676416 | bytes 1048576 | tf_op jit(solution)/shard_map/messages/pallas_call | solution.py:300
  137.9 0.7 copy-done.10
  138.6 0.1 copy-done.11
  138.7 0.1 copy-done.12
  138.7 3.0 %atom_mlp.1 = f32[4,128,128]{2,1,0:T(8,128)} custom-call(s32[4]{0:T(128)} %reshape.45.refs_0_, f32[4,128,128]{2,1,0:T(8,128)} %bitcast.37, f32[4,128,128]{2,1,0:T(8,128)} %messages.2.refs_2_, f32[4,128,128]{2,1,0:T(8,128)} %messages.3.refs_3_, f32[4,128,128]{2,1,0:T(8,128)} %get-tuple-element.15.refs_4_, f32[4,128,128]{2,1,0:T(8,128)} %copy-done.10, ...), custom_call_target="tpu_custom_call" | custom-call | tf_op jit(solution)/shard_map/atom_mlp/pallas_call | solution.py:365
  (66 shorter events, 0.4 us)
Async XLA Ops:
  0.0 13.2 %copy-start = (s32[3,2048]{1,0:T(4,128)S(1)}, s32[3,2048]{1,0:T(4,128)}, u32[]{:S(2)}) copy-start(s32[3,2048]{1,0:T(4,128)} %param.15) | copy-start | bytes 73732
  0.0 14.1 %copy-start.18 = (f32[8,128]{1,0:T(8,128)S(1)}, f32[8,128]{1,0:T(8,128)}, u32[]{:S(2)}) copy-start(f32[8,128]{1,0:T(8,128)} %param.19) | copy-start | bytes 12292
  3.4 13.0 %copy-start.1 = (f32[2,2,1,136,128]{4,3,2,1,0:T(8,128)}, f32[2,2,1,136,128]{4,3,2,1,0:T(8,128)S(1)}, u32[]{:S(2)}) copy-start(f32[2,2,1,136,128]{4,3,2,1,0:T(8,128)S(1)} %concatenate.25) | copy-start | bytes 835588
  3.4 15.4 %collective-permute-start = (f32[2,2,1,136,128]{4,3,2,1,0:T(8,128)S(1)}, f32[2,2,1,136,128]{4,3,2,1,0:T(8,128)S(1)}, u32[]{:S(2)}, u32[]{:S(2)}) collective-permute-start(f32[2,2,1,136,128]{4,3,2,1,0:T(8,128)S(1)} %concatenate.25), channel_id=1, source_target_pairs={{0,4},{4,8},{8,12},{12,0},{1,5},{5,9},{9,13},{13,1},{2,6},{6,10},{... | collective-permute-start | bytes 835592 | tf_op jit(solution)/shard_map/ppermute | solution.py:26
  6.4 13.9 %collective-permute-start.1 = (f32[2,2,1,136,128]{4,3,2,1,0:T(8,128)S(1)}, f32[2,2,1,136,128]{4,3,2,1,0:T(8,128)S(1)}, u32[]{:S(2)}, u32[]{:S(2)}) collective-permute-start(f32[2,2,1,136,128]{4,3,2,1,0:T(8,128)S(1)} %concatenate.25), channel_id=1, source_target_pairs={{0,12},{4,0},{8,4},{12,8},{1,13},{5,1},{9,5},{13,9},{2,14},{6,2},{... | collective-permute-start | bytes 835592 | tf_op jit(solution)/shard_map/ppermute | solution.py:26
  7.4 12.9 %collective-permute-start.10 = (f32[2,2,1,136,128]{4,3,2,1,0:T(8,128)S(1)}, f32[2,2,1,136,128]{4,3,2,1,0:T(8,128)S(1)}, u32[]{:S(2)}, u32[]{:S(2)}) collective-permute-start(f32[2,2,1,136,128]{4,3,2,1,0:T(8,128)S(1)} %concatenate.25), channel_id=1, source_target_pairs={{0,8},{4,12},{8,0},{12,4},{1,9},{5,13},{9,1},{13,5},{2,10},{6,14},... | collective-permute-start | bytes 835592 | tf_op jit(solution)/shard_map/ppermute | solution.py:26
  9.4 24.6 %collective-permute-start.4 = (f32[2,2,1,136,128]{4,3,2,1,0:T(8,128)S(1)}, f32[2,2,1,136,128]{4,3,2,1,0:T(8,128)S(1)}, u32[]{:S(2)}, u32[]{:S(2)}) collective-permute-start(f32[2,2,1,136,128]{4,3,2,1,0:T(8,128)S(1)} %concatenate.25), channel_id=1, source_target_pairs={{0,1},{1,2},{2,3},{3,0},{4,5},{5,6},{6,7},{7,4},{8,9},{9,10},{10,1... | collective-permute-start | bytes 835592 | tf_op jit(solution)/shard_map/ppermute | solution.py:26
  10.9 23.1 %collective-permute-start.5 = (f32[2,2,1,136,128]{4,3,2,1,0:T(8,128)S(1)}, f32[2,2,1,136,128]{4,3,2,1,0:T(8,128)S(1)}, u32[]{:S(2)}, u32[]{:S(2)}) collective-permute-start(f32[2,2,1,136,128]{4,3,2,1,0:T(8,128)S(1)} %concatenate.25), channel_id=1, source_target_pairs={{0,3},{1,0},{2,1},{3,2},{4,7},{5,4},{6,5},{7,6},{8,11},{9,8},{10,9... | collective-permute-start | bytes 835592 | tf_op jit(solution)/shard_map/ppermute | solution.py:26
  13.4 3.6 %copy-start.19 = (s32[2,2,1]{1,2,0:T(1,128)S(1)}, s32[2,2,1]{1,2,0:T(1,128)}, u32[]{:S(2)}) copy-start(s32[2,2,1]{1,2,0:T(1,128)} %param.14) | copy-start | bytes 52
  18.8 1.5 %copy-start.4 = (f32[2,2,1,136,128]{4,3,2,1,0:T(8,128)}, f32[2,2,1,136,128]{4,3,2,1,0:T(8,128)S(1)}, u32[]{:S(2)}) copy-start(f32[2,2,1,136,128]{4,3,2,1,0:T(8,128)S(1)} %collective-permute-done) | copy-start | bytes 835588
  20.3 0.7 copy-start.6
  20.3 0.8 copy-start.9
  33.9 3.2 %copy-start.5 = (f32[2,2,1,136,128]{4,3,2,1,0:T(8,128)S(1)}, f32[2,2,1,136,128]{4,3,2,1,0:T(8,128)}, u32[]{:S(2)}) copy-start(f32[2,2,1,136,128]{4,3,2,1,0:T(8,128)} %copy-done.4) | copy-start | bytes 835588
  33.9 3.9 %collective-permute-start.11 = (f32[512,128]{1,0:T(8,128)S(1)}, f32[512,128]{1,0:T(8,128)S(1)}, u32[]{:S(2)}, u32[]{:S(2)}) collective-permute-start(f32[512,128]{1,0:T(8,128)S(1)} %constant_dynamic-slice_fusion.5), channel_id=1, source_target_pairs={{0,16},{16,0},{1,17},{17,1},{2,18},{18,2},{3,19},{19,3},{4,20},{20... | collective-permute-start | bytes 786440 | tf_op jit(solution)/shard_map/ppermute | solution.py:26
  34.0 3.1 %copy-start.7 = (f32[2,2,1,136,128]{4,3,2,1,0:T(8,128)S(1)}, f32[2,2,1,136,128]{4,3,2,1,0:T(8,128)}, u32[]{:S(2)}) copy-start(f32[2,2,1,136,128]{4,3,2,1,0:T(8,128)} %copy-done.6) | copy-start | bytes 835588
  34.0 3.1 %copy-start.2 = (f32[2,2,1,136,128]{4,3,2,1,0:T(8,128)S(1)}, f32[2,2,1,136,128]{4,3,2,1,0:T(8,128)}, u32[]{:S(2)}) copy-start(f32[2,2,1,136,128]{4,3,2,1,0:T(8,128)} %copy-done.1) | copy-start | bytes 835588
  34.1 10.5 %collective-permute-start.6 = (f32[2,1,2,136,128]{4,3,2,1,0:T(8,128)S(1)}, f32[2,1,2,136,128]{4,3,2,1,0:T(8,128)S(1)}, u32[]{:S(2)}, u32[]{:S(2)}) collective-permute-start(f32[2,1,2,136,128]{4,3,2,1,0:T(8,128)S(1)} %get-tuple-element.21), channel_id=1, source_target_pairs={{0,4},{4,8},{8,12},{12,0},{1,5},{5,9},{9,13},{13,1},{2,6},{6,10},{... | collective-permute-start | bytes 835592 | tf_op jit(solution)/shard_map/ppermute | solution.py:26
  36.0 13.9 %collective-permute-start.7 = (f32[2,1,2,136,128]{4,3,2,1,0:T(8,128)S(1)}, f32[2,1,2,136,128]{4,3,2,1,0:T(8,128)S(1)}, u32[]{:S(2)}, u32[]{:S(2)}) collective-permute-start(f32[2,1,2,136,128]{4,3,2,1,0:T(8,128)S(1)} %get-tuple-element.22), channel_id=1, source_target_pairs={{0,12},{4,0},{8,4},{12,8},{1,13},{5,1},{9,5},{13,9},{2,14},{6,2},{... | collective-permute-start | bytes 835592 | tf_op jit(solution)/shard_map/ppermute | solution.py:26
  37.2 1.0 copy-start.8
  37.3 20.9 %collective-permute-start.2 = (f32[1,4,1,136,128]{4,3,2,1,0:T(8,128)S(1)}, f32[1,4,1,136,128]{4,3,2,1,0:T(8,128)S(1)}, u32[]{:S(2)}, u32[]{:S(2)}) collective-permute-start(f32[1,4,1,136,128]{4,3,2,1,0:T(8,128)S(1)} %get-tuple-element.23), channel_id=1, source_target_pairs={{0,16},{16,0},{1,17},{17,1},{2,18},{18,2},{3,19},{19,3},{4,20},{20... | collective-permute-start | bytes 835592 | tf_op jit(solution)/shard_map/ppermute | solution.py:26
  37.5 25.1 %collective-permute-start.3 = (f32[1,4,1,136,128]{4,3,2,1,0:T(8,128)S(1)}, f32[1,4,1,136,128]{4,3,2,1,0:T(8,128)S(1)}, u32[]{:S(2)}, u32[]{:S(2)}) collective-permute-start(f32[1,4,1,136,128]{4,3,2,1,0:T(8,128)S(1)} %get-tuple-element.24), channel_id=1, source_target_pairs={{0,16},{16,0},{1,17},{17,1},{2,18},{18,2},{3,19},{19,3},{4,20},{20... | collective-permute-start | bytes 835592 | tf_op jit(solution)/shard_map/ppermute | solution.py:26
  38.9 14.8 %collective-permute-start.12 = (f32[128,128]{1,0:T(8,128)S(1)}, f32[128,128]{1,0:T(8,128)S(1)}, u32[]{:S(2)}, u32[]{:S(2)}) collective-permute-start(f32[128,128]{1,0:T(8,128)S(1)} %get-tuple-element.27), channel_id=1, source_target_pairs={{0,1},{1,2},{2,3},{3,0},{4,5},{5,6},{6,7},{7,4},{8,9},{9,10},{10,1... | collective-permute-start | bytes 196616 | tf_op jit(solution)/shard_map/ppermute | solution.py:26
  44.6 9.2 %collective-permute-start.13 = (f32[128,128]{1,0:T(8,128)S(1)}, f32[128,128]{1,0:T(8,128)S(1)}, u32[]{:S(2)}, u32[]{:S(2)}) collective-permute-start(f32[128,128]{1,0:T(8,128)S(1)} %get-tuple-element.26), channel_id=1, source_target_pairs={{0,2},{1,3},{2,0},{3,1},{4,6},{5,7},{6,4},{7,5},{8,10},{9,11},{10,... | collective-permute-start | bytes 196616 | tf_op jit(solution)/shard_map/ppermute | solution.py:26
  50.0 5.5 %collective-permute-start.14 = (f32[128,128]{1,0:T(8,128)S(1)}, f32[128,128]{1,0:T(8,128)S(1)}, u32[]{:S(2)}, u32[]{:S(2)}) collective-permute-start(f32[128,128]{1,0:T(8,128)S(1)} %get-tuple-element.25), channel_id=1, source_target_pairs={{0,3},{1,0},{2,1},{3,2},{4,7},{5,4},{6,5},{7,6},{8,11},{9,8},{10,9... | collective-permute-start | bytes 196616 | tf_op jit(solution)/shard_map/ppermute | solution.py:26
  53.7 1.7 %copy-start.15 = (f32[128,128]{1,0:T(8,128)}, f32[128,128]{1,0:T(8,128)S(1)}, u32[]{:S(2)}) copy-start(f32[128,128]{1,0:T(8,128)S(1)} %collective-permute-done.12.refs_1_) | copy-start | bytes 196612
  53.7 45.4 %collective-permute-start.8 = (f32[1,4,2,136,128]{4,3,2,1,0:T(8,128)S(1)}, f32[1,4,2,136,128]{4,3,2,1,0:T(8,128)S(1)}, u32[]{:S(2)}, u32[]{:S(2)}) collective-permute-start(f32[1,4,2,136,128]{4,3,2,1,0:T(8,128)S(1)} %get-tuple-element.19), channel_id=1, source_target_pairs={{0,16},{16,0},{1,17},{17,1},{2,18},{18,2},{3,19},{19,3},{4,20},{20... | collective-permute-start | bytes 1671176 | tf_op jit(solution)/shard_map/ppermute | solution.py:26
  53.8 1.6 %copy-start.16 = (f32[128,128]{1,0:T(8,128)}, f32[128,128]{1,0:T(8,128)S(1)}, u32[]{:S(2)}) copy-start(f32[128,128]{1,0:T(8,128)S(1)} %collective-permute-done.13.refs_2_) | copy-start | bytes 196612
  53.8 45.3 %collective-permute-start.9 = (f32[1,4,2,136,128]{4,3,2,1,0:T(8,128)S(1)}, f32[1,4,2,136,128]{4,3,2,1,0:T(8,128)S(1)}, u32[]{:S(2)}, u32[]{:S(2)}) collective-permute-start(f32[1,4,2,136,128]{4,3,2,1,0:T(8,128)S(1)} %get-tuple-element.20), channel_id=1, source_target_pairs={{0,16},{16,0},{1,17},{17,1},{2,18},{18,2},{3,19},{19,3},{4,20},{20... | collective-permute-start | bytes 1671176 | tf_op jit(solution)/shard_map/ppermute | solution.py:26
  55.5 0.6 copy-start.17
  57.9 9.4 %copy-start.14 = (f32[128,128]{1,0:T(8,128)S(1)}, f32[128,128]{1,0:T(8,128)}, u32[]{:S(2)}) copy-start(f32[128,128]{1,0:T(8,128)} %filter.1) | copy-start | bytes 196612
  57.9 6.8 %collective-permute-start.15 = (f32[128,128]{1,0:T(8,128)}, f32[128,128]{1,0:T(8,128)S(1)}, u32[]{:S(2)}, u32[]{:S(2)}) collective-permute-start(f32[128,128]{1,0:T(8,128)} %filter.1), channel_id=1, source_target_pairs={{0,1},{1,2},{2,3},{3,0},{4,5},{5,6},{6,7},{7,4},{8,9},{9,10},{10,1... | collective-permute-start | bytes 196616 | tf_op jit(solution)/shard_map/ppermute | solution.py:26
  58.2 8.5 %collective-permute-start.16 = (f32[128,128]{1,0:T(8,128)}, f32[128,128]{1,0:T(8,128)S(1)}, u32[]{:S(2)}, u32[]{:S(2)}) collective-permute-start(f32[128,128]{1,0:T(8,128)} %filter.1), channel_id=1, source_target_pairs={{0,2},{1,3},{2,0},{3,1},{4,6},{5,7},{6,4},{7,5},{8,10},{9,11},{10,... | collective-permute-start | bytes 196616 | tf_op jit(solution)/shard_map/ppermute | solution.py:26
  62.6 4.7 %collective-permute-start.17 = (f32[128,128]{1,0:T(8,128)}, f32[128,128]{1,0:T(8,128)S(1)}, u32[]{:S(2)}, u32[]{:S(2)}) collective-permute-start(f32[128,128]{1,0:T(8,128)} %filter.1), channel_id=1, source_target_pairs={{0,3},{1,0},{2,1},{3,2},{4,7},{5,4},{6,5},{7,6},{8,11},{9,8},{10,9... | collective-permute-start | bytes 196616 | tf_op jit(solution)/shard_map/ppermute | solution.py:26
  67.3 20.4 %copy-start.3 = (f32[512,128]{1,0:T(8,128)}, f32[512,128]{1,0:T(8,128)S(1)}, u32[]{:S(2)}) copy-start(f32[512,128]{1,0:T(8,128)S(1)} %pad_maximum_fusion.4.refs_0_) | copy-start | bytes 786436
  67.3 20.4 %collective-permute-start.18 = (f32[512,128]{1,0:T(8,128)S(1)}, f32[512,128]{1,0:T(8,128)S(1)}, u32[]{:S(2)}, u32[]{:S(2)}) collective-permute-start(f32[512,128]{1,0:T(8,128)S(1)} %pad_maximum_fusion.4.refs_0_), channel_id=1, source_target_pairs={{0,16},{16,0},{1,17},{17,1},{2,18},{18,2},{3,19},{19,3},{4,20},{20... | collective-permute-start | bytes 786440 | tf_op jit(solution)/shard_map/ppermute | solution.py:26
  87.7 0.7 copy-start.13
  95.6 42.3 %collective-permute-start.19 = (f32[4,128,128]{2,1,0:T(8,128)}, f32[4,128,128]{2,1,0:T(8,128)S(1)}, u32[]{:S(2)}, u32[]{:S(2)}) collective-permute-start(f32[4,128,128]{2,1,0:T(8,128)} %get-tuple-element.16), channel_id=1, source_target_pairs={{0,12},{4,0},{8,4},{12,8},{1,13},{5,1},{9,5},{13,9},{2,14},{6,2},{... | collective-permute-start | bytes 786440 | tf_op jit(solution)/shard_map/ppermute | solution.py:26
  97.6 40.3 %collective-permute-start.20 = (f32[4,128,128]{2,1,0:T(8,128)}, f32[4,128,128]{2,1,0:T(8,128)S(1)}, u32[]{:S(2)}, u32[]{:S(2)}) collective-permute-start(f32[4,128,128]{2,1,0:T(8,128)} %get-tuple-element.17), channel_id=1, source_target_pairs={{0,8},{4,12},{8,0},{12,4},{1,9},{5,13},{9,1},{13,5},{2,10},{6,14},... | collective-permute-start | bytes 786440 | tf_op jit(solution)/shard_map/ppermute | solution.py:26
  99.1 38.8 %collective-permute-start.21 = (f32[4,128,128]{2,1,0:T(8,128)}, f32[4,128,128]{2,1,0:T(8,128)S(1)}, u32[]{:S(2)}, u32[]{:S(2)}) collective-permute-start(f32[4,128,128]{2,1,0:T(8,128)} %get-tuple-element.18), channel_id=1, source_target_pairs={{0,4},{4,8},{8,12},{12,0},{1,5},{5,9},{9,13},{13,1},{2,6},{6,10},{... | collective-permute-start | bytes 786440 | tf_op jit(solution)/shard_map/ppermute | solution.py:26
  137.9 0.7 copy-start.10
  137.9 0.8 copy-start.11
  137.9 0.9 copy-start.12

commit v2 on v0

v2 whole, which is shorter than its diff:
```python
import functools
import math

import numpy as np

import jax
import jax.numpy as jnp
from jax import lax
from jax.experimental import pallas as pl
from jax.experimental.pallas import tpu as pltpu
from jax.sharding import PartitionSpec as P


HIGH = lax.Precision.HIGH
message_scale = 0.125
bf16 = jnp.bfloat16
f32 = jnp.float32
VMEM_LIMIT = 28 * 1024 * 1024


LOG2E = math.log2(math.e)


def partner(i, step, count):
    return i ^ step


def exchange(block, axis, step):
    count = lax.axis_size(axis)
    pairs = [(i, partner(i, step, count)) for i in range(count)]
    return lax.ppermute(block, axis, pairs)


def is_even(axis):
    if lax.axis_size(axis) % 2:
        return jnp.bool_(True)
    return lax.rem(lax.axis_index(axis), 2) == 0


def neighbours(low, high, axis, same=False):
    count = lax.axis_size(axis)
    if count == 1:
        return low, high
    if count % 2:
        up = lax.ppermute(low, axis, [(i, (i - 1) % count) for i in range(count)])
        down = lax.ppermute(high, axis, [(i, (i + 1) % count) for i in range(count)])
        return up, down
    even = is_even(axis)
    first = high if same else jnp.where(even, high, low)
    second = low if same else jnp.where(even, low, high)
    one = [(i, i ^ 1) for i in range(count)]
    two = [(i, (i + 1 if i % 2 else i - 1) % count) for i in range(count)]
    return lax.ppermute(first, axis, one), lax.ppermute(second, axis, two)


def below_above(low, high, axis):
    first, second = neighbours(low, high, axis)
    even = is_even(axis)
    return jnp.where(even, second, first), jnp.where(even, first, second)


def split(x):
    high = x.astype(bf16)
    low = (x - high.astype(f32)).astype(bf16)
    return high, low


def whole():
    return pl.BlockSpec(memory_space=pltpu.VMEM)


def params():
    return pltpu.CompilerParams(vmem_limit_bytes=VMEM_LIMIT)


def pack_kernel(grid, place_ref, counts_ref, feature_ref, position_ref, out_ref):
    cells, channels, slots = feature_ref.shape
    slot = lax.broadcasted_iota(jnp.int32, (channels, slots), 1)
    blank = jnp.zeros((2, slots), f32)
    for cell in range(cells):
        out_ref[cell, :channels, :] = jnp.where(slot < counts_ref[cell], feature_ref[cell], 0.0)
        at = position_ref[cell]
        rows = [at]
        for axis in range(3):
            here = place_ref[cell * 3 + axis].astype(f32)
            rows.append((at[axis : axis + 1] + here) * (1.0 / grid[axis]))
        out_ref[cell, channels:, :] = jnp.concatenate(rows + [blank], axis=0)


def pack(grid, place, counts, features, positions):
    cells, channels, slots = features.shape
    smem = pl.BlockSpec(memory_space=pltpu.SMEM)
    return pl.pallas_call(
        functools.partial(pack_kernel, grid),
        in_specs=[smem, smem, whole(), whole()],
        out_specs=whole(),
        out_shape=jax.ShapeDtypeStruct((cells, channels + 8, slots), f32),
        compiler_params=params(),
        name="pack",
    )(place, counts, features, positions)


def fitted(function, terms):
    t = 0.125 * (1.0 + np.cos(np.pi * (np.arange(terms) + 0.5) / terms))
    solved = np.linalg.solve(np.vander(t, terms, increasing=True), function(np.sqrt(t)))
    return [float(c) for c in solved]


SIN = fitted(lambda u: 2.0 * np.sin(np.pi * u) / u, 5)
COS = fitted(lambda u: np.cos(np.pi * u), 5)


def poly(coefficients, t):
    acc = t * coefficients[-1] + coefficients[-2]
    for c in coefficients[-3::-1]:
        acc = acc * t + c
    return acc


def turns(u):
    u = u - jnp.round(u)
    t = u * u
    twice_sine = poly(SIN, t) * u
    cosine = poly(COS, t)
    return 1.0 - 0.5 * twice_sine * twice_sine, twice_sine * cosine


def factor_kernel(parts, chunk, first, at_ref, waves_ref, block_ref, *refs):
    before = refs[: 0 if first else parts]
    refs = refs[len(before) :]
    after, wave_ref, weight_ref = refs[:parts], refs[parts], refs[parts + 1]
    cells, _, slots = block_ref.shape
    channels = after[0].shape[-1]
    span = cells * slots
    total = waves_ref.shape[0]
    for cell in range(cells):
        high, low = split(block_ref[cell, :channels, :])
        for at in (cell * slots, span + cell * slots):
            weight_ref[:channels, at : at + slots] = high
            weight_ref[channels:, at : at + slots] = low

    def some(j, carry):
        here = pl.multiple_of(j * chunk, chunk)
        wave_x = waves_ref[pl.ds(here, chunk), 0:1]
        wave_y = waves_ref[pl.ds(here, chunk), 1:2]
        wave_z = waves_ref[pl.ds(here, chunk), 2:3]
        row = pl.multiple_of(j * 2 * chunk, 2 * chunk)
        for cell in range(cells):
            at = cell * slots
            frac = block_ref[cell, channels + 3 : channels + 6, :]
            u = wave_x * frac[0:1] + wave_y * frac[1:2] + wave_z * frac[2:3]
            cosine, sine = turns(u)
            high, low = split(cosine)
            wave_ref[pl.ds(row, chunk), at : at + slots] = high
            wave_ref[pl.ds(row, chunk), span + at : span + at + slots] = low
            high, low = split(sine)
            wave_ref[pl.ds(row + chunk, chunk), at : at + slots] = high
            wave_ref[pl.ds(row + chunk, chunk), span + at : span + at + slots] = low
        both = lax.dot_general(
            wave_ref[pl.ds(row, 2 * chunk), :], weight_ref[...], (((1,), (1,)), ((), ())),
            preferred_element_type=f32,
        )
        both = both[:, :channels] + both[:, channels:]
        per_part = total // chunk // parts
        part = lax.rem(j // per_part - at_ref[0] + parts, parts)
        row = pl.multiple_of(lax.rem(j, per_part) * 2 * chunk, 2 * chunk)
        for n in range(parts):

            @pl.when(part == n)
            def _(n=n):
                if first:
                    after[n][pl.ds(row, 2 * chunk), :] = both
                else:
                    after[n][pl.ds(row, 2 * chunk), :] = before[n][pl.ds(row, 2 * chunk), :] + both

        return carry

    lax.fori_loop(0, total // chunk, some, 0)


def partial_factors(at, waves, block, before, parts):
    total = waves.shape[0]
    chunk = math.gcd(total // parts, 128)
    cells, rows, slots = block.shape
    channels = rows - 8
    span = cells * slots
    out = [jax.ShapeDtypeStruct((2 * total // parts, channels), f32)] * parts
    return pl.pallas_call(
        functools.partial(factor_kernel, parts, chunk, not before),
        in_specs=[pl.BlockSpec(memory_space=pltpu.SMEM)] + [whole()] * (2 + len(before)),
        out_specs=[whole()] * (parts + 1),
        out_shape=out + [jax.ShapeDtypeStruct((2 * total, 2 * span), bf16)],
        scratch_shapes=[pltpu.VMEM((2 * channels, 2 * span), bf16)],
        compiler_params=params(),
        cost_estimate=pl.CostEstimate(
            flops=8 * total * span * channels, bytes_accessed=8 * total * span, transcendentals=0
        ),
        name="factors",
    )(at, waves, block, *before)


def filter_kernel(*refs):
    parts, (weight_ref, table_ref, out_ref) = refs[:-3], refs[-3:]
    summed = parts[0][...]
    for part in parts[1:]:
        summed = summed + part[...]
    projected = jnp.dot(summed, weight_ref[...], precision=HIGH, preferred_element_type=f32)
    out_ref[...] = projected * table_ref[...]


def filtered_piece(parts, w_charge, table):
    return pl.pallas_call(
        filter_kernel,
        in_specs=[whole()] * (len(parts) + 2),
        out_specs=whole(),
        out_shape=jax.ShapeDtypeStruct(table.shape, f32),
        compiler_params=params(),
        name="filter",
    )(*parts, w_charge, table)


def potential_kernel(groups, pieces, blocks, index_ref, *refs):
    held = refs[:groups]
    waves = refs[groups : groups + blocks]
    outs = refs[groups + blocks : -2]
    ordered_ref, turned_ref = refs[-2:]
    channels = ordered_ref.shape[-1]
    piece = held[0].shape[0] // pieces
    for group in range(groups):
        for n in range(pieces):
            at = pl.multiple_of(index_ref[group * pieces + n] * piece, piece)
            ordered_ref[pl.ds(at, piece), :] = held[group][n * piece : (n + 1) * piece, :]
    high, low = split(ordered_ref[...].T)
    turned_ref[:channels, :] = high
    turned_ref[channels:, :] = low
    for wave_ref, out in zip(waves, outs):
        cells, _, slots = out.shape
        span = cells * slots
        both = jnp.dot(turned_ref[...], wave_ref[:, :span], preferred_element_type=f32)
        third = jnp.dot(turned_ref[:channels, :], wave_ref[:, span:], preferred_element_type=f32)
        potential = both[:channels] + both[channels:] + third
        for cell in range(cells):
            out[cell] = potential[:, cell * slots : (cell + 1) * slots]


def potentials_of(index, held, pieces, waves, cells, slots):
    rows = waves[0].shape[0]
    channels = held[0].shape[-1]
    return pl.pallas_call(
        functools.partial(potential_kernel, len(held), pieces, len(waves)),
        in_specs=[pl.BlockSpec(memory_space=pltpu.SMEM)] + [whole()] * (len(held) + len(waves)),
        out_specs=[whole()] * len(waves),
        scratch_shapes=[
            pltpu.VMEM((rows, channels), f32),
            pltpu.VMEM((2 * channels, rows), bf16),
        ],
        out_shape=[jax.ShapeDtypeStruct((cells, channels, slots), f32)] * len(waves),
        compiler_params=params(),
        cost_estimate=pl.CostEstimate(
            flops=6 * rows * len(waves) * cells * slots * channels,
            bytes_accessed=4 * rows * len(waves) * cells * slots, transcendentals=0,
        ),
        name="potentials",
    )(index, *held, *waves)


def message_kernel(
    basis, own_plane, step_ref, own_ref, ext_ref, mix_ref, value_ref, out_ref,
    cell_ref, own_col_ref, acc_ref, mixed_ref, left_0, left_1, left_2, right_0, right_1, right_2,
):
    count = step_ref.shape[1]
    cells = own_ref.shape[0]
    across, along, planes, _, slots = ext_ref.shape
    channels = value_ref.shape[0]
    lefts, rights = (left_0, left_1, left_2), (right_0, right_1, right_2)

    def turn(n, carry):
        x = n // (along * planes)
        y = (n // planes) % along
        z = n % planes
        high, low = split(ext_ref[x, y, z, :channels, :])
        cell_ref[n, :channels, :] = high
        cell_ref[n, channels:, :] = low
        return carry

    lax.fori_loop(0, across * along * planes, turn, 0, unroll=4)
    for b in range(basis):
        high, low = split(value_ref[...] * mix_ref[b : b + 1, :])
        mixed_ref[b * channels : (b + 1) * channels, :channels] = high
        mixed_ref[b * channels : (b + 1) * channels, channels:] = low
    for cell in range(cells):
        columns = own_ref[cell, channels : channels + 8, :].T
        for axis in range(3):
            own_col_ref[cell, axis] = jnp.broadcast_to(columns[:, axis : axis + 1], (slots, slots))

    def fill(step, move):
        place_x = step_ref[0, step] + 1 + (move - 1)
        place_y = step_ref[1, step]
        plane = step_ref[2, step]
        shift_z = step_ref[3, step].astype(f32)
        left, right = lefts[move], rights[move]
        own = step_ref[4, step]
        near = []
        for n in range(3):
            cell = cell_ref[(place_x * along + place_y + n) * planes + plane]
            right[:, n * slots : (n + 1) * slots] = cell
            right[:, (3 + n) * slots : (4 + n) * slots] = cell
            at = ext_ref[place_x, place_y + n, plane, channels : channels + 3, :]
            near.append((at[0:1] + float(move - 1), at[1:2] + float(n - 1), at[2:3] + shift_z))
        tile = 16
        for m in range(slots // tile):
            at = m * tile
            own_x = own_col_ref[own, 0, at : at + tile, :]
            own_y = own_col_ref[own, 1, at : at + tile, :]
            own_z = own_col_ref[own, 2, at : at + tile, :]
            for n in range(3):
                dx = near[n][0] - own_x
                dy = near[n][1] - own_y
                dz = near[n][2] - own_z
                squared = dx * dx + dy * dy + dz * dz
                distance = squared * lax.rsqrt(jnp.maximum(squared, 1e-30))
                envelope = jnp.maximum(1.0 - squared, 0.0)
                term = envelope * envelope * jnp.exp2(squared * (-float((basis - 1) ** 2) * LOG2E))
                ratio = jnp.exp2(distance * (2.0 * (basis - 1) * LOG2E))
                if own_plane and move == 1 and n == 1:
                    i = lax.broadcasted_iota(jnp.int32, (tile, slots), 0) + at
                    j = lax.broadcasted_iota(jnp.int32, (tile, slots), 1)
                    same = jnp.logical_and(i == j, step_ref[3, step] == 0)
                    term = jnp.where(same, 0.0, term)
                for b in range(basis):
                    if b > 0:
                        term = term * ratio
                    high, low = split(term)
                    row = b * slots + at
                    left[row : row + tile, n * slots : (n + 1) * slots] = high
                    left[row : row + tile, (3 + n) * slots : (4 + n) * slots] = low

    def product(move):
        return lax.dot_general(
            lefts[move][...], rights[move][...], (((1,), (1,)), ((), ())), preferred_element_type=f32
        )

    def finish(own):
        gathered = acc_ref[:, :channels] + acc_ref[:, channels:]
        wide = jnp.concatenate([gathered[b * slots : (b + 1) * slots] for b in range(basis)], axis=1)
        high, low = split(wide)
        both = jnp.dot(high, mixed_ref[...], preferred_element_type=f32)
        both = both + jnp.dot(low, mixed_ref[...], preferred_element_type=f32)
        out_ref[own] = (both[:, :channels] + both[:, channels:]).T

    fill(0, 0)

    def visit(step, carry):
        fresh = step_ref[5, step] == 1
        acc_ref[...] = jnp.where(fresh, 0.0, acc_ref[...]) + product(0)
        fill(step, 1)
        acc_ref[...] += product(1)
        fill(step, 2)
        acc_ref[...] += product(2)
        fill(jnp.minimum(step + 1, count - 1), 0)

        @pl.when(step_ref[6, step] == 1)
        def _():
            finish(step_ref[4, step])

        return carry

    lax.fori_loop(0, count, visit, 0)


def pair_messages(steps, own_plane, own, ext, mix, w_value):
    cells, _, slots = own.shape
    basis, channels = mix.shape
    across, along, planes = ext.shape[:3]
    count = steps.shape[1]
    return pl.pallas_call(
        functools.partial(message_kernel, basis, own_plane),
        in_specs=[pl.BlockSpec(memory_space=pltpu.SMEM)] + [whole()] * 4,
        out_specs=whole(),
        scratch_shapes=[
            pltpu.VMEM((across * along * planes, 2 * channels, slots), bf16),
            pltpu.VMEM((cells, 3, slots, slots), f32),
            pltpu.VMEM((basis * slots, 2 * channels), f32),
            pltpu.VMEM((basis * channels, 2 * channels), bf16),
        ]
        + [pltpu.VMEM((basis * slots, 6 * slots), bf16)] * 3
        + [pltpu.VMEM((2 * channels, 6 * slots), bf16)] * 3,
        out_shape=jax.ShapeDtypeStruct((cells, channels, slots), f32),
        compiler_params=params(),
        cost_estimate=pl.CostEstimate(
            flops=count * 8 * basis * slots * 9 * slots * channels, bytes_accessed=1 << 20,
            transcendentals=0,
        ),
        name="messages",
    )(steps, own, ext, mix, w_value)
def visits(cells_x, cells_y, cells_z, inside):
    table = []
    for x in range(cells_x):
        for y in range(cells_y):
            for z in range(cells_z):
                own = (x * cells_y + y) * cells_z + z
                for shift in (-1, 0, 1):
                    plane = z + shift
                    if (0 <= plane < cells_z) != inside:
                        continue
                    if not inside:
                        plane = 0 if shift > 0 else 1
                    table.append([x, y, plane, shift, own, 1, 1])
    for one, after in zip(table, table[1:]):
        if one[4] == after[4]:
            one[6] = after[5] = 0
    return np.array(table, np.int32).T.copy()


def mlp_kernel(count, *refs):
    counts_ref, feature_ref = refs[:2]
    messages = refs[2:4]
    potentials = refs[4 : 4 + count]
    hidden_ref, back_ref, out_ref = refs[4 + count :]
    cells, channels, slots = feature_ref.shape
    columns = []
    for cell in range(cells):
        mixed = feature_ref[cell] + message_scale * (messages[0][cell] + messages[1][cell])
        for potential in potentials:
            mixed = mixed + potential[cell]
        columns.append(mixed)
    mixed = jnp.concatenate(columns, axis=1)
    inner = jnp.dot(hidden_ref[...].T, mixed, precision=HIGH, preferred_element_type=f32)
    hidden = inner * jax.nn.sigmoid(inner)
    updated = mixed + jnp.dot(back_ref[...].T, hidden, precision=HIGH, preferred_element_type=f32)
    slot = lax.broadcasted_iota(jnp.int32, (channels, slots), 1)
    for cell in range(cells):
        part = updated[:, cell * slots : (cell + 1) * slots]
        out_ref[cell] = jnp.where(slot < counts_ref[cell], part, 0.0)


def atom_mlp(counts, features, messages, potentials, w_hidden, w_out):
    return pl.pallas_call(
        functools.partial(mlp_kernel, len(potentials)),
        in_specs=[pl.BlockSpec(memory_space=pltpu.SMEM)]
        + [whole()] * (5 + len(potentials)),
        out_specs=whole(),
        out_shape=jax.ShapeDtypeStruct(features.shape, f32),
        compiler_params=params(),
        name="atom_mlp",
    )(counts, features, *messages, *potentials, w_hidden, w_out)


def with_x(block):
    below, above = below_above(block[:1], block[-1:], "gx")
    return jnp.concatenate([below, block, above], axis=0)


def shards(
    features, positions, counts, waves, filter_table, w_value, w_charge, radial_mix, w_hidden, w_out
):
    cells_x, cells_y, cells_z, channels, slots = features.shape
    basis = radial_mix.shape[0]
    total_waves = waves.shape[1]
    size_x, size_y, size_z = (lax.axis_size(a) for a in ("gx", "gy", "gz"))
    at_x, at_y, at_z = (lax.axis_index(a) for a in ("gx", "gy", "gz"))
    grid = (cells_x * size_x, cells_y * size_y, cells_z * size_z)
    cells = cells_x * cells_y * cells_z
    flat_counts = counts.reshape(cells)
    flat_features = features.reshape(cells, channels, slots)

    offsets = np.array(
        [(x, y, z) for x in range(cells_x) for y in range(cells_y) for z in range(cells_z)], np.int32
    )
    base = jnp.stack([at_x * cells_x, at_y * cells_y, at_z * cells_z]).astype(jnp.int32)
    own = pack(
        grid, (base + offsets).reshape(-1), flat_counts, flat_features,
        positions.reshape(cells, 3, slots),
    )
    rows = own.shape[1]
    packed = own.reshape(cells_x, cells_y, cells_z, rows, slots)

    gathered = [own] + [exchange(own, "gy", s) for s in range(1, size_y)]
    sides = neighbours(packed[:, :, :1], packed[:, :, -1:], "gz", same=cells_z == 1)

    share = total_waves // size_y
    own_waves = lax.dynamic_slice_in_dim(waves, at_y * share, share, 1).astype(f32).T
    parts, tables = (), []
    for block in gathered:
        *parts, table = partial_factors(at_x.reshape(1), own_waves, block, parts, size_x)
        tables.append(table)

    half = 2 * share // size_x
    summed = parts[0]
    for s in range(1, size_x):
        other = partner(at_x, s, size_x)
        to = parts[1]
        for n in range(2, size_x):
            to = jnp.where(lax.rem(other - at_x + size_x, size_x) == n, parts[n], to)
        summed = summed + exchange(to, "gx", s)
    piece = half // size_z
    pieces = [lax.dynamic_slice_in_dim(summed, at_z * piece, piece, 0)]
    for s in range(1, size_z):
        other = partner(at_z, s, size_z)
        pieces.append(exchange(lax.dynamic_slice_in_dim(summed, other * piece, piece, 0), "gz", s))
    scale = 1.0 / math.sqrt(grid[0] * grid[1] * grid[2] * slots) / math.sqrt(total_waves)
    chunk = math.gcd(share // size_x, 128)
    table = lax.dynamic_slice_in_dim(filter_table, at_y * share, share, 0) * scale
    table = jnp.broadcast_to(
        table.reshape(share // chunk, 1, chunk, channels), (share // chunk, 2, chunk, channels)
    ).reshape(2 * share, channels)
    table = lax.dynamic_slice_in_dim(table, at_x * half + at_z * piece, piece, 0)
    filtered = filtered_piece(pieces, w_charge, table)

    held_z = jnp.concatenate(
        [filtered] + [exchange(filtered, "gz", s) for s in range(1, size_z)], axis=0
    )
    held = [held_z] + [exchange(held_z, "gx", s) for s in range(1, size_x)]
    ranks_x = [at_x] + [partner(at_x, s, size_x) for s in range(1, size_x)]
    ranks_z = [at_z] + [partner(at_z, s, size_z) for s in range(1, size_z)]
    index = jnp.stack([x * size_z + z for x in ranks_x for z in ranks_z]).astype(jnp.int32)

    def of_y(rank, edge):
        found = None
        for s in range(size_y):
            source = at_y if s == 0 else partner(at_y, s, size_y)
            possible = any(
                (i if s == 0 else partner(i, s, size_y)) == (i + rank) % size_y for i in range(size_y)
            )
            if not possible:
                continue
            block = gathered[s].reshape(packed.shape)[:, edge]
            wanted = source == lax.rem(at_y + rank + size_y, size_y)
            found = block if found is None else jnp.where(wanted, block, found)
        return found

    plane = with_x(jnp.concatenate([of_y(-1, slice(-1, None)), packed, of_y(1, slice(0, 1))], axis=1))
    low, high = (
        jnp.concatenate([side[:, edge] for side in sides], axis=2)
        for edge in (slice(0, 1), slice(-1, None))
    )
    low, high, filtered = lax.optimization_barrier((low, high, filtered))
    below, above = below_above(low, high, "gy")
    around = with_x(jnp.concatenate([below, jnp.concatenate(sides, axis=2), above], axis=1))

    mix = radial_mix * np.exp(-np.arange(basis, dtype=np.float64) ** 2).astype(np.float32)[:, None]
    inner = jnp.asarray(visits(cells_x, cells_y, cells_z, True))
    outer = jnp.asarray(visits(cells_x, cells_y, cells_z, False))
    outer = outer.at[2].set(jnp.where(is_even("gz"), outer[2], 1 - outer[2]))
    near = pair_messages(inner, True, own, plane, mix, w_value)
    far = pair_messages(outer, False, own, around, mix, w_value)

    found = potentials_of(index, held, held_z.shape[0] // piece, tables, cells, slots)
    returned = [found[0]] + [exchange(found[s], "gy", s) for s in range(1, size_y)]

    updated = atom_mlp(flat_counts, flat_features, [near, far], returned, w_hidden, w_out)
    return updated.reshape(features.shape)


def solution(mesh):
    placed = (
        P("gx", "gy", "gz", None, None),
        P("gx", "gy", "gz", None, None),
        P("gx", "gy", "gz"),
        P(),
        P(),
        P(),
        P(),
        P(),
        P(),
        P(),
    )
    return jax.shard_map(
        shards,
        mesh=mesh,
        in_specs=placed,
        out_specs=P("gx", "gy", "gz", None, None),
        check_vma=False,
    )
```

time: 512 us -> 101 us (0.20); the launches traced: 502 us -> 101 us
  matrix products: 205 us -> 0 us
  waiting for transfers between devices: 128 us -> 11.5 us
  local copies, waits for them, and re-layouts: 100 us -> 8.8 us
  Pallas kernels: 0 us -> 48.1 us
  other arithmetic: 45.6 us -> 6.1 us
  starting transfers between devices: 8.31 us -> 25.9 us
  between operations: 13.6 us -> 0.46 us
    dot_general x35 -> x0, matrix products: 205 us -> none  [the longest x27 122 us: pair_term(): jnp.einsum('...bij,...bcj->...ci', kernel, weighted, precision=highest)]
    ppermute x6 -> x22, waiting for transfers between devices: 75.7 us -> 11.5 us  [the longest x14 8.42 us: exchange(): return lax.ppermute(block, axis, pairs)]
    psum x1 -> x0, waiting for transfers between devices: 52.6 us -> none  [shards(): owned_share = lax.psum(owned_share, ('gx', 'gy'))]
    mul x28 -> x0, local copies, waits for them, and re-layouts: 50.4 us -> none  [the longest x27 49.5 us: pair_term(): weighted = radial_mix[:, :, None] * nearby[..., None, :channels, :]]
    pallas_call x0 -> x10, Pallas kernels: none -> 48.1 us  [the longest x2 30.3 us: pair_messages(): pl.pallas_call(functools.partial(message_kernel, basis, own_plane), in_sp...]
    while x109 -> x0, local copies, waits for them, and re-layouts: 44.2 us -> none
    sqrt x27 -> x0, other arithmetic: 23.9 us -> none  [radial_kernel(): distance = jnp.sqrt(squared)]
    ppermute x6 -> x22, starting transfers between devices: 8.23 us -> 25.9 us  [the longest x14 17.2 us: exchange(): return lax.ppermute(block, axis, pairs)]
  transfers between devices with their start and end apart: 9 -> 22, of which waited for: 7 -> 6; matrix products, arithmetic and copies ran while one was open for 43% -> 7% of each run, Pallas kernels for 0% -> 45%
where the time goes in v2:
time: 101 us
  Pallas kernels  48.1 us (48%)
  starting transfers between devices  25.9 us (26%)
  waiting for transfers between devices  11.5 us (11%)
  local copies, waits for them, and re-layouts  8.8 us (9%)
  other arithmetic  6.1 us (6%)
    pallas_call x2, Pallas kernels, pair_messages(): pl.pallas_call(functools.partial(message_kernel, basis, own_plane), in_sp...  30.3 us
    ppermute x14, starting transfers between devices, exchange(): return lax.ppermute(block, axis, pairs)  17.2 us
    pallas_call x4, Pallas kernels, partial_factors(): pl.pallas_call(functools.partial(factor_kernel, parts, chunk, not before)...  12.6 us
    ppermute x8, starting transfers between devices, neighbours(): return (lax.ppermute(first, axis, one), lax.ppermute(second, axis, two))  8.75 us
    ppermute x14, waiting for transfers between devices, exchange(): return lax.ppermute(block, axis, pairs)  8.42 us
    unnamed x40, local copies, waits for them, and re-layouts  5.83 us
    ppermute x8, waiting for transfers between devices, neighbours(): return (lax.ppermute(first, axis, one), lax.ppermute(second, axis, two))  3.13 us
    pallas_call x1, Pallas kernels, potentials_of(): pl.pallas_call(functools.partial(potential_kernel, len(held), pieces, len...  2.44 us
  transfers between devices with their start and end apart: 22, of which 6 were waited for; matrix products, arithmetic and copies ran while one was open for 7% of the time, Pallas kernels for 45%

profile of v2, /device:TPU:0, one launch (start us, length us, event | category | flops | bytes accessed | tf_op | source)
XLA Modules:
  0.0 100.9 jit_solution(4593509996958419443)
XLA Ops:
  0.0 0.1 pad_add_fusion
  0.1 0.7 broadcast_add_fusion
  0.8 0.1 reshape.65.place_ref
  0.9 0.5 broadcast.28
  1.4 1.3 %reduce.5 = s32[2,2]{1,0:T(2,128)S(1)} reduce(s32[2,2,1]{1,2,0:T(1,128)} %param.18, s32[]{:T(128)} %broadcast.28), dimensions={2}, to_apply=%param.18.reduce_sub_computation.3 | reduce | bytes 36 | tf_op args[2]
  2.7 0.1 reshape.63.counts_ref.refs_0_
  2.8 0.7 copy.17
  3.5 0.9 copy-done.1
  4.4 0.6 pack.1.own_ref.block_ref
  5.0 3.0 %collective-permute-start.1 = (f32[4,136,128]{2,1,0:T(8,128)S(1)}, f32[4,136,128]{2,1,0:T(8,128)S(1)}, u32[]{:S(2)}, u32[]{:S(2)}) collective-permute-start(f32[4,136,128]{2,1,0:T(8,128)S(1)} %pack.1.own_ref.block_ref), channel_id=1, source_target_pairs={{0,4},{4,0},{8,12},{12,8},{1,5},{5,1},{9,13},{13,9},{2,6},{6,2},{1... | collective-permute-start | bytes 835592 | tf_op jit(solution)/shard_map/ppermute | solution.py:31
  8.0 1.5 %collective-permute-start.6 = (f32[4,136,128]{2,1,0:T(8,128)S(1)}, f32[4,136,128]{2,1,0:T(8,128)S(1)}, u32[]{:S(2)}, u32[]{:S(2)}) collective-permute-start(f32[4,136,128]{2,1,0:T(8,128)S(1)} %pack.1.own_ref.block_ref), channel_id=1, source_target_pairs={{0,8},{4,12},{8,0},{12,4},{1,9},{5,13},{9,1},{13,5},{2,10},{6,14},... | collective-permute-start | bytes 835592 | tf_op jit(solution)/shard_map/ppermute | solution.py:31
  9.6 0.0 collective-permute-start
  9.6 2.0 %collective-permute-start.4 = (f32[2,2,1,136,128]{4,3,2,1,0:T(8,128)S(1)}, f32[2,2,1,136,128]{4,3,2,1,0:T(8,128)}, u32[]{:S(2)}, u32[]{:S(2)}) collective-permute-start(f32[2,2,1,136,128]{4,3,2,1,0:T(8,128)S(1)} %bitcast.25), channel_id=1, source_target_pairs={{0,1},{1,0},{2,3},{3,2},{4,5},{5,4},{6,7},{7,6},{8,9},{9,8},{10,11... | collective-permute-start | bytes 835592 | tf_op jit(solution)/shard_map/ppermute | solution.py:53
  11.6 2.5 %collective-permute-start.5 = (f32[2,2,1,136,128]{4,3,2,1,0:T(8,128)S(1)}, f32[2,2,1,136,128]{4,3,2,1,0:T(8,128)}, u32[]{:S(2)}, u32[]{:S(2)}) collective-permute-start(f32[2,2,1,136,128]{4,3,2,1,0:T(8,128)S(1)} %bitcast.26), channel_id=1, source_target_pairs={{0,3},{1,2},{2,1},{3,0},{4,7},{5,6},{6,5},{7,4},{8,11},{9,10},{10,... | collective-permute-start | bytes 835592 | tf_op jit(solution)/shard_map/ppermute | solution.py:53
  14.1 0.1 copy.21
  14.3 1.0 dynamic-slice_multiply_fusion
  15.3 0.0 copy-start.14
  15.3 0.0 copy-start.15
  15.4 0.6 constant_dynamic-slice_fusion.refs_5_
  16.0 3.1 %factors.4 = (f32[512,128]{1,0:T(8,128)S(1)}, f32[512,128]{1,0:T(8,128)S(1)}, bf16[1024,1024]{1,0:T(8,128)(2,1)S(1)}) custom-call(s32[1]{0:T(128)} %bitcast.8.at_ref, f32[512,3]{1,0:T(8,128)S(1)} %convert_bitcast_fusion.waves_ref, f32[4,136,128]{2,1,0:T(8,128)S(1)} %pack.1.own_ref.block_ref), custom_call_target="tpu_custom_call" | custom-call | flops 268435456 | bytes 2097152 | tf_op jit(solution)/shard_map/factors/pallas_call | solution.py:188
  19.2 0.7 copy-done.4
  19.9 0.7 copy-done.6
  20.6 0.1 stack.51.index_ref
  20.7 0.1 broadcast_multiply_fusion.mix_ref
  20.8 1.0 copy-done.5
  21.7 0.9 copy-done.7
  22.7 3.1 %factors.5 = (f32[512,128]{1,0:T(8,128)S(1)}, f32[512,128]{1,0:T(8,128)S(1)}, bf16[1024,1024]{1,0:T(8,128)(2,1)S(1)}) custom-call(s32[1]{0:T(128)} %bitcast.8.at_ref, f32[512,3]{1,0:T(8,128)S(1)} %convert_bitcast_fusion.waves_ref, f32[4,136,128]{2,1,0:T(8,128)S(1)} %collective-permute-done.1.block_ref, f32[512,128]{1,0:T(8,128)S(1)} %copy-done.5, ...), custom_call_target="tpu_custom_call" | custom-call | flops 268435456 | bytes 2097152 | tf_op jit(solution)/shard_map/factors/pallas_call | solution.py:188
  25.8 3.2 %factors.6 = (f32[512,128]{1,0:T(8,128)S(1)}, f32[512,128]{1,0:T(8,128)S(1)}, bf16[1024,1024]{1,0:T(8,128)(2,1)S(1)}) custom-call(s32[1]{0:T(128)} %bitcast.8.at_ref, f32[512,3]{1,0:T(8,128)S(1)} %convert_bitcast_fusion.waves_ref, f32[4,136,128]{2,1,0:T(8,128)S(1)} %collective-permute-done.6.block_ref, f32[512,128]{1,0:T(8,128)S(1)} %get-tuple-element.37.refs_0_, ...), custom_call_target="tpu_custom_call" | custom-call | flops 268435456 | bytes 2097152 | tf_op jit(solution)/shard_map/factors/pallas_call | solution.py:188
  29.0 3.2 %factors.7 = (f32[512,128]{1,0:T(8,128)S(1)}, f32[512,128]{1,0:T(8,128)S(1)}, bf16[1024,1024]{1,0:T(8,128)(2,1)S(1)}) custom-call(s32[1]{0:T(128)} %bitcast.8.at_ref, f32[512,3]{1,0:T(8,128)S(1)} %convert_bitcast_fusion.waves_ref, f32[4,136,128]{2,1,0:T(8,128)S(1)} %collective-permute-done.block_ref, f32[512,128]{1,0:T(8,128)S(1)} %get-tuple-element.39.refs_0_, ...), custom_call_target="tpu_custom_call" | custom-call | flops 268435456 | bytes 2097152 | tf_op jit(solution)/shard_map/factors/pallas_call | solution.py:188
  32.2 0.1 collective-permute-start.7
  32.4 0.6 collective-permute-start.2
  32.9 0.1 collective-permute-start.3
  33.0 1.0 fusion
  34.0 1.0 fusion.1
  35.1 1.4 %collective-permute-start.10 = (f32[128,128]{1,0:T(8,128)S(1)}, f32[128,128]{1,0:T(8,128)S(1)}, u32[]{:S(2)}, u32[]{:S(2)}) collective-permute-start(f32[128,128]{1,0:T(8,128)S(1)} %get-tuple-element.71), channel_id=1, source_target_pairs={{0,3},{1,2},{2,1},{3,0},{4,7},{5,6},{6,5},{7,4},{8,11},{9,10},{10,... | collective-permute-start | bytes 196616 | tf_op jit(solution)/shard_map/ppermute | solution.py:31
  36.6 3.0 %collective-permute-start.9 = (f32[128,128]{1,0:T(8,128)S(1)}, f32[128,128]{1,0:T(8,128)S(1)}, u32[]{:S(2)}, u32[]{:S(2)}) collective-permute-start(f32[128,128]{1,0:T(8,128)S(1)} %get-tuple-element.72), channel_id=1, source_target_pairs={{0,2},{1,3},{2,0},{3,1},{4,6},{5,7},{6,4},{7,5},{8,10},{9,11},{10,... | collective-permute-start | bytes 196616 | tf_op jit(solution)/shard_map/ppermute | solution.py:31
  39.6 2.3 %collective-permute-done.10.refs_3_ = f32[128,128]{1,0:T(8,128)S(1)} collective-permute-done((f32[128,128]{1,0:T(8,128)S(1)}, f32[128,128]{1,0:T(8,128)S(1)}, u32[]{:S(2)}, u32[]{:S(2)}) %collective-permute-start.10) | collective-permute-done | bytes 65568 | tf_op jit(solution)/shard_map/ppermute | solution.py:31
  42.0 1.6 %collective-permute-done.8.refs_1_ = f32[128,128]{1,0:T(8,128)S(1)} collective-permute-done((f32[128,128]{1,0:T(8,128)S(1)}, f32[128,128]{1,0:T(8,128)S(1)}, u32[]{:S(2)}, u32[]{:S(2)}) %collective-permute-start.8) | collective-permute-done | bytes 65568 | tf_op jit(solution)/shard_map/ppermute | solution.py:31
  43.6 0.2 filter.1
  43.8 2.5 %collective-permute-start.11 = (f32[2,1,2,136,128]{4,3,2,1,0:T(8,128)S(1)}, f32[2,1,2,136,128]{4,3,2,1,0:T(8,128)S(1)}, u32[]{:S(2)}, u32[]{:S(2)}) collective-permute-start(f32[2,1,2,136,128]{4,3,2,1,0:T(8,128)S(1)} %get-tuple-element.59), channel_id=1, source_target_pairs={{0,12},{4,8},{8,4},{12,0},{1,13},{5,9},{9,5},{13,1},{2,14},{6,10},... | collective-permute-start | bytes 835592 | tf_op jit(solution)/shard_map/ppermute | solution.py:53
  46.3 0.5 collective-permute-start.12
  46.9 1.4 %collective-permute-start.15 = (f32[128,128]{1,0:T(8,128)S(1)}, f32[128,128]{1,0:T(8,128)S(1)}, u32[]{:S(2)}, u32[]{:S(2)}) collective-permute-start(f32[128,128]{1,0:T(8,128)S(1)} %filter.1), channel_id=1, source_target_pairs={{0,1},{1,0},{2,3},{3,2},{4,5},{5,4},{6,7},{7,6},{8,9},{9,8},{10,11... | collective-permute-start | bytes 196616 | tf_op jit(solution)/shard_map/ppermute | solution.py:31
  48.3 1.5 %collective-permute-start.16 = (f32[128,128]{1,0:T(8,128)S(1)}, f32[128,128]{1,0:T(8,128)S(1)}, u32[]{:S(2)}, u32[]{:S(2)}) collective-permute-start(f32[128,128]{1,0:T(8,128)S(1)} %filter.1), channel_id=1, source_target_pairs={{0,2},{1,3},{2,0},{3,1},{4,6},{5,7},{6,4},{7,5},{8,10},{9,11},{10,... | collective-permute-start | bytes 196616 | tf_op jit(solution)/shard_map/ppermute | solution.py:31
  49.7 1.6 %collective-permute-start.17 = (f32[128,128]{1,0:T(8,128)S(1)}, f32[128,128]{1,0:T(8,128)S(1)}, u32[]{:S(2)}, u32[]{:S(2)}) collective-permute-start(f32[128,128]{1,0:T(8,128)S(1)} %filter.1), channel_id=1, source_target_pairs={{0,3},{1,2},{2,1},{3,0},{4,7},{5,6},{6,5},{7,4},{8,11},{9,10},{10,... | collective-permute-start | bytes 196616 | tf_op jit(solution)/shard_map/ppermute | solution.py:31
  51.3 0.1 pad_maximum_fusion.1.ext_ref
  51.4 0.5 collective-permute-done.15
  51.9 2.9 %collective-permute-done.16 = f32[128,128]{1,0:T(8,128)S(1)} collective-permute-done((f32[128,128]{1,0:T(8,128)S(1)}, f32[128,128]{1,0:T(8,128)S(1)}, u32[]{:S(2)}, u32[]{:S(2)}) %collective-permute-start.16) | collective-permute-done | bytes 65568 | tf_op jit(solution)/shard_map/ppermute | solution.py:31
  54.8 1.1 %collective-permute-done.17 = f32[128,128]{1,0:T(8,128)S(1)} collective-permute-done((f32[128,128]{1,0:T(8,128)S(1)}, f32[128,128]{1,0:T(8,128)S(1)}, u32[]{:S(2)}, u32[]{:S(2)}) %collective-permute-start.17) | collective-permute-done | bytes 65568 | tf_op jit(solution)/shard_map/ppermute | solution.py:31
  55.9 0.1 collective-permute-start.18
  56.0 3.1 %collective-permute-done.12 = f32[2,1,2,136,128]{4,3,2,1,0:T(8,128)S(1)} collective-permute-done((f32[2,1,2,136,128]{4,3,2,1,0:T(8,128)S(1)}, f32[2,1,2,136,128]{4,3,2,1,0:T(8,128)S(1)}, u32[]{:S(2)}, u32[]{:S(2)}) %collective-permute-start.12) | collective-permute-done | bytes 278560 | tf_op jit(solution)/shard_map/ppermute | solution.py:53
  59.2 1.1 %pad_maximum_fusion.2 = f32[2,4,2,136,128]{4,3,2,1,0:T(8,128)S(1)} fusion(f32[2,1,2,136,128]{4,3,2,1,0:T(8,128)S(1)} %get-tuple-element.58, f32[2,2,1,136,128]{4,3,2,1,0:T(8,128)} %collective-permute-done.5, f32[2,2,1,136,128]{4,3,2,1,0:T(8,128)} %collective-permute-done.4, f32[2,1,2,136,128]{4,3,2,1,0:T(8,128)S(1)} %get-tuple-element.57), kind=kLoop, calls=%fused_computation.2 | loop fusion | flops 835584 | bytes 2228224 | tf_op jit(solution)/shard_map/concatenate | solution.py:539
  60.3 0.1 slice_select_fusion.1
  60.4 0.1 collective-permute-start.13
  60.5 0.5 collective-permute-start.14
  61.0 0.2 copy-done.11
  61.2 11.1 %messages.2.refs_2_ = f32[4,128,128]{2,1,0:T(8,128)S(1)} custom-call(s32[7,4]{1,0:T(8,128)S(1)} %copy-done.12, f32[4,136,128]{2,1,0:T(8,128)S(1)} %pack.1.own_ref.block_ref, f32[4,4,1,136,128]{4,3,2,1,0:T(8,128)S(1)} %pad_maximum_fusion.1.ext_ref, f32[8,128]{1,0:T(8,128)S(1)} %broadcast_multiply_fusion.mix_ref, f32[128,128]{1,0:T(8,128)S(1)} %copy-done.11), custom_call_target="tpu_custom_call" | custom-call | flops 4831838208 | bytes 1048576 | tf_op jit(solution)/shard_map/messages/pallas_call | solution.py:376
  72.3 2.4 %potentials.1 = (f32[4,128,128]{2,1,0:T(8,128)S(1)}, f32[4,128,128]{2,1,0:T(8,128)S(1)}, f32[4,128,128]{2,1,0:T(8,128)S(1)}, f32[4,128,128]{2,1,0:T(8,128)S(1)}) custom-call(s32[8]{0:T(128)S(1)} %stack.51.index_ref, f32[512,128]{1,0:T(8,128)S(1)} %pad_maximum_fusion.6.refs_0_, f32[512,128]{1,0:T(8,128)S(1)} %collective-permute-done.18.refs_1_, ...), custom_call_target="tpu_custom_call" | custom-call | flops 1610612736 | bytes 8388608 | tf_op jit(solution)/shard_map/potentials/pallas_call | solution.py:249
  74.7 1.6 %collective-permute-start.19 = (f32[4,128,128]{2,1,0:T(8,128)S(1)}, f32[4,128,128]{2,1,0:T(8,128)S(1)}, u32[]{:S(2)}, u32[]{:S(2)}) collective-permute-start(f32[4,128,128]{2,1,0:T(8,128)S(1)} %get-tuple-element.50), channel_id=1, source_target_pairs={{0,4},{4,0},{8,12},{12,8},{1,5},{5,1},{9,13},{13,9},{2,6},{6,2},{1... | collective-permute-start | bytes 786440 | tf_op jit(solution)/shard_map/ppermute | solution.py:31
  76.3 0.5 collective-permute-start.20
  76.8 1.5 %collective-permute-start.21 = (f32[4,128,128]{2,1,0:T(8,128)S(1)}, f32[4,128,128]{2,1,0:T(8,128)S(1)}, u32[]{:S(2)}, u32[]{:S(2)}) collective-permute-start(f32[4,128,128]{2,1,0:T(8,128)S(1)} %get-tuple-element.52), channel_id=1, source_target_pairs={{0,12},{4,8},{8,4},{12,0},{1,13},{5,9},{9,5},{13,1},{2,14},{6,10},... | collective-permute-start | bytes 786440 | tf_op jit(solution)/shard_map/ppermute | solution.py:31
  78.3 0.1 broadcast_select_fusion.1
  78.4 1.2 %pad_maximum_fusion.ext_ref = f32[4,4,2,136,128]{4,3,2,1,0:T(8,128)S(1)} fusion(f32[1,4,2,136,128]{4,3,2,1,0:T(8,128)S(1)} %get-tuple-element.54, f32[2,1,2,136,128]{4,3,2,1,0:T(8,128)S(1)} %get-tuple-element.58, f32[2,2,1,136,128]{4,3,2,1,0:T(8,128)} %collective-permute-done.5, f32[2,2,1,136,128]{4,3,2,1,0:T(8,128)} %collective-permute-done.4, ...), kind=kLoop, calls=%fused_computation | loop fusion | flops 2785280 | bytes 4456448 | tf_op jit(solution)/shard_map/concatenate | solution.py:451
  79.6 19.2 %messages.3.refs_3_ = f32[4,128,128]{2,1,0:T(8,128)S(1)} custom-call(s32[7,8]{1,0:T(8,128)S(1)} %scatter.4.step_ref, f32[4,136,128]{2,1,0:T(8,128)S(1)} %pack.1.own_ref.block_ref, f32[4,4,2,136,128]{4,3,2,1,0:T(8,128)S(1)} %pad_maximum_fusion.ext_ref, f32[8,128]{1,0:T(8,128)S(1)} %broadcast_multiply_fusion.mix_ref, f32[128,128]{1,0:T(8,128)S(1)} %copy-done.11), custom_call_target="tpu_custom_call" | custom-call | flops 9663676416 | bytes 1048576 | tf_op jit(solution)/shard_map/messages/pallas_call | solution.py:376
  98.9 2.0 %atom_mlp.1 = f32[4,128,128]{2,1,0:T(8,128)} custom-call(s32[4]{0:T(128)S(1)} %reshape.63.counts_ref.refs_0_, f32[4,128,128]{2,1,0:T(8,128)S(1)} %bitcast.32, f32[4,128,128]{2,1,0:T(8,128)S(1)} %messages.2.refs_2_, f32[4,128,128]{2,1,0:T(8,128)S(1)} %messages.3.refs_3_, f32[4,128,128]{2,1,0:T(8,128)S(1)} %get-tuple-element.49.refs_4_, ...), custom_call_target="tpu_custom_call" | custom-call | tf_op jit(solution)/shard_map/atom_mlp/pallas_call | solution.py:438
  (62 shorter events, 0.6 us)
Async XLA Ops:
  0.0 14.1 %copy-start = (s32[3,2048]{1,0:T(4,128)S(1)}, s32[3,2048]{1,0:T(4,128)}, u32[]{:S(2)}) copy-start(s32[3,2048]{1,0:T(4,128)} %param.19) | copy-start | bytes 73732
  0.0 15.3 %copy-start.16 = (s32[1,8]{1,0:T(1,128)S(1)}, s32[1,8]{1,0:T(1,128)}, u32[]{:S(2)}) copy-start(s32[1,8]{1,0:T(1,128)} %constant.91) | copy-start | bytes 100
  0.0 15.3 %copy-start.17 = (s32[1,8]{1,0:T(1,128)S(1)}, s32[1,8]{1,0:T(1,128)}, u32[]{:S(2)}) copy-start(s32[1,8]{1,0:T(1,128)} %constant.92) | copy-start | bytes 100
  3.5 0.9 copy-start.1
  5.0 15.7 %collective-permute-start.1 = (f32[4,136,128]{2,1,0:T(8,128)S(1)}, f32[4,136,128]{2,1,0:T(8,128)S(1)}, u32[]{:S(2)}, u32[]{:S(2)}) collective-permute-start(f32[4,136,128]{2,1,0:T(8,128)S(1)} %pack.1.own_ref.block_ref), channel_id=1, source_target_pairs={{0,4},{4,0},{8,12},{12,8},{1,5},{5,1},{9,13},{13,9},{2,6},{6,2},{1... | collective-permute-start | bytes 835592 | tf_op jit(solution)/shard_map/ppermute | solution.py:31
  8.0 17.8 %collective-permute-start.6 = (f32[4,136,128]{2,1,0:T(8,128)S(1)}, f32[4,136,128]{2,1,0:T(8,128)S(1)}, u32[]{:S(2)}, u32[]{:S(2)}) collective-permute-start(f32[4,136,128]{2,1,0:T(8,128)S(1)} %pack.1.own_ref.block_ref), channel_id=1, source_target_pairs={{0,8},{4,12},{8,0},{12,4},{1,9},{5,13},{9,1},{13,5},{2,10},{6,14},... | collective-permute-start | bytes 835592 | tf_op jit(solution)/shard_map/ppermute | solution.py:31
  9.6 19.4 %collective-permute-start = (f32[4,136,128]{2,1,0:T(8,128)S(1)}, f32[4,136,128]{2,1,0:T(8,128)S(1)}, u32[]{:S(2)}, u32[]{:S(2)}) collective-permute-start(f32[4,136,128]{2,1,0:T(8,128)S(1)} %pack.1.own_ref.block_ref), channel_id=1, source_target_pairs={{0,12},{4,8},{8,4},{12,0},{1,13},{5,9},{9,5},{13,1},{2,14},{6,10},... | collective-permute-start | bytes 835592 | tf_op jit(solution)/shard_map/ppermute | solution.py:31
  9.6 23.4 %collective-permute-start.4 = (f32[2,2,1,136,128]{4,3,2,1,0:T(8,128)S(1)}, f32[2,2,1,136,128]{4,3,2,1,0:T(8,128)}, u32[]{:S(2)}, u32[]{:S(2)}) collective-permute-start(f32[2,2,1,136,128]{4,3,2,1,0:T(8,128)S(1)} %bitcast.25), channel_id=1, source_target_pairs={{0,1},{1,0},{2,3},{3,2},{4,5},{5,4},{6,7},{7,6},{8,9},{9,8},{10,11... | collective-permute-start | bytes 835592 | tf_op jit(solution)/shard_map/ppermute | solution.py:53
  11.6 22.4 %collective-permute-start.5 = (f32[2,2,1,136,128]{4,3,2,1,0:T(8,128)S(1)}, f32[2,2,1,136,128]{4,3,2,1,0:T(8,128)}, u32[]{:S(2)}, u32[]{:S(2)}) collective-permute-start(f32[2,2,1,136,128]{4,3,2,1,0:T(8,128)S(1)} %bitcast.26), channel_id=1, source_target_pairs={{0,3},{1,2},{2,1},{3,0},{4,7},{5,6},{6,5},{7,4},{8,11},{9,10},{10,... | collective-permute-start | bytes 835592 | tf_op jit(solution)/shard_map/ppermute | solution.py:53
  15.3 5.3 %copy-start.14 = (s32[7,8]{1,0:T(8,128)S(1)}, s32[7,8]{1,0:T(8,128)}, u32[]{:S(2)}) copy-start(s32[7,8]{1,0:T(8,128)} %constant.86.clone) | copy-start | bytes 676
  15.3 5.4 %copy-start.13 = (f32[8,128]{1,0:T(8,128)S(1)}, f32[8,128]{1,0:T(8,128)}, u32[]{:S(2)}) copy-start(f32[8,128]{1,0:T(8,128)} %param.23) | copy-start | bytes 12292
  15.3 5.4 %copy-start.15 = (f32[8]{0:T(128)S(1)}, f32[8]{0:T(128)}, u32[]{:S(2)}) copy-start(f32[8]{0:T(128)} %constant.90) | copy-start | bytes 100
  19.1 0.7 copy-start.4
  19.9 0.7 copy-start.6
  20.7 1.0 copy-start.5
  21.7 0.9 copy-start.7
  32.2 2.9 %collective-permute-start.7 = (f32[512,128]{1,0:T(8,128)S(1)}, f32[512,128]{1,0:T(8,128)S(1)}, u32[]{:S(2)}, u32[]{:S(2)}) collective-permute-start(f32[512,128]{1,0:T(8,128)S(1)} %get-tuple-element.42), channel_id=1, source_target_pairs={{0,16},{16,0},{1,17},{17,1},{2,18},{18,2},{3,19},{19,3},{4,20},{20... | collective-permute-start | bytes 786440 | tf_op jit(solution)/shard_map/ppermute | solution.py:31
  32.4 14.5 %collective-permute-start.2 = (f32[1,4,1,136,128]{4,3,2,1,0:T(8,128)S(1)}, f32[1,4,1,136,128]{4,3,2,1,0:T(8,128)S(1)}, u32[]{:S(2)}, u32[]{:S(2)}) collective-permute-start(f32[1,4,1,136,128]{4,3,2,1,0:T(8,128)S(1)} %get-tuple-element.63), channel_id=1, source_target_pairs={{0,16},{16,0},{1,17},{17,1},{2,18},{18,2},{3,19},{19,3},{4,20},{20... | collective-permute-start | bytes 835592 | tf_op jit(solution)/shard_map/ppermute | solution.py:53
  32.9 13.9 %collective-permute-start.3 = (f32[1,4,1,136,128]{4,3,2,1,0:T(8,128)S(1)}, f32[1,4,1,136,128]{4,3,2,1,0:T(8,128)S(1)}, u32[]{:S(2)}, u32[]{:S(2)}) collective-permute-start(f32[1,4,1,136,128]{4,3,2,1,0:T(8,128)S(1)} %get-tuple-element.64), channel_id=1, source_target_pairs={{0,16},{16,0},{1,17},{17,1},{2,18},{18,2},{3,19},{19,3},{4,20},{20... | collective-permute-start | bytes 835592 | tf_op jit(solution)/shard_map/ppermute | solution.py:53
  35.0 8.5 %copy-start.3 = (f32[128,128]{1,0:T(8,128)S(1)}, f32[128,128]{1,0:T(8,128)}, u32[]{:S(2)}) copy-start(f32[128,128]{1,0:T(8,128)} %constant_dynamic-slice_fusion.refs_5_) | copy-start | bytes 196612
  35.1 8.5 %copy-start.10 = (f32[128,128]{1,0:T(8,128)S(1)}, f32[128,128]{1,0:T(8,128)}, u32[]{:S(2)}) copy-start(f32[128,128]{1,0:T(8,128)} %refs_4_.1) | copy-start | bytes 196612
  35.1 6.8 %collective-permute-start.10 = (f32[128,128]{1,0:T(8,128)S(1)}, f32[128,128]{1,0:T(8,128)S(1)}, u32[]{:S(2)}, u32[]{:S(2)}) collective-permute-start(f32[128,128]{1,0:T(8,128)S(1)} %get-tuple-element.71), channel_id=1, source_target_pairs={{0,3},{1,2},{2,1},{3,0},{4,7},{5,6},{6,5},{7,4},{8,11},{9,10},{10,... | collective-permute-start | bytes 196616 | tf_op jit(solution)/shard_map/ppermute | solution.py:31
  36.6 7.0 %collective-permute-start.8 = (f32[128,128]{1,0:T(8,128)S(1)}, f32[128,128]{1,0:T(8,128)S(1)}, u32[]{:S(2)}, u32[]{:S(2)}) collective-permute-start(f32[128,128]{1,0:T(8,128)S(1)} %get-tuple-element.73), channel_id=1, source_target_pairs={{0,1},{1,0},{2,3},{3,2},{4,5},{5,4},{6,7},{7,6},{8,9},{9,8},{10,11... | collective-permute-start | bytes 196616 | tf_op jit(solution)/shard_map/ppermute | solution.py:31
  36.6 7.0 %collective-permute-start.9 = (f32[128,128]{1,0:T(8,128)S(1)}, f32[128,128]{1,0:T(8,128)S(1)}, u32[]{:S(2)}, u32[]{:S(2)}) collective-permute-start(f32[128,128]{1,0:T(8,128)S(1)} %get-tuple-element.72), channel_id=1, source_target_pairs={{0,2},{1,3},{2,0},{3,1},{4,6},{5,7},{6,4},{7,5},{8,10},{9,11},{10,... | collective-permute-start | bytes 196616 | tf_op jit(solution)/shard_map/ppermute | solution.py:31
  43.8 12.2 %collective-permute-start.11 = (f32[2,1,2,136,128]{4,3,2,1,0:T(8,128)S(1)}, f32[2,1,2,136,128]{4,3,2,1,0:T(8,128)S(1)}, u32[]{:S(2)}, u32[]{:S(2)}) collective-permute-start(f32[2,1,2,136,128]{4,3,2,1,0:T(8,128)S(1)} %get-tuple-element.59), channel_id=1, source_target_pairs={{0,12},{4,8},{8,4},{12,0},{1,13},{5,9},{9,5},{13,1},{2,14},{6,10},... | collective-permute-start | bytes 835592 | tf_op jit(solution)/shard_map/ppermute | solution.py:53
  46.3 12.8 %collective-permute-start.12 = (f32[2,1,2,136,128]{4,3,2,1,0:T(8,128)S(1)}, f32[2,1,2,136,128]{4,3,2,1,0:T(8,128)S(1)}, u32[]{:S(2)}, u32[]{:S(2)}) collective-permute-start(f32[2,1,2,136,128]{4,3,2,1,0:T(8,128)S(1)} %get-tuple-element.60), channel_id=1, source_target_pairs={{0,4},{4,0},{8,12},{12,8},{1,5},{5,1},{9,13},{13,9},{2,6},{6,2},{1... | collective-permute-start | bytes 835592 | tf_op jit(solution)/shard_map/ppermute | solution.py:53
  46.9 5.0 %collective-permute-start.15 = (f32[128,128]{1,0:T(8,128)S(1)}, f32[128,128]{1,0:T(8,128)S(1)}, u32[]{:S(2)}, u32[]{:S(2)}) collective-permute-start(f32[128,128]{1,0:T(8,128)S(1)} %filter.1), channel_id=1, source_target_pairs={{0,1},{1,0},{2,3},{3,2},{4,5},{5,4},{6,7},{7,6},{8,9},{9,8},{10,11... | collective-permute-start | bytes 196616 | tf_op jit(solution)/shard_map/ppermute | solution.py:31
  48.3 6.6 %collective-permute-start.16 = (f32[128,128]{1,0:T(8,128)S(1)}, f32[128,128]{1,0:T(8,128)S(1)}, u32[]{:S(2)}, u32[]{:S(2)}) collective-permute-start(f32[128,128]{1,0:T(8,128)S(1)} %filter.1), channel_id=1, source_target_pairs={{0,2},{1,3},{2,0},{3,1},{4,6},{5,7},{6,4},{7,5},{8,10},{9,11},{10,... | collective-permute-start | bytes 196616 | tf_op jit(solution)/shard_map/ppermute | solution.py:31
  49.7 6.2 %collective-permute-start.17 = (f32[128,128]{1,0:T(8,128)S(1)}, f32[128,128]{1,0:T(8,128)S(1)}, u32[]{:S(2)}, u32[]{:S(2)}) collective-permute-start(f32[128,128]{1,0:T(8,128)S(1)} %filter.1), channel_id=1, source_target_pairs={{0,3},{1,2},{2,1},{3,0},{4,7},{5,6},{6,5},{7,4},{8,11},{9,10},{10,... | collective-permute-start | bytes 196616 | tf_op jit(solution)/shard_map/ppermute | solution.py:31
  55.9 16.3 %collective-permute-start.18 = (f32[512,128]{1,0:T(8,128)S(1)}, f32[512,128]{1,0:T(8,128)S(1)}, u32[]{:S(2)}, u32[]{:S(2)}) collective-permute-start(f32[512,128]{1,0:T(8,128)S(1)} %pad_maximum_fusion.6.refs_0_), channel_id=1, source_target_pairs={{0,16},{16,0},{1,17},{17,1},{2,18},{18,2},{3,19},{19,3},{4,20},{20... | collective-permute-start | bytes 786440 | tf_op jit(solution)/shard_map/ppermute | solution.py:31
  60.3 0.8 copy-start.11
  60.3 0.8 copy-start.12
  60.4 17.9 %collective-permute-start.13 = (f32[1,4,2,136,128]{4,3,2,1,0:T(8,128)S(1)}, f32[1,4,2,136,128]{4,3,2,1,0:T(8,128)S(1)}, u32[]{:S(2)}, u32[]{:S(2)}) collective-permute-start(f32[1,4,2,136,128]{4,3,2,1,0:T(8,128)S(1)} %get-tuple-element.55), channel_id=1, source_target_pairs={{0,16},{16,0},{1,17},{17,1},{2,18},{18,2},{3,19},{19,3},{4,20},{20... | collective-permute-start | bytes 1671176 | tf_op jit(solution)/shard_map/ppermute | solution.py:53
  60.5 17.8 %collective-permute-start.14 = (f32[1,4,2,136,128]{4,3,2,1,0:T(8,128)S(1)}, f32[1,4,2,136,128]{4,3,2,1,0:T(8,128)S(1)}, u32[]{:S(2)}, u32[]{:S(2)}) collective-permute-start(f32[1,4,2,136,128]{4,3,2,1,0:T(8,128)S(1)} %get-tuple-element.56), channel_id=1, source_target_pairs={{0,16},{16,0},{1,17},{17,1},{2,18},{18,2},{3,19},{19,3},{4,20},{20... | collective-permute-start | bytes 1671176 | tf_op jit(solution)/shard_map/ppermute | solution.py:53
  74.7 24.1 %collective-permute-start.19 = (f32[4,128,128]{2,1,0:T(8,128)S(1)}, f32[4,128,128]{2,1,0:T(8,128)S(1)}, u32[]{:S(2)}, u32[]{:S(2)}) collective-permute-start(f32[4,128,128]{2,1,0:T(8,128)S(1)} %get-tuple-element.50), channel_id=1, source_target_pairs={{0,4},{4,0},{8,12},{12,8},{1,5},{5,1},{9,13},{13,9},{2,6},{6,2},{1... | collective-permute-start | bytes 786440 | tf_op jit(solution)/shard_map/ppermute | solution.py:31
  76.3 22.6 %collective-permute-start.20 = (f32[4,128,128]{2,1,0:T(8,128)S(1)}, f32[4,128,128]{2,1,0:T(8,128)S(1)}, u32[]{:S(2)}, u32[]{:S(2)}) collective-permute-start(f32[4,128,128]{2,1,0:T(8,128)S(1)} %get-tuple-element.51), channel_id=1, source_target_pairs={{0,8},{4,12},{8,0},{12,4},{1,9},{5,13},{9,1},{13,5},{2,10},{6,14},... | collective-permute-start | bytes 786440 | tf_op jit(solution)/shard_map/ppermute | solution.py:31
  76.8 22.1 %collective-permute-start.21 = (f32[4,128,128]{2,1,0:T(8,128)S(1)}, f32[4,128,128]{2,1,0:T(8,128)S(1)}, u32[]{:S(2)}, u32[]{:S(2)}) collective-permute-start(f32[4,128,128]{2,1,0:T(8,128)S(1)} %get-tuple-element.52), channel_id=1, source_target_pairs={{0,12},{4,8},{8,4},{12,0},{1,13},{5,9},{9,5},{13,1},{2,14},{6,10},... | collective-permute-start | bytes 786440 | tf_op jit(solution)/shard_map/ppermute | solution.py:31
  79.6 19.3 %copy-start.2 = (f32[2,2,1,128,128]{4,3,2,1,0:T(8,128)S(1)}, f32[2,2,1,128,128]{4,3,2,1,0:T(8,128)}, u32[]{:S(2)}) copy-start(f32[2,2,1,128,128]{4,3,2,1,0:T(8,128)} %param.16) | copy-start | bytes 786436
  79.6 19.3 %copy-start.8 = (f32[128,256]{1,0:T(8,128)S(1)}, f32[128,256]{1,0:T(8,128)}, u32[]{:S(2)}) copy-start(f32[128,256]{1,0:T(8,128)} %refs_8_.1) | copy-start | bytes 393220
  79.6 19.3 %copy-start.9 = (f32[256,128]{1,0:T(8,128)S(1)}, f32[256,128]{1,0:T(8,128)}, u32[]{:S(2)}) copy-start(f32[256,128]{1,0:T(8,128)} %refs_9_.1) | copy-start | bytes 393220

commit v3 on v2

--- a/solution.py
+++ b/solution.py
@@ -73,31 +73,36 @@
     return pltpu.CompilerParams(vmem_limit_bytes=VMEM_LIMIT)
 
 
-def pack_kernel(grid, place_ref, counts_ref, feature_ref, position_ref, out_ref):
+def place_of(cell, shape):
+    return cell // (shape[1] * shape[2]), cell // shape[2] % shape[1], cell % shape[2]
+
+
+def pack_kernel(shape, grid, counts_ref, feature_ref, position_ref, out_ref):
     cells, channels, slots = feature_ref.shape
     slot = lax.broadcasted_iota(jnp.int32, (channels, slots), 1)
     blank = jnp.zeros((2, slots), f32)
+    base = [lax.axis_index(axis) * here for axis, here in zip(("gx", "gy", "gz"), shape)]
     for cell in range(cells):
-        out_ref[cell, :channels, :] = jnp.where(slot < counts_ref[cell], feature_ref[cell], 0.0)
-        at = position_ref[cell]
-        rows = [at]
-        for axis in range(3):
-            here = place_ref[cell * 3 + axis].astype(f32)
-            rows.append((at[axis : axis + 1] + here) * (1.0 / grid[axis]))
+        x, y, z = place_of(cell, shape)
+        held = slot < counts_ref[x, z, y]
+        out_ref[cell, :channels, :] = jnp.where(held, feature_ref[cell], 0.0)
+        at = [position_ref[3 * cell + axis] for axis in range(3)]
+        rows = list(at)
+        for axis, offset in enumerate((x, y, z)):
+            rows.append((at[axis] + (base[axis] + offset).astype(f32)) * (1.0 / grid[axis]))
         out_ref[cell, channels:, :] = jnp.concatenate(rows + [blank], axis=0)
 
 
-def pack(grid, place, counts, features, positions):
+def pack(shape, grid, counts, features, positions):
     cells, channels, slots = features.shape
-    smem = pl.BlockSpec(memory_space=pltpu.SMEM)
     return pl.pallas_call(
-        functools.partial(pack_kernel, grid),
-        in_specs=[smem, smem, whole(), whole()],
+        functools.partial(pack_kernel, shape, grid),
+        in_specs=[pl.BlockSpec(memory_space=pltpu.SMEM), whole(), whole()],
         out_specs=whole(),
         out_shape=jax.ShapeDtypeStruct((cells, channels + 8, slots), f32),
         compiler_params=params(),
         name="pack",
-    )(place, counts, features, positions)
+    )(counts, features, positions)
 
 
 def fitted(function, terms):
@@ -125,14 +130,18 @@
     return 1.0 - 0.5 * twice_sine * twice_sine, twice_sine * cosine
 
 
-def factor_kernel(parts, chunk, first, at_ref, waves_ref, block_ref, *refs):
+def factor_kernel(parts, chunk, first, waves_ref, block_ref, *refs):
     before = refs[: 0 if first else parts]
     refs = refs[len(before) :]
-    after, wave_ref, weight_ref = refs[:parts], refs[parts], refs[parts + 1]
+    after, wave_ref, weight_ref, column_ref = refs[:parts], refs[parts], refs[parts + 1], refs[parts + 2]
     cells, _, slots = block_ref.shape
     channels = after[0].shape[-1]
     span = cells * slots
-    total = waves_ref.shape[0]
+    total = wave_ref.shape[0] // 2
+    at_x = lax.axis_index("gx")
+    begin = pl.multiple_of(lax.axis_index("gy") * total, total)
+    rows = waves_ref[:, pl.ds(begin, total)].astype(f32)
+    column_ref[...] = jnp.concatenate([rows, jnp.zeros((5, total), f32)], axis=0).T
     for cell in range(cells):
         high, low = split(block_ref[cell, :channels, :])
         for at in (cell * slots, span + cell * slots):
@@ -141,9 +150,9 @@
 
     def some(j, carry):
         here = pl.multiple_of(j * chunk, chunk)
-        wave_x = waves_ref[pl.ds(here, chunk), 0:1]
-        wave_y = waves_ref[pl.ds(here, chunk), 1:2]
-        wave_z = waves_ref[pl.ds(here, chunk), 2:3]
+        wave_x = column_ref[pl.ds(here, chunk), 0:1]
+        wave_y = column_ref[pl.ds(here, chunk), 1:2]
+        wave_z = column_ref[pl.ds(here, chunk), 2:3]
         row = pl.multiple_of(j * 2 * chunk, 2 * chunk)
         for cell in range(cells):
             at = cell * slots
@@ -162,7 +171,7 @@
         )
         both = both[:, :channels] + both[:, channels:]
         per_part = total // chunk // parts
-        part = lax.rem(j // per_part - at_ref[0] + parts, parts)
+        part = lax.rem(j // per_part - at_x + parts, parts)
         row = pl.multiple_of(lax.rem(j, per_part) * 2 * chunk, 2 * chunk)
         for n in range(parts):
 
@@ -178,48 +187,59 @@
     lax.fori_loop(0, total // chunk, some, 0)
 
 
-def partial_factors(at, waves, block, before, parts):
-    total = waves.shape[0]
-    chunk = math.gcd(total // parts, 128)
+def partial_factors(waves, total, chunk, block, before, parts):
     cells, rows, slots = block.shape
     channels = rows - 8
     span = cells * slots
     out = [jax.ShapeDtypeStruct((2 * total // parts, channels), f32)] * parts
     return pl.pallas_call(
         functools.partial(factor_kernel, parts, chunk, not before),
-        in_specs=[pl.BlockSpec(memory_space=pltpu.SMEM)] + [whole()] * (2 + len(before)),
+        in_specs=[whole()] * (2 + len(before)),
         out_specs=[whole()] * (parts + 1),
         out_shape=out + [jax.ShapeDtypeStruct((2 * total, 2 * span), bf16)],
-        scratch_shapes=[pltpu.VMEM((2 * channels, 2 * span), bf16)],
+        input_output_aliases={2 + n: n for n in range(len(before))},
+        scratch_shapes=[pltpu.VMEM((2 * channels, 2 * span), bf16), pltpu.VMEM((total, 8), f32)],
         compiler_params=params(),
         cost_estimate=pl.CostEstimate(
             flops=8 * total * span * channels, bytes_accessed=8 * total * span, transcendentals=0
         ),
         name="factors",
-    )(at, waves, block, *before)
-
-
-def filter_kernel(*refs):
+    )(waves, block, *before)
+
+
+def filter_kernel(scale, block_ref, *refs):
     parts, (weight_ref, table_ref, out_ref) = refs[:-3], refs[-3:]
     summed = parts[0][...]
     for part in parts[1:]:
         summed = summed + part[...]
     projected = jnp.dot(summed, weight_ref[...], precision=HIGH, preferred_element_type=f32)
-    out_ref[...] = projected * table_ref[...]
-
-
-def filtered_piece(parts, w_charge, table):
+    table = table_ref[...] * scale
+    for n in range(0, summed.shape[0], table.shape[0]):
+        out_ref[n : n + table.shape[0], :] = projected[n : n + table.shape[0]] * table
+
+
+def filtered_piece(scale, block, chunk, parts, w_charge, table):
+    rows, channels = parts[0].shape
+    fixed = pl.BlockSpec((rows, channels), lambda i, block: (0, 0))
     return pl.pallas_call(
-        filter_kernel,
-        in_specs=[whole()] * (len(parts) + 2),
-        out_specs=whole(),
-        out_shape=jax.ShapeDtypeStruct(table.shape, f32),
+        functools.partial(filter_kernel, scale),
+        grid_spec=pltpu.PrefetchScalarGridSpec(
+            num_scalar_prefetch=1,
+            grid=(1,),
+            in_specs=[fixed] * len(parts)
+            + [
+                pl.BlockSpec(w_charge.shape, lambda i, block: (0, 0)),
+                pl.BlockSpec((chunk, channels), lambda i, block: (block[0], 0)),
+            ],
+            out_specs=fixed,
+        ),
+        out_shape=jax.ShapeDtypeStruct((rows, channels), f32),
         compiler_params=params(),
         name="filter",
-    )(*parts, w_charge, table)
-
-
-def potential_kernel(groups, pieces, blocks, index_ref, *refs):
+    )(block, *parts, w_charge, table)
+
+
+def potential_kernel(groups, pieces, blocks, *refs):
     held = refs[:groups]
     waves = refs[groups : groups + blocks]
     outs = refs[groups + blocks : -2]
@@ -228,7 +248,9 @@
     piece = held[0].shape[0] // pieces
     for group in range(groups):
         for n in range(pieces):
-            at = pl.multiple_of(index_ref[group * pieces + n] * piece, piece)
+            rank_x = partner(lax.axis_index("gx"), group, groups)
+            rank_z = partner(lax.axis_index("gz"), n, pieces)
+            at = pl.multiple_of((rank_x * pieces + rank_z) * piece, piece)
             ordered_ref[pl.ds(at, piece), :] = held[group][n * piece : (n + 1) * piece, :]
     high, low = split(ordered_ref[...].T)
     turned_ref[:channels, :] = high
@@ -243,12 +265,12 @@
             out[cell] = potential[:, cell * slots : (cell + 1) * slots]
 
 
-def potentials_of(index, held, pieces, waves, cells, slots):
+def potentials_of(held, pieces, waves, cells, slots):
     rows = waves[0].shape[0]
     channels = held[0].shape[-1]
     return pl.pallas_call(
         functools.partial(potential_kernel, len(held), pieces, len(waves)),
-        in_specs=[pl.BlockSpec(memory_space=pltpu.SMEM)] + [whole()] * (len(held) + len(waves)),
+        in_specs=[whole()] * (len(held) + len(waves)),
         out_specs=[whole()] * len(waves),
         scratch_shapes=[
             pltpu.VMEM((rows, channels), f32),
@@ -261,31 +283,36 @@
             bytes_accessed=4 * rows * len(waves) * cells * slots, transcendentals=0,
         ),
         name="potentials",
-    )(index, *held, *waves)
+    )(*held, *waves)
 
 
 def message_kernel(
-    basis, own_plane, step_ref, own_ref, ext_ref, mix_ref, value_ref, out_ref,
-    cell_ref, own_col_ref, acc_ref, mixed_ref, left_0, left_1, left_2, right_0, right_1, right_2,
+    basis, sources, table, own_plane, step_ref, own_ref, mix_ref, value_ref, *refs
 ):
+    blocks, out_ref = refs[:sources], refs[sources]
+    cell_ref, at_ref, own_col_ref, acc_ref, mixed_ref = refs[sources + 1 : sources + 6]
+    left_0, left_1, left_2, right_0, right_1, right_2 = refs[sources + 6 :]
     count = step_ref.shape[1]
     cells = own_ref.shape[0]
-    across, along, planes, _, slots = ext_ref.shape
+    slots = own_ref.shape[-1]
+    along, planes = len(table[0]), len(table[0][0])
     channels = value_ref.shape[0]
     lefts, rights = (left_0, left_1, left_2), (right_0, right_1, right_2)
 
-    def turn(n, carry):
-        x = n // (along * planes)
-        y = (n // planes) % along
-        z = n % planes
-        high, low = split(ext_ref[x, y, z, :channels, :])
-        cell_ref[n, :channels, :] = high
-        cell_ref[n, channels:, :] = low
-        return carry
-
-    lax.fori_loop(0, across * along * planes, turn, 0, unroll=4)
+    for x, columns in enumerate(table):
+        for y, column in enumerate(columns):
+            for z, choices in enumerate(column):
+                n = (x * along + y) * planes + z
+                (_, source, index), others = choices[0], choices[1:]
+                block = blocks[source][index]
+                for condition, source, index in others:
+                    block = jnp.where(condition(), blocks[source][index], block)
+                high, low = split(block[:channels])
+                cell_ref[n, :channels, :] = high
+                cell_ref[n, channels:, :] = low
+                at_ref[n] = block[channels:]
     for b in range(basis):
-        high, low = split(value_ref[...] * mix_ref[b : b + 1, :])
+        high, low = split(value_ref[...] * (mix_ref[b : b + 1, :] * math.exp(-b * b)))
         mixed_ref[b * channels : (b + 1) * channels, :channels] = high
         mixed_ref[b * channels : (b + 1) * channels, channels:] = low
     for cell in range(cells):
@@ -297,15 +324,18 @@
         place_x = step_ref[0, step] + 1 + (move - 1)
         place_y = step_ref[1, step]
         plane = step_ref[2, step]
+        if not own_plane:
+            plane = jnp.where(is_even("gz"), plane, 1 - plane)
         shift_z = step_ref[3, step].astype(f32)
         left, right = lefts[move], rights[move]
         own = step_ref[4, step]
         near = []
         for n in range(3):
-            cell = cell_ref[(place_x * along + place_y + n) * planes + plane]
+            number = (place_x * along + place_y + n) * planes + plane
+            cell = cell_ref[number]
             right[:, n * slots : (n + 1) * slots] = cell
             right[:, (3 + n) * slots : (4 + n) * slots] = cell
-            at = ext_ref[place_x, place_y + n, plane, channels : channels + 3, :]
+            at = at_ref[number]
             near.append((at[0:1] + float(move - 1), at[1:2] + float(n - 1), at[2:3] + shift_z))
         tile = 16
         for m in range(slots // tile):
@@ -368,17 +398,18 @@
     lax.fori_loop(0, count, visit, 0)
 
 
-def pair_messages(steps, own_plane, own, ext, mix, w_value):
+def pair_messages(steps, own_plane, own, blocks, table, mix, w_value):
     cells, _, slots = own.shape
     basis, channels = mix.shape
-    across, along, planes = ext.shape[:3]
+    around = len(table) * len(table[0]) * len(table[0][0])
     count = steps.shape[1]
     return pl.pallas_call(
-        functools.partial(message_kernel, basis, own_plane),
-        in_specs=[pl.BlockSpec(memory_space=pltpu.SMEM)] + [whole()] * 4,
+        functools.partial(message_kernel, basis, len(blocks), table, own_plane),
+        in_specs=[pl.BlockSpec(memory_space=pltpu.SMEM)] + [whole()] * (3 + len(blocks)),
         out_specs=whole(),
         scratch_shapes=[
-            pltpu.VMEM((across * along * planes, 2 * channels, slots), bf16),
+            pltpu.VMEM((around, 2 * channels, slots), bf16),
+            pltpu.VMEM((around, 8, slots), f32),
             pltpu.VMEM((cells, 3, slots, slots), f32),
             pltpu.VMEM((basis * slots, 2 * channels), f32),
             pltpu.VMEM((basis * channels, 2 * channels), bf16),
@@ -392,7 +423,7 @@
             transcendentals=0,
         ),
         name="messages",
-    )(steps, own, ext, mix, w_value)
+    )(steps, own, mix, w_value, *blocks)
 def visits(cells_x, cells_y, cells_z, inside):
     table = []
     for x in range(cells_x):
@@ -412,7 +443,7 @@
     return np.array(table, np.int32).T.copy()
 
 
-def mlp_kernel(count, *refs):
+def mlp_kernel(count, shape, *refs):
     counts_ref, feature_ref = refs[:2]
     messages = refs[2:4]
     potentials = refs[4 : 4 + count]
@@ -431,12 +462,13 @@
     slot = lax.broadcasted_iota(jnp.int32, (channels, slots), 1)
     for cell in range(cells):
         part = updated[:, cell * slots : (cell + 1) * slots]
-        out_ref[cell] = jnp.where(slot < counts_ref[cell], part, 0.0)
-
-
-def atom_mlp(counts, features, messages, potentials, w_hidden, w_out):
+        x, y, z = place_of(cell, shape)
+        out_ref[cell] = jnp.where(slot < counts_ref[x, z, y], part, 0.0)
+
+
+def atom_mlp(shape, counts, features, messages, potentials, w_hidden, w_out):
     return pl.pallas_call(
-        functools.partial(mlp_kernel, len(potentials)),
+        functools.partial(mlp_kernel, len(potentials), shape),
         in_specs=[pl.BlockSpec(memory_space=pltpu.SMEM)]
         + [whole()] * (5 + len(potentials)),
         out_specs=whole(),
@@ -446,46 +478,70 @@
     )(counts, features, *messages, *potentials, w_hidden, w_out)
 
 
-def with_x(block):
-    below, above = below_above(block[:1], block[-1:], "gx")
-    return jnp.concatenate([below, block, above], axis=0)
+def next_in_x(block, shape):
+    size = lax.axis_size("gx")
+    if size == 2:
+        other = exchange(block, "gx", 1)
+        return (other, shape[0] - 1), (other, 0)
+    wide = block.reshape(shape + block.shape[1:])
+    below, above = below_above(wide[:1], wide[-1:], "gx")
+    return tuple((side.reshape((-1,) + block.shape[1:]), 0) for side in (below, above))
+
+
+class Sources:
+    def __init__(self):
+        self.arrays = []
+
+    def add(self, array):
+        for n, held in enumerate(self.arrays):
+            if held is array:
+                return n
+        self.arrays.append(array)
+        return len(self.arrays) - 1
+
+    def columns(self, block, shape):
+        below, above = next_in_x(block, shape)
+        inside = [(self.add(block), x) for x in range(shape[0])]
+        return [(self.add(below[0]), below[1])] + inside + [(self.add(above[0]), above[1])]
+
+
+def always():
+    return True
 
 
 def shards(
     features, positions, counts, waves, filter_table, w_value, w_charge, radial_mix, w_hidden, w_out
 ):
-    cells_x, cells_y, cells_z, channels, slots = features.shape
-    basis = radial_mix.shape[0]
+    shape = cells_x, cells_y, cells_z = features.shape[:3]
+    channels, slots = features.shape[3:]
     total_waves = waves.shape[1]
     size_x, size_y, size_z = (lax.axis_size(a) for a in ("gx", "gy", "gz"))
     at_x, at_y, at_z = (lax.axis_index(a) for a in ("gx", "gy", "gz"))
     grid = (cells_x * size_x, cells_y * size_y, cells_z * size_z)
     cells = cells_x * cells_y * cells_z
-    flat_counts = counts.reshape(cells)
+    some_counts = jnp.transpose(counts, (0, 2, 1))
     flat_features = features.reshape(cells, channels, slots)
 
-    offsets = np.array(
-        [(x, y, z) for x in range(cells_x) for y in range(cells_y) for z in range(cells_z)], np.int32
-    )
-    base = jnp.stack([at_x * cells_x, at_y * cells_y, at_z * cells_z]).astype(jnp.int32)
-    own = pack(
-        grid, (base + offsets).reshape(-1), flat_counts, flat_features,
-        positions.reshape(cells, 3, slots),
-    )
+    own = pack(shape, grid, some_counts, flat_features, positions.reshape(cells * 3, 1, slots))
     rows = own.shape[1]
-    packed = own.reshape(cells_x, cells_y, cells_z, rows, slots)
+    packed = own.reshape(shape + (rows, slots))
 
     gathered = [own] + [exchange(own, "gy", s) for s in range(1, size_y)]
-    sides = neighbours(packed[:, :, :1], packed[:, :, -1:], "gz", same=cells_z == 1)
+    if cells_z == 1:
+        sides = neighbours(own, own, "gz", same=True)
+    else:
+        flat = (cells_x * cells_y, rows, slots)
+        sides = neighbours(packed[:, :, 0].reshape(flat), packed[:, :, -1].reshape(flat), "gz")
 
     share = total_waves // size_y
-    own_waves = lax.dynamic_slice_in_dim(waves, at_y * share, share, 1).astype(f32).T
+    half = 2 * share // size_x
+    piece = half // size_z
+    chunk = min(piece, share // size_x)
     parts, tables = (), []
     for block in gathered:
-        *parts, table = partial_factors(at_x.reshape(1), own_waves, block, parts, size_x)
+        *parts, table = partial_factors(waves, share, chunk, block, parts, size_x)
         tables.append(table)
 
-    half = 2 * share // size_x
     summed = parts[0]
     for s in range(1, size_x):
         other = partner(at_x, s, size_x)
@@ -493,62 +549,98 @@
         for n in range(2, size_x):
             to = jnp.where(lax.rem(other - at_x + size_x, size_x) == n, parts[n], to)
         summed = summed + exchange(to, "gx", s)
-    piece = half // size_z
+    value_near, summed = lax.optimization_barrier((w_value, summed))
     pieces = [lax.dynamic_slice_in_dim(summed, at_z * piece, piece, 0)]
     for s in range(1, size_z):
         other = partner(at_z, s, size_z)
         pieces.append(exchange(lax.dynamic_slice_in_dim(summed, other * piece, piece, 0), "gz", s))
+
+    sources = Sources()
+
+    def reaches(step, rank):
+        return any(partner(i, step, size_y) == (i + rank) % size_y for i in range(size_y))
+
+    columns = {
+        step: sources.columns(block, shape)
+        for step, block in enumerate(gathered)
+        if any(reaches(step, rank) for rank in (-1, 0, 1))
+    }
+
+    def at_rank(step, rank):
+        def condition():
+            at = lax.axis_index("gy")
+            return partner(at, step, size_y) == (at + rank) % size_y
+
+        return condition
+
+    def choices(x, y, z):
+        rank = -1 if y < 0 else 1 if y == cells_y else 0
+        y = y % cells_y
+        found = []
+        for step in columns:
+            if reaches(step, rank):
+                source, from_x = columns[step][x + 1]
+                found.append((at_rank(step, rank), source, (from_x * cells_y + y) * cells_z + z))
+        return found
+
+    table = [
+        [[choices(x, y, z) for z in range(cells_z)] for y in range(-1, cells_y + 1)]
+        for x in range(-1, cells_x + 1)
+    ]
+    inner = jnp.asarray(visits(cells_x, cells_y, cells_z, True))
+    near = pair_messages(inner, True, own, sources.arrays, table, radial_mix, value_near)
+
     scale = 1.0 / math.sqrt(grid[0] * grid[1] * grid[2] * slots) / math.sqrt(total_waves)
-    chunk = math.gcd(share // size_x, 128)
-    table = lax.dynamic_slice_in_dim(filter_table, at_y * share, share, 0) * scale
-    table = jnp.broadcast_to(
-        table.reshape(share // chunk, 1, chunk, channels), (share // chunk, 2, chunk, channels)
-    ).reshape(2 * share, channels)
-    table = lax.dynamic_slice_in_dim(table, at_x * half + at_z * piece, piece, 0)
-    filtered = filtered_piece(pieces, w_charge, table)
-
-    held_z = jnp.concatenate(
-        [filtered] + [exchange(filtered, "gz", s) for s in range(1, size_z)], axis=0
+    rank = at_x * size_z + at_z
+    block = at_y * (share // chunk) + (rank * piece) // (2 * chunk)
+    charge, near = lax.optimization_barrier((w_charge, near))
+    filtered = filtered_piece(scale, block.reshape(1), chunk, pieces, charge, filter_table)
+
+    held_z = [filtered] + [exchange(filtered, "gz", s) for s in range(1, size_z)]
+    started = held_z[min(1, size_z - 1)]
+    held_z = jnp.concatenate(held_z, axis=0)
+    held = [held_z] + [exchange(held_z, "gx", s) for s in range(1, size_x)]
+
+    low, high = (
+        jnp.concatenate(
+            [side[n : n + 1] for n in range(y, cells_x * cells_y, cells_y) for side in sides], axis=0
+        )
+        for y in (0, cells_y - 1)
     )
-    held = [held_z] + [exchange(held_z, "gx", s) for s in range(1, size_x)]
-    ranks_x = [at_x] + [partner(at_x, s, size_x) for s in range(1, size_x)]
-    ranks_z = [at_z] + [partner(at_z, s, size_z) for s in range(1, size_z)]
-    index = jnp.stack([x * size_z + z for x in ranks_x for z in ranks_z]).astype(jnp.int32)
-
-    def of_y(rank, edge):
-        found = None
-        for s in range(size_y):
-            source = at_y if s == 0 else partner(at_y, s, size_y)
-            possible = any(
-                (i if s == 0 else partner(i, s, size_y)) == (i + rank) % size_y for i in range(size_y)
+    low, high, started = lax.optimization_barrier((low, high, started))
+    edges = neighbours(low, high, "gy")
+    sources = Sources()
+    flat = (cells_x, cells_y, 1)
+    side_columns = [sources.columns(side, flat) for side in sides]
+    edge_columns = [sources.columns(edge, (cells_x, 1, 2)) for edge in edges]
+
+    def choices(x, y, z):
+        if 0 <= y < cells_y:
+            source, from_x = side_columns[z][x + 1]
+            return [(always, source, from_x * cells_y + y)]
+        found = []
+        for n, columns in enumerate(edge_columns):
+            source, from_x = columns[x + 1]
+            first_is_here = y == cells_y
+            condition = (lambda: is_even("gy")) if (n == 0) == first_is_here else (
+                lambda: jnp.logical_not(is_even("gy"))
             )
-            if not possible:
-                continue
-            block = gathered[s].reshape(packed.shape)[:, edge]
-            wanted = source == lax.rem(at_y + rank + size_y, size_y)
-            found = block if found is None else jnp.where(wanted, block, found)
+            found.append((condition, source, from_x * 2 + z))
         return found
 
-    plane = with_x(jnp.concatenate([of_y(-1, slice(-1, None)), packed, of_y(1, slice(0, 1))], axis=1))
-    low, high = (
-        jnp.concatenate([side[:, edge] for side in sides], axis=2)
-        for edge in (slice(0, 1), slice(-1, None))
+    table = [
+        [[choices(x, y, z) for z in range(2)] for y in range(-1, cells_y + 1)]
+        for x in range(-1, cells_x + 1)
+    ]
+    found = potentials_of(held, held_z.shape[0] // piece, tables, cells, slots)
+    value_far, *found = lax.optimization_barrier((w_value, *found))
+    returned = [found[0]] + [exchange(found[s], "gy", s) for s in range(1, size_y)]
+    outer = jnp.asarray(visits(cells_x, cells_y, cells_z, False))
+    far = pair_messages(outer, False, own, sources.arrays, table, radial_mix, value_far)
+
+    updated = atom_mlp(
+        shape, some_counts, flat_features, [near, far], returned, w_hidden, w_out
     )
-    low, high, filtered = lax.optimization_barrier((low, high, filtered))
-    below, above = below_above(low, high, "gy")
-    around = with_x(jnp.concatenate([below, jnp.concatenate(sides, axis=2), above], axis=1))
-
-    mix = radial_mix * np.exp(-np.arange(basis, dtype=np.float64) ** 2).astype(np.float32)[:, None]
-    inner = jnp.asarray(visits(cells_x, cells_y, cells_z, True))
-    outer = jnp.asarray(visits(cells_x, cells_y, cells_z, False))
-    outer = outer.at[2].set(jnp.where(is_even("gz"), outer[2], 1 - outer[2]))
-    near = pair_messages(inner, True, own, plane, mix, w_value)
-    far = pair_messages(outer, False, own, around, mix, w_value)
-
-    found = potentials_of(index, held, held_z.shape[0] // piece, tables, cells, slots)
-    returned = [found[0]] + [exchange(found[s], "gy", s) for s in range(1, size_y)]
-
-    updated = atom_mlp(flat_counts, flat_features, [near, far], returned, w_hidden, w_out)
     return updated.reshape(features.shape)
 
 

time: 101 us -> 89.7 us (0.89)
  other arithmetic: 6.1 us -> 0.13 us
  local copies, waits for them, and re-layouts: 8.8 us -> 3.2 us
  waiting for transfers between devices: 11.5 us -> 12.6 us
    ppermute x8 -> x4, waiting for transfers between devices: 3.13 us -> 7.99 us  [neighbours(): return (lax.ppermute(first, axis, one), lax.ppermute(second, axis, two))]
    ppermute x14 -> x21, waiting for transfers between devices: 8.42 us -> 4.63 us  [exchange(): return lax.ppermute(block, axis, pairs)]
    unnamed x40 -> x28, local copies, waits for them, and re-layouts: 5.83 us -> 3.12 us
    concatenate x6 -> x2, other arithmetic: 2.52 us -> 0.07 us  [the longest x1 0.05 us: shards(): jnp.concatenate([side[n:n + 1] for n in range(y, cells_x * cells_y, cells...]
    slice x2, local copies, waits for them, and re-layouts: 1.99 us -> 0.04 us  [shards(): side[n:n + 1]]
    ppermute x8 -> x4, starting transfers between devices: 8.75 us -> 7.18 us  [neighbours(): return (lax.ppermute(first, axis, one), lax.ppermute(second, axis, two))]
    unnamed x1 -> x0, other arithmetic: 1.34 us -> none
    ppermute x14 -> x21, starting transfers between devices: 17.2 us -> 18.2 us  [exchange(): return lax.ppermute(block, axis, pairs)]
  transfers between devices with their start and end apart: 22 -> 25, of which waited for: 6 -> 5; matrix products, arithmetic and copies ran while one was open for 7% -> 0% of each run, Pallas kernels for 45% -> 50%
where the time goes in v3:
time: 89.7 us; the launch traced here: 89.5 us
  Pallas kernels  47.8 us (53%)
  starting transfers between devices  25.4 us (28%)
  waiting for transfers between devices  12.6 us (14%)
  local copies, waits for them, and re-layouts  3.2 us (4%)
    pallas_call x2, Pallas kernels, pair_messages(): pl.pallas_call(functools.partial(message_kernel, basis, len(blocks), tabl...  30.1 us
    ppermute x21, starting transfers between devices, exchange(): return lax.ppermute(block, axis, pairs)  18.2 us
    pallas_call x4, Pallas kernels, partial_factors(): pl.pallas_call(functools.partial(factor_kernel, parts, chunk, not before)...  13 us
    ppermute x4, waiting for transfers between devices, neighbours(): return (lax.ppermute(first, axis, one), lax.ppermute(second, axis, two))  7.99 us
    ppermute x4, starting transfers between devices, neighbours(): return (lax.ppermute(first, axis, one), lax.ppermute(second, axis, two))  7.18 us
    ppermute x21, waiting for transfers between devices, exchange(): return lax.ppermute(block, axis, pairs)  4.63 us
    unnamed x28, local copies, waits for them, and re-layouts  3.12 us
    pallas_call x1, Pallas kernels, atom_mlp(): pl.pallas_call(functools.partial(mlp_kernel, len(potentials), shape), in_...  2.03 us
  transfers between devices with their start and end apart: 25, of which 5 were waited for; matrix products, arithmetic and copies ran while one was open for 0% of the time, Pallas kernels for 50%

profile of v3, /device:TPU:0, one launch (start us, length us, event | category | flops | bytes accessed | tf_op | source)
XLA Modules:
  0.0 89.5 jit_solution(10850723429412304974)
XLA Ops:
  0.0 0.9 %copy-done = f32[2,2,1,128,128]{4,3,2,1,0:T(8,128)S(1)} copy-done((f32[2,2,1,128,128]{4,3,2,1,0:T(8,128)S(1)}, f32[2,2,1,128,128]{4,3,2,1,0:T(8,128)}, u32[]{:S(2)}) %copy-start) | copy-done | bytes 262168
  1.0 0.7 copy-done.6
  1.6 0.7 copy-done.7
  2.3 0.6 pack.1.block_ref.own_ref.refs_0_
  2.9 3.0 %collective-permute-start.2 = (f32[4,136,128]{2,1,0:T(8,128)S(1)}, f32[4,136,128]{2,1,0:T(8,128)S(1)}, u32[]{:S(2)}, u32[]{:S(2)}) collective-permute-start(f32[4,136,128]{2,1,0:T(8,128)S(1)} %pack.1.block_ref.own_ref.refs_0_), channel_id=1, source_target_pairs={{0,4},{4,0},{8,12},{12,8},{1,5},{5,1},{9,13},{13,9},{2,6},{6,2},{1... | collective-permute-start | bytes 835592 | tf_op jit(solution)/shard_map/ppermute | solution.py:31
  5.9 1.5 %collective-permute-start.1 = (f32[4,136,128]{2,1,0:T(8,128)S(1)}, f32[4,136,128]{2,1,0:T(8,128)S(1)}, u32[]{:S(2)}, u32[]{:S(2)}) collective-permute-start(f32[4,136,128]{2,1,0:T(8,128)S(1)} %pack.1.block_ref.own_ref.refs_0_), channel_id=1, source_target_pairs={{0,8},{4,12},{8,0},{12,4},{1,9},{5,13},{9,1},{13,5},{2,10},{6,14},... | collective-permute-start | bytes 835592 | tf_op jit(solution)/shard_map/ppermute | solution.py:31
  7.4 0.0 collective-permute-start
  7.5 4.1 %collective-permute-start.16 = (f32[4,136,128]{2,1,0:T(8,128)S(1)}, f32[4,136,128]{2,1,0:T(8,128)S(1)}, u32[]{:S(2)}, u32[]{:S(2)}) collective-permute-start(f32[4,136,128]{2,1,0:T(8,128)S(1)} %pack.1.block_ref.own_ref.refs_0_), channel_id=1, source_target_pairs={{0,3},{1,2},{2,1},{3,0},{4,7},{5,6},{6,5},{7,4},{8,11},{9,10},{10,... | collective-permute-start | bytes 835592 | tf_op jit(solution)/shard_map/ppermute | solution.py:53
  11.5 0.0 collective-permute-start.4
  11.5 0.8 copy-done.10
  12.3 3.2 %factors.4 = (f32[512,128]{1,0:T(8,128)S(1)}, f32[512,128]{1,0:T(8,128)S(1)}, bf16[1024,1024]{1,0:T(8,128)(2,1)S(1)}) custom-call(s32[3,2048]{1,0:T(4,128)S(1)} %copy-done.10, f32[4,136,128]{2,1,0:T(8,128)S(1)} %pack.1.block_ref.own_ref.refs_0_), custom_call_target="tpu_custom_call" | custom-call | flops 268435456 | bytes 2097152 | tf_op jit(solution)/shard_map/factors/pallas_call | solution.py:195
  15.5 0.0 collective-permute-done.2.block_ref.refs_2_
  15.5 0.1 collective-permute-start.14
  15.6 3.3 %factors.5 = (f32[512,128]{1,0:T(8,128)S(1)}, f32[512,128]{1,0:T(8,128)S(1)}, bf16[1024,1024]{1,0:T(8,128)(2,1)S(1)}) custom-call(s32[3,2048]{1,0:T(4,128)S(1)} %copy-done.10, f32[4,136,128]{2,1,0:T(8,128)S(1)} %collective-permute-done.2.block_ref.refs_2_, f32[512,128]{1,0:T(8,128)S(1)} %get-tuple-element.32.refs_0_, ...), custom_call_target="tpu_custom_call", output_to_operand_aliasing={{0}: (2, {}), {1}: (3, {})} | custom-call | flops 268435456 | bytes 2097152 | tf_op jit(solution)/shard_map/factors/pallas_call | solution.py:195
  18.9 1.1 %collective-permute-done.1.block_ref = f32[4,136,128]{2,1,0:T(8,128)S(1)} collective-permute-done((f32[4,136,128]{2,1,0:T(8,128)S(1)}, f32[4,136,128]{2,1,0:T(8,128)S(1)}, u32[]{:S(2)}, u32[]{:S(2)}) %collective-permute-start.1) | collective-permute-done | bytes 278560 | tf_op jit(solution)/shard_map/ppermute | solution.py:31
  20.0 3.3 %factors.6 = (f32[512,128]{1,0:T(8,128)S(1)}, f32[512,128]{1,0:T(8,128)S(1)}, bf16[1024,1024]{1,0:T(8,128)(2,1)S(1)}) custom-call(s32[3,2048]{1,0:T(4,128)S(1)} %copy-done.10, f32[4,136,128]{2,1,0:T(8,128)S(1)} %collective-permute-done.1.block_ref, f32[512,128]{1,0:T(8,128)S(1)} %get-tuple-element.34.refs_0_, ...), custom_call_target="tpu_custom_call", output_to_operand_aliasing={{0}: (2, {}), {1}: (3, {})} | custom-call | flops 268435456 | bytes 2097152 | tf_op jit(solution)/shard_map/factors/pallas_call | solution.py:195
  23.3 0.0 collective-permute-done.block_ref.refs_4_
  23.3 3.3 %factors.7 = (f32[512,128]{1,0:T(8,128)S(1)}, f32[512,128]{1,0:T(8,128)S(1)}, bf16[1024,1024]{1,0:T(8,128)(2,1)S(1)}) custom-call(s32[3,2048]{1,0:T(4,128)S(1)} %copy-done.10, f32[4,136,128]{2,1,0:T(8,128)S(1)} %collective-permute-done.block_ref.refs_4_, f32[512,128]{1,0:T(8,128)S(1)} %get-tuple-element.36.refs_0_, ...), custom_call_target="tpu_custom_call", output_to_operand_aliasing={{0}: (2, {}), {1}: (3, {})} | custom-call | flops 268435456 | bytes 2097152 | tf_op jit(solution)/shard_map/factors/pallas_call | solution.py:195
  26.5 0.1 collective-permute-start.3
  26.6 0.5 collective-permute-start.5
  27.1 0.0 collective-permute-done.16.refs_2_
  27.1 0.1 collective-permute-start.6
  27.2 0.0 collective-permute-done.14.refs_0_
  27.3 0.9 collective-permute-done.3
  28.2 1.6 %collective-permute-start.7 = (f32[128,128]{1,0:T(8,128)S(1)}, f32[128,128]{1,0:T(8,128)S(1)}, u32[]{:S(2)}, u32[]{:S(2)}) collective-permute-start(f32[128,128]{1,0:T(8,128)S(1)} %get-tuple-element.71), channel_id=1, source_target_pairs={{0,1},{1,0},{2,3},{3,2},{4,5},{5,4},{6,7},{7,6},{8,9},{9,8},{10,11... | collective-permute-start | bytes 196616 | tf_op jit(solution)/shard_map/ppermute | solution.py:31
  29.9 2.6 %collective-permute-start.8 = (f32[128,128]{1,0:T(8,128)S(1)}, f32[128,128]{1,0:T(8,128)S(1)}, u32[]{:S(2)}, u32[]{:S(2)}) collective-permute-start(f32[128,128]{1,0:T(8,128)S(1)} %get-tuple-element.70), channel_id=1, source_target_pairs={{0,2},{1,3},{2,0},{3,1},{4,6},{5,7},{6,4},{7,5},{8,10},{9,11},{10,... | collective-permute-start | bytes 196616 | tf_op jit(solution)/shard_map/ppermute | solution.py:31
  32.4 0.0 collective-permute-done.4.refs_1_
  32.5 0.2 collective-permute-start.9
  32.7 0.0 collective-permute-done.5.refs_3_
  32.7 0.0 collective-permute-done.6.refs_5_
  32.7 11.0 %messages.2.refs_2_ = f32[4,128,128]{2,1,0:T(8,128)S(1)} custom-call(s32[7,4]{1,0:T(8,128)S(1)} %copy-done.13, f32[4,136,128]{2,1,0:T(8,128)S(1)} %pack.1.block_ref.own_ref.refs_0_, f32[8,128]{1,0:T(8,128)S(1)} %copy-done.11, f32[128,128]{1,0:T(8,128)S(1)} %copy-done.9, f32[4,136,128]{2,1,0:T(8,128)S(1)} %pack.1.block_ref.own_ref.refs_0_, ...), custom_call_target="tpu_custom_call" | custom-call | flops 4831838208 | bytes 1048576 | tf_op jit(solution)/shard_map/messages/pallas_call | solution.py:406
  43.7 0.0 collective-permute-done.7.refs_1_
  43.7 0.0 collective-permute-done.8.refs_2_
  43.8 0.0 collective-permute-done.9.refs_3_
  43.8 0.2 filter.1
  44.0 0.8 collective-permute-start.10
  44.8 3.0 %collective-permute-start.12 = (f32[128,128]{1,0:T(8,128)S(1)}, f32[128,128]{1,0:T(8,128)S(1)}, u32[]{:S(2)}, u32[]{:S(2)}) collective-permute-start(f32[128,128]{1,0:T(8,128)S(1)} %filter.1), channel_id=1, source_target_pairs={{0,3},{1,2},{2,1},{3,0},{4,7},{5,6},{6,5},{7,4},{8,11},{9,10},{10,... | collective-permute-start | bytes 196616 | tf_op jit(solution)/shard_map/ppermute | solution.py:31
  47.8 0.6 collective-permute-start.11
  48.4 0.0 collective-permute-done.10
  48.4 0.5 collective-permute-start.18
  49.0 2.5 %collective-permute-start.20 = (f32[4,136,128]{2,1,0:T(8,128)S(1)}, f32[4,136,128]{2,1,0:T(8,128)S(1)}, u32[]{:S(2)}, u32[]{:S(2)}) collective-permute-start(f32[4,136,128]{2,1,0:T(8,128)S(1)} %get-tuple-element.59), channel_id=1, source_target_pairs={{0,12},{4,8},{8,4},{12,0},{1,13},{5,9},{9,5},{13,1},{2,14},{6,10},... | collective-permute-start | bytes 835592 | tf_op jit(solution)/shard_map/ppermute | solution.py:53
  51.5 0.0 collective-permute-done.12
  51.5 2.6 %collective-permute-done.11 = f32[128,128]{1,0:T(8,128)S(1)} collective-permute-done((f32[128,128]{1,0:T(8,128)S(1)}, f32[128,128]{1,0:T(8,128)S(1)}, u32[]{:S(2)}, u32[]{:S(2)}) %collective-permute-start.11) | collective-permute-done | bytes 65568 | tf_op jit(solution)/shard_map/ppermute | solution.py:31
  54.1 0.1 collective-permute-start.13
  54.2 0.5 collective-permute-start.15
  54.7 0.1 collective-permute-start.17
  54.7 3.3 %collective-permute-done.18.refs_4_ = f32[4,136,128]{2,1,0:T(8,128)S(1)} collective-permute-done((f32[4,136,128]{2,1,0:T(8,128)S(1)}, f32[4,136,128]{2,1,0:T(8,128)S(1)}, u32[]{:S(2)}, u32[]{:S(2)}) %collective-permute-start.18) | collective-permute-done | bytes 278560 | tf_op jit(solution)/shard_map/ppermute | solution.py:53
  58.1 0.0 collective-permute-start.19
  58.1 4.6 %collective-permute-done.20.refs_6_ = f32[4,136,128]{2,1,0:T(8,128)S(1)} collective-permute-done((f32[4,136,128]{2,1,0:T(8,128)S(1)}, f32[4,136,128]{2,1,0:T(8,128)S(1)}, u32[]{:S(2)}, u32[]{:S(2)}) %collective-permute-start.20) | collective-permute-done | bytes 278560 | tf_op jit(solution)/shard_map/ppermute | solution.py:53
  62.7 0.0 collective-permute-start.21
  62.7 0.0 collective-permute-done.13.refs_1_
  62.7 1.9 %potentials.1 = (f32[4,128,128]{2,1,0:T(8,128)S(1)}, f32[4,128,128]{2,1,0:T(8,128)S(1)}, f32[4,128,128]{2,1,0:T(8,128)S(1)}, f32[4,128,128]{2,1,0:T(8,128)S(1)}) custom-call(f32[512,128]{1,0:T(8,128)S(1)} %pad_maximum_fusion.2.refs_0_, f32[512,128]{1,0:T(8,128)S(1)} %collective-permute-done.13.refs_1_, bf16[1024,1024]{1,0:T(8,128)(2,1)S(1)} %get-tuple-element.44.refs_2_, ...), custom_call_target="tpu_custom_call" | custom-call | flops 1610612736 | bytes 8388608 | tf_op jit(solution)/shard_map/potentials/pallas_call | solution.py:271
  64.6 0.0 copy-start.1
  64.6 0.0 copy-start.3
  64.7 0.0 copy-start.4
  64.7 0.0 copy-start.8
  64.7 0.6 collective-permute-start.22
  65.3 0.3 collective-permute-start.23
  65.5 2.7 %collective-permute-start.24 = (f32[4,128,128]{2,1,0:T(8,128)S(1)}, f32[4,128,128]{2,1,0:T(8,128)S(1)}, u32[]{:S(2)}, u32[]{:S(2)}) collective-permute-start(f32[4,128,128]{2,1,0:T(8,128)S(1)} %get-tuple-element.58), channel_id=1, source_target_pairs={{0,12},{4,8},{8,4},{12,0},{1,13},{5,9},{9,5},{13,1},{2,14},{6,10},... | collective-permute-start | bytes 786440 | tf_op jit(solution)/shard_map/ppermute | solution.py:31
  68.2 0.0 collective-permute-done.19.refs_5_
  68.3 19.1 %messages.3.refs_3_ = f32[4,128,128]{2,1,0:T(8,128)S(1)} custom-call(s32[7,8]{1,0:T(8,128)S(1)} %copy-done.12, f32[4,136,128]{2,1,0:T(8,128)S(1)} %pack.1.block_ref.own_ref.refs_0_, f32[8,128]{1,0:T(8,128)S(1)} %copy-done.11, f32[128,128]{1,0:T(8,128)S(1)} %copy-done.9, f32[4,136,128]{2,1,0:T(8,128)S(1)} %collective-permute-done.14.refs_0_, ...), custom_call_target="tpu_custom_call" | custom-call | flops 9663676416 | bytes 1048576 | tf_op jit(solution)/shard_map/messages/pallas_call | solution.py:406
  87.4 0.0 collective-permute-done.23.refs_6_
  87.4 0.0 collective-permute-done.24.refs_7_
  87.4 2.0 %atom_mlp.1 = f32[4,128,128]{2,1,0:T(8,128)} custom-call(s32[2,1,2]{2,1,0:T(1,128)S(1)} %bitcast.13, f32[4,128,128]{2,1,0:T(8,128)S(1)} %bitcast.10, f32[4,128,128]{2,1,0:T(8,128)S(1)} %messages.2.refs_2_, f32[4,128,128]{2,1,0:T(8,128)S(1)} %messages.3.refs_3_, f32[4,128,128]{2,1,0:T(8,128)S(1)} %get-tuple-element.55.refs_4_, ...), custom_call_target="tpu_custom_call" | custom-call | tf_op jit(solution)/shard_map/atom_mlp/pallas_call | solution.py:470
  (31 shorter events, 0.3 us)
Async XLA Ops:
  0.0 0.9 %copy-start = (f32[2,2,1,128,128]{4,3,2,1,0:T(8,128)S(1)}, f32[2,2,1,128,128]{4,3,2,1,0:T(8,128)}, u32[]{:S(2)}) copy-start(f32[2,2,1,128,128]{4,3,2,1,0:T(8,128)} %param.12) | copy-start | bytes 786436
  1.0 0.7 copy-start.6
  1.6 0.7 copy-start.7
  2.9 12.6 %collective-permute-start.2 = (f32[4,136,128]{2,1,0:T(8,128)S(1)}, f32[4,136,128]{2,1,0:T(8,128)S(1)}, u32[]{:S(2)}, u32[]{:S(2)}) collective-permute-start(f32[4,136,128]{2,1,0:T(8,128)S(1)} %pack.1.block_ref.own_ref.refs_0_), channel_id=1, source_target_pairs={{0,4},{4,0},{8,12},{12,8},{1,5},{5,1},{9,13},{13,9},{2,6},{6,2},{1... | collective-permute-start | bytes 835592 | tf_op jit(solution)/shard_map/ppermute | solution.py:31
  5.9 14.1 %collective-permute-start.1 = (f32[4,136,128]{2,1,0:T(8,128)S(1)}, f32[4,136,128]{2,1,0:T(8,128)S(1)}, u32[]{:S(2)}, u32[]{:S(2)}) collective-permute-start(f32[4,136,128]{2,1,0:T(8,128)S(1)} %pack.1.block_ref.own_ref.refs_0_), channel_id=1, source_target_pairs={{0,8},{4,12},{8,0},{12,4},{1,9},{5,13},{9,1},{13,5},{2,10},{6,14},... | collective-permute-start | bytes 835592 | tf_op jit(solution)/shard_map/ppermute | solution.py:31
  7.4 15.8 %collective-permute-start = (f32[4,136,128]{2,1,0:T(8,128)S(1)}, f32[4,136,128]{2,1,0:T(8,128)S(1)}, u32[]{:S(2)}, u32[]{:S(2)}) collective-permute-start(f32[4,136,128]{2,1,0:T(8,128)S(1)} %pack.1.block_ref.own_ref.refs_0_), channel_id=1, source_target_pairs={{0,12},{4,8},{8,4},{12,0},{1,13},{5,9},{9,5},{13,1},{2,14},{6,10},... | collective-permute-start | bytes 835592 | tf_op jit(solution)/shard_map/ppermute | solution.py:31
  7.5 19.7 %collective-permute-start.16 = (f32[4,136,128]{2,1,0:T(8,128)S(1)}, f32[4,136,128]{2,1,0:T(8,128)S(1)}, u32[]{:S(2)}, u32[]{:S(2)}) collective-permute-start(f32[4,136,128]{2,1,0:T(8,128)S(1)} %pack.1.block_ref.own_ref.refs_0_), channel_id=1, source_target_pairs={{0,3},{1,2},{2,1},{3,0},{4,7},{5,6},{6,5},{7,4},{8,11},{9,10},{10,... | collective-permute-start | bytes 835592 | tf_op jit(solution)/shard_map/ppermute | solution.py:53
  11.5 20.9 %collective-permute-start.4 = (f32[4,136,128]{2,1,0:T(8,128)S(1)}, f32[4,136,128]{2,1,0:T(8,128)S(1)}, u32[]{:S(2)}, u32[]{:S(2)}) collective-permute-start(f32[4,136,128]{2,1,0:T(8,128)S(1)} %pack.1.block_ref.own_ref.refs_0_), channel_id=1, source_target_pairs={{0,16},{16,0},{1,17},{17,1},{2,18},{18,2},{3,19},{19,3},{4,20},{20... | collective-permute-start | bytes 835592 | tf_op jit(solution)/shard_map/ppermute | solution.py:31
  11.5 0.8 copy-start.10
  15.5 11.7 %collective-permute-start.14 = (f32[4,136,128]{2,1,0:T(8,128)S(1)}, f32[4,136,128]{2,1,0:T(8,128)S(1)}, u32[]{:S(2)}, u32[]{:S(2)}) collective-permute-start(f32[4,136,128]{2,1,0:T(8,128)S(1)} %pack.1.block_ref.own_ref.refs_0_), channel_id=1, source_target_pairs={{0,1},{1,0},{2,3},{3,2},{4,5},{5,4},{6,7},{7,6},{8,9},{9,8},{10,11... | collective-permute-start | bytes 835592 | tf_op jit(solution)/shard_map/ppermute | solution.py:53
  20.0 12.7 %copy-start.9 = (f32[128,128]{1,0:T(8,128)S(1)}, f32[128,128]{1,0:T(8,128)}, u32[]{:S(2)}) copy-start(f32[128,128]{1,0:T(8,128)} %value_ref.1) | copy-start | bytes 196612
  20.0 12.7 %copy-start.11 = (f32[8,128]{1,0:T(8,128)S(1)}, f32[8,128]{1,0:T(8,128)}, u32[]{:S(2)}) copy-start(f32[8,128]{1,0:T(8,128)} %mix_ref.3) | copy-start | bytes 12292
  20.0 12.7 %copy-start.13 = (s32[7,4]{1,0:T(8,128)S(1)}, s32[7,4]{1,0:T(8,128)}, u32[]{:S(2)}) copy-start(s32[7,4]{1,0:T(8,128)} %constant.47.clone.step_ref) | copy-start | bytes 340
  26.5 1.6 %collective-permute-start.3 = (f32[512,128]{1,0:T(8,128)S(1)}, f32[512,128]{1,0:T(8,128)S(1)}, u32[]{:S(2)}, u32[]{:S(2)}) collective-permute-start(f32[512,128]{1,0:T(8,128)S(1)} %get-tuple-element.39), channel_id=1, source_target_pairs={{0,16},{16,0},{1,17},{17,1},{2,18},{18,2},{3,19},{19,3},{4,20},{20... | collective-permute-start | bytes 786440 | tf_op jit(solution)/shard_map/ppermute | solution.py:31
  26.6 6.1 %collective-permute-start.5 = (f32[4,136,128]{2,1,0:T(8,128)S(1)}, f32[4,136,128]{2,1,0:T(8,128)S(1)}, u32[]{:S(2)}, u32[]{:S(2)}) collective-permute-start(f32[4,136,128]{2,1,0:T(8,128)S(1)} %collective-permute-done.2.block_ref.refs_2_), channel_id=1, source_target_pairs={{0,16},{16,0},{1,17},{17,1},{2,18},{18,2},{3,19},{19,3},{4,20},{20... | collective-permute-start | bytes 835592 | tf_op jit(solution)/shard_map/ppermute | solution.py:31
  27.1 5.6 %collective-permute-start.6 = (f32[4,136,128]{2,1,0:T(8,128)S(1)}, f32[4,136,128]{2,1,0:T(8,128)S(1)}, u32[]{:S(2)}, u32[]{:S(2)}) collective-permute-start(f32[4,136,128]{2,1,0:T(8,128)S(1)} %collective-permute-done.block_ref.refs_4_), channel_id=1, source_target_pairs={{0,16},{16,0},{1,17},{17,1},{2,18},{18,2},{3,19},{19,3},{4,20},{20... | collective-permute-start | bytes 835592 | tf_op jit(solution)/shard_map/ppermute | solution.py:31
  28.2 15.5 %collective-permute-start.7 = (f32[128,128]{1,0:T(8,128)S(1)}, f32[128,128]{1,0:T(8,128)S(1)}, u32[]{:S(2)}, u32[]{:S(2)}) collective-permute-start(f32[128,128]{1,0:T(8,128)S(1)} %get-tuple-element.71), channel_id=1, source_target_pairs={{0,1},{1,0},{2,3},{3,2},{4,5},{5,4},{6,7},{7,6},{8,9},{9,8},{10,11... | collective-permute-start | bytes 196616 | tf_op jit(solution)/shard_map/ppermute | solution.py:31
  29.9 13.9 %collective-permute-start.8 = (f32[128,128]{1,0:T(8,128)S(1)}, f32[128,128]{1,0:T(8,128)S(1)}, u32[]{:S(2)}, u32[]{:S(2)}) collective-permute-start(f32[128,128]{1,0:T(8,128)S(1)} %get-tuple-element.70), channel_id=1, source_target_pairs={{0,2},{1,3},{2,0},{3,1},{4,6},{5,7},{6,4},{7,5},{8,10},{9,11},{10,... | collective-permute-start | bytes 196616 | tf_op jit(solution)/shard_map/ppermute | solution.py:31
  32.4 11.3 %copy-start.2 = (f32[2048,128]{1,0:T(8,128)S(1)}, f32[2048,128]{1,0:T(8,128)}, u32[]{:S(2)}) copy-start(f32[2048,128]{1,0:T(8,128)} %refs_5_.1) | copy-start | bytes 3145732
  32.4 11.3 %copy-start.5 = (f32[128,128]{1,0:T(8,128)S(1)}, f32[128,128]{1,0:T(8,128)}, u32[]{:S(2)}) copy-start(f32[128,128]{1,0:T(8,128)} %refs_4_) | copy-start | bytes 196612
  32.5 11.3 %collective-permute-start.9 = (f32[128,128]{1,0:T(8,128)S(1)}, f32[128,128]{1,0:T(8,128)S(1)}, u32[]{:S(2)}, u32[]{:S(2)}) collective-permute-start(f32[128,128]{1,0:T(8,128)S(1)} %get-tuple-element.69), channel_id=1, source_target_pairs={{0,3},{1,2},{2,1},{3,0},{4,7},{5,6},{6,5},{7,4},{8,11},{9,10},{10,... | collective-permute-start | bytes 196616 | tf_op jit(solution)/shard_map/ppermute | solution.py:31
  44.0 4.4 %collective-permute-start.10 = (f32[128,128]{1,0:T(8,128)S(1)}, f32[128,128]{1,0:T(8,128)S(1)}, u32[]{:S(2)}, u32[]{:S(2)}) collective-permute-start(f32[128,128]{1,0:T(8,128)S(1)} %filter.1), channel_id=1, source_target_pairs={{0,1},{1,0},{2,3},{3,2},{4,5},{5,4},{6,7},{7,6},{8,9},{9,8},{10,11... | collective-permute-start | bytes 196616 | tf_op jit(solution)/shard_map/ppermute | solution.py:31
  44.8 6.7 %collective-permute-start.12 = (f32[128,128]{1,0:T(8,128)S(1)}, f32[128,128]{1,0:T(8,128)S(1)}, u32[]{:S(2)}, u32[]{:S(2)}) collective-permute-start(f32[128,128]{1,0:T(8,128)S(1)} %filter.1), channel_id=1, source_target_pairs={{0,3},{1,2},{2,1},{3,0},{4,7},{5,6},{6,5},{7,4},{8,11},{9,10},{10,... | collective-permute-start | bytes 196616 | tf_op jit(solution)/shard_map/ppermute | solution.py:31
  47.8 6.3 %collective-permute-start.11 = (f32[128,128]{1,0:T(8,128)S(1)}, f32[128,128]{1,0:T(8,128)S(1)}, u32[]{:S(2)}, u32[]{:S(2)}) collective-permute-start(f32[128,128]{1,0:T(8,128)S(1)} %filter.1), channel_id=1, source_target_pairs={{0,2},{1,3},{2,0},{3,1},{4,6},{5,7},{6,4},{7,5},{8,10},{9,11},{10,... | collective-permute-start | bytes 196616 | tf_op jit(solution)/shard_map/ppermute | solution.py:31
  48.4 9.7 %collective-permute-start.18 = (f32[4,136,128]{2,1,0:T(8,128)S(1)}, f32[4,136,128]{2,1,0:T(8,128)S(1)}, u32[]{:S(2)}, u32[]{:S(2)}) collective-permute-start(f32[4,136,128]{2,1,0:T(8,128)S(1)} %get-tuple-element.60), channel_id=1, source_target_pairs={{0,4},{4,0},{8,12},{12,8},{1,5},{5,1},{9,13},{13,9},{2,6},{6,2},{1... | collective-permute-start | bytes 835592 | tf_op jit(solution)/shard_map/ppermute | solution.py:53
  49.0 13.8 %collective-permute-start.20 = (f32[4,136,128]{2,1,0:T(8,128)S(1)}, f32[4,136,128]{2,1,0:T(8,128)S(1)}, u32[]{:S(2)}, u32[]{:S(2)}) collective-permute-start(f32[4,136,128]{2,1,0:T(8,128)S(1)} %get-tuple-element.59), channel_id=1, source_target_pairs={{0,12},{4,8},{8,4},{12,0},{1,13},{5,9},{9,5},{13,1},{2,14},{6,10},... | collective-permute-start | bytes 835592 | tf_op jit(solution)/shard_map/ppermute | solution.py:53
  54.1 8.7 %collective-permute-start.13 = (f32[512,128]{1,0:T(8,128)S(1)}, f32[512,128]{1,0:T(8,128)S(1)}, u32[]{:S(2)}, u32[]{:S(2)}) collective-permute-start(f32[512,128]{1,0:T(8,128)S(1)} %pad_maximum_fusion.2.refs_0_), channel_id=1, source_target_pairs={{0,16},{16,0},{1,17},{17,1},{2,18},{18,2},{3,19},{19,3},{4,20},{20... | collective-permute-start | bytes 786440 | tf_op jit(solution)/shard_map/ppermute | solution.py:31
  54.2 11.1 %collective-permute-start.15 = (f32[4,136,128]{2,1,0:T(8,128)S(1)}, f32[4,136,128]{2,1,0:T(8,128)S(1)}, u32[]{:S(2)}, u32[]{:S(2)}) collective-permute-start(f32[4,136,128]{2,1,0:T(8,128)S(1)} %collective-permute-done.14.refs_0_), channel_id=1, source_target_pairs={{0,16},{16,0},{1,17},{17,1},{2,18},{18,2},{3,19},{19,3},{4,20},{20... | collective-permute-start | bytes 835592 | tf_op jit(solution)/shard_map/ppermute | solution.py:31
  54.7 10.9 %collective-permute-start.17 = (f32[4,136,128]{2,1,0:T(8,128)S(1)}, f32[4,136,128]{2,1,0:T(8,128)S(1)}, u32[]{:S(2)}, u32[]{:S(2)}) collective-permute-start(f32[4,136,128]{2,1,0:T(8,128)S(1)} %collective-permute-done.16.refs_2_), channel_id=1, source_target_pairs={{0,16},{16,0},{1,17},{17,1},{2,18},{18,2},{3,19},{19,3},{4,20},{20... | collective-permute-start | bytes 835592 | tf_op jit(solution)/shard_map/ppermute | solution.py:31
  58.1 10.2 %collective-permute-start.19 = (f32[4,136,128]{2,1,0:T(8,128)S(1)}, f32[4,136,128]{2,1,0:T(8,128)S(1)}, u32[]{:S(2)}, u32[]{:S(2)}) collective-permute-start(f32[4,136,128]{2,1,0:T(8,128)S(1)} %collective-permute-done.18.refs_4_), channel_id=1, source_target_pairs={{0,16},{16,0},{1,17},{17,1},{2,18},{18,2},{3,19},{19,3},{4,20},{20... | collective-permute-start | bytes 835592 | tf_op jit(solution)/shard_map/ppermute | solution.py:31
  62.7 5.5 %collective-permute-start.21 = (f32[4,136,128]{2,1,0:T(8,128)S(1)}, f32[4,136,128]{2,1,0:T(8,128)S(1)}, u32[]{:S(2)}, u32[]{:S(2)}) collective-permute-start(f32[4,136,128]{2,1,0:T(8,128)S(1)} %collective-permute-done.20.refs_6_), channel_id=1, source_target_pairs={{0,16},{16,0},{1,17},{17,1},{2,18},{18,2},{3,19},{19,3},{4,20},{20... | collective-permute-start | bytes 835592 | tf_op jit(solution)/shard_map/ppermute | solution.py:31
  62.7 5.5 %copy-start.12 = (s32[7,8]{1,0:T(8,128)S(1)}, s32[7,8]{1,0:T(8,128)}, u32[]{:S(2)}) copy-start(s32[7,8]{1,0:T(8,128)} %constant.48.clone.step_ref) | copy-start | bytes 676
  64.6 22.8 %copy-start.1 = (f32[2,2,1,128,128]{4,3,2,1,0:T(8,128)S(1)}, f32[2,2,1,128,128]{4,3,2,1,0:T(8,128)}, u32[]{:S(2)}) copy-start(f32[2,2,1,128,128]{4,3,2,1,0:T(8,128)} %param.12) | copy-start | bytes 786436
  64.6 22.8 %copy-start.3 = (f32[128,256]{1,0:T(8,128)S(1)}, f32[128,256]{1,0:T(8,128)}, u32[]{:S(2)}) copy-start(f32[128,256]{1,0:T(8,128)} %refs_8_.1) | copy-start | bytes 393220
  64.7 22.8 %copy-start.4 = (f32[256,128]{1,0:T(8,128)S(1)}, f32[256,128]{1,0:T(8,128)}, u32[]{:S(2)}) copy-start(f32[256,128]{1,0:T(8,128)} %refs_9_.1) | copy-start | bytes 393220
  64.7 22.8 %copy-start.8 = (s32[2,2,1]{1,2,0:T(1,128)S(1)}, s32[2,2,1]{1,2,0:T(1,128)}, u32[]{:S(2)}) copy-start(s32[2,2,1]{1,2,0:T(1,128)} %param.14) | copy-start | bytes 52
  64.7 22.7 %collective-permute-start.22 = (f32[4,128,128]{2,1,0:T(8,128)S(1)}, f32[4,128,128]{2,1,0:T(8,128)S(1)}, u32[]{:S(2)}, u32[]{:S(2)}) collective-permute-start(f32[4,128,128]{2,1,0:T(8,128)S(1)} %get-tuple-element.56), channel_id=1, source_target_pairs={{0,4},{4,0},{8,12},{12,8},{1,5},{5,1},{9,13},{13,9},{2,6},{6,2},{1... | collective-permute-start | bytes 786440 | tf_op jit(solution)/shard_map/ppermute | solution.py:31
  65.3 22.1 %collective-permute-start.23 = (f32[4,128,128]{2,1,0:T(8,128)S(1)}, f32[4,128,128]{2,1,0:T(8,128)S(1)}, u32[]{:S(2)}, u32[]{:S(2)}) collective-permute-start(f32[4,128,128]{2,1,0:T(8,128)S(1)} %get-tuple-element.57), channel_id=1, source_target_pairs={{0,8},{4,12},{8,0},{12,4},{1,9},{5,13},{9,1},{13,5},{2,10},{6,14},... | collective-permute-start | bytes 786440 | tf_op jit(solution)/shard_map/ppermute | solution.py:31
  65.5 21.8 %collective-permute-start.24 = (f32[4,128,128]{2,1,0:T(8,128)S(1)}, f32[4,128,128]{2,1,0:T(8,128)S(1)}, u32[]{:S(2)}, u32[]{:S(2)}) collective-permute-start(f32[4,128,128]{2,1,0:T(8,128)S(1)} %get-tuple-element.58), channel_id=1, source_target_pairs={{0,12},{4,8},{8,4},{12,0},{1,13},{5,9},{9,5},{13,1},{2,14},{6,10},... | collective-permute-start | bytes 786440 | tf_op jit(solution)/shard_map/ppermute | solution.py:31

commit v4 on v3

--- a/solution.py
+++ b/solution.py
@@ -77,29 +77,43 @@
     return cell // (shape[1] * shape[2]), cell // shape[2] % shape[1], cell % shape[2]
 
 
-def pack_kernel(shape, grid, counts_ref, feature_ref, position_ref, out_ref):
+def pack_kernel(shape, grid, counts_hbm, feature_hbm, position_hbm, out_ref, counts_ref, feature_ref, position_ref, sems):
     cells, channels, slots = feature_ref.shape
+    copies = [
+        pltpu.make_async_copy(counts_hbm, counts_ref, sems.at[0]),
+        pltpu.make_async_copy(position_hbm, position_ref, sems.at[1]),
+        pltpu.make_async_copy(feature_hbm, feature_ref, sems.at[2]),
+    ]
+    for copy in copies:
+        copy.start()
+    for copy in copies:
+        copy.wait()
     slot = lax.broadcasted_iota(jnp.int32, (channels, slots), 1)
-    blank = jnp.zeros((2, slots), f32)
-    base = [lax.axis_index(axis) * here for axis, here in zip(("gx", "gy", "gz"), shape)]
     for cell in range(cells):
-        x, y, z = place_of(cell, shape)
-        held = slot < counts_ref[x, z, y]
+        place = place_of(cell, shape)
+        held = slot < counts_ref[place[0], place[2], place[1]]
         out_ref[cell, :channels, :] = jnp.where(held, feature_ref[cell], 0.0)
         at = [position_ref[3 * cell + axis] for axis in range(3)]
         rows = list(at)
-        for axis, offset in enumerate((x, y, z)):
-            rows.append((at[axis] + (base[axis] + offset).astype(f32)) * (1.0 / grid[axis]))
-        out_ref[cell, channels:, :] = jnp.concatenate(rows + [blank], axis=0)
+        for axis, name in enumerate(("gx", "gy", "gz")):
+            here = lax.axis_index(name) * shape[axis] + place[axis]
+            rows.append((at[axis] + here.astype(f32)) * (1.0 / grid[axis]))
+        out_ref[cell, channels:, :] = jnp.concatenate(rows + [jnp.zeros((2, slots), f32)], axis=0)
 
 
 def pack(shape, grid, counts, features, positions):
     cells, channels, slots = features.shape
     return pl.pallas_call(
         functools.partial(pack_kernel, shape, grid),
-        in_specs=[pl.BlockSpec(memory_space=pltpu.SMEM), whole(), whole()],
+        in_specs=[pl.BlockSpec(memory_space=pltpu.HBM)] * 3,
         out_specs=whole(),
         out_shape=jax.ShapeDtypeStruct((cells, channels + 8, slots), f32),
+        scratch_shapes=[
+            pltpu.SMEM(counts.shape, jnp.int32),
+            pltpu.VMEM(features.shape, f32),
+            pltpu.VMEM(positions.shape, f32),
+            pltpu.SemaphoreType.DMA((3,)),
+        ],
         compiler_params=params(),
         name="pack",
     )(counts, features, positions)
@@ -111,8 +125,8 @@
     return [float(c) for c in solved]
 
 
-SIN = fitted(lambda u: 2.0 * np.sin(np.pi * u) / u, 5)
-COS = fitted(lambda u: np.cos(np.pi * u), 5)
+SIN = fitted(lambda u: math.sqrt(2.0) * np.sin(np.pi * u) / u, 5)
+COS = fitted(lambda u: math.sqrt(2.0) * np.cos(np.pi * u), 5)
 
 
 def poly(coefficients, t):
@@ -125,9 +139,9 @@
 def turns(u):
     u = u - jnp.round(u)
     t = u * u
-    twice_sine = poly(SIN, t) * u
+    sine = poly(SIN, t) * u
     cosine = poly(COS, t)
-    return 1.0 - 0.5 * twice_sine * twice_sine, twice_sine * cosine
+    return 1.0 - sine * sine, sine * cosine
 
 
 def factor_kernel(parts, chunk, first, waves_ref, block_ref, *refs):
@@ -165,26 +179,18 @@
             high, low = split(sine)
             wave_ref[pl.ds(row + chunk, chunk), at : at + slots] = high
             wave_ref[pl.ds(row + chunk, chunk), span + at : span + at + slots] = low
+        return carry
+
+    lax.fori_loop(0, total // chunk, some, 0)
+    half = 2 * total // parts
+    for n in range(parts):
+        row = pl.multiple_of(lax.rem(at_x + n, parts) * half, half)
         both = lax.dot_general(
-            wave_ref[pl.ds(row, 2 * chunk), :], weight_ref[...], (((1,), (1,)), ((), ())),
+            wave_ref[pl.ds(row, half), :], weight_ref[...], (((1,), (1,)), ((), ())),
             preferred_element_type=f32,
         )
         both = both[:, :channels] + both[:, channels:]
-        per_part = total // chunk // parts
-        part = lax.rem(j // per_part - at_x + parts, parts)
-        row = pl.multiple_of(lax.rem(j, per_part) * 2 * chunk, 2 * chunk)
-        for n in range(parts):
-
-            @pl.when(part == n)
-            def _(n=n):
-                if first:
-                    after[n][pl.ds(row, 2 * chunk), :] = both
-                else:
-                    after[n][pl.ds(row, 2 * chunk), :] = before[n][pl.ds(row, 2 * chunk), :] + both
-
-        return carry
-
-    lax.fori_loop(0, total // chunk, some, 0)
+        after[n][...] = both if first else before[n][...] + both
 
 
 def partial_factors(waves, total, chunk, block, before, parts):
@@ -287,11 +293,14 @@
 
 
 def message_kernel(
-    basis, sources, table, own_plane, step_ref, own_ref, mix_ref, value_ref, *refs
+    basis, sources, table, last, step_ref, own_ref, mix_ref, value_ref, *refs
 ):
-    blocks, out_ref = refs[:sources], refs[sources]
-    cell_ref, at_ref, own_col_ref, acc_ref, mixed_ref = refs[sources + 1 : sources + 6]
-    left_0, left_1, left_2, right_0, right_1, right_2 = refs[sources + 6 :]
+    blocks, refs = refs[:sources], refs[sources:]
+    if last:
+        before_ref, out_ref, cell_ref, at_ref, own_col_ref, acc_ref, mixed_ref, wide_ref = refs[:8]
+    else:
+        out_ref, cell_ref, at_ref, own_col_ref, acc_ref = refs[:5]
+    left_0, left_1, left_2, right_0, right_1, right_2 = refs[-6:]
     count = step_ref.shape[1]
     cells = own_ref.shape[0]
     slots = own_ref.shape[-1]
@@ -311,7 +320,7 @@
                 cell_ref[n, :channels, :] = high
                 cell_ref[n, channels:, :] = low
                 at_ref[n] = block[channels:]
-    for b in range(basis):
+    for b in range(basis) if last else ():
         high, low = split(value_ref[...] * (mix_ref[b : b + 1, :] * math.exp(-b * b)))
         mixed_ref[b * channels : (b + 1) * channels, :channels] = high
         mixed_ref[b * channels : (b + 1) * channels, channels:] = low
@@ -324,7 +333,7 @@
         place_x = step_ref[0, step] + 1 + (move - 1)
         place_y = step_ref[1, step]
         plane = step_ref[2, step]
-        if not own_plane:
+        if last:
             plane = jnp.where(is_even("gz"), plane, 1 - plane)
         shift_z = step_ref[3, step].astype(f32)
         left, right = lefts[move], rights[move]
@@ -352,7 +361,7 @@
                 envelope = jnp.maximum(1.0 - squared, 0.0)
                 term = envelope * envelope * jnp.exp2(squared * (-float((basis - 1) ** 2) * LOG2E))
                 ratio = jnp.exp2(distance * (2.0 * (basis - 1) * LOG2E))
-                if own_plane and move == 1 and n == 1:
+                if not last and move == 1 and n == 1:
                     i = lax.broadcasted_iota(jnp.int32, (tile, slots), 0) + at
                     j = lax.broadcasted_iota(jnp.int32, (tile, slots), 1)
                     same = jnp.logical_and(i == j, step_ref[3, step] == 0)
@@ -370,60 +379,73 @@
             lefts[move][...], rights[move][...], (((1,), (1,)), ((), ())), preferred_element_type=f32
         )
 
-    def finish(own):
-        gathered = acc_ref[:, :channels] + acc_ref[:, channels:]
-        wide = jnp.concatenate([gathered[b * slots : (b + 1) * slots] for b in range(basis)], axis=1)
-        high, low = split(wide)
-        both = jnp.dot(high, mixed_ref[...], preferred_element_type=f32)
-        both = both + jnp.dot(low, mixed_ref[...], preferred_element_type=f32)
-        out_ref[own] = (both[:, :channels] + both[:, channels:]).T
-
     fill(0, 0)
 
     def visit(step, carry):
+        own = step_ref[4, step]
         fresh = step_ref[5, step] == 1
-        acc_ref[...] = jnp.where(fresh, 0.0, acc_ref[...]) + product(0)
+        acc_ref[own] = jnp.where(fresh, 0.0, acc_ref[own]) + product(0)
         fill(step, 1)
-        acc_ref[...] += product(1)
+        acc_ref[own] += product(1)
         fill(step, 2)
-        acc_ref[...] += product(2)
+        acc_ref[own] += product(2)
         fill(jnp.minimum(step + 1, count - 1), 0)
-
-        @pl.when(step_ref[6, step] == 1)
-        def _():
-            finish(step_ref[4, step])
-
         return carry
 
     lax.fori_loop(0, count, visit, 0)
-
-
-def pair_messages(steps, own_plane, own, blocks, table, mix, w_value):
+    wide = basis * channels
+    for cell in range(cells):
+        gathered = acc_ref[cell, :, :channels] + acc_ref[cell, :, channels:]
+        if not last:
+            out_ref[cell] = gathered
+            continue
+        high, low = split(gathered + before_ref[cell])
+        here = slice(cell * slots, (cell + 1) * slots)
+        for b in range(basis):
+            wide_ref[here, b * channels : (b + 1) * channels] = high[b * slots : (b + 1) * slots]
+            wide_ref[here, wide + b * channels : wide + (b + 1) * channels] = low[b * slots : (b + 1) * slots]
+    if last:
+        both = jnp.dot(wide_ref[:, :wide], mixed_ref[...], preferred_element_type=f32)
+        both = both + jnp.dot(wide_ref[:, wide:], mixed_ref[...], preferred_element_type=f32)
+        for cell in range(cells):
+            part = both[cell * slots : (cell + 1) * slots]
+            out_ref[cell] = (part[:, :channels] + part[:, channels:]).T
+
+
+def pair_messages(steps, own, blocks, table, mix, w_value, before=None):
     cells, _, slots = own.shape
     basis, channels = mix.shape
     around = len(table) * len(table[0]) * len(table[0][0])
     count = steps.shape[1]
+    last = before is not None
+    sums = (cells, basis * slots, channels)
+    closing = [
+        pltpu.VMEM((basis * channels, 2 * channels), bf16),
+        pltpu.VMEM((cells * slots, 2 * basis * channels), bf16),
+    ]
     return pl.pallas_call(
-        functools.partial(message_kernel, basis, len(blocks), table, own_plane),
-        in_specs=[pl.BlockSpec(memory_space=pltpu.SMEM)] + [whole()] * (3 + len(blocks)),
+        functools.partial(message_kernel, basis, len(blocks), table, last),
+        in_specs=[pl.BlockSpec(memory_space=pltpu.SMEM)] + [whole()] * (3 + len(blocks) + last),
         out_specs=whole(),
         scratch_shapes=[
             pltpu.VMEM((around, 2 * channels, slots), bf16),
             pltpu.VMEM((around, 8, slots), f32),
             pltpu.VMEM((cells, 3, slots, slots), f32),
-            pltpu.VMEM((basis * slots, 2 * channels), f32),
-            pltpu.VMEM((basis * channels, 2 * channels), bf16),
+            pltpu.VMEM((cells, basis * slots, 2 * channels), f32),
         ]
+        + closing * last
         + [pltpu.VMEM((basis * slots, 6 * slots), bf16)] * 3
         + [pltpu.VMEM((2 * channels, 6 * slots), bf16)] * 3,
-        out_shape=jax.ShapeDtypeStruct((cells, channels, slots), f32),
+        out_shape=jax.ShapeDtypeStruct((cells, channels, slots) if last else sums, f32),
         compiler_params=params(),
         cost_estimate=pl.CostEstimate(
             flops=count * 8 * basis * slots * 9 * slots * channels, bytes_accessed=1 << 20,
             transcendentals=0,
         ),
         name="messages",
-    )(steps, own, mix, w_value, *blocks)
+    )(steps, own, mix, w_value, *blocks, *([before] if last else []))
+
+
 def visits(cells_x, cells_y, cells_z, inside):
     table = []
     for x in range(cells_x):
@@ -445,13 +467,13 @@
 
 def mlp_kernel(count, shape, *refs):
     counts_ref, feature_ref = refs[:2]
-    messages = refs[2:4]
-    potentials = refs[4 : 4 + count]
-    hidden_ref, back_ref, out_ref = refs[4 + count :]
+    message_ref = refs[2]
+    potentials = refs[3 : 3 + count]
+    hidden_ref, back_ref, out_ref = refs[3 + count :]
     cells, channels, slots = feature_ref.shape
     columns = []
     for cell in range(cells):
-        mixed = feature_ref[cell] + message_scale * (messages[0][cell] + messages[1][cell])
+        mixed = feature_ref[cell] + message_scale * message_ref[cell]
         for potential in potentials:
             mixed = mixed + potential[cell]
         columns.append(mixed)
@@ -470,12 +492,12 @@
     return pl.pallas_call(
         functools.partial(mlp_kernel, len(potentials), shape),
         in_specs=[pl.BlockSpec(memory_space=pltpu.SMEM)]
-        + [whole()] * (5 + len(potentials)),
+        + [whole()] * (4 + len(potentials)),
         out_specs=whole(),
         out_shape=jax.ShapeDtypeStruct(features.shape, f32),
         compiler_params=params(),
         name="atom_mlp",
-    )(counts, features, *messages, *potentials, w_hidden, w_out)
+    )(counts, features, messages, *potentials, w_hidden, w_out)
 
 
 def next_in_x(block, shape):
@@ -549,6 +571,13 @@
         for n in range(2, size_x):
             to = jnp.where(lax.rem(other - at_x + size_x, size_x) == n, parts[n], to)
         summed = summed + exchange(to, "gx", s)
+    low, high = (
+        jnp.concatenate(
+            [side[n : n + 1] for n in range(y, cells_x * cells_y, cells_y) for side in sides], axis=0
+        )
+        for y in (0, cells_y - 1)
+    )
+    edges = neighbours(low, high, "gy")
     value_near, summed = lax.optimization_barrier((w_value, summed))
     pieces = [lax.dynamic_slice_in_dim(summed, at_z * piece, piece, 0)]
     for s in range(1, size_z):
@@ -588,27 +617,19 @@
         for x in range(-1, cells_x + 1)
     ]
     inner = jnp.asarray(visits(cells_x, cells_y, cells_z, True))
-    near = pair_messages(inner, True, own, sources.arrays, table, radial_mix, value_near)
+    near = pair_messages(inner, own, sources.arrays, table, radial_mix, value_near)
 
     scale = 1.0 / math.sqrt(grid[0] * grid[1] * grid[2] * slots) / math.sqrt(total_waves)
     rank = at_x * size_z + at_z
     block = at_y * (share // chunk) + (rank * piece) // (2 * chunk)
-    charge, near = lax.optimization_barrier((w_charge, near))
+    charge, near, *edges = lax.optimization_barrier((w_charge, near, *edges))
     filtered = filtered_piece(scale, block.reshape(1), chunk, pieces, charge, filter_table)
 
-    held_z = [filtered] + [exchange(filtered, "gz", s) for s in range(1, size_z)]
-    started = held_z[min(1, size_z - 1)]
-    held_z = jnp.concatenate(held_z, axis=0)
+    held_z = jnp.concatenate(
+        [filtered] + [exchange(filtered, "gz", s) for s in range(1, size_z)], axis=0
+    )
     held = [held_z] + [exchange(held_z, "gx", s) for s in range(1, size_x)]
 
-    low, high = (
-        jnp.concatenate(
-            [side[n : n + 1] for n in range(y, cells_x * cells_y, cells_y) for side in sides], axis=0
-        )
-        for y in (0, cells_y - 1)
-    )
-    low, high, started = lax.optimization_barrier((low, high, started))
-    edges = neighbours(low, high, "gy")
     sources = Sources()
     flat = (cells_x, cells_y, 1)
     side_columns = [sources.columns(side, flat) for side in sides]
@@ -636,10 +657,10 @@
     value_far, *found = lax.optimization_barrier((w_value, *found))
     returned = [found[0]] + [exchange(found[s], "gy", s) for s in range(1, size_y)]
     outer = jnp.asarray(visits(cells_x, cells_y, cells_z, False))
-    far = pair_messages(outer, False, own, sources.arrays, table, radial_mix, value_far)
+    messages = pair_messages(outer, own, sources.arrays, table, radial_mix, value_far, near)
 
     updated = atom_mlp(
-        shape, some_counts, flat_features, [near, far], returned, w_hidden, w_out
+        shape, some_counts, flat_features, messages, returned, w_hidden, w_out
     )
     return updated.reshape(features.shape)
 

time: 89.7 us -> 82.6 us (0.921)
  waiting for transfers between devices: 12.6 us -> 5.46 us
  starting transfers between devices: 25.4 us -> 29.3 us
  Pallas kernels: 47.8 us -> 44 us
    ppermute x4, waiting for transfers between devices: 7.99 us -> 0.01 us  [neighbours(): return (lax.ppermute(first, axis, one), lax.ppermute(second, axis, two))]
    ppermute x4, starting transfers between devices: 7.18 us -> 9.47 us  [neighbours(): return (lax.ppermute(first, axis, one), lax.ppermute(second, axis, two))]
    pallas_call x2, Pallas kernels: 30.1 us -> 28.2 us  [pair_messages(): pl.pallas_call(functools.partial(message_kernel, basis, len(blocks), tabl...]
    pallas_call x4, Pallas kernels: 13 us -> 11.1 us  [partial_factors(): pl.pallas_call(functools.partial(factor_kernel, parts, chunk, not before)...]
    ppermute x21, starting transfers between devices: 18.2 us -> 19.8 us  [exchange(): return lax.ppermute(block, axis, pairs)]
  transfers between devices with their start and end apart: 25 -> 25, of which waited for: 5 -> 4; matrix products, arithmetic and copies ran while one was open for 0% -> 0% of each run, Pallas kernels for 50% -> 50%
where the time goes in v4:
time: 82.6 us; the launch traced here: 82.3 us
  Pallas kernels  44 us (53%)
  starting transfers between devices  29.3 us (35%)
  waiting for transfers between devices  5.46 us (7%)
  local copies, waits for them, and re-layouts  3.2 us (4%)
    pallas_call x2, Pallas kernels, pair_messages(): pl.pallas_call(functools.partial(message_kernel, basis, len(blocks), tabl...  28.2 us
    ppermute x21, starting transfers between devices, exchange(): return lax.ppermute(block, axis, pairs)  19.8 us
    pallas_call x4, Pallas kernels, partial_factors(): pl.pallas_call(functools.partial(factor_kernel, parts, chunk, not before)...  11.1 us
    ppermute x4, starting transfers between devices, neighbours(): return (lax.ppermute(first, axis, one), lax.ppermute(second, axis, two))  9.47 us
    ppermute x21, waiting for transfers between devices, exchange(): return lax.ppermute(block, axis, pairs)  5.45 us
    unnamed x28, local copies, waits for them, and re-layouts  3.13 us
    pallas_call x1, Pallas kernels, atom_mlp(): pl.pallas_call(functools.partial(mlp_kernel, len(potentials), shape), in_...  2 us
    pallas_call x1, Pallas kernels, potentials_of(): pl.pallas_call(functools.partial(potential_kernel, len(held), pieces, len...  1.89 us
  transfers between devices with their start and end apart: 25, of which 4 were waited for; matrix products, arithmetic and copies ran while one was open for 0% of the time, Pallas kernels for 50%

profile of v4, /device:TPU:0, one launch (start us, length us, event | category | flops | bytes accessed | tf_op | source)
XLA Modules:
  0.0 82.3 jit_solution(7136587294567297827)
XLA Ops:
  0.0 0.9 %copy-done.1 = f32[2,2,1,128,128]{4,3,2,1,0:T(8,128)S(1)} copy-done((f32[2,2,1,128,128]{4,3,2,1,0:T(8,128)S(1)}, f32[2,2,1,128,128]{4,3,2,1,0:T(8,128)}, u32[]{:S(2)}) %copy-start.1) | copy-done | bytes 262168
  1.0 0.7 copy-done.6
  1.6 0.7 copy-done.7
  2.3 0.6 pack.1.block_ref.own_ref.refs_0_
  2.9 3.0 %collective-permute-start.2 = (f32[4,136,128]{2,1,0:T(8,128)S(1)}, f32[4,136,128]{2,1,0:T(8,128)S(1)}, u32[]{:S(2)}, u32[]{:S(2)}) collective-permute-start(f32[4,136,128]{2,1,0:T(8,128)S(1)} %pack.1.block_ref.own_ref.refs_0_), channel_id=1, source_target_pairs={{0,4},{4,0},{8,12},{12,8},{1,5},{5,1},{9,13},{13,9},{2,6},{6,2},{1... | collective-permute-start | bytes 835592 | tf_op jit(solution)/shard_map/ppermute | solution.py:31
  5.9 1.5 %collective-permute-start.1 = (f32[4,136,128]{2,1,0:T(8,128)S(1)}, f32[4,136,128]{2,1,0:T(8,128)S(1)}, u32[]{:S(2)}, u32[]{:S(2)}) collective-permute-start(f32[4,136,128]{2,1,0:T(8,128)S(1)} %pack.1.block_ref.own_ref.refs_0_), channel_id=1, source_target_pairs={{0,8},{4,12},{8,0},{12,4},{1,9},{5,13},{9,1},{13,5},{2,10},{6,14},... | collective-permute-start | bytes 835592 | tf_op jit(solution)/shard_map/ppermute | solution.py:31
  7.5 0.0 collective-permute-start
  7.5 2.0 %collective-permute-start.10 = (f32[4,136,128]{2,1,0:T(8,128)S(1)}, f32[4,136,128]{2,1,0:T(8,128)S(1)}, u32[]{:S(2)}, u32[]{:S(2)}) collective-permute-start(f32[4,136,128]{2,1,0:T(8,128)S(1)} %pack.1.block_ref.own_ref.refs_0_), channel_id=1, source_target_pairs={{0,1},{1,0},{2,3},{3,2},{4,5},{5,4},{6,7},{7,6},{8,9},{9,8},{10,11... | collective-permute-start | bytes 835592 | tf_op jit(solution)/shard_map/ppermute | solution.py:53
  9.5 0.0 collective-permute-start.7
  9.5 0.8 copy-done.10
  10.3 2.8 %factors.4 = (f32[512,128]{1,0:T(8,128)S(1)}, f32[512,128]{1,0:T(8,128)S(1)}, bf16[1024,1024]{1,0:T(8,128)(2,1)S(1)}) custom-call(s32[3,2048]{1,0:T(4,128)S(1)} %copy-done.10, f32[4,136,128]{2,1,0:T(8,128)S(1)} %pack.1.block_ref.own_ref.refs_0_), custom_call_target="tpu_custom_call" | custom-call | flops 268435456 | bytes 2097152 | tf_op jit(solution)/shard_map/factors/pallas_call | solution.py:201
  13.0 0.4 collective-permute-done.2.block_ref.refs_2_
  13.4 4.2 %collective-permute-start.11 = (f32[4,136,128]{2,1,0:T(8,128)S(1)}, f32[4,136,128]{2,1,0:T(8,128)S(1)}, u32[]{:S(2)}, u32[]{:S(2)}) collective-permute-start(f32[4,136,128]{2,1,0:T(8,128)S(1)} %pack.1.block_ref.own_ref.refs_0_), channel_id=1, source_target_pairs={{0,3},{1,2},{2,1},{3,0},{4,7},{5,6},{6,5},{7,4},{8,11},{9,10},{10,... | collective-permute-start | bytes 835592 | tf_op jit(solution)/shard_map/ppermute | solution.py:53
  17.6 2.8 %factors.5 = (f32[512,128]{1,0:T(8,128)S(1)}, f32[512,128]{1,0:T(8,128)S(1)}, bf16[1024,1024]{1,0:T(8,128)(2,1)S(1)}) custom-call(s32[3,2048]{1,0:T(4,128)S(1)} %copy-done.10, f32[4,136,128]{2,1,0:T(8,128)S(1)} %collective-permute-done.2.block_ref.refs_2_, f32[512,128]{1,0:T(8,128)S(1)} %get-tuple-element.32.refs_0_, ...), custom_call_target="tpu_custom_call", output_to_operand_aliasing={{0}: (2, {}), {1}: (3, {})} | custom-call | flops 268435456 | bytes 2097152 | tf_op jit(solution)/shard_map/factors/pallas_call | solution.py:201
  20.4 0.0 collective-permute-done.1.block_ref
  20.4 2.8 %factors.6 = (f32[512,128]{1,0:T(8,128)S(1)}, f32[512,128]{1,0:T(8,128)S(1)}, bf16[1024,1024]{1,0:T(8,128)(2,1)S(1)}) custom-call(s32[3,2048]{1,0:T(4,128)S(1)} %copy-done.10, f32[4,136,128]{2,1,0:T(8,128)S(1)} %collective-permute-done.1.block_ref, f32[512,128]{1,0:T(8,128)S(1)} %get-tuple-element.34.refs_0_, ...), custom_call_target="tpu_custom_call", output_to_operand_aliasing={{0}: (2, {}), {1}: (3, {})} | custom-call | flops 268435456 | bytes 2097152 | tf_op jit(solution)/shard_map/factors/pallas_call | solution.py:201
  23.2 0.0 collective-permute-done.block_ref.refs_4_
  23.2 0.0 copy-start.9
  23.2 0.0 copy-start.11
  23.2 0.0 copy-start.13
  23.2 2.8 %factors.7 = (f32[512,128]{1,0:T(8,128)S(1)}, f32[512,128]{1,0:T(8,128)S(1)}, bf16[1024,1024]{1,0:T(8,128)(2,1)S(1)}) custom-call(s32[3,2048]{1,0:T(4,128)S(1)} %copy-done.10, f32[4,136,128]{2,1,0:T(8,128)S(1)} %collective-permute-done.block_ref.refs_4_, f32[512,128]{1,0:T(8,128)S(1)} %get-tuple-element.36.refs_0_, ...), custom_call_target="tpu_custom_call", output_to_operand_aliasing={{0}: (2, {}), {1}: (3, {})} | custom-call | flops 268435456 | bytes 2097152 | tf_op jit(solution)/shard_map/factors/pallas_call | solution.py:201
  26.0 0.1 collective-permute-start.3
  26.1 0.5 collective-permute-start.8
  26.6 0.0 collective-permute-done.10.refs_0_
  26.6 0.1 collective-permute-start.9
  26.7 0.1 fusion
  26.8 1.6 %collective-permute-start.12 = (f32[4,136,128]{2,1,0:T(8,128)S(1)}, f32[4,136,128]{2,1,0:T(8,128)S(1)}, u32[]{:S(2)}, u32[]{:S(2)}) collective-permute-start(f32[4,136,128]{2,1,0:T(8,128)S(1)} %get-tuple-element.60), channel_id=1, source_target_pairs={{0,4},{4,0},{8,12},{12,8},{1,5},{5,1},{9,13},{13,9},{2,6},{6,2},{1... | collective-permute-start | bytes 835592 | tf_op jit(solution)/shard_map/ppermute | solution.py:53
  28.3 0.0 collective-permute-done.3
  28.4 1.7 %collective-permute-start.13 = (f32[4,136,128]{2,1,0:T(8,128)S(1)}, f32[4,136,128]{2,1,0:T(8,128)S(1)}, u32[]{:S(2)}, u32[]{:S(2)}) collective-permute-start(f32[4,136,128]{2,1,0:T(8,128)S(1)} %get-tuple-element.59), channel_id=1, source_target_pairs={{0,12},{4,8},{8,4},{12,0},{1,13},{5,9},{9,5},{13,1},{2,14},{6,10},... | collective-permute-start | bytes 835592 | tf_op jit(solution)/shard_map/ppermute | solution.py:53
  30.1 0.0 collective-permute-done.7.refs_1_
  30.1 2.7 %collective-permute-start.4 = (f32[128,128]{1,0:T(8,128)S(1)}, f32[128,128]{1,0:T(8,128)S(1)}, u32[]{:S(2)}, u32[]{:S(2)}) collective-permute-start(f32[128,128]{1,0:T(8,128)S(1)} %get-tuple-element.71), channel_id=1, source_target_pairs={{0,1},{1,0},{2,3},{3,2},{4,5},{5,4},{6,7},{7,6},{8,9},{9,8},{10,11... | collective-permute-start | bytes 196616 | tf_op jit(solution)/shard_map/ppermute | solution.py:31
  32.9 0.0 collective-permute-done.8.refs_3_
  32.9 1.3 %collective-permute-start.5 = (f32[128,128]{1,0:T(8,128)S(1)}, f32[128,128]{1,0:T(8,128)S(1)}, u32[]{:S(2)}, u32[]{:S(2)}) collective-permute-start(f32[128,128]{1,0:T(8,128)S(1)} %get-tuple-element.70), channel_id=1, source_target_pairs={{0,2},{1,3},{2,0},{3,1},{4,6},{5,7},{6,4},{7,5},{8,10},{9,11},{10,... | collective-permute-start | bytes 196616 | tf_op jit(solution)/shard_map/ppermute | solution.py:31
  34.1 1.5 %collective-permute-start.6 = (f32[128,128]{1,0:T(8,128)S(1)}, f32[128,128]{1,0:T(8,128)S(1)}, u32[]{:S(2)}, u32[]{:S(2)}) collective-permute-start(f32[128,128]{1,0:T(8,128)S(1)} %get-tuple-element.69), channel_id=1, source_target_pairs={{0,3},{1,2},{2,1},{3,0},{4,7},{5,6},{6,5},{7,4},{8,11},{9,10},{10,... | collective-permute-start | bytes 196616 | tf_op jit(solution)/shard_map/ppermute | solution.py:31
  35.6 9.6 %messages.2.refs_8_ = f32[4,1024,128]{2,1,0:T(8,128)S(1)} custom-call(s32[7,4]{1,0:T(8,128)S(1)} %copy-done.13, f32[4,136,128]{2,1,0:T(8,128)S(1)} %pack.1.block_ref.own_ref.refs_0_, f32[8,128]{1,0:T(8,128)S(1)} %copy-done.11, f32[128,128]{1,0:T(8,128)S(1)} %copy-done.9, f32[4,136,128]{2,1,0:T(8,128)S(1)} %pack.1.block_ref.own_ref.refs_0_, ...), custom_call_target="tpu_custom_call" | custom-call | flops 4831838208 | bytes 1048576 | tf_op jit(solution)/shard_map/messages/pallas_call | solution.py:426
  45.3 0.0 collective-permute-done.13.refs_6_
  45.3 0.0 collective-permute-done.4.refs_1_
  45.3 0.0 collective-permute-done.6.refs_3_
  45.3 0.2 filter.1
  45.5 0.8 %collective-permute-start.14 = (f32[128,128]{1,0:T(8,128)S(1)}, f32[128,128]{1,0:T(8,128)S(1)}, u32[]{:S(2)}, u32[]{:S(2)}) collective-permute-start(f32[128,128]{1,0:T(8,128)S(1)} %filter.1), channel_id=1, source_target_pairs={{0,1},{1,0},{2,3},{3,2},{4,5},{5,4},{6,7},{7,6},{8,9},{9,8},{10,11... | collective-permute-start | bytes 196616 | tf_op jit(solution)/shard_map/ppermute | solution.py:31
  46.3 2.2 %collective-permute-start.15 = (f32[128,128]{1,0:T(8,128)S(1)}, f32[128,128]{1,0:T(8,128)S(1)}, u32[]{:S(2)}, u32[]{:S(2)}) collective-permute-start(f32[128,128]{1,0:T(8,128)S(1)} %filter.1), channel_id=1, source_target_pairs={{0,2},{1,3},{2,0},{3,1},{4,6},{5,7},{6,4},{7,5},{8,10},{9,11},{10,... | collective-permute-start | bytes 196616 | tf_op jit(solution)/shard_map/ppermute | solution.py:31
  48.5 1.5 %collective-permute-start.16 = (f32[128,128]{1,0:T(8,128)S(1)}, f32[128,128]{1,0:T(8,128)S(1)}, u32[]{:S(2)}, u32[]{:S(2)}) collective-permute-start(f32[128,128]{1,0:T(8,128)S(1)} %filter.1), channel_id=1, source_target_pairs={{0,3},{1,2},{2,1},{3,0},{4,7},{5,6},{6,5},{7,4},{8,11},{9,10},{10,... | collective-permute-start | bytes 196616 | tf_op jit(solution)/shard_map/ppermute | solution.py:31
  50.0 0.0 collective-permute-done.14
  50.0 2.9 %collective-permute-done.15 = f32[128,128]{1,0:T(8,128)S(1)} collective-permute-done((f32[128,128]{1,0:T(8,128)S(1)}, f32[128,128]{1,0:T(8,128)S(1)}, u32[]{:S(2)}, u32[]{:S(2)}) %collective-permute-start.15) | collective-permute-done | bytes 65568 | tf_op jit(solution)/shard_map/ppermute | solution.py:31
  52.9 1.7 %collective-permute-done.16 = f32[128,128]{1,0:T(8,128)S(1)} collective-permute-done((f32[128,128]{1,0:T(8,128)S(1)}, f32[128,128]{1,0:T(8,128)S(1)}, u32[]{:S(2)}, u32[]{:S(2)}) %collective-permute-start.16) | collective-permute-done | bytes 65568 | tf_op jit(solution)/shard_map/ppermute | solution.py:31
  54.6 0.1 collective-permute-start.17
  54.7 0.5 collective-permute-start.18
  55.2 0.1 collective-permute-start.19
  55.2 0.4 collective-permute-start.20
  55.7 0.1 collective-permute-start.21
  55.7 0.4 collective-permute-done.17.refs_1_
  56.2 1.9 %potentials.1 = (f32[4,128,128]{2,1,0:T(8,128)S(1)}, f32[4,128,128]{2,1,0:T(8,128)S(1)}, f32[4,128,128]{2,1,0:T(8,128)S(1)}, f32[4,128,128]{2,1,0:T(8,128)S(1)}) custom-call(f32[512,128]{1,0:T(8,128)S(1)} %pad_maximum_fusion.2.refs_0_, f32[512,128]{1,0:T(8,128)S(1)} %collective-permute-done.17.refs_1_, bf16[1024,1024]{1,0:T(8,128)(2,1)S(1)} %get-tuple-element.43.refs_2_, ...), custom_call_target="tpu_custom_call" | custom-call | flops 1610612736 | bytes 8388608 | tf_op jit(solution)/shard_map/potentials/pallas_call | solution.py:277
  58.1 0.0 copy-start.2
  58.1 0.0 copy-start.3
  58.1 0.0 copy-start.4
  58.1 0.0 copy-start.8
  58.1 1.6 %collective-permute-start.22 = (f32[4,128,128]{2,1,0:T(8,128)S(1)}, f32[4,128,128]{2,1,0:T(8,128)S(1)}, u32[]{:S(2)}, u32[]{:S(2)}) collective-permute-start(f32[4,128,128]{2,1,0:T(8,128)S(1)} %get-tuple-element.56), channel_id=1, source_target_pairs={{0,4},{4,0},{8,12},{12,8},{1,5},{5,1},{9,13},{13,9},{2,6},{6,2},{1... | collective-permute-start | bytes 786440 | tf_op jit(solution)/shard_map/ppermute | solution.py:31
  59.7 0.5 collective-permute-start.23
  60.2 0.0 collective-permute-done.19.refs_3_
  60.2 1.5 %collective-permute-start.24 = (f32[4,128,128]{2,1,0:T(8,128)S(1)}, f32[4,128,128]{2,1,0:T(8,128)S(1)}, u32[]{:S(2)}, u32[]{:S(2)}) collective-permute-start(f32[4,128,128]{2,1,0:T(8,128)S(1)} %get-tuple-element.58), channel_id=1, source_target_pairs={{0,12},{4,8},{8,4},{12,0},{1,13},{5,9},{9,5},{13,1},{2,14},{6,10},... | collective-permute-start | bytes 786440 | tf_op jit(solution)/shard_map/ppermute | solution.py:31
  61.7 18.6 %messages.3.refs_2_ = f32[4,128,128]{2,1,0:T(8,128)S(1)} custom-call(s32[7,8]{1,0:T(8,128)S(1)} %copy-done.12, f32[4,136,128]{2,1,0:T(8,128)S(1)} %pack.1.block_ref.own_ref.refs_0_, f32[8,128]{1,0:T(8,128)S(1)} %copy-done.11, f32[128,128]{1,0:T(8,128)S(1)} %copy-done.9, f32[4,136,128]{2,1,0:T(8,128)S(1)} %collective-permute-done.10.refs_0_, ...), custom_call_target="tpu_custom_call" | custom-call | flops 9663676416 | bytes 1048576 | tf_op jit(solution)/shard_map/messages/pallas_call | solution.py:426
  80.3 0.0 collective-permute-done.22.refs_4_
  80.3 0.0 collective-permute-done.23.refs_5_
  80.3 2.0 %atom_mlp.1 = f32[4,128,128]{2,1,0:T(8,128)} custom-call(s32[2,1,2]{2,1,0:T(1,128)S(1)} %bitcast.13, f32[4,128,128]{2,1,0:T(8,128)S(1)} %bitcast.10, f32[4,128,128]{2,1,0:T(8,128)S(1)} %messages.3.refs_2_, f32[4,128,128]{2,1,0:T(8,128)S(1)} %get-tuple-element.55.refs_3_, f32[4,128,128]{2,1,0:T(8,128)S(1)} %collective-permute-done.22.refs_4_, ...), custom_call_target="tpu_custom_call" | custom-call | tf_op jit(solution)/shard_map/atom_mlp/pallas_call | solution.py:492
  (30 shorter events, 0.2 us)
Async XLA Ops:
  0.0 0.9 %copy-start.1 = (f32[2,2,1,128,128]{4,3,2,1,0:T(8,128)S(1)}, f32[2,2,1,128,128]{4,3,2,1,0:T(8,128)}, u32[]{:S(2)}) copy-start(f32[2,2,1,128,128]{4,3,2,1,0:T(8,128)} %param.12) | copy-start | bytes 786436
  1.0 0.7 copy-start.6
  1.6 0.7 copy-start.7
  2.9 10.5 %collective-permute-start.2 = (f32[4,136,128]{2,1,0:T(8,128)S(1)}, f32[4,136,128]{2,1,0:T(8,128)S(1)}, u32[]{:S(2)}, u32[]{:S(2)}) collective-permute-start(f32[4,136,128]{2,1,0:T(8,128)S(1)} %pack.1.block_ref.own_ref.refs_0_), channel_id=1, source_target_pairs={{0,4},{4,0},{8,12},{12,8},{1,5},{5,1},{9,13},{13,9},{2,6},{6,2},{1... | collective-permute-start | bytes 835592 | tf_op jit(solution)/shard_map/ppermute | solution.py:31
  5.9 14.4 %collective-permute-start.1 = (f32[4,136,128]{2,1,0:T(8,128)S(1)}, f32[4,136,128]{2,1,0:T(8,128)S(1)}, u32[]{:S(2)}, u32[]{:S(2)}) collective-permute-start(f32[4,136,128]{2,1,0:T(8,128)S(1)} %pack.1.block_ref.own_ref.refs_0_), channel_id=1, source_target_pairs={{0,8},{4,12},{8,0},{12,4},{1,9},{5,13},{9,1},{13,5},{2,10},{6,14},... | collective-permute-start | bytes 835592 | tf_op jit(solution)/shard_map/ppermute | solution.py:31
  7.5 15.7 %collective-permute-start = (f32[4,136,128]{2,1,0:T(8,128)S(1)}, f32[4,136,128]{2,1,0:T(8,128)S(1)}, u32[]{:S(2)}, u32[]{:S(2)}) collective-permute-start(f32[4,136,128]{2,1,0:T(8,128)S(1)} %pack.1.block_ref.own_ref.refs_0_), channel_id=1, source_target_pairs={{0,12},{4,8},{8,4},{12,0},{1,13},{5,9},{9,5},{13,1},{2,14},{6,10},... | collective-permute-start | bytes 835592 | tf_op jit(solution)/shard_map/ppermute | solution.py:31
  7.5 19.1 %collective-permute-start.10 = (f32[4,136,128]{2,1,0:T(8,128)S(1)}, f32[4,136,128]{2,1,0:T(8,128)S(1)}, u32[]{:S(2)}, u32[]{:S(2)}) collective-permute-start(f32[4,136,128]{2,1,0:T(8,128)S(1)} %pack.1.block_ref.own_ref.refs_0_), channel_id=1, source_target_pairs={{0,1},{1,0},{2,3},{3,2},{4,5},{5,4},{6,7},{7,6},{8,9},{9,8},{10,11... | collective-permute-start | bytes 835592 | tf_op jit(solution)/shard_map/ppermute | solution.py:53
  9.5 20.6 %collective-permute-start.7 = (f32[4,136,128]{2,1,0:T(8,128)S(1)}, f32[4,136,128]{2,1,0:T(8,128)S(1)}, u32[]{:S(2)}, u32[]{:S(2)}) collective-permute-start(f32[4,136,128]{2,1,0:T(8,128)S(1)} %pack.1.block_ref.own_ref.refs_0_), channel_id=1, source_target_pairs={{0,16},{16,0},{1,17},{17,1},{2,18},{18,2},{3,19},{19,3},{4,20},{20... | collective-permute-start | bytes 835592 | tf_op jit(solution)/shard_map/ppermute | solution.py:31
  9.5 0.8 copy-start.10
  13.4 13.3 %collective-permute-start.11 = (f32[4,136,128]{2,1,0:T(8,128)S(1)}, f32[4,136,128]{2,1,0:T(8,128)S(1)}, u32[]{:S(2)}, u32[]{:S(2)}) collective-permute-start(f32[4,136,128]{2,1,0:T(8,128)S(1)} %pack.1.block_ref.own_ref.refs_0_), channel_id=1, source_target_pairs={{0,3},{1,2},{2,1},{3,0},{4,7},{5,6},{6,5},{7,4},{8,11},{9,10},{10,... | collective-permute-start | bytes 835592 | tf_op jit(solution)/shard_map/ppermute | solution.py:53
  23.2 12.4 %copy-start.9 = (f32[128,128]{1,0:T(8,128)S(1)}, f32[128,128]{1,0:T(8,128)}, u32[]{:S(2)}) copy-start(f32[128,128]{1,0:T(8,128)} %value_ref.1) | copy-start | bytes 196612
  23.2 12.4 %copy-start.11 = (f32[8,128]{1,0:T(8,128)S(1)}, f32[8,128]{1,0:T(8,128)}, u32[]{:S(2)}) copy-start(f32[8,128]{1,0:T(8,128)} %mix_ref.3) | copy-start | bytes 12292
  23.2 12.4 %copy-start.13 = (s32[7,4]{1,0:T(8,128)S(1)}, s32[7,4]{1,0:T(8,128)}, u32[]{:S(2)}) copy-start(s32[7,4]{1,0:T(8,128)} %constant.47.clone.step_ref) | copy-start | bytes 340
  26.0 2.3 %collective-permute-start.3 = (f32[512,128]{1,0:T(8,128)S(1)}, f32[512,128]{1,0:T(8,128)S(1)}, u32[]{:S(2)}, u32[]{:S(2)}) collective-permute-start(f32[512,128]{1,0:T(8,128)S(1)} %get-tuple-element.39), channel_id=1, source_target_pairs={{0,16},{16,0},{1,17},{17,1},{2,18},{18,2},{3,19},{19,3},{4,20},{20... | collective-permute-start | bytes 786440 | tf_op jit(solution)/shard_map/ppermute | solution.py:31
  26.1 6.8 %collective-permute-start.8 = (f32[4,136,128]{2,1,0:T(8,128)S(1)}, f32[4,136,128]{2,1,0:T(8,128)S(1)}, u32[]{:S(2)}, u32[]{:S(2)}) collective-permute-start(f32[4,136,128]{2,1,0:T(8,128)S(1)} %collective-permute-done.2.block_ref.refs_2_), channel_id=1, source_target_pairs={{0,16},{16,0},{1,17},{17,1},{2,18},{18,2},{3,19},{19,3},{4,20},{20... | collective-permute-start | bytes 835592 | tf_op jit(solution)/shard_map/ppermute | solution.py:31
  26.6 7.5 %collective-permute-start.9 = (f32[4,136,128]{2,1,0:T(8,128)S(1)}, f32[4,136,128]{2,1,0:T(8,128)S(1)}, u32[]{:S(2)}, u32[]{:S(2)}) collective-permute-start(f32[4,136,128]{2,1,0:T(8,128)S(1)} %collective-permute-done.block_ref.refs_4_), channel_id=1, source_target_pairs={{0,16},{16,0},{1,17},{17,1},{2,18},{18,2},{3,19},{19,3},{4,20},{20... | collective-permute-start | bytes 835592 | tf_op jit(solution)/shard_map/ppermute | solution.py:31
  26.8 18.5 %collective-permute-start.12 = (f32[4,136,128]{2,1,0:T(8,128)S(1)}, f32[4,136,128]{2,1,0:T(8,128)S(1)}, u32[]{:S(2)}, u32[]{:S(2)}) collective-permute-start(f32[4,136,128]{2,1,0:T(8,128)S(1)} %get-tuple-element.60), channel_id=1, source_target_pairs={{0,4},{4,0},{8,12},{12,8},{1,5},{5,1},{9,13},{13,9},{2,6},{6,2},{1... | collective-permute-start | bytes 835592 | tf_op jit(solution)/shard_map/ppermute | solution.py:53
  28.4 16.9 %collective-permute-start.13 = (f32[4,136,128]{2,1,0:T(8,128)S(1)}, f32[4,136,128]{2,1,0:T(8,128)S(1)}, u32[]{:S(2)}, u32[]{:S(2)}) collective-permute-start(f32[4,136,128]{2,1,0:T(8,128)S(1)} %get-tuple-element.59), channel_id=1, source_target_pairs={{0,12},{4,8},{8,4},{12,0},{1,13},{5,9},{9,5},{13,1},{2,14},{6,10},... | collective-permute-start | bytes 835592 | tf_op jit(solution)/shard_map/ppermute | solution.py:53
  30.1 15.1 %collective-permute-start.4 = (f32[128,128]{1,0:T(8,128)S(1)}, f32[128,128]{1,0:T(8,128)S(1)}, u32[]{:S(2)}, u32[]{:S(2)}) collective-permute-start(f32[128,128]{1,0:T(8,128)S(1)} %get-tuple-element.71), channel_id=1, source_target_pairs={{0,1},{1,0},{2,3},{3,2},{4,5},{5,4},{6,7},{7,6},{8,9},{9,8},{10,11... | collective-permute-start | bytes 196616 | tf_op jit(solution)/shard_map/ppermute | solution.py:31
  32.9 12.4 %collective-permute-start.5 = (f32[128,128]{1,0:T(8,128)S(1)}, f32[128,128]{1,0:T(8,128)S(1)}, u32[]{:S(2)}, u32[]{:S(2)}) collective-permute-start(f32[128,128]{1,0:T(8,128)S(1)} %get-tuple-element.70), channel_id=1, source_target_pairs={{0,2},{1,3},{2,0},{3,1},{4,6},{5,7},{6,4},{7,5},{8,10},{9,11},{10,... | collective-permute-start | bytes 196616 | tf_op jit(solution)/shard_map/ppermute | solution.py:31
  34.1 11.2 %copy-start = (f32[2048,128]{1,0:T(8,128)S(1)}, f32[2048,128]{1,0:T(8,128)}, u32[]{:S(2)}) copy-start(f32[2048,128]{1,0:T(8,128)} %refs_5_.1) | copy-start | bytes 3145732
  34.1 11.2 %copy-start.5 = (f32[128,128]{1,0:T(8,128)S(1)}, f32[128,128]{1,0:T(8,128)}, u32[]{:S(2)}) copy-start(f32[128,128]{1,0:T(8,128)} %refs_4_) | copy-start | bytes 196612
  34.1 11.2 %collective-permute-start.6 = (f32[128,128]{1,0:T(8,128)S(1)}, f32[128,128]{1,0:T(8,128)S(1)}, u32[]{:S(2)}, u32[]{:S(2)}) collective-permute-start(f32[128,128]{1,0:T(8,128)S(1)} %get-tuple-element.69), channel_id=1, source_target_pairs={{0,3},{1,2},{2,1},{3,0},{4,7},{5,6},{6,5},{7,4},{8,11},{9,10},{10,... | collective-permute-start | bytes 196616 | tf_op jit(solution)/shard_map/ppermute | solution.py:31
  45.5 4.5 %collective-permute-start.14 = (f32[128,128]{1,0:T(8,128)S(1)}, f32[128,128]{1,0:T(8,128)S(1)}, u32[]{:S(2)}, u32[]{:S(2)}) collective-permute-start(f32[128,128]{1,0:T(8,128)S(1)} %filter.1), channel_id=1, source_target_pairs={{0,1},{1,0},{2,3},{3,2},{4,5},{5,4},{6,7},{7,6},{8,9},{9,8},{10,11... | collective-permute-start | bytes 196616 | tf_op jit(solution)/shard_map/ppermute | solution.py:31
  46.3 6.6 %collective-permute-start.15 = (f32[128,128]{1,0:T(8,128)S(1)}, f32[128,128]{1,0:T(8,128)S(1)}, u32[]{:S(2)}, u32[]{:S(2)}) collective-permute-start(f32[128,128]{1,0:T(8,128)S(1)} %filter.1), channel_id=1, source_target_pairs={{0,2},{1,3},{2,0},{3,1},{4,6},{5,7},{6,4},{7,5},{8,10},{9,11},{10,... | collective-permute-start | bytes 196616 | tf_op jit(solution)/shard_map/ppermute | solution.py:31
  48.5 6.1 %collective-permute-start.16 = (f32[128,128]{1,0:T(8,128)S(1)}, f32[128,128]{1,0:T(8,128)S(1)}, u32[]{:S(2)}, u32[]{:S(2)}) collective-permute-start(f32[128,128]{1,0:T(8,128)S(1)} %filter.1), channel_id=1, source_target_pairs={{0,3},{1,2},{2,1},{3,0},{4,7},{5,6},{6,5},{7,4},{8,11},{9,10},{10,... | collective-permute-start | bytes 196616 | tf_op jit(solution)/shard_map/ppermute | solution.py:31
  54.6 1.6 %collective-permute-start.17 = (f32[512,128]{1,0:T(8,128)S(1)}, f32[512,128]{1,0:T(8,128)S(1)}, u32[]{:S(2)}, u32[]{:S(2)}) collective-permute-start(f32[512,128]{1,0:T(8,128)S(1)} %pad_maximum_fusion.2.refs_0_), channel_id=1, source_target_pairs={{0,16},{16,0},{1,17},{17,1},{2,18},{18,2},{3,19},{19,3},{4,20},{20... | collective-permute-start | bytes 786440 | tf_op jit(solution)/shard_map/ppermute | solution.py:31
  54.7 5.0 %collective-permute-start.18 = (f32[4,136,128]{2,1,0:T(8,128)S(1)}, f32[4,136,128]{2,1,0:T(8,128)S(1)}, u32[]{:S(2)}, u32[]{:S(2)}) collective-permute-start(f32[4,136,128]{2,1,0:T(8,128)S(1)} %collective-permute-done.10.refs_0_), channel_id=1, source_target_pairs={{0,16},{16,0},{1,17},{17,1},{2,18},{18,2},{3,19},{19,3},{4,20},{20... | collective-permute-start | bytes 835592 | tf_op jit(solution)/shard_map/ppermute | solution.py:31
  55.2 5.0 %collective-permute-start.19 = (f32[4,136,128]{2,1,0:T(8,128)S(1)}, f32[4,136,128]{2,1,0:T(8,128)S(1)}, u32[]{:S(2)}, u32[]{:S(2)}) collective-permute-start(f32[4,136,128]{2,1,0:T(8,128)S(1)} %collective-permute-done.11.refs_2_), channel_id=1, source_target_pairs={{0,16},{16,0},{1,17},{17,1},{2,18},{18,2},{3,19},{19,3},{4,20},{20... | collective-permute-start | bytes 835592 | tf_op jit(solution)/shard_map/ppermute | solution.py:31
  55.2 6.5 %collective-permute-start.20 = (f32[4,136,128]{2,1,0:T(8,128)S(1)}, f32[4,136,128]{2,1,0:T(8,128)S(1)}, u32[]{:S(2)}, u32[]{:S(2)}) collective-permute-start(f32[4,136,128]{2,1,0:T(8,128)S(1)} %collective-permute-done.12.refs_4_), channel_id=1, source_target_pairs={{0,16},{16,0},{1,17},{17,1},{2,18},{18,2},{3,19},{19,3},{4,20},{20... | collective-permute-start | bytes 835592 | tf_op jit(solution)/shard_map/ppermute | solution.py:31
  55.7 6.0 %collective-permute-start.21 = (f32[4,136,128]{2,1,0:T(8,128)S(1)}, f32[4,136,128]{2,1,0:T(8,128)S(1)}, u32[]{:S(2)}, u32[]{:S(2)}) collective-permute-start(f32[4,136,128]{2,1,0:T(8,128)S(1)} %collective-permute-done.13.refs_6_), channel_id=1, source_target_pairs={{0,16},{16,0},{1,17},{17,1},{2,18},{18,2},{3,19},{19,3},{4,20},{20... | collective-permute-start | bytes 835592 | tf_op jit(solution)/shard_map/ppermute | solution.py:31
  56.2 5.5 %copy-start.12 = (s32[7,8]{1,0:T(8,128)S(1)}, s32[7,8]{1,0:T(8,128)}, u32[]{:S(2)}) copy-start(s32[7,8]{1,0:T(8,128)} %constant.48.clone.step_ref) | copy-start | bytes 676
  58.1 22.2 %copy-start.2 = (f32[2,2,1,128,128]{4,3,2,1,0:T(8,128)S(1)}, f32[2,2,1,128,128]{4,3,2,1,0:T(8,128)}, u32[]{:S(2)}) copy-start(f32[2,2,1,128,128]{4,3,2,1,0:T(8,128)} %param.12) | copy-start | bytes 786436
  58.1 22.2 %copy-start.3 = (f32[128,256]{1,0:T(8,128)S(1)}, f32[128,256]{1,0:T(8,128)}, u32[]{:S(2)}) copy-start(f32[128,256]{1,0:T(8,128)} %refs_7_.1) | copy-start | bytes 393220
  58.1 22.2 %copy-start.4 = (f32[256,128]{1,0:T(8,128)S(1)}, f32[256,128]{1,0:T(8,128)}, u32[]{:S(2)}) copy-start(f32[256,128]{1,0:T(8,128)} %refs_8_.1) | copy-start | bytes 393220
  58.1 22.2 %copy-start.8 = (s32[2,2,1]{1,2,0:T(1,128)S(1)}, s32[2,2,1]{1,2,0:T(1,128)}, u32[]{:S(2)}) copy-start(s32[2,2,1]{1,2,0:T(1,128)} %param.14) | copy-start | bytes 52
  58.1 22.1 %collective-permute-start.22 = (f32[4,128,128]{2,1,0:T(8,128)S(1)}, f32[4,128,128]{2,1,0:T(8,128)S(1)}, u32[]{:S(2)}, u32[]{:S(2)}) collective-permute-start(f32[4,128,128]{2,1,0:T(8,128)S(1)} %get-tuple-element.56), channel_id=1, source_target_pairs={{0,4},{4,0},{8,12},{12,8},{1,5},{5,1},{9,13},{13,9},{2,6},{6,2},{1... | collective-permute-start | bytes 786440 | tf_op jit(solution)/shard_map/ppermute | solution.py:31
  59.7 20.6 %collective-permute-start.23 = (f32[4,128,128]{2,1,0:T(8,128)S(1)}, f32[4,128,128]{2,1,0:T(8,128)S(1)}, u32[]{:S(2)}, u32[]{:S(2)}) collective-permute-start(f32[4,128,128]{2,1,0:T(8,128)S(1)} %get-tuple-element.57), channel_id=1, source_target_pairs={{0,8},{4,12},{8,0},{12,4},{1,9},{5,13},{9,1},{13,5},{2,10},{6,14},... | collective-permute-start | bytes 786440 | tf_op jit(solution)/shard_map/ppermute | solution.py:31
  60.2 20.1 %collective-permute-start.24 = (f32[4,128,128]{2,1,0:T(8,128)S(1)}, f32[4,128,128]{2,1,0:T(8,128)S(1)}, u32[]{:S(2)}, u32[]{:S(2)}) collective-permute-start(f32[4,128,128]{2,1,0:T(8,128)S(1)} %get-tuple-element.58), channel_id=1, source_target_pairs={{0,12},{4,8},{8,4},{12,0},{1,13},{5,9},{9,5},{13,1},{2,14},{6,10},... | collective-permute-start | bytes 786440 | tf_op jit(solution)/shard_map/ppermute | solution.py:31

commit v5 on v4

--- a/solution.py
+++ b/solution.py
@@ -16,6 +16,7 @@
 bf16 = jnp.bfloat16
 f32 = jnp.float32
 VMEM_LIMIT = 28 * 1024 * 1024
+PACK_LIMIT = 62 * 1024 * 1024
 
 
 LOG2E = math.log2(math.e)
@@ -69,25 +70,34 @@
     return pl.BlockSpec(memory_space=pltpu.VMEM)
 
 
-def params():
-    return pltpu.CompilerParams(vmem_limit_bytes=VMEM_LIMIT)
+def params(limit=VMEM_LIMIT):
+    return pltpu.CompilerParams(vmem_limit_bytes=limit)
 
 
 def place_of(cell, shape):
     return cell // (shape[1] * shape[2]), cell // shape[2] % shape[1], cell % shape[2]
 
 
-def pack_kernel(shape, grid, counts_hbm, feature_hbm, position_hbm, out_ref, counts_ref, feature_ref, position_ref, sems):
+def pack_kernel(
+    shape, grid, counts_hbm, feature_hbm, position_hbm, waves_hbm, out_ref, column_ref,
+    counts_ref, feature_ref, position_ref, waves_ref, sems,
+):
+    total = column_ref.shape[0]
+    begin = pl.multiple_of(lax.axis_index("gy") * total, total)
     cells, channels, slots = feature_ref.shape
     copies = [
         pltpu.make_async_copy(counts_hbm, counts_ref, sems.at[0]),
         pltpu.make_async_copy(position_hbm, position_ref, sems.at[1]),
-        pltpu.make_async_copy(feature_hbm, feature_ref, sems.at[2]),
+        pltpu.make_async_copy(waves_hbm.at[:, pl.ds(begin, total)], waves_ref, sems.at[2]),
+        pltpu.make_async_copy(feature_hbm, feature_ref, sems.at[3]),
     ]
     for copy in copies:
         copy.start()
-    for copy in copies:
+    for copy in copies[:3]:
         copy.wait()
+    waves = waves_ref[...].astype(f32)
+    column_ref[...] = jnp.concatenate([waves, jnp.zeros((5, total), f32)], axis=0).T
+    copies[3].wait()
     slot = lax.broadcasted_iota(jnp.int32, (channels, slots), 1)
     for cell in range(cells):
         place = place_of(cell, shape)
@@ -101,22 +111,26 @@
         out_ref[cell, channels:, :] = jnp.concatenate(rows + [jnp.zeros((2, slots), f32)], axis=0)
 
 
-def pack(shape, grid, counts, features, positions):
+def pack(shape, grid, counts, features, positions, waves, total):
     cells, channels, slots = features.shape
     return pl.pallas_call(
         functools.partial(pack_kernel, shape, grid),
-        in_specs=[pl.BlockSpec(memory_space=pltpu.HBM)] * 3,
-        out_specs=whole(),
-        out_shape=jax.ShapeDtypeStruct((cells, channels + 8, slots), f32),
+        in_specs=[pl.BlockSpec(memory_space=pltpu.HBM)] * 4,
+        out_specs=[whole()] * 2,
+        out_shape=[
+            jax.ShapeDtypeStruct((cells, channels + 8, slots), f32),
+            jax.ShapeDtypeStruct((total, 8), f32),
+        ],
         scratch_shapes=[
             pltpu.SMEM(counts.shape, jnp.int32),
             pltpu.VMEM(features.shape, f32),
             pltpu.VMEM(positions.shape, f32),
-            pltpu.SemaphoreType.DMA((3,)),
+            pltpu.VMEM((3, total), jnp.int32),
+            pltpu.SemaphoreType.DMA((4,)),
         ],
-        compiler_params=params(),
+        compiler_params=params(PACK_LIMIT),
         name="pack",
-    )(counts, features, positions)
+    )(counts, features, positions, waves)
 
 
 def fitted(function, terms):
@@ -144,18 +158,15 @@
     return 1.0 - sine * sine, sine * cosine
 
 
-def factor_kernel(parts, chunk, first, waves_ref, block_ref, *refs):
+def factor_kernel(parts, chunk, first, column_ref, block_ref, *refs):
     before = refs[: 0 if first else parts]
     refs = refs[len(before) :]
-    after, wave_ref, weight_ref, column_ref = refs[:parts], refs[parts], refs[parts + 1], refs[parts + 2]
+    after, wave_ref, weight_ref = refs[:parts], refs[parts], refs[parts + 1]
     cells, _, slots = block_ref.shape
     channels = after[0].shape[-1]
     span = cells * slots
     total = wave_ref.shape[0] // 2
     at_x = lax.axis_index("gx")
-    begin = pl.multiple_of(lax.axis_index("gy") * total, total)
-    rows = waves_ref[:, pl.ds(begin, total)].astype(f32)
-    column_ref[...] = jnp.concatenate([rows, jnp.zeros((5, total), f32)], axis=0).T
     for cell in range(cells):
         high, low = split(block_ref[cell, :channels, :])
         for at in (cell * slots, span + cell * slots):
@@ -181,7 +192,7 @@
             wave_ref[pl.ds(row + chunk, chunk), span + at : span + at + slots] = low
         return carry
 
-    lax.fori_loop(0, total // chunk, some, 0)
+    lax.fori_loop(0, total // chunk, some, 0, unroll=total // chunk <= 8)
     half = 2 * total // parts
     for n in range(parts):
         row = pl.multiple_of(lax.rem(at_x + n, parts) * half, half)
@@ -193,7 +204,8 @@
         after[n][...] = both if first else before[n][...] + both
 
 
-def partial_factors(waves, total, chunk, block, before, parts):
+def partial_factors(columns, chunk, block, before, parts):
+    total = columns.shape[0]
     cells, rows, slots = block.shape
     channels = rows - 8
     span = cells * slots
@@ -204,13 +216,13 @@
         out_specs=[whole()] * (parts + 1),
         out_shape=out + [jax.ShapeDtypeStruct((2 * total, 2 * span), bf16)],
         input_output_aliases={2 + n: n for n in range(len(before))},
-        scratch_shapes=[pltpu.VMEM((2 * channels, 2 * span), bf16), pltpu.VMEM((total, 8), f32)],
+        scratch_shapes=[pltpu.VMEM((2 * channels, 2 * span), bf16)],
         compiler_params=params(),
         cost_estimate=pl.CostEstimate(
             flops=8 * total * span * channels, bytes_accessed=8 * total * span, transcendentals=0
         ),
         name="factors",
-    )(waves, block, *before)
+    )(columns, block, *before)
 
 
 def filter_kernel(scale, block_ref, *refs):
@@ -293,16 +305,17 @@
 
 
 def message_kernel(
-    basis, sources, table, last, step_ref, own_ref, mix_ref, value_ref, *refs
+    basis, sources, table, last, first, step_ref, own_ref, mix_ref, value_ref, *refs
 ):
     blocks, refs = refs[:sources], refs[sources:]
     if last:
-        before_ref, out_ref, cell_ref, at_ref, own_col_ref, acc_ref, mixed_ref, wide_ref = refs[:8]
+        before, refs = refs[:last], refs[last:]
+        out_ref, cell_ref, at_ref, own_col_ref, acc_ref, mixed_ref, wide_ref = refs[:7]
     else:
         out_ref, cell_ref, at_ref, own_col_ref, acc_ref = refs[:5]
     left_0, left_1, left_2, right_0, right_1, right_2 = refs[-6:]
     count = step_ref.shape[1]
-    cells = own_ref.shape[0]
+    cells = acc_ref.shape[0]
     slots = own_ref.shape[-1]
     along, planes = len(table[0]), len(table[0][0])
     channels = value_ref.shape[0]
@@ -325,7 +338,7 @@
         mixed_ref[b * channels : (b + 1) * channels, :channels] = high
         mixed_ref[b * channels : (b + 1) * channels, channels:] = low
     for cell in range(cells):
-        columns = own_ref[cell, channels : channels + 8, :].T
+        columns = own_ref[first + cell, channels : channels + 8, :].T
         for axis in range(3):
             own_col_ref[cell, axis] = jnp.broadcast_to(columns[:, axis : axis + 1], (slots, slots))
 
@@ -399,7 +412,8 @@
         if not last:
             out_ref[cell] = gathered
             continue
-        high, low = split(gathered + before_ref[cell])
+        per = cells // last
+        high, low = split(gathered + before[cell // per][cell % per])
         here = slice(cell * slots, (cell + 1) * slots)
         for b in range(basis):
             wide_ref[here, b * channels : (b + 1) * channels] = high[b * slots : (b + 1) * slots]
@@ -412,19 +426,19 @@
             out_ref[cell] = (part[:, :channels] + part[:, channels:]).T
 
 
-def pair_messages(steps, own, blocks, table, mix, w_value, before=None):
-    cells, _, slots = own.shape
+def pair_messages(steps, own, blocks, table, mix, w_value, cells, first, before=()):
+    slots = own.shape[-1]
     basis, channels = mix.shape
     around = len(table) * len(table[0]) * len(table[0][0])
     count = steps.shape[1]
-    last = before is not None
+    last = len(before)
     sums = (cells, basis * slots, channels)
     closing = [
         pltpu.VMEM((basis * channels, 2 * channels), bf16),
         pltpu.VMEM((cells * slots, 2 * basis * channels), bf16),
     ]
     return pl.pallas_call(
-        functools.partial(message_kernel, basis, len(blocks), table, last),
+        functools.partial(message_kernel, basis, len(blocks), table, last, first),
         in_specs=[pl.BlockSpec(memory_space=pltpu.SMEM)] + [whole()] * (3 + len(blocks) + last),
         out_specs=whole(),
         scratch_shapes=[
@@ -433,7 +447,7 @@
             pltpu.VMEM((cells, 3, slots, slots), f32),
             pltpu.VMEM((cells, basis * slots, 2 * channels), f32),
         ]
-        + closing * last
+        + closing * bool(last)
         + [pltpu.VMEM((basis * slots, 6 * slots), bf16)] * 3
         + [pltpu.VMEM((2 * channels, 6 * slots), bf16)] * 3,
         out_shape=jax.ShapeDtypeStruct((cells, channels, slots) if last else sums, f32),
@@ -443,22 +457,24 @@
             transcendentals=0,
         ),
         name="messages",
-    )(steps, own, mix, w_value, *blocks, *([before] if last else []))
-
-
-def visits(cells_x, cells_y, cells_z, inside):
+    )(steps, own, mix, w_value, *blocks, *before)
+
+
+def visits(cells_x, cells_y, cells_z, inside, first=0, end=None):
     table = []
     for x in range(cells_x):
         for y in range(cells_y):
             for z in range(cells_z):
                 own = (x * cells_y + y) * cells_z + z
+                if not first <= own < (cells_x * cells_y * cells_z if end is None else end):
+                    continue
                 for shift in (-1, 0, 1):
                     plane = z + shift
                     if (0 <= plane < cells_z) != inside:
                         continue
                     if not inside:
                         plane = 0 if shift > 0 else 1
-                    table.append([x, y, plane, shift, own, 1, 1])
+                    table.append([x - first // (cells_y * cells_z), y, plane, shift, own - first, 1, 1])
     for one, after in zip(table, table[1:]):
         if one[4] == after[4]:
             one[6] = after[5] = 0
@@ -478,9 +494,13 @@
             mixed = mixed + potential[cell]
         columns.append(mixed)
     mixed = jnp.concatenate(columns, axis=1)
-    inner = jnp.dot(hidden_ref[...].T, mixed, precision=HIGH, preferred_element_type=f32)
+    inner = lax.dot_general(
+        hidden_ref[...], mixed, (((0,), (0,)), ((), ())), precision=HIGH, preferred_element_type=f32
+    )
     hidden = inner * jax.nn.sigmoid(inner)
-    updated = mixed + jnp.dot(back_ref[...].T, hidden, precision=HIGH, preferred_element_type=f32)
+    updated = mixed + lax.dot_general(
+        back_ref[...], hidden, (((0,), (0,)), ((), ())), precision=HIGH, preferred_element_type=f32
+    )
     slot = lax.broadcasted_iota(jnp.int32, (channels, slots), 1)
     for cell in range(cells):
         part = updated[:, cell * slots : (cell + 1) * slots]
@@ -544,7 +564,10 @@
     some_counts = jnp.transpose(counts, (0, 2, 1))
     flat_features = features.reshape(cells, channels, slots)
 
-    own = pack(shape, grid, some_counts, flat_features, positions.reshape(cells * 3, 1, slots))
+    share = total_waves // size_y
+    own, columns = pack(
+        shape, grid, some_counts, flat_features, positions.reshape(cells * 3, 1, slots), waves, share
+    )
     rows = own.shape[1]
     packed = own.reshape(shape + (rows, slots))
 
@@ -555,13 +578,12 @@
         flat = (cells_x * cells_y, rows, slots)
         sides = neighbours(packed[:, :, 0].reshape(flat), packed[:, :, -1].reshape(flat), "gz")
 
-    share = total_waves // size_y
     half = 2 * share // size_x
     piece = half // size_z
     chunk = min(piece, share // size_x)
     parts, tables = (), []
     for block in gathered:
-        *parts, table = partial_factors(waves, share, chunk, block, parts, size_x)
+        *parts, table = partial_factors(columns, chunk, block, parts, size_x)
         tables.append(table)
 
     summed = parts[0]
@@ -616,18 +638,33 @@
         [[choices(x, y, z) for z in range(cells_z)] for y in range(-1, cells_y + 1)]
         for x in range(-1, cells_x + 1)
     ]
-    inner = jnp.asarray(visits(cells_x, cells_y, cells_z, True))
-    near = pair_messages(inner, own, sources.arrays, table, radial_mix, value_near)
+    layer = cells_y * cells_z
+    at_once = (cells_x + 1) // 2
+    near = []
+
+    def near_messages(begin, value):
+        end = min(begin + at_once, cells_x)
+        inner = visits(cells_x, cells_y, cells_z, True, begin * layer, end * layer)
+        return pair_messages(
+            jnp.asarray(inner), own, sources.arrays, table[begin : end + 2], radial_mix, value,
+            (end - begin) * layer, begin * layer,
+        )
+
+    near.append(near_messages(0, value_near))
 
     scale = 1.0 / math.sqrt(grid[0] * grid[1] * grid[2] * slots) / math.sqrt(total_waves)
     rank = at_x * size_z + at_z
     block = at_y * (share // chunk) + (rank * piece) // (2 * chunk)
-    charge, near, *edges = lax.optimization_barrier((w_charge, near, *edges))
+    charge, near[0], *edges = lax.optimization_barrier((w_charge, near[0], *edges))
     filtered = filtered_piece(scale, block.reshape(1), chunk, pieces, charge, filter_table)
 
+    value_near, filtered = lax.optimization_barrier((w_value, filtered))
+    if cells_x > 1:
+        near.append(near_messages(at_once, value_near))
     held_z = jnp.concatenate(
         [filtered] + [exchange(filtered, "gz", s) for s in range(1, size_z)], axis=0
     )
+    held_z, *near = lax.optimization_barrier((held_z, *near))
     held = [held_z] + [exchange(held_z, "gx", s) for s in range(1, size_x)]
 
     sources = Sources()
@@ -657,7 +694,9 @@
     value_far, *found = lax.optimization_barrier((w_value, *found))
     returned = [found[0]] + [exchange(found[s], "gy", s) for s in range(1, size_y)]
     outer = jnp.asarray(visits(cells_x, cells_y, cells_z, False))
-    messages = pair_messages(outer, own, sources.arrays, table, radial_mix, value_far, near)
+    messages = pair_messages(
+        outer, own, sources.arrays, table, radial_mix, value_far, cells, 0, near
+    )
 
     updated = atom_mlp(
         shape, some_counts, flat_features, messages, returned, w_hidden, w_out

time: 82.6 us -> 81.2 us (0.983)
  waiting for transfers between devices: 5.46 us -> 0.61 us
  starting transfers between devices: 29.3 us -> 31.8 us
  Pallas kernels: 44 us -> 46 us
  local copies, waits for them, and re-layouts: 3.2 us -> 2.03 us
    ppermute x21, waiting for transfers between devices: 5.45 us -> 0.6 us  [exchange(): return lax.ppermute(block, axis, pairs)]
    pallas_call x2 -> x3, Pallas kernels: 28.2 us -> 30.8 us  [pair_messages(): pl.pallas_call(functools.partial(message_kernel, basis, len(blocks), tabl...]
    ppermute x21, starting transfers between devices: 19.8 us -> 22.3 us  [exchange(): return lax.ppermute(block, axis, pairs)]
    pallas_call x4, Pallas kernels: 11.1 us -> 9.3 us  [partial_factors(): pl.pallas_call(functools.partial(factor_kernel, parts, chunk, not before)...]
    pallas_call x1, Pallas kernels: 0.61 us -> 1.85 us  [pack(): pl.pallas_call(functools.partial(pack_kernel, shape, grid), in_specs=[pl....]
    unnamed x28 -> x24, local copies, waits for them, and re-layouts: 3.13 us -> 1.96 us
  transfers between devices with their start and end apart: 25 -> 25, of which waited for: 4 -> 2; matrix products, arithmetic and copies ran while one was open for 0% -> 0% of each run, Pallas kernels for 50% -> 52%
where the time goes in v5:
time: 81.2 us; the launch traced here: 80.9 us
  Pallas kernels  46 us (57%)
  starting transfers between devices  31.8 us (39%)
  local copies, waits for them, and re-layouts  2.03 us (2%)
    pallas_call x3, Pallas kernels, pair_messages(): pl.pallas_call(functools.partial(message_kernel, basis, len(blocks), tabl...  30.8 us
    ppermute x21, starting transfers between devices, exchange(): return lax.ppermute(block, axis, pairs)  22.3 us
    ppermute x4, starting transfers between devices, neighbours(): return (lax.ppermute(first, axis, one), lax.ppermute(second, axis, two))  9.47 us
    pallas_call x4, Pallas kernels, partial_factors(): pl.pallas_call(functools.partial(factor_kernel, parts, chunk, not before)...  9.3 us
    pallas_call x1, Pallas kernels, atom_mlp(): pl.pallas_call(functools.partial(mlp_kernel, len(potentials), shape), in_...  1.98 us
    unnamed x24, local copies, waits for them, and re-layouts  1.96 us
    pallas_call x1, Pallas kernels, potentials_of(): pl.pallas_call(functools.partial(potential_kernel, len(held), pieces, len...  1.88 us
    pallas_call x1, Pallas kernels, pack(): pl.pallas_call(functools.partial(pack_kernel, shape, grid), in_specs=[pl....  1.85 us
  transfers between devices with their start and end apart: 25, of which 2 were waited for; matrix products, arithmetic and copies ran while one was open for 0% of the time, Pallas kernels for 52%

profile of v5, /device:TPU:0, one launch (start us, length us, event | category | flops | bytes accessed | tf_op | source)
XLA Modules:
  0.0 80.9 jit_solution(14496722924096771060)
XLA Ops:
  0.0 1.8 %pack.1 = (f32[4,136,128]{2,1,0:T(8,128)}, f32[512,8]{1,0:T(8,128)}) custom-call(s32[2,1,2]{2,1,0:T(1,128)} %bitcast.11, f32[4,128,128]{2,1,0:T(8,128)} %bitcast.9, f32[12,1,128]{2,1,0:T(1,128)} %bitcast.13, s32[3,2048]{1,0:T(4,128)} %waves_hbm.1), custom_call_target="tpu_custom_call" | custom-call | tf_op jit(solution)/shard_map/pack/pallas_call | solution.py:116
  1.9 3.0 %collective-permute-start.2 = (f32[4,136,128]{2,1,0:T(8,128)}, f32[4,136,128]{2,1,0:T(8,128)S(1)}, u32[]{:S(2)}, u32[]{:S(2)}) collective-permute-start(f32[4,136,128]{2,1,0:T(8,128)} %get-tuple-element.39.block_ref.own_ref.refs_0_), channel_id=1, source_target_pairs={{0,4},{4,0},{8,12},{12,8},{1,5},{5,1},{9,13},{13,9},{2,6},{6,2},{1... | collective-permute-start | bytes 835592 | tf_op jit(solution)/shard_map/ppermute | solution.py:32
  4.9 1.5 %collective-permute-start.1 = (f32[4,136,128]{2,1,0:T(8,128)}, f32[4,136,128]{2,1,0:T(8,128)S(1)}, u32[]{:S(2)}, u32[]{:S(2)}) collective-permute-start(f32[4,136,128]{2,1,0:T(8,128)} %get-tuple-element.39.block_ref.own_ref.refs_0_), channel_id=1, source_target_pairs={{0,8},{4,12},{8,0},{12,4},{1,9},{5,13},{9,1},{13,5},{2,10},{6,14},... | collective-permute-start | bytes 835592 | tf_op jit(solution)/shard_map/ppermute | solution.py:32
  6.4 0.0 collective-permute-start
  6.4 2.0 %collective-permute-start.10 = (f32[4,136,128]{2,1,0:T(8,128)}, f32[4,136,128]{2,1,0:T(8,128)S(1)}, u32[]{:S(2)}, u32[]{:S(2)}) collective-permute-start(f32[4,136,128]{2,1,0:T(8,128)} %get-tuple-element.39.block_ref.own_ref.refs_0_), channel_id=1, source_target_pairs={{0,1},{1,0},{2,3},{3,2},{4,5},{5,4},{6,7},{7,6},{8,9},{9,8},{10,11... | collective-permute-start | bytes 835592 | tf_op jit(solution)/shard_map/ppermute | solution.py:54
  8.4 0.0 collective-permute-start.7
  8.4 0.9 %copy-done = f32[512,8]{1,0:T(8,128)S(1)} copy-done((f32[512,8]{1,0:T(8,128)S(1)}, f32[512,8]{1,0:T(8,128)}, u32[]{:S(2)}) %copy-start) | copy-done | bytes 16408
  9.4 3.0 %factors.4 = (f32[512,128]{1,0:T(8,128)S(1)}, f32[512,128]{1,0:T(8,128)S(1)}, bf16[1024,1024]{1,0:T(8,128)(2,1)S(1)}) custom-call(f32[512,8]{1,0:T(8,128)S(1)} %copy-done, f32[4,136,128]{2,1,0:T(8,128)} %get-tuple-element.39.block_ref.own_ref.refs_0_), custom_call_target="tpu_custom_call" | custom-call | flops 268435456 | bytes 2097152 | tf_op jit(solution)/shard_map/factors/pallas_call | solution.py:213
  12.4 0.1 collective-permute-done.2.block_ref.refs_2_
  12.6 4.2 %collective-permute-start.11 = (f32[4,136,128]{2,1,0:T(8,128)}, f32[4,136,128]{2,1,0:T(8,128)S(1)}, u32[]{:S(2)}, u32[]{:S(2)}) collective-permute-start(f32[4,136,128]{2,1,0:T(8,128)} %get-tuple-element.39.block_ref.own_ref.refs_0_), channel_id=1, source_target_pairs={{0,3},{1,2},{2,1},{3,0},{4,7},{5,6},{6,5},{7,4},{8,11},{9,10},{10,... | collective-permute-start | bytes 835592 | tf_op jit(solution)/shard_map/ppermute | solution.py:54
  16.7 0.9 %copy-done.1 = f32[512,8]{1,0:T(8,128)S(1)} copy-done((f32[512,8]{1,0:T(8,128)S(1)}, f32[512,8]{1,0:T(8,128)}, u32[]{:S(2)}) %copy-start.1) | copy-done | bytes 16408
  17.7 2.1 %factors.5 = (f32[512,128]{1,0:T(8,128)S(1)}, f32[512,128]{1,0:T(8,128)S(1)}, bf16[1024,1024]{1,0:T(8,128)(2,1)S(1)}) custom-call(f32[512,8]{1,0:T(8,128)S(1)} %copy-done.1, f32[4,136,128]{2,1,0:T(8,128)S(1)} %collective-permute-done.2.block_ref.refs_2_, f32[512,128]{1,0:T(8,128)S(1)} %get-tuple-element.41.refs_0_, ...), custom_call_target="tpu_custom_call", output_to_operand_aliasing={{0}: (2, {}), {1}: (3, {})} | custom-call | flops 268435456 | bytes 2097152 | tf_op jit(solution)/shard_map/factors/pallas_call | solution.py:213
  19.8 0.0 collective-permute-done.1.block_ref
  19.8 2.1 %factors.6 = (f32[512,128]{1,0:T(8,128)S(1)}, f32[512,128]{1,0:T(8,128)S(1)}, bf16[1024,1024]{1,0:T(8,128)(2,1)S(1)}) custom-call(f32[512,8]{1,0:T(8,128)S(1)} %copy-done.1, f32[4,136,128]{2,1,0:T(8,128)S(1)} %collective-permute-done.1.block_ref, f32[512,128]{1,0:T(8,128)S(1)} %get-tuple-element.43.refs_0_, ...), custom_call_target="tpu_custom_call", output_to_operand_aliasing={{0}: (2, {}), {1}: (3, {})} | custom-call | flops 268435456 | bytes 2097152 | tf_op jit(solution)/shard_map/factors/pallas_call | solution.py:213
  21.9 0.0 collective-permute-done.block_ref.refs_4_
  21.9 0.0 copy-start.8
  21.9 0.0 copy-start.9
  21.9 0.0 copy-start.11
  21.9 2.1 %factors.7 = (f32[512,128]{1,0:T(8,128)S(1)}, f32[512,128]{1,0:T(8,128)S(1)}, bf16[1024,1024]{1,0:T(8,128)(2,1)S(1)}) custom-call(f32[512,8]{1,0:T(8,128)S(1)} %copy-done.1, f32[4,136,128]{2,1,0:T(8,128)S(1)} %collective-permute-done.block_ref.refs_4_, f32[512,128]{1,0:T(8,128)S(1)} %get-tuple-element.45.refs_0_, ...), custom_call_target="tpu_custom_call", output_to_operand_aliasing={{0}: (2, {}), {1}: (3, {})} | custom-call | flops 268435456 | bytes 2097152 | tf_op jit(solution)/shard_map/factors/pallas_call | solution.py:213
  24.0 0.1 collective-permute-start.3
  24.1 0.5 collective-permute-start.8
  24.6 0.0 collective-permute-done.10.refs_0_
  24.6 0.1 collective-permute-start.9
  24.7 0.0 collective-permute-done.11.refs_2_
  24.7 0.1 fusion
  24.8 1.6 %collective-permute-start.12 = (f32[4,136,128]{2,1,0:T(8,128)S(1)}, f32[4,136,128]{2,1,0:T(8,128)S(1)}, u32[]{:S(2)}, u32[]{:S(2)}) collective-permute-start(f32[4,136,128]{2,1,0:T(8,128)S(1)} %get-tuple-element.74), channel_id=1, source_target_pairs={{0,4},{4,0},{8,12},{12,8},{1,5},{5,1},{9,13},{13,9},{2,6},{6,2},{1... | collective-permute-start | bytes 835592 | tf_op jit(solution)/shard_map/ppermute | solution.py:54
  26.4 0.0 collective-permute-done.3
  26.4 1.7 %collective-permute-start.13 = (f32[4,136,128]{2,1,0:T(8,128)S(1)}, f32[4,136,128]{2,1,0:T(8,128)S(1)}, u32[]{:S(2)}, u32[]{:S(2)}) collective-permute-start(f32[4,136,128]{2,1,0:T(8,128)S(1)} %get-tuple-element.73), channel_id=1, source_target_pairs={{0,12},{4,8},{8,4},{12,0},{1,13},{5,9},{9,5},{13,1},{2,14},{6,10},... | collective-permute-start | bytes 835592 | tf_op jit(solution)/shard_map/ppermute | solution.py:54
  28.1 0.0 collective-permute-done.7.refs_1_
  28.1 4.3 %collective-permute-start.4 = (f32[128,128]{1,0:T(8,128)S(1)}, f32[128,128]{1,0:T(8,128)S(1)}, u32[]{:S(2)}, u32[]{:S(2)}) collective-permute-start(f32[128,128]{1,0:T(8,128)S(1)} %get-tuple-element.85), channel_id=1, source_target_pairs={{0,1},{1,0},{2,3},{3,2},{4,5},{5,4},{6,7},{7,6},{8,9},{9,8},{10,11... | collective-permute-start | bytes 196616 | tf_op jit(solution)/shard_map/ppermute | solution.py:32
  32.4 0.0 collective-permute-done.8.refs_3_
  32.4 1.3 %collective-permute-start.5 = (f32[128,128]{1,0:T(8,128)S(1)}, f32[128,128]{1,0:T(8,128)S(1)}, u32[]{:S(2)}, u32[]{:S(2)}) collective-permute-start(f32[128,128]{1,0:T(8,128)S(1)} %get-tuple-element.84), channel_id=1, source_target_pairs={{0,2},{1,3},{2,0},{3,1},{4,6},{5,7},{6,4},{7,5},{8,10},{9,11},{10,... | collective-permute-start | bytes 196616 | tf_op jit(solution)/shard_map/ppermute | solution.py:32
  33.7 0.0 collective-permute-done.9.refs_5_
  33.7 1.5 %collective-permute-start.6 = (f32[128,128]{1,0:T(8,128)S(1)}, f32[128,128]{1,0:T(8,128)S(1)}, u32[]{:S(2)}, u32[]{:S(2)}) collective-permute-start(f32[128,128]{1,0:T(8,128)S(1)} %get-tuple-element.83), channel_id=1, source_target_pairs={{0,3},{1,2},{2,1},{3,0},{4,7},{5,6},{6,5},{7,4},{8,11},{9,10},{10,... | collective-permute-start | bytes 196616 | tf_op jit(solution)/shard_map/ppermute | solution.py:32
  35.2 6.1 %messages.3.refs_8_ = f32[2,1024,128]{2,1,0:T(8,128)S(1)} custom-call(s32[7,2]{1,0:T(8,128)S(1)} %copy-done.11, f32[4,136,128]{2,1,0:T(8,128)} %get-tuple-element.39.block_ref.own_ref.refs_0_, f32[8,128]{1,0:T(8,128)S(1)} %copy-done.9, f32[128,128]{1,0:T(8,128)S(1)} %copy-done.8, f32[4,136,128]{2,1,0:T(8,128)} %get-tuple-element.39.block_ref.own_ref.refs_0_, ...), custom_call_target="tpu_custom_call" | custom-call | flops 2415919104 | bytes 1048576 | tf_op jit(solution)/shard_map/messages/pallas_call | solution.py:440
  41.3 0.0 collective-permute-done.12.refs_4_
  41.3 0.0 collective-permute-done.4.refs_1_
  41.3 0.0 collective-permute-done.5.refs_2_
  41.3 0.2 filter.1
  41.5 2.6 %collective-permute-start.14 = (f32[128,128]{1,0:T(8,128)S(1)}, f32[128,128]{1,0:T(8,128)S(1)}, u32[]{:S(2)}, u32[]{:S(2)}) collective-permute-start(f32[128,128]{1,0:T(8,128)S(1)} %filter.1), channel_id=1, source_target_pairs={{0,1},{1,0},{2,3},{3,2},{4,5},{5,4},{6,7},{7,6},{8,9},{9,8},{10,11... | collective-permute-start | bytes 196616 | tf_op jit(solution)/shard_map/ppermute | solution.py:32
  44.1 1.4 %collective-permute-start.15 = (f32[128,128]{1,0:T(8,128)S(1)}, f32[128,128]{1,0:T(8,128)S(1)}, u32[]{:S(2)}, u32[]{:S(2)}) collective-permute-start(f32[128,128]{1,0:T(8,128)S(1)} %filter.1), channel_id=1, source_target_pairs={{0,2},{1,3},{2,0},{3,1},{4,6},{5,7},{6,4},{7,5},{8,10},{9,11},{10,... | collective-permute-start | bytes 196616 | tf_op jit(solution)/shard_map/ppermute | solution.py:32
  45.5 1.4 %collective-permute-start.16 = (f32[128,128]{1,0:T(8,128)S(1)}, f32[128,128]{1,0:T(8,128)S(1)}, u32[]{:S(2)}, u32[]{:S(2)}) collective-permute-start(f32[128,128]{1,0:T(8,128)S(1)} %filter.1), channel_id=1, source_target_pairs={{0,3},{1,2},{2,1},{3,0},{4,7},{5,6},{6,5},{7,4},{8,11},{9,10},{10,... | collective-permute-start | bytes 196616 | tf_op jit(solution)/shard_map/ppermute | solution.py:32
  46.9 5.9 %messages.4.refs_9_ = f32[2,1024,128]{2,1,0:T(8,128)S(1)} custom-call(s32[7,2]{1,0:T(8,128)S(1)} %copy-done.11, f32[4,136,128]{2,1,0:T(8,128)} %get-tuple-element.39.block_ref.own_ref.refs_0_, f32[8,128]{1,0:T(8,128)S(1)} %copy-done.9, f32[128,128]{1,0:T(8,128)S(1)} %copy-done.8, f32[4,136,128]{2,1,0:T(8,128)} %get-tuple-element.39.block_ref.own_ref.refs_0_, ...), custom_call_target="tpu_custom_call" | custom-call | flops 2415919104 | bytes 1048576 | tf_op jit(solution)/shard_map/messages/pallas_call | solution.py:440
  52.8 0.0 collective-permute-done.14
  52.8 0.0 collective-permute-done.15
  52.9 0.1 collective-permute-start.17
  53.0 0.5 collective-permute-start.18
  53.5 0.1 collective-permute-start.19
  53.5 0.4 collective-permute-start.20
  54.0 0.1 collective-permute-start.21
  54.1 0.4 collective-permute-done.17.refs_1_
  54.5 1.9 %potentials.1 = (f32[4,128,128]{2,1,0:T(8,128)S(1)}, f32[4,128,128]{2,1,0:T(8,128)S(1)}, f32[4,128,128]{2,1,0:T(8,128)S(1)}, f32[4,128,128]{2,1,0:T(8,128)S(1)}) custom-call(f32[512,128]{1,0:T(8,128)S(1)} %pad_maximum_fusion.2.refs_0_, f32[512,128]{1,0:T(8,128)S(1)} %collective-permute-done.17.refs_1_, bf16[1024,1024]{1,0:T(8,128)(2,1)S(1)} %get-tuple-element.56.refs_2_, ...), custom_call_target="tpu_custom_call" | custom-call | flops 1610612736 | bytes 8388608 | tf_op jit(solution)/shard_map/potentials/pallas_call | solution.py:289
  56.4 0.0 copy-start.3
  56.4 0.0 copy-start.4
  56.4 0.0 copy-start.5
  56.4 0.0 copy-start.7
  56.4 1.6 %collective-permute-start.22 = (f32[4,128,128]{2,1,0:T(8,128)S(1)}, f32[4,128,128]{2,1,0:T(8,128)S(1)}, u32[]{:S(2)}, u32[]{:S(2)}) collective-permute-start(f32[4,128,128]{2,1,0:T(8,128)S(1)} %get-tuple-element.70), channel_id=1, source_target_pairs={{0,4},{4,0},{8,12},{12,8},{1,5},{5,1},{9,13},{13,9},{2,6},{6,2},{1... | collective-permute-start | bytes 786440 | tf_op jit(solution)/shard_map/ppermute | solution.py:32
  58.0 0.0 collective-permute-done.18.refs_1_
  58.0 0.5 collective-permute-start.23
  58.5 1.5 %collective-permute-start.24 = (f32[4,128,128]{2,1,0:T(8,128)S(1)}, f32[4,128,128]{2,1,0:T(8,128)S(1)}, u32[]{:S(2)}, u32[]{:S(2)}) collective-permute-start(f32[4,128,128]{2,1,0:T(8,128)S(1)} %get-tuple-element.72), channel_id=1, source_target_pairs={{0,12},{4,8},{8,4},{12,0},{1,13},{5,9},{9,5},{13,1},{2,14},{6,10},... | collective-permute-start | bytes 786440 | tf_op jit(solution)/shard_map/ppermute | solution.py:32
  60.0 18.8 %messages.5.refs_2_ = f32[4,128,128]{2,1,0:T(8,128)S(1)} custom-call(s32[7,8]{1,0:T(8,128)S(1)} %copy-done.10, f32[4,136,128]{2,1,0:T(8,128)} %get-tuple-element.39.block_ref.own_ref.refs_0_, f32[8,128]{1,0:T(8,128)S(1)} %copy-done.9, f32[128,128]{1,0:T(8,128)S(1)} %copy-done.8, f32[4,136,128]{2,1,0:T(8,128)S(1)} %collective-permute-done.10.refs_0_, ...), custom_call_target="tpu_custom_call" | custom-call | flops 9663676416 | bytes 1048576 | tf_op jit(solution)/shard_map/messages/pallas_call | solution.py:440
  78.8 0.0 collective-permute-done.22.refs_4_
  78.8 0.0 collective-permute-done.23.refs_5_
  78.9 2.0 %atom_mlp.1 = f32[4,128,128]{2,1,0:T(8,128)} custom-call(s32[2,1,2]{2,1,0:T(1,128)S(1)} %bitcast.12, f32[4,128,128]{2,1,0:T(8,128)S(1)} %bitcast.10, f32[4,128,128]{2,1,0:T(8,128)S(1)} %messages.5.refs_2_, f32[4,128,128]{2,1,0:T(8,128)S(1)} %get-tuple-element.69.refs_3_, f32[4,128,128]{2,1,0:T(8,128)S(1)} %collective-permute-done.22.refs_4_, ...), custom_call_target="tpu_custom_call" | custom-call | tf_op jit(solution)/shard_map/atom_mlp/pallas_call | solution.py:512
  (27 shorter events, 0.2 us)
Async XLA Ops:
  1.9 10.7 %collective-permute-start.2 = (f32[4,136,128]{2,1,0:T(8,128)}, f32[4,136,128]{2,1,0:T(8,128)S(1)}, u32[]{:S(2)}, u32[]{:S(2)}) collective-permute-start(f32[4,136,128]{2,1,0:T(8,128)} %get-tuple-element.39.block_ref.own_ref.refs_0_), channel_id=1, source_target_pairs={{0,4},{4,0},{8,12},{12,8},{1,5},{5,1},{9,13},{13,9},{2,6},{6,2},{1... | collective-permute-start | bytes 835592 | tf_op jit(solution)/shard_map/ppermute | solution.py:32
  4.9 14.9 %collective-permute-start.1 = (f32[4,136,128]{2,1,0:T(8,128)}, f32[4,136,128]{2,1,0:T(8,128)S(1)}, u32[]{:S(2)}, u32[]{:S(2)}) collective-permute-start(f32[4,136,128]{2,1,0:T(8,128)} %get-tuple-element.39.block_ref.own_ref.refs_0_), channel_id=1, source_target_pairs={{0,8},{4,12},{8,0},{12,4},{1,9},{5,13},{9,1},{13,5},{2,10},{6,14},... | collective-permute-start | bytes 835592 | tf_op jit(solution)/shard_map/ppermute | solution.py:32
  6.4 15.5 %collective-permute-start = (f32[4,136,128]{2,1,0:T(8,128)}, f32[4,136,128]{2,1,0:T(8,128)S(1)}, u32[]{:S(2)}, u32[]{:S(2)}) collective-permute-start(f32[4,136,128]{2,1,0:T(8,128)} %get-tuple-element.39.block_ref.own_ref.refs_0_), channel_id=1, source_target_pairs={{0,12},{4,8},{8,4},{12,0},{1,13},{5,9},{9,5},{13,1},{2,14},{6,10},... | collective-permute-start | bytes 835592 | tf_op jit(solution)/shard_map/ppermute | solution.py:32
  6.4 18.2 %collective-permute-start.10 = (f32[4,136,128]{2,1,0:T(8,128)}, f32[4,136,128]{2,1,0:T(8,128)S(1)}, u32[]{:S(2)}, u32[]{:S(2)}) collective-permute-start(f32[4,136,128]{2,1,0:T(8,128)} %get-tuple-element.39.block_ref.own_ref.refs_0_), channel_id=1, source_target_pairs={{0,1},{1,0},{2,3},{3,2},{4,5},{5,4},{6,7},{7,6},{8,9},{9,8},{10,11... | collective-permute-start | bytes 835592 | tf_op jit(solution)/shard_map/ppermute | solution.py:54
  8.4 19.7 %collective-permute-start.7 = (f32[4,136,128]{2,1,0:T(8,128)}, f32[4,136,128]{2,1,0:T(8,128)S(1)}, u32[]{:S(2)}, u32[]{:S(2)}) collective-permute-start(f32[4,136,128]{2,1,0:T(8,128)} %get-tuple-element.39.block_ref.own_ref.refs_0_), channel_id=1, source_target_pairs={{0,16},{16,0},{1,17},{17,1},{2,18},{18,2},{3,19},{19,3},{4,20},{20... | collective-permute-start | bytes 835592 | tf_op jit(solution)/shard_map/ppermute | solution.py:32
  8.4 1.0 %copy-start = (f32[512,8]{1,0:T(8,128)S(1)}, f32[512,8]{1,0:T(8,128)}, u32[]{:S(2)}) copy-start(f32[512,8]{1,0:T(8,128)} %get-tuple-element.40.column_ref) | copy-start | bytes 49156
  12.6 12.2 %collective-permute-start.11 = (f32[4,136,128]{2,1,0:T(8,128)}, f32[4,136,128]{2,1,0:T(8,128)S(1)}, u32[]{:S(2)}, u32[]{:S(2)}) collective-permute-start(f32[4,136,128]{2,1,0:T(8,128)} %get-tuple-element.39.block_ref.own_ref.refs_0_), channel_id=1, source_target_pairs={{0,3},{1,2},{2,1},{3,0},{4,7},{5,6},{6,5},{7,4},{8,11},{9,10},{10,... | collective-permute-start | bytes 835592 | tf_op jit(solution)/shard_map/ppermute | solution.py:54
  16.7 0.9 %copy-start.1 = (f32[512,8]{1,0:T(8,128)S(1)}, f32[512,8]{1,0:T(8,128)}, u32[]{:S(2)}) copy-start(f32[512,8]{1,0:T(8,128)} %get-tuple-element.40.column_ref) | copy-start | bytes 49156
  21.9 13.3 %copy-start.8 = (f32[128,128]{1,0:T(8,128)S(1)}, f32[128,128]{1,0:T(8,128)}, u32[]{:S(2)}) copy-start(f32[128,128]{1,0:T(8,128)} %value_ref.2) | copy-start | bytes 196612
  21.9 13.3 %copy-start.9 = (f32[8,128]{1,0:T(8,128)S(1)}, f32[8,128]{1,0:T(8,128)}, u32[]{:S(2)}) copy-start(f32[8,128]{1,0:T(8,128)} %mix_ref.5) | copy-start | bytes 12292
  21.9 13.3 %copy-start.11 = (s32[7,2]{1,0:T(8,128)S(1)}, s32[7,2]{1,0:T(8,128)}, u32[]{:S(2)}) copy-start(s32[7,2]{1,0:T(8,128)} %constant.47.clone.step_ref) | copy-start | bytes 172
  24.0 2.3 %collective-permute-start.3 = (f32[512,128]{1,0:T(8,128)S(1)}, f32[512,128]{1,0:T(8,128)S(1)}, u32[]{:S(2)}, u32[]{:S(2)}) collective-permute-start(f32[512,128]{1,0:T(8,128)S(1)} %get-tuple-element.48), channel_id=1, source_target_pairs={{0,16},{16,0},{1,17},{17,1},{2,18},{18,2},{3,19},{19,3},{4,20},{20... | collective-permute-start | bytes 786440 | tf_op jit(solution)/shard_map/ppermute | solution.py:32
  24.1 8.3 %collective-permute-start.8 = (f32[4,136,128]{2,1,0:T(8,128)S(1)}, f32[4,136,128]{2,1,0:T(8,128)S(1)}, u32[]{:S(2)}, u32[]{:S(2)}) collective-permute-start(f32[4,136,128]{2,1,0:T(8,128)S(1)} %collective-permute-done.2.block_ref.refs_2_), channel_id=1, source_target_pairs={{0,16},{16,0},{1,17},{17,1},{2,18},{18,2},{3,19},{19,3},{4,20},{20... | collective-permute-start | bytes 835592 | tf_op jit(solution)/shard_map/ppermute | solution.py:32
  24.6 9.1 %collective-permute-start.9 = (f32[4,136,128]{2,1,0:T(8,128)S(1)}, f32[4,136,128]{2,1,0:T(8,128)S(1)}, u32[]{:S(2)}, u32[]{:S(2)}) collective-permute-start(f32[4,136,128]{2,1,0:T(8,128)S(1)} %collective-permute-done.block_ref.refs_4_), channel_id=1, source_target_pairs={{0,16},{16,0},{1,17},{17,1},{2,18},{18,2},{3,19},{19,3},{4,20},{20... | collective-permute-start | bytes 835592 | tf_op jit(solution)/shard_map/ppermute | solution.py:32
  24.8 16.5 %collective-permute-start.12 = (f32[4,136,128]{2,1,0:T(8,128)S(1)}, f32[4,136,128]{2,1,0:T(8,128)S(1)}, u32[]{:S(2)}, u32[]{:S(2)}) collective-permute-start(f32[4,136,128]{2,1,0:T(8,128)S(1)} %get-tuple-element.74), channel_id=1, source_target_pairs={{0,4},{4,0},{8,12},{12,8},{1,5},{5,1},{9,13},{13,9},{2,6},{6,2},{1... | collective-permute-start | bytes 835592 | tf_op jit(solution)/shard_map/ppermute | solution.py:54
  26.4 14.9 %collective-permute-start.13 = (f32[4,136,128]{2,1,0:T(8,128)S(1)}, f32[4,136,128]{2,1,0:T(8,128)S(1)}, u32[]{:S(2)}, u32[]{:S(2)}) collective-permute-start(f32[4,136,128]{2,1,0:T(8,128)S(1)} %get-tuple-element.73), channel_id=1, source_target_pairs={{0,12},{4,8},{8,4},{12,0},{1,13},{5,9},{9,5},{13,1},{2,14},{6,10},... | collective-permute-start | bytes 835592 | tf_op jit(solution)/shard_map/ppermute | solution.py:54
  28.1 13.2 %collective-permute-start.4 = (f32[128,128]{1,0:T(8,128)S(1)}, f32[128,128]{1,0:T(8,128)S(1)}, u32[]{:S(2)}, u32[]{:S(2)}) collective-permute-start(f32[128,128]{1,0:T(8,128)S(1)} %get-tuple-element.85), channel_id=1, source_target_pairs={{0,1},{1,0},{2,3},{3,2},{4,5},{5,4},{6,7},{7,6},{8,9},{9,8},{10,11... | collective-permute-start | bytes 196616 | tf_op jit(solution)/shard_map/ppermute | solution.py:32
  32.4 8.9 %collective-permute-start.5 = (f32[128,128]{1,0:T(8,128)S(1)}, f32[128,128]{1,0:T(8,128)S(1)}, u32[]{:S(2)}, u32[]{:S(2)}) collective-permute-start(f32[128,128]{1,0:T(8,128)S(1)} %get-tuple-element.84), channel_id=1, source_target_pairs={{0,2},{1,3},{2,0},{3,1},{4,6},{5,7},{6,4},{7,5},{8,10},{9,11},{10,... | collective-permute-start | bytes 196616 | tf_op jit(solution)/shard_map/ppermute | solution.py:32
  33.7 7.6 %copy-start.2 = (f32[2048,128]{1,0:T(8,128)S(1)}, f32[2048,128]{1,0:T(8,128)}, u32[]{:S(2)}) copy-start(f32[2048,128]{1,0:T(8,128)} %refs_5_.1) | copy-start | bytes 3145732
  33.7 7.6 %copy-start.6 = (f32[128,128]{1,0:T(8,128)S(1)}, f32[128,128]{1,0:T(8,128)}, u32[]{:S(2)}) copy-start(f32[128,128]{1,0:T(8,128)} %refs_4_) | copy-start | bytes 196612
  33.7 7.6 %collective-permute-start.6 = (f32[128,128]{1,0:T(8,128)S(1)}, f32[128,128]{1,0:T(8,128)S(1)}, u32[]{:S(2)}, u32[]{:S(2)}) collective-permute-start(f32[128,128]{1,0:T(8,128)S(1)} %get-tuple-element.83), channel_id=1, source_target_pairs={{0,3},{1,2},{2,1},{3,0},{4,7},{5,6},{6,5},{7,4},{8,11},{9,10},{10,... | collective-permute-start | bytes 196616 | tf_op jit(solution)/shard_map/ppermute | solution.py:32
  41.5 11.3 %collective-permute-start.14 = (f32[128,128]{1,0:T(8,128)S(1)}, f32[128,128]{1,0:T(8,128)S(1)}, u32[]{:S(2)}, u32[]{:S(2)}) collective-permute-start(f32[128,128]{1,0:T(8,128)S(1)} %filter.1), channel_id=1, source_target_pairs={{0,1},{1,0},{2,3},{3,2},{4,5},{5,4},{6,7},{7,6},{8,9},{9,8},{10,11... | collective-permute-start | bytes 196616 | tf_op jit(solution)/shard_map/ppermute | solution.py:32
  44.1 8.7 %collective-permute-start.15 = (f32[128,128]{1,0:T(8,128)S(1)}, f32[128,128]{1,0:T(8,128)S(1)}, u32[]{:S(2)}, u32[]{:S(2)}) collective-permute-start(f32[128,128]{1,0:T(8,128)S(1)} %filter.1), channel_id=1, source_target_pairs={{0,2},{1,3},{2,0},{3,1},{4,6},{5,7},{6,4},{7,5},{8,10},{9,11},{10,... | collective-permute-start | bytes 196616 | tf_op jit(solution)/shard_map/ppermute | solution.py:32
  45.5 7.3 %collective-permute-start.16 = (f32[128,128]{1,0:T(8,128)S(1)}, f32[128,128]{1,0:T(8,128)S(1)}, u32[]{:S(2)}, u32[]{:S(2)}) collective-permute-start(f32[128,128]{1,0:T(8,128)S(1)} %filter.1), channel_id=1, source_target_pairs={{0,3},{1,2},{2,1},{3,0},{4,7},{5,6},{6,5},{7,4},{8,11},{9,10},{10,... | collective-permute-start | bytes 196616 | tf_op jit(solution)/shard_map/ppermute | solution.py:32
  52.9 1.6 %collective-permute-start.17 = (f32[512,128]{1,0:T(8,128)S(1)}, f32[512,128]{1,0:T(8,128)S(1)}, u32[]{:S(2)}, u32[]{:S(2)}) collective-permute-start(f32[512,128]{1,0:T(8,128)S(1)} %pad_maximum_fusion.2.refs_0_), channel_id=1, source_target_pairs={{0,16},{16,0},{1,17},{17,1},{2,18},{18,2},{3,19},{19,3},{4,20},{20... | collective-permute-start | bytes 786440 | tf_op jit(solution)/shard_map/ppermute | solution.py:32
  53.0 5.0 %collective-permute-start.18 = (f32[4,136,128]{2,1,0:T(8,128)S(1)}, f32[4,136,128]{2,1,0:T(8,128)S(1)}, u32[]{:S(2)}, u32[]{:S(2)}) collective-permute-start(f32[4,136,128]{2,1,0:T(8,128)S(1)} %collective-permute-done.10.refs_0_), channel_id=1, source_target_pairs={{0,16},{16,0},{1,17},{17,1},{2,18},{18,2},{3,19},{19,3},{4,20},{20... | collective-permute-start | bytes 835592 | tf_op jit(solution)/shard_map/ppermute | solution.py:32
  53.5 5.0 %collective-permute-start.19 = (f32[4,136,128]{2,1,0:T(8,128)S(1)}, f32[4,136,128]{2,1,0:T(8,128)S(1)}, u32[]{:S(2)}, u32[]{:S(2)}) collective-permute-start(f32[4,136,128]{2,1,0:T(8,128)S(1)} %collective-permute-done.11.refs_2_), channel_id=1, source_target_pairs={{0,16},{16,0},{1,17},{17,1},{2,18},{18,2},{3,19},{19,3},{4,20},{20... | collective-permute-start | bytes 835592 | tf_op jit(solution)/shard_map/ppermute | solution.py:32
  53.5 6.5 %collective-permute-start.20 = (f32[4,136,128]{2,1,0:T(8,128)S(1)}, f32[4,136,128]{2,1,0:T(8,128)S(1)}, u32[]{:S(2)}, u32[]{:S(2)}) collective-permute-start(f32[4,136,128]{2,1,0:T(8,128)S(1)} %collective-permute-done.12.refs_4_), channel_id=1, source_target_pairs={{0,16},{16,0},{1,17},{17,1},{2,18},{18,2},{3,19},{19,3},{4,20},{20... | collective-permute-start | bytes 835592 | tf_op jit(solution)/shard_map/ppermute | solution.py:32
  54.0 6.0 %collective-permute-start.21 = (f32[4,136,128]{2,1,0:T(8,128)S(1)}, f32[4,136,128]{2,1,0:T(8,128)S(1)}, u32[]{:S(2)}, u32[]{:S(2)}) collective-permute-start(f32[4,136,128]{2,1,0:T(8,128)S(1)} %collective-permute-done.13.refs_6_), channel_id=1, source_target_pairs={{0,16},{16,0},{1,17},{17,1},{2,18},{18,2},{3,19},{19,3},{4,20},{20... | collective-permute-start | bytes 835592 | tf_op jit(solution)/shard_map/ppermute | solution.py:32
  54.5 5.5 %copy-start.10 = (s32[7,8]{1,0:T(8,128)S(1)}, s32[7,8]{1,0:T(8,128)}, u32[]{:S(2)}) copy-start(s32[7,8]{1,0:T(8,128)} %constant.48.clone.step_ref) | copy-start | bytes 676
  56.4 22.5 %copy-start.3 = (f32[2,2,1,128,128]{4,3,2,1,0:T(8,128)S(1)}, f32[2,2,1,128,128]{4,3,2,1,0:T(8,128)}, u32[]{:S(2)}) copy-start(f32[2,2,1,128,128]{4,3,2,1,0:T(8,128)} %param.13) | copy-start | bytes 786436
  56.4 22.5 %copy-start.4 = (f32[128,256]{1,0:T(8,128)S(1)}, f32[128,256]{1,0:T(8,128)}, u32[]{:S(2)}) copy-start(f32[128,256]{1,0:T(8,128)} %refs_7_.1) | copy-start | bytes 393220
  56.4 22.5 %copy-start.5 = (f32[256,128]{1,0:T(8,128)S(1)}, f32[256,128]{1,0:T(8,128)}, u32[]{:S(2)}) copy-start(f32[256,128]{1,0:T(8,128)} %refs_8_.1) | copy-start | bytes 393220
  56.4 22.5 %copy-start.7 = (s32[2,2,1]{1,2,0:T(1,128)S(1)}, s32[2,2,1]{1,2,0:T(1,128)}, u32[]{:S(2)}) copy-start(s32[2,2,1]{1,2,0:T(1,128)} %param.15) | copy-start | bytes 52
  56.4 22.4 %collective-permute-start.22 = (f32[4,128,128]{2,1,0:T(8,128)S(1)}, f32[4,128,128]{2,1,0:T(8,128)S(1)}, u32[]{:S(2)}, u32[]{:S(2)}) collective-permute-start(f32[4,128,128]{2,1,0:T(8,128)S(1)} %get-tuple-element.70), channel_id=1, source_target_pairs={{0,4},{4,0},{8,12},{12,8},{1,5},{5,1},{9,13},{13,9},{2,6},{6,2},{1... | collective-permute-start | bytes 786440 | tf_op jit(solution)/shard_map/ppermute | solution.py:32
  58.0 20.8 %collective-permute-start.23 = (f32[4,128,128]{2,1,0:T(8,128)S(1)}, f32[4,128,128]{2,1,0:T(8,128)S(1)}, u32[]{:S(2)}, u32[]{:S(2)}) collective-permute-start(f32[4,128,128]{2,1,0:T(8,128)S(1)} %get-tuple-element.71), channel_id=1, source_target_pairs={{0,8},{4,12},{8,0},{12,4},{1,9},{5,13},{9,1},{13,5},{2,10},{6,14},... | collective-permute-start | bytes 786440 | tf_op jit(solution)/shard_map/ppermute | solution.py:32
  58.5 20.3 %collective-permute-start.24 = (f32[4,128,128]{2,1,0:T(8,128)S(1)}, f32[4,128,128]{2,1,0:T(8,128)S(1)}, u32[]{:S(2)}, u32[]{:S(2)}) collective-permute-start(f32[4,128,128]{2,1,0:T(8,128)S(1)} %get-tuple-element.72), channel_id=1, source_target_pairs={{0,12},{4,8},{8,4},{12,0},{1,13},{5,9},{9,5},{13,1},{2,14},{6,10},... | collective-permute-start | bytes 786440 | tf_op jit(solution)/shard_map/ppermute | solution.py:32

commit v6 on v5

--- a/solution.py
+++ b/solution.py
@@ -161,7 +161,19 @@
 def factor_kernel(parts, chunk, first, column_ref, block_ref, *refs):
     before = refs[: 0 if first else parts]
     refs = refs[len(before) :]
-    after, wave_ref, weight_ref = refs[:parts], refs[parts], refs[parts + 1]
+    after, wave_ref, refs = refs[:parts], refs[parts], refs[parts + 1 :]
+    weight_ref = refs[-1]
+    if first:
+        columns_out, block_out, sems = refs[0], refs[1], refs[2]
+        copies = [
+            pltpu.make_async_copy(column_ref, columns_out, sems.at[0]),
+            pltpu.make_async_copy(block_ref, block_out, sems.at[1]),
+        ]
+        for copy in copies:
+            copy.start()
+        for copy in copies:
+            copy.wait()
+        column_ref, block_ref = columns_out, block_out
     cells, _, slots = block_ref.shape
     channels = after[0].shape[-1]
     span = cells * slots
@@ -210,13 +222,20 @@
     channels = rows - 8
     span = cells * slots
     out = [jax.ShapeDtypeStruct((2 * total // parts, channels), f32)] * parts
+    out.append(jax.ShapeDtypeStruct((2 * total, 2 * span), bf16))
+    in_specs = [whole()] * (2 + len(before))
+    scratch = [pltpu.VMEM((2 * channels, 2 * span), bf16)]
+    if not before:
+        in_specs = [pl.BlockSpec(memory_space=pltpu.HBM)] * 2
+        out += [jax.ShapeDtypeStruct(columns.shape, f32), jax.ShapeDtypeStruct(block.shape, f32)]
+        scratch = [pltpu.SemaphoreType.DMA((2,))] + scratch
     return pl.pallas_call(
         functools.partial(factor_kernel, parts, chunk, not before),
-        in_specs=[whole()] * (2 + len(before)),
-        out_specs=[whole()] * (parts + 1),
-        out_shape=out + [jax.ShapeDtypeStruct((2 * total, 2 * span), bf16)],
+        in_specs=in_specs,
+        out_specs=[whole()] * len(out),
+        out_shape=out,
         input_output_aliases={2 + n: n for n in range(len(before))},
-        scratch_shapes=[pltpu.VMEM((2 * channels, 2 * span), bf16)],
+        scratch_shapes=scratch,
         compiler_params=params(),
         cost_estimate=pl.CostEstimate(
             flops=8 * total * span * channels, bytes_accessed=8 * total * span, transcendentals=0
@@ -305,9 +324,10 @@
 
 
 def message_kernel(
-    basis, sources, table, last, first, step_ref, own_ref, mix_ref, value_ref, *refs
+    basis, sources, table, last, first, own_source, step_ref, mix_ref, value_ref, *refs
 ):
     blocks, refs = refs[:sources], refs[sources:]
+    own_ref = blocks[own_source]
     if last:
         before, refs = refs[:last], refs[last:]
         out_ref, cell_ref, at_ref, own_col_ref, acc_ref, mixed_ref, wide_ref = refs[:7]
@@ -427,7 +447,7 @@
 
 
 def pair_messages(steps, own, blocks, table, mix, w_value, cells, first, before=()):
-    slots = own.shape[-1]
+    slots = blocks[own].shape[-1]
     basis, channels = mix.shape
     around = len(table) * len(table[0]) * len(table[0][0])
     count = steps.shape[1]
@@ -438,8 +458,8 @@
         pltpu.VMEM((cells * slots, 2 * basis * channels), bf16),
     ]
     return pl.pallas_call(
-        functools.partial(message_kernel, basis, len(blocks), table, last, first),
-        in_specs=[pl.BlockSpec(memory_space=pltpu.SMEM)] + [whole()] * (3 + len(blocks) + last),
+        functools.partial(message_kernel, basis, len(blocks), table, last, first, own),
+        in_specs=[pl.BlockSpec(memory_space=pltpu.SMEM)] + [whole()] * (2 + len(blocks) + last),
         out_specs=whole(),
         scratch_shapes=[
             pltpu.VMEM((around, 2 * channels, slots), bf16),
@@ -457,7 +477,7 @@
             transcendentals=0,
         ),
         name="messages",
-    )(steps, own, mix, w_value, *blocks, *before)
+    )(steps, mix, w_value, *blocks, *before)
 
 
 def visits(cells_x, cells_y, cells_z, inside, first=0, end=None):
@@ -581,8 +601,10 @@
     half = 2 * share // size_x
     piece = half // size_z
     chunk = min(piece, share // size_x)
-    parts, tables = (), []
-    for block in gathered:
+    *parts, table, columns, own = partial_factors(columns, chunk, own, (), size_x)
+    gathered[0] = own
+    tables = [table]
+    for block in gathered[1:]:
         *parts, table = partial_factors(columns, chunk, block, parts, size_x)
         tables.append(table)
 
@@ -593,13 +615,6 @@
         for n in range(2, size_x):
             to = jnp.where(lax.rem(other - at_x + size_x, size_x) == n, parts[n], to)
         summed = summed + exchange(to, "gx", s)
-    low, high = (
-        jnp.concatenate(
-            [side[n : n + 1] for n in range(y, cells_x * cells_y, cells_y) for side in sides], axis=0
-        )
-        for y in (0, cells_y - 1)
-    )
-    edges = neighbours(low, high, "gy")
     value_near, summed = lax.optimization_barrier((w_value, summed))
     pieces = [lax.dynamic_slice_in_dim(summed, at_z * piece, piece, 0)]
     for s in range(1, size_z):
@@ -646,7 +661,7 @@
         end = min(begin + at_once, cells_x)
         inner = visits(cells_x, cells_y, cells_z, True, begin * layer, end * layer)
         return pair_messages(
-            jnp.asarray(inner), own, sources.arrays, table[begin : end + 2], radial_mix, value,
+            jnp.asarray(inner), sources.add(own), sources.arrays, table[begin : end + 2], radial_mix, value,
             (end - begin) * layer, begin * layer,
         )
 
@@ -655,10 +670,17 @@
     scale = 1.0 / math.sqrt(grid[0] * grid[1] * grid[2] * slots) / math.sqrt(total_waves)
     rank = at_x * size_z + at_z
     block = at_y * (share // chunk) + (rank * piece) // (2 * chunk)
-    charge, near[0], *edges = lax.optimization_barrier((w_charge, near[0], *edges))
+    charge, near[0], *sides = lax.optimization_barrier((w_charge, near[0], *sides))
     filtered = filtered_piece(scale, block.reshape(1), chunk, pieces, charge, filter_table)
 
-    value_near, filtered = lax.optimization_barrier((w_value, filtered))
+    low, high = (
+        jnp.concatenate(
+            [side[n : n + 1] for n in range(y, cells_x * cells_y, cells_y) for side in sides], axis=0
+        )
+        for y in (0, cells_y - 1)
+    )
+    value_near, filtered, low, high = lax.optimization_barrier((w_value, filtered, low, high))
+    edges = neighbours(low, high, "gy")
     if cells_x > 1:
         near.append(near_messages(at_once, value_near))
     held_z = jnp.concatenate(
@@ -666,6 +688,10 @@
     )
     held_z, *near = lax.optimization_barrier((held_z, *near))
     held = [held_z] + [exchange(held_z, "gx", s) for s in range(1, size_x)]
+
+    found = potentials_of(held, held_z.shape[0] // piece, tables, cells, slots)
+    value_far, first, second, *found = lax.optimization_barrier((w_value, *edges, *found))
+    edges = first, second
 
     sources = Sources()
     flat = (cells_x, cells_y, 1)
@@ -690,12 +716,10 @@
         [[choices(x, y, z) for z in range(2)] for y in range(-1, cells_y + 1)]
         for x in range(-1, cells_x + 1)
     ]
-    found = potentials_of(held, held_z.shape[0] // piece, tables, cells, slots)
-    value_far, *found = lax.optimization_barrier((w_value, *found))
     returned = [found[0]] + [exchange(found[s], "gy", s) for s in range(1, size_y)]
     outer = jnp.asarray(visits(cells_x, cells_y, cells_z, False))
     messages = pair_messages(
-        outer, own, sources.arrays, table, radial_mix, value_far, cells, 0, near
+        outer, sources.add(own), sources.arrays, table, radial_mix, value_far, cells, 0, near
     )
 
     updated = atom_mlp(

time: 81.2 us -> 101 us (1.24)
  waiting for transfers between devices: 0.61 us -> 21.2 us
  starting transfers between devices: 31.8 us -> 26.7 us
  local copies, waits for them, and re-layouts: 2.03 us -> 5.08 us
    ppermute x4, waiting for transfers between devices: 0.01 us -> 12 us  [neighbours(): return (lax.ppermute(first, axis, one), lax.ppermute(second, axis, two))]
    ppermute x21, waiting for transfers between devices: 0.6 us -> 9.22 us  [exchange(): return lax.ppermute(block, axis, pairs)]
    ppermute x21, starting transfers between devices: 22.3 us -> 19.1 us  [exchange(): return lax.ppermute(block, axis, pairs)]
    unnamed x24 -> x34, local copies, waits for them, and re-layouts: 1.96 us -> 5.01 us
    ppermute x4, starting transfers between devices: 9.47 us -> 7.63 us  [neighbours(): return (lax.ppermute(first, axis, one), lax.ppermute(second, axis, two))]
  transfers between devices with their start and end apart: 25 -> 25, of which waited for: 2 -> 6; matrix products, arithmetic and copies ran while one was open for 0% -> 1% of each run, Pallas kernels for 52% -> 40%
where the time goes in v6:
time: 101 us
  Pallas kernels  46.5 us (46%)
  starting transfers between devices  26.7 us (26%)
  waiting for transfers between devices  21.2 us (21%)
  local copies, waits for them, and re-layouts  5.08 us (5%)
  other arithmetic  1.09 us (1%)
    pallas_call x3, Pallas kernels, pair_messages(): pl.pallas_call(functools.partial(message_kernel, basis, len(blocks), tabl...  31.3 us
    ppermute x21, starting transfers between devices, exchange(): return lax.ppermute(block, axis, pairs)  19.1 us
    ppermute x4, waiting for transfers between devices, neighbours(): return (lax.ppermute(first, axis, one), lax.ppermute(second, axis, two))  12 us
    pallas_call x4, Pallas kernels, partial_factors(): pl.pallas_call(functools.partial(factor_kernel, parts, chunk, not before)...  9.33 us
    ppermute x21, waiting for transfers between devices, exchange(): return lax.ppermute(block, axis, pairs)  9.22 us
    ppermute x4, starting transfers between devices, neighbours(): return (lax.ppermute(first, axis, one), lax.ppermute(second, axis, two))  7.63 us
    unnamed x34, local copies, waits for them, and re-layouts  5.01 us
  transfers between devices with their start and end apart: 25, of which 6 were waited for; matrix products, arithmetic and copies ran while one was open for 1% of the time, Pallas kernels for 40%

profile of v6, /device:TPU:0, one launch (start us, length us, event | category | flops | bytes accessed | tf_op | source)
XLA Modules:
  0.0 100.9 jit_solution(889658932727892085)
XLA Ops:
  0.0 1.8 %pack.1 = (f32[4,136,128]{2,1,0:T(8,128)}, f32[512,8]{1,0:T(8,128)}) custom-call(s32[2,1,2]{2,1,0:T(1,128)} %bitcast.11, f32[4,128,128]{2,1,0:T(8,128)} %bitcast.9, f32[12,1,128]{2,1,0:T(1,128)} %bitcast.13, s32[3,2048]{1,0:T(4,128)} %waves_hbm.1), custom_call_target="tpu_custom_call" | custom-call | tf_op jit(solution)/shard_map/pack/pallas_call | solution.py:116
  1.8 3.0 %collective-permute-start.2 = (f32[4,136,128]{2,1,0:T(8,128)}, f32[4,136,128]{2,1,0:T(8,128)S(1)}, u32[]{:S(2)}, u32[]{:S(2)}) collective-permute-start(f32[4,136,128]{2,1,0:T(8,128)} %get-tuple-element.46.block_ref), channel_id=1, source_target_pairs={{0,4},{4,0},{8,12},{12,8},{1,5},{5,1},{9,13},{13,9},{2,6},{6,2},{1... | collective-permute-start | bytes 835592 | tf_op jit(solution)/shard_map/ppermute | solution.py:32
  4.9 1.5 %collective-permute-start.1 = (f32[4,136,128]{2,1,0:T(8,128)}, f32[4,136,128]{2,1,0:T(8,128)S(1)}, u32[]{:S(2)}, u32[]{:S(2)}) collective-permute-start(f32[4,136,128]{2,1,0:T(8,128)} %get-tuple-element.46.block_ref), channel_id=1, source_target_pairs={{0,8},{4,12},{8,0},{12,4},{1,9},{5,13},{9,1},{13,5},{2,10},{6,14},... | collective-permute-start | bytes 835592 | tf_op jit(solution)/shard_map/ppermute | solution.py:32
  6.4 0.0 collective-permute-start
  6.4 0.9 copy-done.12
  7.3 3.1 %factors.4 = (f32[512,128]{1,0:T(8,128)S(1)}, f32[512,128]{1,0:T(8,128)S(1)}, bf16[1024,1024]{1,0:T(8,128)(2,1)S(1)}, f32[512,8]{1,0:T(8,128)S(1)}, f32[4,136,128]{2,1,0:T(8,128)}) custom-call(f32[512,8]{1,0:T(8,128)S(1)} %copy-done.12, f32[4,136,128]{2,1,0:T(8,128)} %get-tuple-element.46.block_ref), custom_call_target="tpu_custom_call" | custom-call | flops 268435456 | bytes 2097152 | tf_op jit(solution)/shard_map/factors/pallas_call | solution.py:232
  10.4 2.1 %collective-permute-done.2.block_ref.refs_2_ = f32[4,136,128]{2,1,0:T(8,128)S(1)} collective-permute-done((f32[4,136,128]{2,1,0:T(8,128)}, f32[4,136,128]{2,1,0:T(8,128)S(1)}, u32[]{:S(2)}, u32[]{:S(2)}) %collective-permute-start.2) | collective-permute-done | bytes 278560 | tf_op jit(solution)/shard_map/ppermute | solution.py:32
  12.6 2.1 %factors.5 = (f32[512,128]{1,0:T(8,128)S(1)}, f32[512,128]{1,0:T(8,128)S(1)}, bf16[1024,1024]{1,0:T(8,128)(2,1)S(1)}) custom-call(f32[512,8]{1,0:T(8,128)S(1)} %get-tuple-element.47.column_ref, f32[4,136,128]{2,1,0:T(8,128)S(1)} %collective-permute-done.2.block_ref.refs_2_, ...), custom_call_target="tpu_custom_call", output_to_operand_aliasing={{0}: (2, {}), {1}: (3, {})} | custom-call | flops 268435456 | bytes 2097152 | tf_op jit(solution)/shard_map/factors/pallas_call | solution.py:232
  14.7 1.3 %copy-done = bf16[1024,1024]{1,0:T(8,128)(2,1)} copy-done((bf16[1024,1024]{1,0:T(8,128)(2,1)}, bf16[1024,1024]{1,0:T(8,128)(2,1)S(1)}, u32[]{:S(2)}) %copy-start) | copy-done | bytes 2097176
  16.0 3.2 %collective-permute-done.1.block_ref = f32[4,136,128]{2,1,0:T(8,128)S(1)} collective-permute-done((f32[4,136,128]{2,1,0:T(8,128)}, f32[4,136,128]{2,1,0:T(8,128)S(1)}, u32[]{:S(2)}, u32[]{:S(2)}) %collective-permute-start.1) | collective-permute-done | bytes 278560 | tf_op jit(solution)/shard_map/ppermute | solution.py:32
  19.1 2.1 %factors.6 = (f32[512,128]{1,0:T(8,128)S(1)}, f32[512,128]{1,0:T(8,128)S(1)}, bf16[1024,1024]{1,0:T(8,128)(2,1)S(1)}) custom-call(f32[512,8]{1,0:T(8,128)S(1)} %get-tuple-element.47.column_ref, f32[4,136,128]{2,1,0:T(8,128)S(1)} %collective-permute-done.1.block_ref, ...), custom_call_target="tpu_custom_call", output_to_operand_aliasing={{0}: (2, {}), {1}: (3, {})} | custom-call | flops 268435456 | bytes 2097152 | tf_op jit(solution)/shard_map/factors/pallas_call | solution.py:232
  21.2 1.3 %copy-done.2 = bf16[1024,1024]{1,0:T(8,128)(2,1)} copy-done((bf16[1024,1024]{1,0:T(8,128)(2,1)}, bf16[1024,1024]{1,0:T(8,128)(2,1)S(1)}, u32[]{:S(2)}) %copy-start.2) | copy-done | bytes 2097176
  22.6 0.0 collective-permute-done.block_ref.refs_4_
  22.6 2.1 %factors.7 = (f32[512,128]{1,0:T(8,128)S(1)}, f32[512,128]{1,0:T(8,128)S(1)}, bf16[1024,1024]{1,0:T(8,128)(2,1)S(1)}) custom-call(f32[512,8]{1,0:T(8,128)S(1)} %get-tuple-element.47.column_ref, f32[4,136,128]{2,1,0:T(8,128)S(1)} %collective-permute-done.block_ref.refs_4_, ...), custom_call_target="tpu_custom_call", output_to_operand_aliasing={{0}: (2, {}), {1}: (3, {})} | custom-call | flops 268435456 | bytes 2097152 | tf_op jit(solution)/shard_map/factors/pallas_call | solution.py:232
  24.7 1.3 %copy-done.4 = bf16[1024,1024]{1,0:T(8,128)(2,1)} copy-done((bf16[1024,1024]{1,0:T(8,128)(2,1)}, bf16[1024,1024]{1,0:T(8,128)(2,1)S(1)}, u32[]{:S(2)}) %copy-start.4) | copy-done | bytes 2097176
  26.0 0.0 collective-permute-start.3
  26.0 0.5 collective-permute-start.7
  26.5 0.0 collective-permute-start.8
  26.5 0.5 collective-permute-start.9
  27.0 1.6 %collective-permute-start.10 = (f32[4,136,128]{2,1,0:T(8,128)}, f32[4,136,128]{2,1,0:T(8,128)S(1)}, u32[]{:S(2)}, u32[]{:S(2)}) collective-permute-start(f32[4,136,128]{2,1,0:T(8,128)} %get-tuple-element.46.block_ref), channel_id=1, source_target_pairs={{0,1},{1,0},{2,3},{3,2},{4,5},{5,4},{6,7},{7,6},{8,9},{9,8},{10,11... | collective-permute-start | bytes 835592 | tf_op jit(solution)/shard_map/ppermute | solution.py:54
  28.6 0.0 collective-permute-done.3
  28.6 3.0 %collective-permute-start.11 = (f32[4,136,128]{2,1,0:T(8,128)}, f32[4,136,128]{2,1,0:T(8,128)S(1)}, u32[]{:S(2)}, u32[]{:S(2)}) collective-permute-start(f32[4,136,128]{2,1,0:T(8,128)} %get-tuple-element.46.block_ref), channel_id=1, source_target_pairs={{0,3},{1,2},{2,1},{3,0},{4,7},{5,6},{6,5},{7,4},{8,11},{9,10},{10,... | collective-permute-start | bytes 835592 | tf_op jit(solution)/shard_map/ppermute | solution.py:54
  31.6 1.0 add.24
  32.7 0.0 collective-permute-done.7.refs_1_
  32.7 0.2 collective-permute-start.4
  32.9 0.0 collective-permute-done.8.refs_3_
  32.9 1.2 %collective-permute-start.5 = (f32[128,128]{1,0:T(8,128)S(1)}, f32[128,128]{1,0:T(8,128)S(1)}, u32[]{:S(2)}, u32[]{:S(2)}) collective-permute-start(f32[128,128]{1,0:T(8,128)S(1)} %get-tuple-element.96), channel_id=1, source_target_pairs={{0,2},{1,3},{2,0},{3,1},{4,6},{5,7},{6,4},{7,5},{8,10},{9,11},{10,... | collective-permute-start | bytes 196616 | tf_op jit(solution)/shard_map/ppermute | solution.py:32
  34.1 0.0 collective-permute-done.9.refs_5_
  34.1 3.0 %collective-permute-start.6 = (f32[128,128]{1,0:T(8,128)S(1)}, f32[128,128]{1,0:T(8,128)S(1)}, u32[]{:S(2)}, u32[]{:S(2)}) collective-permute-start(f32[128,128]{1,0:T(8,128)S(1)} %get-tuple-element.95), channel_id=1, source_target_pairs={{0,3},{1,2},{2,1},{3,0},{4,7},{5,6},{6,5},{7,4},{8,11},{9,10},{10,... | collective-permute-start | bytes 196616 | tf_op jit(solution)/shard_map/ppermute | solution.py:32
  37.1 6.2 %messages.3.refs_9_ = f32[2,1024,128]{2,1,0:T(8,128)S(1)} custom-call(s32[7,2]{1,0:T(8,128)S(1)} %copy-done.16, f32[8,128]{1,0:T(8,128)S(1)} %copy-done.14, f32[128,128]{1,0:T(8,128)S(1)} %copy-done.13, f32[4,136,128]{2,1,0:T(8,128)} %get-tuple-element.58.refs_0_.refs_8_, f32[4,136,128]{2,1,0:T(8,128)} %collective-permute-done.7.refs_1_, ...), custom_call_target="tpu_custom_call" | custom-call | flops 2415919104 | bytes 1048576 | tf_op jit(solution)/shard_map/messages/pallas_call | solution.py:460
  43.4 0.0 copy-start.6
  43.4 0.0 copy-start.10
  43.4 0.0 collective-permute-done.10.refs_0_
  43.4 1.4 %collective-permute-done.11.refs_2_ = f32[4,136,128]{2,1,0:T(8,128)S(1)} collective-permute-done((f32[4,136,128]{2,1,0:T(8,128)}, f32[4,136,128]{2,1,0:T(8,128)S(1)}, u32[]{:S(2)}, u32[]{:S(2)}) %collective-permute-start.11) | collective-permute-done | bytes 278560 | tf_op jit(solution)/shard_map/ppermute | solution.py:54
  45.0 3.9 %collective-permute-done.5.refs_2_ = f32[128,128]{1,0:T(8,128)S(1)} collective-permute-done((f32[128,128]{1,0:T(8,128)S(1)}, f32[128,128]{1,0:T(8,128)S(1)}, u32[]{:S(2)}, u32[]{:S(2)}) %collective-permute-start.5) | collective-permute-done | bytes 65568 | tf_op jit(solution)/shard_map/ppermute | solution.py:32
  48.9 0.0 collective-permute-done.6.refs_3_
  48.9 0.2 filter.1
  49.1 1.3 %collective-permute-start.14 = (f32[128,128]{1,0:T(8,128)S(1)}, f32[128,128]{1,0:T(8,128)S(1)}, u32[]{:S(2)}, u32[]{:S(2)}) collective-permute-start(f32[128,128]{1,0:T(8,128)S(1)} %filter.1), channel_id=1, source_target_pairs={{0,1},{1,0},{2,3},{3,2},{4,5},{5,4},{6,7},{7,6},{8,9},{9,8},{10,11... | collective-permute-start | bytes 196616 | tf_op jit(solution)/shard_map/ppermute | solution.py:32
  50.4 1.9 %collective-permute-start.15 = (f32[128,128]{1,0:T(8,128)S(1)}, f32[128,128]{1,0:T(8,128)S(1)}, u32[]{:S(2)}, u32[]{:S(2)}) collective-permute-start(f32[128,128]{1,0:T(8,128)S(1)} %filter.1), channel_id=1, source_target_pairs={{0,2},{1,3},{2,0},{3,1},{4,6},{5,7},{6,4},{7,5},{8,10},{9,11},{10,... | collective-permute-start | bytes 196616 | tf_op jit(solution)/shard_map/ppermute | solution.py:32
  52.3 1.2 %collective-permute-start.16 = (f32[128,128]{1,0:T(8,128)S(1)}, f32[128,128]{1,0:T(8,128)S(1)}, u32[]{:S(2)}, u32[]{:S(2)}) collective-permute-start(f32[128,128]{1,0:T(8,128)S(1)} %filter.1), channel_id=1, source_target_pairs={{0,3},{1,2},{2,1},{3,0},{4,7},{5,6},{6,5},{7,4},{8,11},{9,10},{10,... | collective-permute-start | bytes 196616 | tf_op jit(solution)/shard_map/ppermute | solution.py:32
  53.5 6.2 %messages.4.refs_10_ = f32[2,1024,128]{2,1,0:T(8,128)S(1)} custom-call(s32[7,2]{1,0:T(8,128)S(1)} %copy-done.16, f32[8,128]{1,0:T(8,128)S(1)} %copy-done.14, f32[128,128]{1,0:T(8,128)S(1)} %copy-done.13, f32[4,136,128]{2,1,0:T(8,128)} %get-tuple-element.58.refs_0_.refs_8_, f32[4,136,128]{2,1,0:T(8,128)} %collective-permute-done.7.refs_1_, ...), custom_call_target="tpu_custom_call" | custom-call | flops 2415919104 | bytes 1048576 | tf_op jit(solution)/shard_map/messages/pallas_call | solution.py:460
  59.8 0.0 collective-permute-done.14
  59.8 0.0 collective-permute-done.15
  59.8 0.1 collective-permute-start.17
  59.9 0.1 collective-permute-start.12
  60.0 3.0 %collective-permute-start.13 = (f32[4,136,128]{2,1,0:T(8,128)S(1)}, f32[4,136,128]{2,1,0:T(8,128)S(1)}, u32[]{:S(2)}, u32[]{:S(2)}) collective-permute-start(f32[4,136,128]{2,1,0:T(8,128)S(1)} %get-tuple-element.85), channel_id=1, source_target_pairs={{0,12},{4,8},{8,4},{12,0},{1,13},{5,9},{9,5},{13,1},{2,14},{6,10},... | collective-permute-start | bytes 835592 | tf_op jit(solution)/shard_map/ppermute | solution.py:54
  63.0 0.5 collective-permute-start.19
  63.5 0.0 collective-permute-done.17.refs_1_
  63.5 0.0 copy-start.15
  63.5 1.9 %potentials.1 = (f32[4,128,128]{2,1,0:T(8,128)S(1)}, f32[4,128,128]{2,1,0:T(8,128)S(1)}, f32[4,128,128]{2,1,0:T(8,128)S(1)}, f32[4,128,128]{2,1,0:T(8,128)S(1)}) custom-call(f32[512,128]{1,0:T(8,128)S(1)} %pad_maximum_fusion.2.refs_0_, f32[512,128]{1,0:T(8,128)S(1)} %collective-permute-done.17.refs_1_, bf16[1024,1024]{1,0:T(8,128)(2,1)S(1)} %get-tuple-element.68.refs_2_, ...), custom_call_target="tpu_custom_call" | custom-call | flops 1610612736 | bytes 8388608 | tf_op jit(solution)/shard_map/potentials/pallas_call | solution.py:308
  65.4 4.0 %collective-permute-done.12.refs_4_ = f32[4,136,128]{2,1,0:T(8,128)S(1)} collective-permute-done((f32[4,136,128]{2,1,0:T(8,128)S(1)}, f32[4,136,128]{2,1,0:T(8,128)S(1)}, u32[]{:S(2)}, u32[]{:S(2)}) %collective-permute-start.12) | collective-permute-done | bytes 278560 | tf_op jit(solution)/shard_map/ppermute | solution.py:54
  69.5 6.5 %collective-permute-done.13.refs_6_ = f32[4,136,128]{2,1,0:T(8,128)S(1)} collective-permute-done((f32[4,136,128]{2,1,0:T(8,128)S(1)}, f32[4,136,128]{2,1,0:T(8,128)S(1)}, u32[]{:S(2)}, u32[]{:S(2)}) %collective-permute-start.13) | collective-permute-done | bytes 278560 | tf_op jit(solution)/shard_map/ppermute | solution.py:54
  76.0 0.1 collective-permute-start.20
  76.1 0.5 collective-permute-start.21
  76.6 0.5 collective-permute-start.22
  77.1 0.3 collective-permute-start.23
  77.4 2.7 %collective-permute-start.24 = (f32[4,128,128]{2,1,0:T(8,128)S(1)}, f32[4,128,128]{2,1,0:T(8,128)S(1)}, u32[]{:S(2)}, u32[]{:S(2)}) collective-permute-start(f32[4,128,128]{2,1,0:T(8,128)S(1)} %get-tuple-element.84), channel_id=1, source_target_pairs={{0,12},{4,8},{8,4},{12,0},{1,13},{5,9},{9,5},{13,1},{2,14},{6,10},... | collective-permute-start | bytes 786440 | tf_op jit(solution)/shard_map/ppermute | solution.py:32
  80.1 0.0 collective-permute-done.20.refs_5_
  80.1 0.0 collective-permute-done.21.refs_7_
  80.1 18.8 %messages.5.refs_2_ = f32[4,128,128]{2,1,0:T(8,128)S(1)} custom-call(s32[7,8]{1,0:T(8,128)S(1)} %copy-done.15, f32[8,128]{1,0:T(8,128)S(1)} %copy-done.14, f32[128,128]{1,0:T(8,128)S(1)} %copy-done.13, f32[4,136,128]{2,1,0:T(8,128)S(1)} %collective-permute-done.10.refs_0_, f32[4,136,128]{2,1,0:T(8,128)S(1)} %collective-permute-done.18.refs_1_, ...), custom_call_target="tpu_custom_call" | custom-call | flops 9663676416 | bytes 1048576 | tf_op jit(solution)/shard_map/messages/pallas_call | solution.py:460
  98.9 0.0 collective-permute-done.22.refs_4_
  98.9 0.0 collective-permute-done.23.refs_5_
  98.9 0.0 collective-permute-done.24.refs_6_
  99.0 2.0 %atom_mlp.1 = f32[4,128,128]{2,1,0:T(8,128)} custom-call(s32[2,1,2]{2,1,0:T(1,128)S(1)} %bitcast.12, f32[4,128,128]{2,1,0:T(8,128)S(1)} %bitcast.10, f32[4,128,128]{2,1,0:T(8,128)S(1)} %messages.5.refs_2_, f32[4,128,128]{2,1,0:T(8,128)S(1)} %get-tuple-element.81.refs_3_, f32[4,128,128]{2,1,0:T(8,128)S(1)} %collective-permute-done.22.refs_4_, ...), custom_call_target="tpu_custom_call" | custom-call | tf_op jit(solution)/shard_map/atom_mlp/pallas_call | solution.py:532
  (38 shorter events, 0.2 us)
Async XLA Ops:
  1.8 10.7 %collective-permute-start.2 = (f32[4,136,128]{2,1,0:T(8,128)}, f32[4,136,128]{2,1,0:T(8,128)S(1)}, u32[]{:S(2)}, u32[]{:S(2)}) collective-permute-start(f32[4,136,128]{2,1,0:T(8,128)} %get-tuple-element.46.block_ref), channel_id=1, source_target_pairs={{0,4},{4,0},{8,12},{12,8},{1,5},{5,1},{9,13},{13,9},{2,6},{6,2},{1... | collective-permute-start | bytes 835592 | tf_op jit(solution)/shard_map/ppermute | solution.py:32
  4.9 14.3 %collective-permute-start.1 = (f32[4,136,128]{2,1,0:T(8,128)}, f32[4,136,128]{2,1,0:T(8,128)S(1)}, u32[]{:S(2)}, u32[]{:S(2)}) collective-permute-start(f32[4,136,128]{2,1,0:T(8,128)} %get-tuple-element.46.block_ref), channel_id=1, source_target_pairs={{0,8},{4,12},{8,0},{12,4},{1,9},{5,13},{9,1},{13,5},{2,10},{6,14},... | collective-permute-start | bytes 835592 | tf_op jit(solution)/shard_map/ppermute | solution.py:32
  6.4 16.2 %collective-permute-start = (f32[4,136,128]{2,1,0:T(8,128)}, f32[4,136,128]{2,1,0:T(8,128)S(1)}, u32[]{:S(2)}, u32[]{:S(2)}) collective-permute-start(f32[4,136,128]{2,1,0:T(8,128)} %get-tuple-element.46.block_ref), channel_id=1, source_target_pairs={{0,12},{4,8},{8,4},{12,0},{1,13},{5,9},{9,5},{13,1},{2,14},{6,10},... | collective-permute-start | bytes 835592 | tf_op jit(solution)/shard_map/ppermute | solution.py:32
  6.4 0.9 copy-start.12
  12.5 24.6 %copy-start.13 = (f32[128,128]{1,0:T(8,128)S(1)}, f32[128,128]{1,0:T(8,128)}, u32[]{:S(2)}) copy-start(f32[128,128]{1,0:T(8,128)} %value_ref.2) | copy-start | bytes 196612
  12.6 24.6 %copy-start.14 = (f32[8,128]{1,0:T(8,128)S(1)}, f32[8,128]{1,0:T(8,128)}, u32[]{:S(2)}) copy-start(f32[8,128]{1,0:T(8,128)} %mix_ref.5) | copy-start | bytes 12292
  12.6 24.6 %copy-start.16 = (s32[7,2]{1,0:T(8,128)S(1)}, s32[7,2]{1,0:T(8,128)}, u32[]{:S(2)}) copy-start(s32[7,2]{1,0:T(8,128)} %constant.47.clone.step_ref) | copy-start | bytes 172
  14.6 1.3 %copy-start = (bf16[1024,1024]{1,0:T(8,128)(2,1)}, bf16[1024,1024]{1,0:T(8,128)(2,1)S(1)}, u32[]{:S(2)}) copy-start(bf16[1024,1024]{1,0:T(8,128)(2,1)S(1)} %get-tuple-element.69.refs_3_) | copy-start | bytes 6291460
  21.2 1.3 %copy-start.2 = (bf16[1024,1024]{1,0:T(8,128)(2,1)}, bf16[1024,1024]{1,0:T(8,128)(2,1)S(1)}, u32[]{:S(2)}) copy-start(bf16[1024,1024]{1,0:T(8,128)(2,1)S(1)} %get-tuple-element.70.refs_4_) | copy-start | bytes 6291460
  24.7 1.4 %copy-start.4 = (bf16[1024,1024]{1,0:T(8,128)(2,1)}, bf16[1024,1024]{1,0:T(8,128)(2,1)S(1)}, u32[]{:S(2)}) copy-start(bf16[1024,1024]{1,0:T(8,128)(2,1)S(1)} %get-tuple-element.71.refs_5_) | copy-start | bytes 6291460
  26.0 2.6 %collective-permute-start.3 = (f32[512,128]{1,0:T(8,128)S(1)}, f32[512,128]{1,0:T(8,128)}, u32[]{:S(2)}, u32[]{:S(2)}) collective-permute-start(f32[512,128]{1,0:T(8,128)S(1)} %get-tuple-element.55), channel_id=1, source_target_pairs={{0,16},{16,0},{1,17},{17,1},{2,18},{18,2},{3,19},{19,3},{4,20},{20... | collective-permute-start | bytes 786440 | tf_op jit(solution)/shard_map/ppermute | solution.py:32
  26.0 6.6 %collective-permute-start.7 = (f32[4,136,128]{2,1,0:T(8,128)}, f32[4,136,128]{2,1,0:T(8,128)}, u32[]{:S(2)}, u32[]{:S(2)}) collective-permute-start(f32[4,136,128]{2,1,0:T(8,128)} %get-tuple-element.58.refs_0_.refs_8_), channel_id=1, source_target_pairs={{0,16},{16,0},{1,17},{17,1},{2,18},{18,2},{3,19},{19,3},{4,20},{20... | collective-permute-start | bytes 835592 | tf_op jit(solution)/shard_map/ppermute | solution.py:32
  26.5 6.3 %collective-permute-start.8 = (f32[4,136,128]{2,1,0:T(8,128)S(1)}, f32[4,136,128]{2,1,0:T(8,128)}, u32[]{:S(2)}, u32[]{:S(2)}) collective-permute-start(f32[4,136,128]{2,1,0:T(8,128)S(1)} %collective-permute-done.2.block_ref.refs_2_), channel_id=1, source_target_pairs={{0,16},{16,0},{1,17},{17,1},{2,18},{18,2},{3,19},{19,3},{4,20},{20... | collective-permute-start | bytes 835592 | tf_op jit(solution)/shard_map/ppermute | solution.py:32
  26.5 7.6 %collective-permute-start.9 = (f32[4,136,128]{2,1,0:T(8,128)S(1)}, f32[4,136,128]{2,1,0:T(8,128)}, u32[]{:S(2)}, u32[]{:S(2)}) collective-permute-start(f32[4,136,128]{2,1,0:T(8,128)S(1)} %collective-permute-done.block_ref.refs_4_), channel_id=1, source_target_pairs={{0,16},{16,0},{1,17},{17,1},{2,18},{18,2},{3,19},{19,3},{4,20},{20... | collective-permute-start | bytes 835592 | tf_op jit(solution)/shard_map/ppermute | solution.py:32
  27.0 16.4 %collective-permute-start.10 = (f32[4,136,128]{2,1,0:T(8,128)}, f32[4,136,128]{2,1,0:T(8,128)S(1)}, u32[]{:S(2)}, u32[]{:S(2)}) collective-permute-start(f32[4,136,128]{2,1,0:T(8,128)} %get-tuple-element.46.block_ref), channel_id=1, source_target_pairs={{0,1},{1,0},{2,3},{3,2},{4,5},{5,4},{6,7},{7,6},{8,9},{9,8},{10,11... | collective-permute-start | bytes 835592 | tf_op jit(solution)/shard_map/ppermute | solution.py:54
  28.6 16.2 %collective-permute-start.11 = (f32[4,136,128]{2,1,0:T(8,128)}, f32[4,136,128]{2,1,0:T(8,128)S(1)}, u32[]{:S(2)}, u32[]{:S(2)}) collective-permute-start(f32[4,136,128]{2,1,0:T(8,128)} %get-tuple-element.46.block_ref), channel_id=1, source_target_pairs={{0,3},{1,2},{2,1},{3,0},{4,7},{5,6},{6,5},{7,4},{8,11},{9,10},{10,... | collective-permute-start | bytes 835592 | tf_op jit(solution)/shard_map/ppermute | solution.py:54
  32.7 12.3 %collective-permute-start.4 = (f32[128,128]{1,0:T(8,128)S(1)}, f32[128,128]{1,0:T(8,128)S(1)}, u32[]{:S(2)}, u32[]{:S(2)}) collective-permute-start(f32[128,128]{1,0:T(8,128)S(1)} %get-tuple-element.97), channel_id=1, source_target_pairs={{0,1},{1,0},{2,3},{3,2},{4,5},{5,4},{6,7},{7,6},{8,9},{9,8},{10,11... | collective-permute-start | bytes 196616 | tf_op jit(solution)/shard_map/ppermute | solution.py:32
  32.9 16.0 %collective-permute-start.5 = (f32[128,128]{1,0:T(8,128)S(1)}, f32[128,128]{1,0:T(8,128)S(1)}, u32[]{:S(2)}, u32[]{:S(2)}) collective-permute-start(f32[128,128]{1,0:T(8,128)S(1)} %get-tuple-element.96), channel_id=1, source_target_pairs={{0,2},{1,3},{2,0},{3,1},{4,6},{5,7},{6,4},{7,5},{8,10},{9,11},{10,... | collective-permute-start | bytes 196616 | tf_op jit(solution)/shard_map/ppermute | solution.py:32
  34.1 14.8 %collective-permute-start.6 = (f32[128,128]{1,0:T(8,128)S(1)}, f32[128,128]{1,0:T(8,128)S(1)}, u32[]{:S(2)}, u32[]{:S(2)}) collective-permute-start(f32[128,128]{1,0:T(8,128)S(1)} %get-tuple-element.95), channel_id=1, source_target_pairs={{0,3},{1,2},{2,1},{3,0},{4,7},{5,6},{6,5},{7,4},{8,11},{9,10},{10,... | collective-permute-start | bytes 196616 | tf_op jit(solution)/shard_map/ppermute | solution.py:32
  43.4 5.5 %copy-start.6 = (f32[2048,128]{1,0:T(8,128)S(1)}, f32[2048,128]{1,0:T(8,128)}, u32[]{:S(2)}) copy-start(f32[2048,128]{1,0:T(8,128)} %refs_5_.1) | copy-start | bytes 3145732
  43.4 5.5 %copy-start.10 = (f32[128,128]{1,0:T(8,128)S(1)}, f32[128,128]{1,0:T(8,128)}, u32[]{:S(2)}) copy-start(f32[128,128]{1,0:T(8,128)} %refs_4_) | copy-start | bytes 196612
  49.1 10.7 %collective-permute-start.14 = (f32[128,128]{1,0:T(8,128)S(1)}, f32[128,128]{1,0:T(8,128)S(1)}, u32[]{:S(2)}, u32[]{:S(2)}) collective-permute-start(f32[128,128]{1,0:T(8,128)S(1)} %filter.1), channel_id=1, source_target_pairs={{0,1},{1,0},{2,3},{3,2},{4,5},{5,4},{6,7},{7,6},{8,9},{9,8},{10,11... | collective-permute-start | bytes 196616 | tf_op jit(solution)/shard_map/ppermute | solution.py:32
  50.4 9.4 %collective-permute-start.15 = (f32[128,128]{1,0:T(8,128)S(1)}, f32[128,128]{1,0:T(8,128)S(1)}, u32[]{:S(2)}, u32[]{:S(2)}) collective-permute-start(f32[128,128]{1,0:T(8,128)S(1)} %filter.1), channel_id=1, source_target_pairs={{0,2},{1,3},{2,0},{3,1},{4,6},{5,7},{6,4},{7,5},{8,10},{9,11},{10,... | collective-permute-start | bytes 196616 | tf_op jit(solution)/shard_map/ppermute | solution.py:32
  52.3 7.5 %collective-permute-start.16 = (f32[128,128]{1,0:T(8,128)S(1)}, f32[128,128]{1,0:T(8,128)S(1)}, u32[]{:S(2)}, u32[]{:S(2)}) collective-permute-start(f32[128,128]{1,0:T(8,128)S(1)} %filter.1), channel_id=1, source_target_pairs={{0,3},{1,2},{2,1},{3,0},{4,7},{5,6},{6,5},{7,4},{8,11},{9,10},{10,... | collective-permute-start | bytes 196616 | tf_op jit(solution)/shard_map/ppermute | solution.py:32
  53.5 10.0 %copy-start.1 = (bf16[1024,1024]{1,0:T(8,128)(2,1)S(1)}, bf16[1024,1024]{1,0:T(8,128)(2,1)}, u32[]{:S(2)}) copy-start(bf16[1024,1024]{1,0:T(8,128)(2,1)} %copy-done) | copy-start | bytes 6291460
  53.5 10.0 %copy-start.3 = (bf16[1024,1024]{1,0:T(8,128)(2,1)S(1)}, bf16[1024,1024]{1,0:T(8,128)(2,1)}, u32[]{:S(2)}) copy-start(bf16[1024,1024]{1,0:T(8,128)(2,1)} %copy-done.2) | copy-start | bytes 6291460
  53.5 10.0 %copy-start.5 = (bf16[1024,1024]{1,0:T(8,128)(2,1)S(1)}, bf16[1024,1024]{1,0:T(8,128)(2,1)}, u32[]{:S(2)}) copy-start(bf16[1024,1024]{1,0:T(8,128)(2,1)} %copy-done.4) | copy-start | bytes 6291460
  59.8 3.7 %collective-permute-start.17 = (f32[512,128]{1,0:T(8,128)S(1)}, f32[512,128]{1,0:T(8,128)S(1)}, u32[]{:S(2)}, u32[]{:S(2)}) collective-permute-start(f32[512,128]{1,0:T(8,128)S(1)} %pad_maximum_fusion.2.refs_0_), channel_id=1, source_target_pairs={{0,16},{16,0},{1,17},{17,1},{2,18},{18,2},{3,19},{19,3},{4,20},{20... | collective-permute-start | bytes 786440 | tf_op jit(solution)/shard_map/ppermute | solution.py:32
  59.9 9.5 %collective-permute-start.12 = (f32[4,136,128]{2,1,0:T(8,128)S(1)}, f32[4,136,128]{2,1,0:T(8,128)S(1)}, u32[]{:S(2)}, u32[]{:S(2)}) collective-permute-start(f32[4,136,128]{2,1,0:T(8,128)S(1)} %get-tuple-element.86), channel_id=1, source_target_pairs={{0,4},{4,0},{8,12},{12,8},{1,5},{5,1},{9,13},{13,9},{2,6},{6,2},{1... | collective-permute-start | bytes 835592 | tf_op jit(solution)/shard_map/ppermute | solution.py:54
  60.0 16.0 %collective-permute-start.13 = (f32[4,136,128]{2,1,0:T(8,128)S(1)}, f32[4,136,128]{2,1,0:T(8,128)S(1)}, u32[]{:S(2)}, u32[]{:S(2)}) collective-permute-start(f32[4,136,128]{2,1,0:T(8,128)S(1)} %get-tuple-element.85), channel_id=1, source_target_pairs={{0,12},{4,8},{8,4},{12,0},{1,13},{5,9},{9,5},{13,1},{2,14},{6,10},... | collective-permute-start | bytes 835592 | tf_op jit(solution)/shard_map/ppermute | solution.py:54
  63.0 14.1 %collective-permute-start.18 = (f32[4,136,128]{2,1,0:T(8,128)S(1)}, f32[4,136,128]{2,1,0:T(8,128)S(1)}, u32[]{:S(2)}, u32[]{:S(2)}) collective-permute-start(f32[4,136,128]{2,1,0:T(8,128)S(1)} %collective-permute-done.10.refs_0_), channel_id=1, source_target_pairs={{0,16},{16,0},{1,17},{17,1},{2,18},{18,2},{3,19},{19,3},{4,20},{20... | collective-permute-start | bytes 835592 | tf_op jit(solution)/shard_map/ppermute | solution.py:32
  63.0 14.4 %collective-permute-start.19 = (f32[4,136,128]{2,1,0:T(8,128)S(1)}, f32[4,136,128]{2,1,0:T(8,128)S(1)}, u32[]{:S(2)}, u32[]{:S(2)}) collective-permute-start(f32[4,136,128]{2,1,0:T(8,128)S(1)} %collective-permute-done.11.refs_2_), channel_id=1, source_target_pairs={{0,16},{16,0},{1,17},{17,1},{2,18},{18,2},{3,19},{19,3},{4,20},{20... | collective-permute-start | bytes 835592 | tf_op jit(solution)/shard_map/ppermute | solution.py:32
  63.5 16.6 %copy-start.15 = (s32[7,8]{1,0:T(8,128)S(1)}, s32[7,8]{1,0:T(8,128)}, u32[]{:S(2)}) copy-start(s32[7,8]{1,0:T(8,128)} %constant.48.clone.step_ref) | copy-start | bytes 676
  76.0 22.9 %copy-start.7 = (f32[2,2,1,128,128]{4,3,2,1,0:T(8,128)S(1)}, f32[2,2,1,128,128]{4,3,2,1,0:T(8,128)}, u32[]{:S(2)}) copy-start(f32[2,2,1,128,128]{4,3,2,1,0:T(8,128)} %param.13) | copy-start | bytes 786436
  76.0 22.9 %copy-start.8 = (f32[128,256]{1,0:T(8,128)S(1)}, f32[128,256]{1,0:T(8,128)}, u32[]{:S(2)}) copy-start(f32[128,256]{1,0:T(8,128)} %refs_7_.1) | copy-start | bytes 393220
  76.0 23.0 %copy-start.9 = (f32[256,128]{1,0:T(8,128)S(1)}, f32[256,128]{1,0:T(8,128)}, u32[]{:S(2)}) copy-start(f32[256,128]{1,0:T(8,128)} %refs_8_.1) | copy-start | bytes 393220
  76.0 23.0 %copy-start.11 = (s32[2,2,1]{1,2,0:T(1,128)S(1)}, s32[2,2,1]{1,2,0:T(1,128)}, u32[]{:S(2)}) copy-start(s32[2,2,1]{1,2,0:T(1,128)} %param.15) | copy-start | bytes 52
  76.0 4.1 %collective-permute-start.20 = (f32[4,136,128]{2,1,0:T(8,128)S(1)}, f32[4,136,128]{2,1,0:T(8,128)S(1)}, u32[]{:S(2)}, u32[]{:S(2)}) collective-permute-start(f32[4,136,128]{2,1,0:T(8,128)S(1)} %collective-permute-done.12.refs_4_), channel_id=1, source_target_pairs={{0,16},{16,0},{1,17},{17,1},{2,18},{18,2},{3,19},{19,3},{4,20},{20... | collective-permute-start | bytes 835592 | tf_op jit(solution)/shard_map/ppermute | solution.py:32
  76.1 4.0 %collective-permute-start.21 = (f32[4,136,128]{2,1,0:T(8,128)S(1)}, f32[4,136,128]{2,1,0:T(8,128)S(1)}, u32[]{:S(2)}, u32[]{:S(2)}) collective-permute-start(f32[4,136,128]{2,1,0:T(8,128)S(1)} %collective-permute-done.13.refs_6_), channel_id=1, source_target_pairs={{0,16},{16,0},{1,17},{17,1},{2,18},{18,2},{3,19},{19,3},{4,20},{20... | collective-permute-start | bytes 835592 | tf_op jit(solution)/shard_map/ppermute | solution.py:32
  76.6 22.3 %collective-permute-start.22 = (f32[4,128,128]{2,1,0:T(8,128)S(1)}, f32[4,128,128]{2,1,0:T(8,128)S(1)}, u32[]{:S(2)}, u32[]{:S(2)}) collective-permute-start(f32[4,128,128]{2,1,0:T(8,128)S(1)} %get-tuple-element.82), channel_id=1, source_target_pairs={{0,4},{4,0},{8,12},{12,8},{1,5},{5,1},{9,13},{13,9},{2,6},{6,2},{1... | collective-permute-start | bytes 786440 | tf_op jit(solution)/shard_map/ppermute | solution.py:32
  77.1 21.8 %collective-permute-start.23 = (f32[4,128,128]{2,1,0:T(8,128)S(1)}, f32[4,128,128]{2,1,0:T(8,128)S(1)}, u32[]{:S(2)}, u32[]{:S(2)}) collective-permute-start(f32[4,128,128]{2,1,0:T(8,128)S(1)} %get-tuple-element.83), channel_id=1, source_target_pairs={{0,8},{4,12},{8,0},{12,4},{1,9},{5,13},{9,1},{13,5},{2,10},{6,14},... | collective-permute-start | bytes 786440 | tf_op jit(solution)/shard_map/ppermute | solution.py:32
  77.4 21.5 %collective-permute-start.24 = (f32[4,128,128]{2,1,0:T(8,128)S(1)}, f32[4,128,128]{2,1,0:T(8,128)S(1)}, u32[]{:S(2)}, u32[]{:S(2)}) collective-permute-start(f32[4,128,128]{2,1,0:T(8,128)S(1)} %get-tuple-element.84), channel_id=1, source_target_pairs={{0,12},{4,8},{8,4},{12,0},{1,13},{5,9},{9,5},{13,1},{2,14},{6,10},... | collective-permute-start | bytes 786440 | tf_op jit(solution)/shard_map/ppermute | solution.py:32

commit v7 on v5

--- a/solution.py
+++ b/solution.py
@@ -79,25 +79,19 @@
 
 
 def pack_kernel(
-    shape, grid, counts_hbm, feature_hbm, position_hbm, waves_hbm, out_ref, column_ref,
-    counts_ref, feature_ref, position_ref, waves_ref, sems,
+    shape, grid, counts_hbm, feature_hbm, position_hbm, out_ref,
+    counts_ref, feature_ref, position_ref, sems,
 ):
-    total = column_ref.shape[0]
-    begin = pl.multiple_of(lax.axis_index("gy") * total, total)
     cells, channels, slots = feature_ref.shape
     copies = [
         pltpu.make_async_copy(counts_hbm, counts_ref, sems.at[0]),
         pltpu.make_async_copy(position_hbm, position_ref, sems.at[1]),
-        pltpu.make_async_copy(waves_hbm.at[:, pl.ds(begin, total)], waves_ref, sems.at[2]),
-        pltpu.make_async_copy(feature_hbm, feature_ref, sems.at[3]),
+        pltpu.make_async_copy(feature_hbm, feature_ref, sems.at[2]),
     ]
     for copy in copies:
         copy.start()
-    for copy in copies[:3]:
+    for copy in copies:
         copy.wait()
-    waves = waves_ref[...].astype(f32)
-    column_ref[...] = jnp.concatenate([waves, jnp.zeros((5, total), f32)], axis=0).T
-    copies[3].wait()
     slot = lax.broadcasted_iota(jnp.int32, (channels, slots), 1)
     for cell in range(cells):
         place = place_of(cell, shape)
@@ -111,26 +105,22 @@
         out_ref[cell, channels:, :] = jnp.concatenate(rows + [jnp.zeros((2, slots), f32)], axis=0)
 
 
-def pack(shape, grid, counts, features, positions, waves, total):
+def pack(shape, grid, counts, features, positions):
     cells, channels, slots = features.shape
     return pl.pallas_call(
         functools.partial(pack_kernel, shape, grid),
-        in_specs=[pl.BlockSpec(memory_space=pltpu.HBM)] * 4,
-        out_specs=[whole()] * 2,
-        out_shape=[
-            jax.ShapeDtypeStruct((cells, channels + 8, slots), f32),
-            jax.ShapeDtypeStruct((total, 8), f32),
-        ],
+        in_specs=[pl.BlockSpec(memory_space=pltpu.HBM)] * 3,
+        out_specs=whole(),
+        out_shape=jax.ShapeDtypeStruct((cells, channels + 8, slots), f32),
         scratch_shapes=[
             pltpu.SMEM(counts.shape, jnp.int32),
             pltpu.VMEM(features.shape, f32),
             pltpu.VMEM(positions.shape, f32),
-            pltpu.VMEM((3, total), jnp.int32),
-            pltpu.SemaphoreType.DMA((4,)),
+            pltpu.SemaphoreType.DMA((3,)),
         ],
-        compiler_params=params(PACK_LIMIT),
+        compiler_params=params(),
         name="pack",
-    )(counts, features, positions, waves)
+    )(counts, features, positions)
 
 
 def fitted(function, terms):
@@ -161,12 +151,18 @@
 def factor_kernel(parts, chunk, first, column_ref, block_ref, *refs):
     before = refs[: 0 if first else parts]
     refs = refs[len(before) :]
-    after, wave_ref, weight_ref = refs[:parts], refs[parts], refs[parts + 1]
+    after, wave_ref, refs = refs[:parts], refs[parts], refs[parts + 1 :]
+    weight_ref = refs[-1]
     cells, _, slots = block_ref.shape
     channels = after[0].shape[-1]
     span = cells * slots
     total = wave_ref.shape[0] // 2
     at_x = lax.axis_index("gx")
+    if first:
+        begin = pl.multiple_of(lax.axis_index("gy") * total, total)
+        rows = column_ref[:, pl.ds(begin, total)].astype(f32)
+        column_ref = refs[0]
+        column_ref[...] = jnp.concatenate([rows, jnp.zeros((5, total), f32)], axis=0).T
     for cell in range(cells):
         high, low = split(block_ref[cell, :channels, :])
         for at in (cell * slots, span + cell * slots):
@@ -204,17 +200,19 @@
         after[n][...] = both if first else before[n][...] + both
 
 
-def partial_factors(columns, chunk, block, before, parts):
-    total = columns.shape[0]
+def partial_factors(columns, total, chunk, block, before, parts):
     cells, rows, slots = block.shape
     channels = rows - 8
     span = cells * slots
     out = [jax.ShapeDtypeStruct((2 * total // parts, channels), f32)] * parts
+    out.append(jax.ShapeDtypeStruct((2 * total, 2 * span), bf16))
+    if not before:
+        out.append(jax.ShapeDtypeStruct((total, 8), f32))
     return pl.pallas_call(
         functools.partial(factor_kernel, parts, chunk, not before),
         in_specs=[whole()] * (2 + len(before)),
-        out_specs=[whole()] * (parts + 1),
-        out_shape=out + [jax.ShapeDtypeStruct((2 * total, 2 * span), bf16)],
+        out_specs=[whole()] * len(out),
+        out_shape=out,
         input_output_aliases={2 + n: n for n in range(len(before))},
         scratch_shapes=[pltpu.VMEM((2 * channels, 2 * span), bf16)],
         compiler_params=params(),
@@ -305,9 +303,10 @@
 
 
 def message_kernel(
-    basis, sources, table, last, first, step_ref, own_ref, mix_ref, value_ref, *refs
+    basis, sources, table, last, first, own_source, step_ref, mix_ref, value_ref, *refs
 ):
     blocks, refs = refs[:sources], refs[sources:]
+    own_ref = blocks[own_source]
     if last:
         before, refs = refs[:last], refs[last:]
         out_ref, cell_ref, at_ref, own_col_ref, acc_ref, mixed_ref, wide_ref = refs[:7]
@@ -427,7 +426,7 @@
 
 
 def pair_messages(steps, own, blocks, table, mix, w_value, cells, first, before=()):
-    slots = own.shape[-1]
+    slots = blocks[own].shape[-1]
     basis, channels = mix.shape
     around = len(table) * len(table[0]) * len(table[0][0])
     count = steps.shape[1]
@@ -438,8 +437,8 @@
         pltpu.VMEM((cells * slots, 2 * basis * channels), bf16),
     ]
     return pl.pallas_call(
-        functools.partial(message_kernel, basis, len(blocks), table, last, first),
-        in_specs=[pl.BlockSpec(memory_space=pltpu.SMEM)] + [whole()] * (3 + len(blocks) + last),
+        functools.partial(message_kernel, basis, len(blocks), table, last, first, own),
+        in_specs=[pl.BlockSpec(memory_space=pltpu.SMEM)] + [whole()] * (2 + len(blocks) + last),
         out_specs=whole(),
         scratch_shapes=[
             pltpu.VMEM((around, 2 * channels, slots), bf16),
@@ -457,7 +456,7 @@
             transcendentals=0,
         ),
         name="messages",
-    )(steps, own, mix, w_value, *blocks, *before)
+    )(steps, mix, w_value, *blocks, *before)
 
 
 def visits(cells_x, cells_y, cells_z, inside, first=0, end=None):
@@ -565,13 +564,14 @@
     flat_features = features.reshape(cells, channels, slots)
 
     share = total_waves // size_y
-    own, columns = pack(
-        shape, grid, some_counts, flat_features, positions.reshape(cells * 3, 1, slots), waves, share
-    )
+    own = pack(shape, grid, some_counts, flat_features, positions.reshape(cells * 3, 1, slots))
     rows = own.shape[1]
     packed = own.reshape(shape + (rows, slots))
 
-    gathered = [own] + [exchange(own, "gy", s) for s in range(1, size_y)]
+    gathered = [own]
+    for s in range(1, size_y):
+        high = 1 << (s.bit_length() - 1)
+        gathered.append(exchange(gathered[s - high], "gy", high))
     if cells_z == 1:
         sides = neighbours(own, own, "gz", same=True)
     else:
@@ -581,9 +581,12 @@
     half = 2 * share // size_x
     piece = half // size_z
     chunk = min(piece, share // size_x)
-    parts, tables = (), []
-    for block in gathered:
-        *parts, table = partial_factors(columns, chunk, block, parts, size_x)
+    first = min(1, size_y - 1)
+    waves, gathered[first] = lax.optimization_barrier((waves, gathered[first]))
+    *parts, table, columns = partial_factors(waves, share, chunk, own, (), size_x)
+    tables = [table]
+    for block in gathered[1:]:
+        *parts, table = partial_factors(columns, share, chunk, block, parts, size_x)
         tables.append(table)
 
     summed = parts[0]
@@ -646,7 +649,7 @@
         end = min(begin + at_once, cells_x)
         inner = visits(cells_x, cells_y, cells_z, True, begin * layer, end * layer)
         return pair_messages(
-            jnp.asarray(inner), own, sources.arrays, table[begin : end + 2], radial_mix, value,
+            jnp.asarray(inner), sources.add(own), sources.arrays, table[begin : end + 2], radial_mix, value,
             (end - begin) * layer, begin * layer,
         )
 
@@ -655,7 +658,7 @@
     scale = 1.0 / math.sqrt(grid[0] * grid[1] * grid[2] * slots) / math.sqrt(total_waves)
     rank = at_x * size_z + at_z
     block = at_y * (share // chunk) + (rank * piece) // (2 * chunk)
-    charge, near[0], *edges = lax.optimization_barrier((w_charge, near[0], *edges))
+    charge, near[0] = lax.optimization_barrier((w_charge, near[0]))
     filtered = filtered_piece(scale, block.reshape(1), chunk, pieces, charge, filter_table)
 
     value_near, filtered = lax.optimization_barrier((w_value, filtered))
@@ -664,7 +667,8 @@
     held_z = jnp.concatenate(
         [filtered] + [exchange(filtered, "gz", s) for s in range(1, size_z)], axis=0
     )
-    held_z, *near = lax.optimization_barrier((held_z, *near))
+    held_z, *rest = lax.optimization_barrier((held_z, *near, *edges))
+    near, edges = rest[:-2], rest[-2:]
     held = [held_z] + [exchange(held_z, "gx", s) for s in range(1, size_x)]
 
     sources = Sources()
@@ -695,7 +699,7 @@
     returned = [found[0]] + [exchange(found[s], "gy", s) for s in range(1, size_y)]
     outer = jnp.asarray(visits(cells_x, cells_y, cells_z, False))
     messages = pair_messages(
-        outer, own, sources.arrays, table, radial_mix, value_far, cells, 0, near
+        outer, sources.add(own), sources.arrays, table, radial_mix, value_far, cells, 0, near
     )
 
     updated = atom_mlp(

time: 81.2 us -> 75.7 us (0.932)
  starting transfers between devices: 31.8 us -> 27.1 us
  Pallas kernels: 46 us -> 42.7 us
  waiting for transfers between devices: 0.61 us -> 1.98 us
  local copies, waits for them, and re-layouts: 2.03 us -> 3.2 us
    ppermute x4, starting transfers between devices: 9.47 us -> 6.5 us  [neighbours(): return (lax.ppermute(first, axis, one), lax.ppermute(second, axis, two))]
    ppermute x21, starting transfers between devices: 22.3 us -> 20.6 us  [exchange(): return lax.ppermute(block, axis, pairs)]
    ppermute x21, waiting for transfers between devices: 0.6 us -> 1.97 us  [exchange(): return lax.ppermute(block, axis, pairs)]
    pallas_call x3, Pallas kernels: 30.8 us -> 29.5 us  [pair_messages(): pl.pallas_call(functools.partial(message_kernel, basis, len(blocks), tabl...]
    pallas_call x1, Pallas kernels: 1.85 us -> 0.61 us  [pack(): pl.pallas_call(functools.partial(pack_kernel, shape, grid), in_specs=[pl....]
    unnamed x24 -> x28, local copies, waits for them, and re-layouts: 1.96 us -> 3.13 us
  transfers between devices with their start and end apart: 25 -> 25, of which waited for: 2 -> 4; matrix products, arithmetic and copies ran while one was open for 0% -> 0% of each run, Pallas kernels for 52% -> 53%
where the time goes in v7:
time: 75.7 us; the launch traced here: 75.4 us
  Pallas kernels  42.7 us (56%)
  starting transfers between devices  27.1 us (36%)
  local copies, waits for them, and re-layouts  3.2 us (4%)
  waiting for transfers between devices  1.98 us (3%)
    pallas_call x3, Pallas kernels, pair_messages(): pl.pallas_call(functools.partial(message_kernel, basis, len(blocks), tabl...  29.5 us
    ppermute x21, starting transfers between devices, exchange(): return lax.ppermute(block, axis, pairs)  20.6 us
    pallas_call x4, Pallas kernels, partial_factors(): pl.pallas_call(functools.partial(factor_kernel, parts, chunk, not before)...  8.52 us
    ppermute x4, starting transfers between devices, neighbours(): return (lax.ppermute(first, axis, one), lax.ppermute(second, axis, two))  6.5 us
    unnamed x28, local copies, waits for them, and re-layouts  3.13 us
    pallas_call x1, Pallas kernels, atom_mlp(): pl.pallas_call(functools.partial(mlp_kernel, len(potentials), shape), in_...  2 us
    ppermute x21, waiting for transfers between devices, exchange(): return lax.ppermute(block, axis, pairs)  1.97 us
    pallas_call x1, Pallas kernels, potentials_of(): pl.pallas_call(functools.partial(potential_kernel, len(held), pieces, len...  1.88 us
  transfers between devices with their start and end apart: 25, of which 4 were waited for; matrix products, arithmetic and copies ran while one was open for 0% of the time, Pallas kernels for 53%

profile of v7, /device:TPU:0, one launch (start us, length us, event | category | flops | bytes accessed | tf_op | source)
XLA Modules:
  0.0 75.4 jit_solution(1769337204391216561)
XLA Ops:
  0.0 0.9 %copy-done.1 = f32[2,2,1,128,128]{4,3,2,1,0:T(8,128)S(1)} copy-done((f32[2,2,1,128,128]{4,3,2,1,0:T(8,128)S(1)}, f32[2,2,1,128,128]{4,3,2,1,0:T(8,128)}, u32[]{:S(2)}) %copy-start.1) | copy-done | bytes 262168
  1.0 0.7 copy-done.6
  1.6 0.7 copy-done.7
  2.3 0.6 pack.1.block_ref.refs_0_.refs_8_
  2.9 3.0 %collective-permute-start = (f32[4,136,128]{2,1,0:T(8,128)S(1)}, f32[4,136,128]{2,1,0:T(8,128)S(1)}, u32[]{:S(2)}, u32[]{:S(2)}) collective-permute-start(f32[4,136,128]{2,1,0:T(8,128)S(1)} %pack.1.block_ref.refs_0_.refs_8_), channel_id=1, source_target_pairs={{0,4},{4,0},{8,12},{12,8},{1,5},{5,1},{9,13},{13,9},{2,6},{6,2},{1... | collective-permute-start | bytes 835592 | tf_op jit(solution)/shard_map/ppermute | solution.py:32
  5.9 1.5 %collective-permute-start.2 = (f32[4,136,128]{2,1,0:T(8,128)S(1)}, f32[4,136,128]{2,1,0:T(8,128)S(1)}, u32[]{:S(2)}, u32[]{:S(2)}) collective-permute-start(f32[4,136,128]{2,1,0:T(8,128)S(1)} %pack.1.block_ref.refs_0_.refs_8_), channel_id=1, source_target_pairs={{0,8},{4,12},{8,0},{12,4},{1,9},{5,13},{9,1},{13,5},{2,10},{6,14},... | collective-permute-start | bytes 835592 | tf_op jit(solution)/shard_map/ppermute | solution.py:32
  7.5 1.6 %collective-permute-start.13 = (f32[4,136,128]{2,1,0:T(8,128)S(1)}, f32[4,136,128]{2,1,0:T(8,128)S(1)}, u32[]{:S(2)}, u32[]{:S(2)}) collective-permute-start(f32[4,136,128]{2,1,0:T(8,128)S(1)} %pack.1.block_ref.refs_0_.refs_8_), channel_id=1, source_target_pairs={{0,1},{1,0},{2,3},{3,2},{4,5},{5,4},{6,7},{7,6},{8,9},{9,8},{10,11... | collective-permute-start | bytes 835592 | tf_op jit(solution)/shard_map/ppermute | solution.py:54
  9.0 0.0 collective-permute-start.7
  9.0 2.5 %collective-permute-start.14 = (f32[4,136,128]{2,1,0:T(8,128)S(1)}, f32[4,136,128]{2,1,0:T(8,128)S(1)}, u32[]{:S(2)}, u32[]{:S(2)}) collective-permute-start(f32[4,136,128]{2,1,0:T(8,128)S(1)} %pack.1.block_ref.refs_0_.refs_8_), channel_id=1, source_target_pairs={{0,3},{1,2},{2,1},{3,0},{4,7},{5,6},{6,5},{7,4},{8,11},{9,10},{10,... | collective-permute-start | bytes 835592 | tf_op jit(solution)/shard_map/ppermute | solution.py:54
  11.5 1.1 %collective-permute-done.block_ref.refs_2_ = f32[4,136,128]{2,1,0:T(8,128)S(1)} collective-permute-done((f32[4,136,128]{2,1,0:T(8,128)S(1)}, f32[4,136,128]{2,1,0:T(8,128)S(1)}, u32[]{:S(2)}, u32[]{:S(2)}) %collective-permute-start) | collective-permute-done | bytes 278560 | tf_op jit(solution)/shard_map/ppermute | solution.py:32
  12.6 1.8 %collective-permute-start.1 = (f32[4,136,128]{2,1,0:T(8,128)S(1)}, f32[4,136,128]{2,1,0:T(8,128)S(1)}, u32[]{:S(2)}, u32[]{:S(2)}) collective-permute-start(f32[4,136,128]{2,1,0:T(8,128)S(1)} %collective-permute-done.block_ref.refs_2_), channel_id=1, source_target_pairs={{0,8},{4,12},{8,0},{12,4},{1,9},{5,13},{9,1},{13,5},{2,10},{6,14},... | collective-permute-start | bytes 835592 | tf_op jit(solution)/shard_map/ppermute | solution.py:32
  14.4 0.8 %copy-done.10 = s32[3,2048]{1,0:T(4,128)S(1)} copy-done((s32[3,2048]{1,0:T(4,128)S(1)}, s32[3,2048]{1,0:T(4,128)}, u32[]{:S(2)}) %copy-start.10) | copy-done | bytes 24600
  15.1 2.3 %factors.4 = (f32[512,128]{1,0:T(8,128)S(1)}, f32[512,128]{1,0:T(8,128)S(1)}, bf16[1024,1024]{1,0:T(8,128)(2,1)S(1)}, f32[512,8]{1,0:T(8,128)S(1)}) custom-call(s32[3,2048]{1,0:T(4,128)S(1)} %copy-done.10, f32[4,136,128]{2,1,0:T(8,128)S(1)} %pack.1.block_ref.refs_0_.refs_8_), custom_call_target="tpu_custom_call" | custom-call | flops 268435456 | bytes 2097152 | tf_op jit(solution)/shard_map/factors/pallas_call | solution.py:211
  17.4 2.1 %factors.5 = (f32[512,128]{1,0:T(8,128)S(1)}, f32[512,128]{1,0:T(8,128)S(1)}, bf16[1024,1024]{1,0:T(8,128)(2,1)S(1)}) custom-call(f32[512,8]{1,0:T(8,128)S(1)} %get-tuple-element.41.column_ref, f32[4,136,128]{2,1,0:T(8,128)S(1)} %collective-permute-done.block_ref.refs_2_, ...), custom_call_target="tpu_custom_call", output_to_operand_aliasing={{0}: (2, {}), {1}: (3, {})} | custom-call | flops 268435456 | bytes 2097152 | tf_op jit(solution)/shard_map/factors/pallas_call | solution.py:211
  19.5 0.0 collective-permute-done.2.block_ref
  19.5 0.1 collective-permute-start.8
  19.6 2.1 %factors.6 = (f32[512,128]{1,0:T(8,128)S(1)}, f32[512,128]{1,0:T(8,128)S(1)}, bf16[1024,1024]{1,0:T(8,128)(2,1)S(1)}) custom-call(f32[512,8]{1,0:T(8,128)S(1)} %get-tuple-element.41.column_ref, f32[4,136,128]{2,1,0:T(8,128)S(1)} %collective-permute-done.2.block_ref, ...), custom_call_target="tpu_custom_call", output_to_operand_aliasing={{0}: (2, {}), {1}: (3, {})} | custom-call | flops 268435456 | bytes 2097152 | tf_op jit(solution)/shard_map/factors/pallas_call | solution.py:211
  21.7 0.0 collective-permute-done.13.refs_0_
  21.7 0.0 copy-start.9
  21.7 0.0 copy-start.11
  21.7 0.0 copy-start.13
  21.7 0.0 collective-permute-done.1.block_ref.refs_4_
  21.8 2.1 %factors.7 = (f32[512,128]{1,0:T(8,128)S(1)}, f32[512,128]{1,0:T(8,128)S(1)}, bf16[1024,1024]{1,0:T(8,128)(2,1)S(1)}) custom-call(f32[512,8]{1,0:T(8,128)S(1)} %get-tuple-element.41.column_ref, f32[4,136,128]{2,1,0:T(8,128)S(1)} %collective-permute-done.1.block_ref.refs_4_, ...), custom_call_target="tpu_custom_call", output_to_operand_aliasing={{0}: (2, {}), {1}: (3, {})} | custom-call | flops 268435456 | bytes 2097152 | tf_op jit(solution)/shard_map/factors/pallas_call | solution.py:211
  23.9 0.6 collective-permute-start.3
  24.4 0.1 collective-permute-start.9
  24.6 1.6 %collective-permute-start.15 = (f32[4,136,128]{2,1,0:T(8,128)S(1)}, f32[4,136,128]{2,1,0:T(8,128)S(1)}, u32[]{:S(2)}, u32[]{:S(2)}) collective-permute-start(f32[4,136,128]{2,1,0:T(8,128)S(1)} %get-tuple-element.76), channel_id=1, source_target_pairs={{0,4},{4,0},{8,12},{12,8},{1,5},{5,1},{9,13},{13,9},{2,6},{6,2},{1... | collective-permute-start | bytes 835592 | tf_op jit(solution)/shard_map/ppermute | solution.py:54
  26.2 0.0 collective-permute-done.3
  26.2 0.9 %collective-permute-start.16 = (f32[4,136,128]{2,1,0:T(8,128)S(1)}, f32[4,136,128]{2,1,0:T(8,128)S(1)}, u32[]{:S(2)}, u32[]{:S(2)}) collective-permute-start(f32[4,136,128]{2,1,0:T(8,128)S(1)} %get-tuple-element.75), channel_id=1, source_target_pairs={{0,12},{4,8},{8,4},{12,0},{1,13},{5,9},{9,5},{13,1},{2,14},{6,10},... | collective-permute-start | bytes 835592 | tf_op jit(solution)/shard_map/ppermute | solution.py:54
  27.1 1.6 %collective-permute-start.4 = (f32[128,128]{1,0:T(8,128)S(1)}, f32[128,128]{1,0:T(8,128)S(1)}, u32[]{:S(2)}, u32[]{:S(2)}) collective-permute-start(f32[128,128]{1,0:T(8,128)S(1)} %get-tuple-element.87), channel_id=1, source_target_pairs={{0,1},{1,0},{2,3},{3,2},{4,5},{5,4},{6,7},{7,6},{8,9},{9,8},{10,11... | collective-permute-start | bytes 196616 | tf_op jit(solution)/shard_map/ppermute | solution.py:32
  28.8 0.0 collective-permute-done.8.refs_3_
  28.8 2.6 %collective-permute-start.5 = (f32[128,128]{1,0:T(8,128)S(1)}, f32[128,128]{1,0:T(8,128)S(1)}, u32[]{:S(2)}, u32[]{:S(2)}) collective-permute-start(f32[128,128]{1,0:T(8,128)S(1)} %get-tuple-element.86), channel_id=1, source_target_pairs={{0,2},{1,3},{2,0},{3,1},{4,6},{5,7},{6,4},{7,5},{8,10},{9,11},{10,... | collective-permute-start | bytes 196616 | tf_op jit(solution)/shard_map/ppermute | solution.py:32
  31.4 0.0 collective-permute-done.9.refs_5_
  31.4 0.2 collective-permute-start.6
  31.6 5.6 %messages.3.refs_9_ = f32[2,1024,128]{2,1,0:T(8,128)S(1)} custom-call(s32[7,2]{1,0:T(8,128)S(1)} %copy-done.13, f32[8,128]{1,0:T(8,128)S(1)} %copy-done.11, f32[128,128]{1,0:T(8,128)S(1)} %copy-done.9, f32[4,136,128]{2,1,0:T(8,128)S(1)} %pack.1.block_ref.refs_0_.refs_8_, f32[4,136,128]{2,1,0:T(8,128)S(1)} %collective-permute-done.7.refs_1_, ...), custom_call_target="tpu_custom_call" | custom-call | flops 2415919104 | bytes 1048576 | tf_op jit(solution)/shard_map/messages/pallas_call | solution.py:439
  37.2 0.0 collective-permute-done.5.refs_2_
  37.2 0.3 collective-permute-done.6.refs_3_
  37.5 0.2 filter.1
  37.7 0.8 %collective-permute-start.10 = (f32[128,128]{1,0:T(8,128)S(1)}, f32[128,128]{1,0:T(8,128)S(1)}, u32[]{:S(2)}, u32[]{:S(2)}) collective-permute-start(f32[128,128]{1,0:T(8,128)S(1)} %filter.1), channel_id=1, source_target_pairs={{0,1},{1,0},{2,3},{3,2},{4,5},{5,4},{6,7},{7,6},{8,9},{9,8},{10,11... | collective-permute-start | bytes 196616 | tf_op jit(solution)/shard_map/ppermute | solution.py:32
  38.5 3.2 %collective-permute-start.11 = (f32[128,128]{1,0:T(8,128)S(1)}, f32[128,128]{1,0:T(8,128)S(1)}, u32[]{:S(2)}, u32[]{:S(2)}) collective-permute-start(f32[128,128]{1,0:T(8,128)S(1)} %filter.1), channel_id=1, source_target_pairs={{0,2},{1,3},{2,0},{3,1},{4,6},{5,7},{6,4},{7,5},{8,10},{9,11},{10,... | collective-permute-start | bytes 196616 | tf_op jit(solution)/shard_map/ppermute | solution.py:32
  41.7 0.5 collective-permute-start.12
  42.2 5.5 %messages.4.refs_10_ = f32[2,1024,128]{2,1,0:T(8,128)S(1)} custom-call(s32[7,2]{1,0:T(8,128)S(1)} %copy-done.13, f32[8,128]{1,0:T(8,128)S(1)} %copy-done.11, f32[128,128]{1,0:T(8,128)S(1)} %copy-done.9, f32[4,136,128]{2,1,0:T(8,128)S(1)} %pack.1.block_ref.refs_0_.refs_8_, f32[4,136,128]{2,1,0:T(8,128)S(1)} %collective-permute-done.7.refs_1_, ...), custom_call_target="tpu_custom_call" | custom-call | flops 2415919104 | bytes 1048576 | tf_op jit(solution)/shard_map/messages/pallas_call | solution.py:439
  47.6 0.0 collective-permute-done.10
  47.7 0.1 collective-permute-done.12
  47.8 0.0 collective-permute-done.16.refs_6_
  47.8 0.1 collective-permute-start.17
  47.9 0.5 collective-permute-start.18
  48.4 0.1 collective-permute-start.19
  48.5 0.4 collective-permute-start.20
  48.9 0.1 collective-permute-start.21
  49.0 0.4 collective-permute-done.17.refs_1_
  49.4 1.9 %potentials.1 = (f32[4,128,128]{2,1,0:T(8,128)S(1)}, f32[4,128,128]{2,1,0:T(8,128)S(1)}, f32[4,128,128]{2,1,0:T(8,128)S(1)}, f32[4,128,128]{2,1,0:T(8,128)S(1)}) custom-call(f32[512,128]{1,0:T(8,128)S(1)} %pad_maximum_fusion.2.refs_0_, f32[512,128]{1,0:T(8,128)S(1)} %collective-permute-done.17.refs_1_, bf16[1024,1024]{1,0:T(8,128)(2,1)S(1)} %get-tuple-element.58.refs_2_, ...), custom_call_target="tpu_custom_call" | custom-call | flops 1610612736 | bytes 8388608 | tf_op jit(solution)/shard_map/potentials/pallas_call | solution.py:287
  51.3 0.0 copy-start.2
  51.3 0.0 copy-start.3
  51.3 0.0 copy-start.4
  51.3 0.0 copy-start.8
  51.4 1.1 %collective-permute-start.22 = (f32[4,128,128]{2,1,0:T(8,128)S(1)}, f32[4,128,128]{2,1,0:T(8,128)S(1)}, u32[]{:S(2)}, u32[]{:S(2)}) collective-permute-start(f32[4,128,128]{2,1,0:T(8,128)S(1)} %get-tuple-element.72), channel_id=1, source_target_pairs={{0,4},{4,0},{8,12},{12,8},{1,5},{5,1},{9,13},{13,9},{2,6},{6,2},{1... | collective-permute-start | bytes 786440 | tf_op jit(solution)/shard_map/ppermute | solution.py:32
  52.5 0.0 collective-permute-done.18.refs_1_
  52.5 1.5 %collective-permute-start.23 = (f32[4,128,128]{2,1,0:T(8,128)S(1)}, f32[4,128,128]{2,1,0:T(8,128)S(1)}, u32[]{:S(2)}, u32[]{:S(2)}) collective-permute-start(f32[4,128,128]{2,1,0:T(8,128)S(1)} %get-tuple-element.73), channel_id=1, source_target_pairs={{0,8},{4,12},{8,0},{12,4},{1,9},{5,13},{9,1},{13,5},{2,10},{6,14},... | collective-permute-start | bytes 786440 | tf_op jit(solution)/shard_map/ppermute | solution.py:32
  54.0 0.0 collective-permute-done.19.refs_3_
  54.0 0.9 %collective-permute-start.24 = (f32[4,128,128]{2,1,0:T(8,128)S(1)}, f32[4,128,128]{2,1,0:T(8,128)S(1)}, u32[]{:S(2)}, u32[]{:S(2)}) collective-permute-start(f32[4,128,128]{2,1,0:T(8,128)S(1)} %get-tuple-element.74), channel_id=1, source_target_pairs={{0,12},{4,8},{8,4},{12,0},{1,13},{5,9},{9,5},{13,1},{2,14},{6,10},... | collective-permute-start | bytes 786440 | tf_op jit(solution)/shard_map/ppermute | solution.py:32
  54.9 18.4 %messages.5.refs_2_ = f32[4,128,128]{2,1,0:T(8,128)S(1)} custom-call(s32[7,8]{1,0:T(8,128)S(1)} %copy-done.12, f32[8,128]{1,0:T(8,128)S(1)} %copy-done.11, f32[128,128]{1,0:T(8,128)S(1)} %copy-done.9, f32[4,136,128]{2,1,0:T(8,128)S(1)} %collective-permute-done.13.refs_0_, f32[4,136,128]{2,1,0:T(8,128)S(1)} %collective-permute-done.18.refs_1_, ...), custom_call_target="tpu_custom_call" | custom-call | flops 9663676416 | bytes 1048576 | tf_op jit(solution)/shard_map/messages/pallas_call | solution.py:439
  73.3 0.0 collective-permute-done.22.refs_4_
  73.3 0.0 collective-permute-done.23.refs_5_
  73.4 2.0 %atom_mlp.1 = f32[4,128,128]{2,1,0:T(8,128)} custom-call(s32[2,1,2]{2,1,0:T(1,128)S(1)} %bitcast.13, f32[4,128,128]{2,1,0:T(8,128)S(1)} %bitcast.10, f32[4,128,128]{2,1,0:T(8,128)S(1)} %messages.5.refs_2_, f32[4,128,128]{2,1,0:T(8,128)S(1)} %get-tuple-element.71.refs_3_, f32[4,128,128]{2,1,0:T(8,128)S(1)} %collective-permute-done.22.refs_4_, ...), custom_call_target="tpu_custom_call" | custom-call | tf_op jit(solution)/shard_map/atom_mlp/pallas_call | solution.py:511
  (31 shorter events, 0.2 us)
Async XLA Ops:
  0.0 0.9 %copy-start.1 = (f32[2,2,1,128,128]{4,3,2,1,0:T(8,128)S(1)}, f32[2,2,1,128,128]{4,3,2,1,0:T(8,128)}, u32[]{:S(2)}) copy-start(f32[2,2,1,128,128]{4,3,2,1,0:T(8,128)} %param.13) | copy-start | bytes 786436
  1.0 0.7 copy-start.6
  1.6 0.7 copy-start.7
  2.9 9.7 %collective-permute-start = (f32[4,136,128]{2,1,0:T(8,128)S(1)}, f32[4,136,128]{2,1,0:T(8,128)S(1)}, u32[]{:S(2)}, u32[]{:S(2)}) collective-permute-start(f32[4,136,128]{2,1,0:T(8,128)S(1)} %pack.1.block_ref.refs_0_.refs_8_), channel_id=1, source_target_pairs={{0,4},{4,0},{8,12},{12,8},{1,5},{5,1},{9,13},{13,9},{2,6},{6,2},{1... | collective-permute-start | bytes 835592 | tf_op jit(solution)/shard_map/ppermute | solution.py:32
  5.9 13.5 %collective-permute-start.2 = (f32[4,136,128]{2,1,0:T(8,128)S(1)}, f32[4,136,128]{2,1,0:T(8,128)S(1)}, u32[]{:S(2)}, u32[]{:S(2)}) collective-permute-start(f32[4,136,128]{2,1,0:T(8,128)S(1)} %pack.1.block_ref.refs_0_.refs_8_), channel_id=1, source_target_pairs={{0,8},{4,12},{8,0},{12,4},{1,9},{5,13},{9,1},{13,5},{2,10},{6,14},... | collective-permute-start | bytes 835592 | tf_op jit(solution)/shard_map/ppermute | solution.py:32
  7.5 14.2 %collective-permute-start.13 = (f32[4,136,128]{2,1,0:T(8,128)S(1)}, f32[4,136,128]{2,1,0:T(8,128)S(1)}, u32[]{:S(2)}, u32[]{:S(2)}) collective-permute-start(f32[4,136,128]{2,1,0:T(8,128)S(1)} %pack.1.block_ref.refs_0_.refs_8_), channel_id=1, source_target_pairs={{0,1},{1,0},{2,3},{3,2},{4,5},{5,4},{6,7},{7,6},{8,9},{9,8},{10,11... | collective-permute-start | bytes 835592 | tf_op jit(solution)/shard_map/ppermute | solution.py:54
  9.0 18.1 %collective-permute-start.7 = (f32[4,136,128]{2,1,0:T(8,128)S(1)}, f32[4,136,128]{2,1,0:T(8,128)S(1)}, u32[]{:S(2)}, u32[]{:S(2)}) collective-permute-start(f32[4,136,128]{2,1,0:T(8,128)S(1)} %pack.1.block_ref.refs_0_.refs_8_), channel_id=1, source_target_pairs={{0,16},{16,0},{1,17},{17,1},{2,18},{18,2},{3,19},{19,3},{4,20},{20... | collective-permute-start | bytes 835592 | tf_op jit(solution)/shard_map/ppermute | solution.py:32
  9.0 15.5 %collective-permute-start.14 = (f32[4,136,128]{2,1,0:T(8,128)S(1)}, f32[4,136,128]{2,1,0:T(8,128)S(1)}, u32[]{:S(2)}, u32[]{:S(2)}) collective-permute-start(f32[4,136,128]{2,1,0:T(8,128)S(1)} %pack.1.block_ref.refs_0_.refs_8_), channel_id=1, source_target_pairs={{0,3},{1,2},{2,1},{3,0},{4,7},{5,6},{6,5},{7,4},{8,11},{9,10},{10,... | collective-permute-start | bytes 835592 | tf_op jit(solution)/shard_map/ppermute | solution.py:54
  12.6 9.1 %collective-permute-start.1 = (f32[4,136,128]{2,1,0:T(8,128)S(1)}, f32[4,136,128]{2,1,0:T(8,128)S(1)}, u32[]{:S(2)}, u32[]{:S(2)}) collective-permute-start(f32[4,136,128]{2,1,0:T(8,128)S(1)} %collective-permute-done.block_ref.refs_2_), channel_id=1, source_target_pairs={{0,8},{4,12},{8,0},{12,4},{1,9},{5,13},{9,1},{13,5},{2,10},{6,14},... | collective-permute-start | bytes 835592 | tf_op jit(solution)/shard_map/ppermute | solution.py:32
  14.4 0.8 %copy-start.10 = (s32[3,2048]{1,0:T(4,128)S(1)}, s32[3,2048]{1,0:T(4,128)}, u32[]{:S(2)}) copy-start(s32[3,2048]{1,0:T(4,128)} %column_ref) | copy-start | bytes 73732
  19.5 9.3 %collective-permute-start.8 = (f32[4,136,128]{2,1,0:T(8,128)S(1)}, f32[4,136,128]{2,1,0:T(8,128)S(1)}, u32[]{:S(2)}, u32[]{:S(2)}) collective-permute-start(f32[4,136,128]{2,1,0:T(8,128)S(1)} %collective-permute-done.block_ref.refs_2_), channel_id=1, source_target_pairs={{0,16},{16,0},{1,17},{17,1},{2,18},{18,2},{3,19},{19,3},{4,20},{20... | collective-permute-start | bytes 835592 | tf_op jit(solution)/shard_map/ppermute | solution.py:32
  21.7 9.9 %copy-start.9 = (f32[128,128]{1,0:T(8,128)S(1)}, f32[128,128]{1,0:T(8,128)}, u32[]{:S(2)}) copy-start(f32[128,128]{1,0:T(8,128)} %value_ref.2) | copy-start | bytes 196612
  21.7 9.9 %copy-start.11 = (f32[8,128]{1,0:T(8,128)S(1)}, f32[8,128]{1,0:T(8,128)}, u32[]{:S(2)}) copy-start(f32[8,128]{1,0:T(8,128)} %mix_ref.5) | copy-start | bytes 12292
  21.7 9.8 %copy-start.13 = (s32[7,2]{1,0:T(8,128)S(1)}, s32[7,2]{1,0:T(8,128)}, u32[]{:S(2)}) copy-start(s32[7,2]{1,0:T(8,128)} %constant.47.clone.step_ref) | copy-start | bytes 172
  23.9 2.3 %collective-permute-start.3 = (f32[512,128]{1,0:T(8,128)S(1)}, f32[512,128]{1,0:T(8,128)S(1)}, u32[]{:S(2)}, u32[]{:S(2)}) collective-permute-start(f32[512,128]{1,0:T(8,128)S(1)} %get-tuple-element.50), channel_id=1, source_target_pairs={{0,16},{16,0},{1,17},{17,1},{2,18},{18,2},{3,19},{19,3},{4,20},{20... | collective-permute-start | bytes 786440 | tf_op jit(solution)/shard_map/ppermute | solution.py:32
  24.4 7.0 %collective-permute-start.9 = (f32[4,136,128]{2,1,0:T(8,128)S(1)}, f32[4,136,128]{2,1,0:T(8,128)S(1)}, u32[]{:S(2)}, u32[]{:S(2)}) collective-permute-start(f32[4,136,128]{2,1,0:T(8,128)S(1)} %collective-permute-done.1.block_ref.refs_4_), channel_id=1, source_target_pairs={{0,16},{16,0},{1,17},{17,1},{2,18},{18,2},{3,19},{19,3},{4,20},{20... | collective-permute-start | bytes 835592 | tf_op jit(solution)/shard_map/ppermute | solution.py:32
  24.6 23.2 %collective-permute-start.15 = (f32[4,136,128]{2,1,0:T(8,128)S(1)}, f32[4,136,128]{2,1,0:T(8,128)S(1)}, u32[]{:S(2)}, u32[]{:S(2)}) collective-permute-start(f32[4,136,128]{2,1,0:T(8,128)S(1)} %get-tuple-element.76), channel_id=1, source_target_pairs={{0,4},{4,0},{8,12},{12,8},{1,5},{5,1},{9,13},{13,9},{2,6},{6,2},{1... | collective-permute-start | bytes 835592 | tf_op jit(solution)/shard_map/ppermute | solution.py:54
  26.2 21.7 %collective-permute-start.16 = (f32[4,136,128]{2,1,0:T(8,128)S(1)}, f32[4,136,128]{2,1,0:T(8,128)S(1)}, u32[]{:S(2)}, u32[]{:S(2)}) collective-permute-start(f32[4,136,128]{2,1,0:T(8,128)S(1)} %get-tuple-element.75), channel_id=1, source_target_pairs={{0,12},{4,8},{8,4},{12,0},{1,13},{5,9},{9,5},{13,1},{2,14},{6,10},... | collective-permute-start | bytes 835592 | tf_op jit(solution)/shard_map/ppermute | solution.py:54
  27.1 10.1 %collective-permute-start.4 = (f32[128,128]{1,0:T(8,128)S(1)}, f32[128,128]{1,0:T(8,128)S(1)}, u32[]{:S(2)}, u32[]{:S(2)}) collective-permute-start(f32[128,128]{1,0:T(8,128)S(1)} %get-tuple-element.87), channel_id=1, source_target_pairs={{0,1},{1,0},{2,3},{3,2},{4,5},{5,4},{6,7},{7,6},{8,9},{9,8},{10,11... | collective-permute-start | bytes 196616 | tf_op jit(solution)/shard_map/ppermute | solution.py:32
  28.8 8.5 %collective-permute-start.5 = (f32[128,128]{1,0:T(8,128)S(1)}, f32[128,128]{1,0:T(8,128)S(1)}, u32[]{:S(2)}, u32[]{:S(2)}) collective-permute-start(f32[128,128]{1,0:T(8,128)S(1)} %get-tuple-element.86), channel_id=1, source_target_pairs={{0,2},{1,3},{2,0},{3,1},{4,6},{5,7},{6,4},{7,5},{8,10},{9,11},{10,... | collective-permute-start | bytes 196616 | tf_op jit(solution)/shard_map/ppermute | solution.py:32
  31.4 6.2 %copy-start = (f32[2048,128]{1,0:T(8,128)S(1)}, f32[2048,128]{1,0:T(8,128)}, u32[]{:S(2)}) copy-start(f32[2048,128]{1,0:T(8,128)} %refs_5_.1) | copy-start | bytes 3145732
  31.4 6.2 %copy-start.5 = (f32[128,128]{1,0:T(8,128)S(1)}, f32[128,128]{1,0:T(8,128)}, u32[]{:S(2)}) copy-start(f32[128,128]{1,0:T(8,128)} %refs_4_) | copy-start | bytes 196612
  31.4 6.2 %collective-permute-start.6 = (f32[128,128]{1,0:T(8,128)S(1)}, f32[128,128]{1,0:T(8,128)S(1)}, u32[]{:S(2)}, u32[]{:S(2)}) collective-permute-start(f32[128,128]{1,0:T(8,128)S(1)} %get-tuple-element.85), channel_id=1, source_target_pairs={{0,3},{1,2},{2,1},{3,0},{4,7},{5,6},{6,5},{7,4},{8,11},{9,10},{10,... | collective-permute-start | bytes 196616 | tf_op jit(solution)/shard_map/ppermute | solution.py:32
  37.7 9.9 %collective-permute-start.10 = (f32[128,128]{1,0:T(8,128)S(1)}, f32[128,128]{1,0:T(8,128)S(1)}, u32[]{:S(2)}, u32[]{:S(2)}) collective-permute-start(f32[128,128]{1,0:T(8,128)S(1)} %filter.1), channel_id=1, source_target_pairs={{0,1},{1,0},{2,3},{3,2},{4,5},{5,4},{6,7},{7,6},{8,9},{9,8},{10,11... | collective-permute-start | bytes 196616 | tf_op jit(solution)/shard_map/ppermute | solution.py:32
  38.5 9.1 %collective-permute-start.11 = (f32[128,128]{1,0:T(8,128)S(1)}, f32[128,128]{1,0:T(8,128)S(1)}, u32[]{:S(2)}, u32[]{:S(2)}) collective-permute-start(f32[128,128]{1,0:T(8,128)S(1)} %filter.1), channel_id=1, source_target_pairs={{0,2},{1,3},{2,0},{3,1},{4,6},{5,7},{6,4},{7,5},{8,10},{9,11},{10,... | collective-permute-start | bytes 196616 | tf_op jit(solution)/shard_map/ppermute | solution.py:32
  41.7 6.1 %collective-permute-start.12 = (f32[128,128]{1,0:T(8,128)S(1)}, f32[128,128]{1,0:T(8,128)S(1)}, u32[]{:S(2)}, u32[]{:S(2)}) collective-permute-start(f32[128,128]{1,0:T(8,128)S(1)} %filter.1), channel_id=1, source_target_pairs={{0,3},{1,2},{2,1},{3,0},{4,7},{5,6},{6,5},{7,4},{8,11},{9,10},{10,... | collective-permute-start | bytes 196616 | tf_op jit(solution)/shard_map/ppermute | solution.py:32
  47.8 1.6 %collective-permute-start.17 = (f32[512,128]{1,0:T(8,128)S(1)}, f32[512,128]{1,0:T(8,128)S(1)}, u32[]{:S(2)}, u32[]{:S(2)}) collective-permute-start(f32[512,128]{1,0:T(8,128)S(1)} %pad_maximum_fusion.2.refs_0_), channel_id=1, source_target_pairs={{0,16},{16,0},{1,17},{17,1},{2,18},{18,2},{3,19},{19,3},{4,20},{20... | collective-permute-start | bytes 786440 | tf_op jit(solution)/shard_map/ppermute | solution.py:32
  47.9 4.6 %collective-permute-start.18 = (f32[4,136,128]{2,1,0:T(8,128)S(1)}, f32[4,136,128]{2,1,0:T(8,128)S(1)}, u32[]{:S(2)}, u32[]{:S(2)}) collective-permute-start(f32[4,136,128]{2,1,0:T(8,128)S(1)} %collective-permute-done.13.refs_0_), channel_id=1, source_target_pairs={{0,16},{16,0},{1,17},{17,1},{2,18},{18,2},{3,19},{19,3},{4,20},{20... | collective-permute-start | bytes 835592 | tf_op jit(solution)/shard_map/ppermute | solution.py:32
  48.4 5.6 %collective-permute-start.19 = (f32[4,136,128]{2,1,0:T(8,128)S(1)}, f32[4,136,128]{2,1,0:T(8,128)S(1)}, u32[]{:S(2)}, u32[]{:S(2)}) collective-permute-start(f32[4,136,128]{2,1,0:T(8,128)S(1)} %collective-permute-done.14.refs_2_), channel_id=1, source_target_pairs={{0,16},{16,0},{1,17},{17,1},{2,18},{18,2},{3,19},{19,3},{4,20},{20... | collective-permute-start | bytes 835592 | tf_op jit(solution)/shard_map/ppermute | solution.py:32
  48.5 6.4 %collective-permute-start.20 = (f32[4,136,128]{2,1,0:T(8,128)S(1)}, f32[4,136,128]{2,1,0:T(8,128)S(1)}, u32[]{:S(2)}, u32[]{:S(2)}) collective-permute-start(f32[4,136,128]{2,1,0:T(8,128)S(1)} %collective-permute-done.15.refs_4_), channel_id=1, source_target_pairs={{0,16},{16,0},{1,17},{17,1},{2,18},{18,2},{3,19},{19,3},{4,20},{20... | collective-permute-start | bytes 835592 | tf_op jit(solution)/shard_map/ppermute | solution.py:32
  48.9 6.0 %collective-permute-start.21 = (f32[4,136,128]{2,1,0:T(8,128)S(1)}, f32[4,136,128]{2,1,0:T(8,128)S(1)}, u32[]{:S(2)}, u32[]{:S(2)}) collective-permute-start(f32[4,136,128]{2,1,0:T(8,128)S(1)} %collective-permute-done.16.refs_6_), channel_id=1, source_target_pairs={{0,16},{16,0},{1,17},{17,1},{2,18},{18,2},{3,19},{19,3},{4,20},{20... | collective-permute-start | bytes 835592 | tf_op jit(solution)/shard_map/ppermute | solution.py:32
  49.4 5.5 %copy-start.12 = (s32[7,8]{1,0:T(8,128)S(1)}, s32[7,8]{1,0:T(8,128)}, u32[]{:S(2)}) copy-start(s32[7,8]{1,0:T(8,128)} %constant.48.clone.step_ref) | copy-start | bytes 676
  51.3 22.1 %copy-start.2 = (f32[2,2,1,128,128]{4,3,2,1,0:T(8,128)S(1)}, f32[2,2,1,128,128]{4,3,2,1,0:T(8,128)}, u32[]{:S(2)}) copy-start(f32[2,2,1,128,128]{4,3,2,1,0:T(8,128)} %param.13) | copy-start | bytes 786436
  51.3 22.1 %copy-start.3 = (f32[128,256]{1,0:T(8,128)S(1)}, f32[128,256]{1,0:T(8,128)}, u32[]{:S(2)}) copy-start(f32[128,256]{1,0:T(8,128)} %refs_7_.1) | copy-start | bytes 393220
  51.3 22.1 %copy-start.4 = (f32[256,128]{1,0:T(8,128)S(1)}, f32[256,128]{1,0:T(8,128)}, u32[]{:S(2)}) copy-start(f32[256,128]{1,0:T(8,128)} %refs_8_.1) | copy-start | bytes 393220
  51.3 22.1 %copy-start.8 = (s32[2,2,1]{1,2,0:T(1,128)S(1)}, s32[2,2,1]{1,2,0:T(1,128)}, u32[]{:S(2)}) copy-start(s32[2,2,1]{1,2,0:T(1,128)} %param.15) | copy-start | bytes 52
  51.4 22.0 %collective-permute-start.22 = (f32[4,128,128]{2,1,0:T(8,128)S(1)}, f32[4,128,128]{2,1,0:T(8,128)S(1)}, u32[]{:S(2)}, u32[]{:S(2)}) collective-permute-start(f32[4,128,128]{2,1,0:T(8,128)S(1)} %get-tuple-element.72), channel_id=1, source_target_pairs={{0,4},{4,0},{8,12},{12,8},{1,5},{5,1},{9,13},{13,9},{2,6},{6,2},{1... | collective-permute-start | bytes 786440 | tf_op jit(solution)/shard_map/ppermute | solution.py:32
  52.5 20.8 %collective-permute-start.23 = (f32[4,128,128]{2,1,0:T(8,128)S(1)}, f32[4,128,128]{2,1,0:T(8,128)S(1)}, u32[]{:S(2)}, u32[]{:S(2)}) collective-permute-start(f32[4,128,128]{2,1,0:T(8,128)S(1)} %get-tuple-element.73), channel_id=1, source_target_pairs={{0,8},{4,12},{8,0},{12,4},{1,9},{5,13},{9,1},{13,5},{2,10},{6,14},... | collective-permute-start | bytes 786440 | tf_op jit(solution)/shard_map/ppermute | solution.py:32
  54.0 19.4 %collective-permute-start.24 = (f32[4,128,128]{2,1,0:T(8,128)S(1)}, f32[4,128,128]{2,1,0:T(8,128)S(1)}, u32[]{:S(2)}, u32[]{:S(2)}) collective-permute-start(f32[4,128,128]{2,1,0:T(8,128)S(1)} %get-tuple-element.74), channel_id=1, source_target_pairs={{0,12},{4,8},{8,4},{12,0},{1,13},{5,9},{9,5},{13,1},{2,14},{6,10},... | collective-permute-start | bytes 786440 | tf_op jit(solution)/shard_map/ppermute | solution.py:32

commit v8 on v7

--- a/solution.py
+++ b/solution.py
@@ -303,7 +303,7 @@
 
 
 def message_kernel(
-    basis, sources, table, last, first, own_source, step_ref, mix_ref, value_ref, *refs
+    basis, sources, table, together, once, last, first, own_source, step_ref, mix_ref, value_ref, *refs
 ):
     blocks, refs = refs[:sources], refs[sources:]
     own_ref = blocks[own_source]
@@ -312,13 +312,12 @@
         out_ref, cell_ref, at_ref, own_col_ref, acc_ref, mixed_ref, wide_ref = refs[:7]
     else:
         out_ref, cell_ref, at_ref, own_col_ref, acc_ref = refs[:5]
-    left_0, left_1, left_2, right_0, right_1, right_2 = refs[-6:]
+    left_ref = refs[-1]
     count = step_ref.shape[1]
     cells = acc_ref.shape[0]
     slots = own_ref.shape[-1]
     along, planes = len(table[0]), len(table[0][0])
     channels = value_ref.shape[0]
-    lefts, rights = (left_0, left_1, left_2), (right_0, right_1, right_2)
 
     for x, columns in enumerate(table):
         for y, column in enumerate(columns):
@@ -341,21 +340,15 @@
         for axis in range(3):
             own_col_ref[cell, axis] = jnp.broadcast_to(columns[:, axis : axis + 1], (slots, slots))
 
-    def fill(step, move):
+    def fill(step, visit, move):
         place_x = step_ref[0, step] + 1 + (move - 1)
         place_y = step_ref[1, step]
-        plane = step_ref[2, step]
-        if last:
-            plane = jnp.where(is_even("gz"), plane, 1 - plane)
+        plane = plane_of(step)
         shift_z = step_ref[3, step].astype(f32)
-        left, right = lefts[move], rights[move]
         own = step_ref[4, step]
         near = []
         for n in range(3):
             number = (place_x * along + place_y + n) * planes + plane
-            cell = cell_ref[number]
-            right[:, n * slots : (n + 1) * slots] = cell
-            right[:, (3 + n) * slots : (4 + n) * slots] = cell
             at = at_ref[number]
             near.append((at[0:1] + float(move - 1), at[1:2] + float(n - 1), at[2:3] + shift_z))
         tile = 16
@@ -383,28 +376,46 @@
                         term = term * ratio
                     high, low = split(term)
                     row = b * slots + at
-                    left[row : row + tile, n * slots : (n + 1) * slots] = high
-                    left[row : row + tile, (3 + n) * slots : (4 + n) * slots] = low
-
-    def product(move):
+                    here = 9 * visit + 3 * move + n
+                    left_ref[row : row + tile, here * slots : (here + 1) * slots] = high
+                    here += 9 * together
+                    left_ref[row : row + tile, here * slots : (here + 1) * slots] = low
+
+    def plane_of(step):
+        plane = step_ref[2, step]
+        return jnp.where(is_even("gz"), plane, 1 - plane) if last else plane
+
+    def near_of(step):
+        held = []
+        for n in range(together):
+            x, y = step_ref[0, step + n], step_ref[1, step + n]
+            plane = plane_of(step + n)
+            held += [
+                cell_ref[((x + over_x) * along + y + over_y) * planes + plane]
+                for over_x in range(3)
+                for over_y in range(3)
+            ]
+        return jnp.concatenate(held + held, axis=1)
+
+    def product(step):
         return lax.dot_general(
-            lefts[move][...], rights[move][...], (((1,), (1,)), ((), ())), preferred_element_type=f32
+            left_ref[...], near_of(step), (((1,), (1,)), ((), ())), preferred_element_type=f32
         )
 
-    fill(0, 0)
-
-    def visit(step, carry):
+    def visit(group, carry):
+        step = group * together
         own = step_ref[4, step]
-        fresh = step_ref[5, step] == 1
-        acc_ref[own] = jnp.where(fresh, 0.0, acc_ref[own]) + product(0)
-        fill(step, 1)
-        acc_ref[own] += product(1)
-        fill(step, 2)
-        acc_ref[own] += product(2)
-        fill(jnp.minimum(step + 1, count - 1), 0)
+        for n in range(together):
+            for move in range(3):
+                fill(step + n, n, move)
+        if once:
+            acc_ref[own] = product(step)
+        else:
+            fresh = step_ref[5, step] == 1
+            acc_ref[own] = jnp.where(fresh, 0.0, acc_ref[own]) + product(step)
         return carry
 
-    lax.fori_loop(0, count, visit, 0)
+    lax.fori_loop(0, count // together, visit, 0)
     wide = basis * channels
     for cell in range(cells):
         gathered = acc_ref[cell, :, :channels] + acc_ref[cell, :, channels:]
@@ -430,6 +441,9 @@
     basis, channels = mix.shape
     around = len(table) * len(table[0]) * len(table[0][0])
     count = steps.shape[1]
+    per_cell = np.bincount(steps[4], minlength=cells)
+    once = bool(np.all(per_cell == per_cell[0]))
+    together = int(per_cell[0]) if once else 1
     last = len(before)
     sums = (cells, basis * slots, channels)
     closing = [
@@ -437,7 +451,9 @@
         pltpu.VMEM((cells * slots, 2 * basis * channels), bf16),
     ]
     return pl.pallas_call(
-        functools.partial(message_kernel, basis, len(blocks), table, last, first, own),
+        functools.partial(
+            message_kernel, basis, len(blocks), table, together, once, last, first, own
+        ),
         in_specs=[pl.BlockSpec(memory_space=pltpu.SMEM)] + [whole()] * (2 + len(blocks) + last),
         out_specs=whole(),
         scratch_shapes=[
@@ -447,8 +463,7 @@
             pltpu.VMEM((cells, basis * slots, 2 * channels), f32),
         ]
         + closing * bool(last)
-        + [pltpu.VMEM((basis * slots, 6 * slots), bf16)] * 3
-        + [pltpu.VMEM((2 * channels, 6 * slots), bf16)] * 3,
+        + [pltpu.VMEM((basis * slots, 18 * together * slots), bf16)],
         out_shape=jax.ShapeDtypeStruct((cells, channels, slots) if last else sums, f32),
         compiler_params=params(),
         cost_estimate=pl.CostEstimate(
@@ -456,7 +471,7 @@
             transcendentals=0,
         ),
         name="messages",
-    )(steps, mix, w_value, *blocks, *before)
+    )(jnp.asarray(steps), mix, w_value, *blocks, *before)
 
 
 def visits(cells_x, cells_y, cells_z, inside, first=0, end=None):
@@ -649,7 +664,7 @@
         end = min(begin + at_once, cells_x)
         inner = visits(cells_x, cells_y, cells_z, True, begin * layer, end * layer)
         return pair_messages(
-            jnp.asarray(inner), sources.add(own), sources.arrays, table[begin : end + 2], radial_mix, value,
+            inner, sources.add(own), sources.arrays, table[begin : end + 2], radial_mix, value,
             (end - begin) * layer, begin * layer,
         )
 
@@ -697,7 +712,7 @@
     found = potentials_of(held, held_z.shape[0] // piece, tables, cells, slots)
     value_far, *found = lax.optimization_barrier((w_value, *found))
     returned = [found[0]] + [exchange(found[s], "gy", s) for s in range(1, size_y)]
-    outer = jnp.asarray(visits(cells_x, cells_y, cells_z, False))
+    outer = visits(cells_x, cells_y, cells_z, False)
     messages = pair_messages(
         outer, sources.add(own), sources.arrays, table, radial_mix, value_far, cells, 0, near
     )

time: 75.7 us -> 70.3 us (0.929)
  Pallas kernels: 42.7 us -> 36.2 us
  waiting for transfers between devices: 1.98 us -> 3.13 us
    pallas_call x3, Pallas kernels: 29.5 us -> 23 us  [pair_messages(): pl.pallas_call(functools.partial(message_kernel, basis, len(blocks), tabl...]
    ppermute x21, waiting for transfers between devices: 1.97 us -> 3.12 us  [exchange(): return lax.ppermute(block, axis, pairs)]
  transfers between devices with their start and end apart: 25 -> 25, of which waited for: 4 -> 4; matrix products, arithmetic and copies ran while one was open for 0% -> 0% of each run, Pallas kernels for 53% -> 48%
where the time goes in v8:
time: 70.3 us; the launch traced here: 70 us
  Pallas kernels  36.2 us (51%)
  starting transfers between devices  27.1 us (39%)
  local copies, waits for them, and re-layouts  3.2 us (5%)
  waiting for transfers between devices  3.13 us (4%)
    pallas_call x3, Pallas kernels, pair_messages(): pl.pallas_call(functools.partial(message_kernel, basis, len(blocks), tabl...  23 us
    ppermute x21, starting transfers between devices, exchange(): return lax.ppermute(block, axis, pairs)  20.6 us
    pallas_call x4, Pallas kernels, partial_factors(): pl.pallas_call(functools.partial(factor_kernel, parts, chunk, not before)...  8.52 us
    ppermute x4, starting transfers between devices, neighbours(): return (lax.ppermute(first, axis, one), lax.ppermute(second, axis, two))  6.5 us
    unnamed x28, local copies, waits for them, and re-layouts  3.13 us
    ppermute x21, waiting for transfers between devices, exchange(): return lax.ppermute(block, axis, pairs)  3.12 us
    pallas_call x1, Pallas kernels, atom_mlp(): pl.pallas_call(functools.partial(mlp_kernel, len(potentials), shape), in_...  2 us
    pallas_call x1, Pallas kernels, potentials_of(): pl.pallas_call(functools.partial(potential_kernel, len(held), pieces, len...  1.89 us
  transfers between devices with their start and end apart: 25, of which 4 were waited for; matrix products, arithmetic and copies ran while one was open for 0% of the time, Pallas kernels for 48%

profile of v8, /device:TPU:0, one launch (start us, length us, event | category | flops | bytes accessed | tf_op | source)
XLA Modules:
  0.0 70.0 jit_solution(9218141842541392950)
XLA Ops:
  0.0 0.9 %copy-done.1 = f32[2,2,1,128,128]{4,3,2,1,0:T(8,128)S(1)} copy-done((f32[2,2,1,128,128]{4,3,2,1,0:T(8,128)S(1)}, f32[2,2,1,128,128]{4,3,2,1,0:T(8,128)}, u32[]{:S(2)}) %copy-start.1) | copy-done | bytes 262168
  1.0 0.7 copy-done.6
  1.6 0.7 copy-done.7
  2.3 0.6 pack.1.block_ref.refs_0_.refs_8_
  2.9 3.0 %collective-permute-start = (f32[4,136,128]{2,1,0:T(8,128)S(1)}, f32[4,136,128]{2,1,0:T(8,128)S(1)}, u32[]{:S(2)}, u32[]{:S(2)}) collective-permute-start(f32[4,136,128]{2,1,0:T(8,128)S(1)} %pack.1.block_ref.refs_0_.refs_8_), channel_id=1, source_target_pairs={{0,4},{4,0},{8,12},{12,8},{1,5},{5,1},{9,13},{13,9},{2,6},{6,2},{1... | collective-permute-start | bytes 835592 | tf_op jit(solution)/shard_map/ppermute | solution.py:32
  5.9 1.5 %collective-permute-start.2 = (f32[4,136,128]{2,1,0:T(8,128)S(1)}, f32[4,136,128]{2,1,0:T(8,128)S(1)}, u32[]{:S(2)}, u32[]{:S(2)}) collective-permute-start(f32[4,136,128]{2,1,0:T(8,128)S(1)} %pack.1.block_ref.refs_0_.refs_8_), channel_id=1, source_target_pairs={{0,8},{4,12},{8,0},{12,4},{1,9},{5,13},{9,1},{13,5},{2,10},{6,14},... | collective-permute-start | bytes 835592 | tf_op jit(solution)/shard_map/ppermute | solution.py:32
  7.5 1.6 %collective-permute-start.13 = (f32[4,136,128]{2,1,0:T(8,128)S(1)}, f32[4,136,128]{2,1,0:T(8,128)S(1)}, u32[]{:S(2)}, u32[]{:S(2)}) collective-permute-start(f32[4,136,128]{2,1,0:T(8,128)S(1)} %pack.1.block_ref.refs_0_.refs_8_), channel_id=1, source_target_pairs={{0,1},{1,0},{2,3},{3,2},{4,5},{5,4},{6,7},{7,6},{8,9},{9,8},{10,11... | collective-permute-start | bytes 835592 | tf_op jit(solution)/shard_map/ppermute | solution.py:54
  9.0 0.0 collective-permute-start.7
  9.0 2.5 %collective-permute-start.14 = (f32[4,136,128]{2,1,0:T(8,128)S(1)}, f32[4,136,128]{2,1,0:T(8,128)S(1)}, u32[]{:S(2)}, u32[]{:S(2)}) collective-permute-start(f32[4,136,128]{2,1,0:T(8,128)S(1)} %pack.1.block_ref.refs_0_.refs_8_), channel_id=1, source_target_pairs={{0,3},{1,2},{2,1},{3,0},{4,7},{5,6},{6,5},{7,4},{8,11},{9,10},{10,... | collective-permute-start | bytes 835592 | tf_op jit(solution)/shard_map/ppermute | solution.py:54
  11.5 1.1 %collective-permute-done.block_ref.refs_2_ = f32[4,136,128]{2,1,0:T(8,128)S(1)} collective-permute-done((f32[4,136,128]{2,1,0:T(8,128)S(1)}, f32[4,136,128]{2,1,0:T(8,128)S(1)}, u32[]{:S(2)}, u32[]{:S(2)}) %collective-permute-start) | collective-permute-done | bytes 278560 | tf_op jit(solution)/shard_map/ppermute | solution.py:32
  12.6 1.8 %collective-permute-start.1 = (f32[4,136,128]{2,1,0:T(8,128)S(1)}, f32[4,136,128]{2,1,0:T(8,128)S(1)}, u32[]{:S(2)}, u32[]{:S(2)}) collective-permute-start(f32[4,136,128]{2,1,0:T(8,128)S(1)} %collective-permute-done.block_ref.refs_2_), channel_id=1, source_target_pairs={{0,8},{4,12},{8,0},{12,4},{1,9},{5,13},{9,1},{13,5},{2,10},{6,14},... | collective-permute-start | bytes 835592 | tf_op jit(solution)/shard_map/ppermute | solution.py:32
  14.4 0.8 %copy-done.10 = s32[3,2048]{1,0:T(4,128)S(1)} copy-done((s32[3,2048]{1,0:T(4,128)S(1)}, s32[3,2048]{1,0:T(4,128)}, u32[]{:S(2)}) %copy-start.10) | copy-done | bytes 24600
  15.1 2.3 %factors.4 = (f32[512,128]{1,0:T(8,128)S(1)}, f32[512,128]{1,0:T(8,128)S(1)}, bf16[1024,1024]{1,0:T(8,128)(2,1)S(1)}, f32[512,8]{1,0:T(8,128)S(1)}) custom-call(s32[3,2048]{1,0:T(4,128)S(1)} %copy-done.10, f32[4,136,128]{2,1,0:T(8,128)S(1)} %pack.1.block_ref.refs_0_.refs_8_), custom_call_target="tpu_custom_call" | custom-call | flops 268435456 | bytes 2097152 | tf_op jit(solution)/shard_map/factors/pallas_call | solution.py:211
  17.4 2.1 %factors.5 = (f32[512,128]{1,0:T(8,128)S(1)}, f32[512,128]{1,0:T(8,128)S(1)}, bf16[1024,1024]{1,0:T(8,128)(2,1)S(1)}) custom-call(f32[512,8]{1,0:T(8,128)S(1)} %get-tuple-element.41.column_ref, f32[4,136,128]{2,1,0:T(8,128)S(1)} %collective-permute-done.block_ref.refs_2_, ...), custom_call_target="tpu_custom_call", output_to_operand_aliasing={{0}: (2, {}), {1}: (3, {})} | custom-call | flops 268435456 | bytes 2097152 | tf_op jit(solution)/shard_map/factors/pallas_call | solution.py:211
  19.5 0.1 collective-permute-start.8
  19.6 2.1 %factors.6 = (f32[512,128]{1,0:T(8,128)S(1)}, f32[512,128]{1,0:T(8,128)S(1)}, bf16[1024,1024]{1,0:T(8,128)(2,1)S(1)}) custom-call(f32[512,8]{1,0:T(8,128)S(1)} %get-tuple-element.41.column_ref, f32[4,136,128]{2,1,0:T(8,128)S(1)} %collective-permute-done.2.block_ref, ...), custom_call_target="tpu_custom_call", output_to_operand_aliasing={{0}: (2, {}), {1}: (3, {})} | custom-call | flops 268435456 | bytes 2097152 | tf_op jit(solution)/shard_map/factors/pallas_call | solution.py:211
  21.7 0.0 collective-permute-done.13.refs_0_
  21.7 0.0 copy-start.9
  21.7 0.0 copy-start.11
  21.7 0.0 copy-start.13
  21.7 0.0 collective-permute-done.1.block_ref.refs_4_
  21.8 2.1 %factors.7 = (f32[512,128]{1,0:T(8,128)S(1)}, f32[512,128]{1,0:T(8,128)S(1)}, bf16[1024,1024]{1,0:T(8,128)(2,1)S(1)}) custom-call(f32[512,8]{1,0:T(8,128)S(1)} %get-tuple-element.41.column_ref, f32[4,136,128]{2,1,0:T(8,128)S(1)} %collective-permute-done.1.block_ref.refs_4_, ...), custom_call_target="tpu_custom_call", output_to_operand_aliasing={{0}: (2, {}), {1}: (3, {})} | custom-call | flops 268435456 | bytes 2097152 | tf_op jit(solution)/shard_map/factors/pallas_call | solution.py:211
  23.9 0.6 collective-permute-start.3
  24.4 0.1 collective-permute-start.9
  24.5 0.0 collective-permute-done.14.refs_2_
  24.6 1.6 %collective-permute-start.15 = (f32[4,136,128]{2,1,0:T(8,128)S(1)}, f32[4,136,128]{2,1,0:T(8,128)S(1)}, u32[]{:S(2)}, u32[]{:S(2)}) collective-permute-start(f32[4,136,128]{2,1,0:T(8,128)S(1)} %get-tuple-element.76), channel_id=1, source_target_pairs={{0,4},{4,0},{8,12},{12,8},{1,5},{5,1},{9,13},{13,9},{2,6},{6,2},{1... | collective-permute-start | bytes 835592 | tf_op jit(solution)/shard_map/ppermute | solution.py:54
  26.2 0.0 collective-permute-done.3
  26.2 0.9 %collective-permute-start.16 = (f32[4,136,128]{2,1,0:T(8,128)S(1)}, f32[4,136,128]{2,1,0:T(8,128)S(1)}, u32[]{:S(2)}, u32[]{:S(2)}) collective-permute-start(f32[4,136,128]{2,1,0:T(8,128)S(1)} %get-tuple-element.75), channel_id=1, source_target_pairs={{0,12},{4,8},{8,4},{12,0},{1,13},{5,9},{9,5},{13,1},{2,14},{6,10},... | collective-permute-start | bytes 835592 | tf_op jit(solution)/shard_map/ppermute | solution.py:54
  27.1 0.0 collective-permute-done.7.refs_1_
  27.1 1.6 %collective-permute-start.4 = (f32[128,128]{1,0:T(8,128)S(1)}, f32[128,128]{1,0:T(8,128)S(1)}, u32[]{:S(2)}, u32[]{:S(2)}) collective-permute-start(f32[128,128]{1,0:T(8,128)S(1)} %get-tuple-element.87), channel_id=1, source_target_pairs={{0,1},{1,0},{2,3},{3,2},{4,5},{5,4},{6,7},{7,6},{8,9},{9,8},{10,11... | collective-permute-start | bytes 196616 | tf_op jit(solution)/shard_map/ppermute | solution.py:32
  28.8 0.0 collective-permute-done.8.refs_3_
  28.8 2.6 %collective-permute-start.5 = (f32[128,128]{1,0:T(8,128)S(1)}, f32[128,128]{1,0:T(8,128)S(1)}, u32[]{:S(2)}, u32[]{:S(2)}) collective-permute-start(f32[128,128]{1,0:T(8,128)S(1)} %get-tuple-element.86), channel_id=1, source_target_pairs={{0,2},{1,3},{2,0},{3,1},{4,6},{5,7},{6,4},{7,5},{8,10},{9,11},{10,... | collective-permute-start | bytes 196616 | tf_op jit(solution)/shard_map/ppermute | solution.py:32
  31.4 0.0 collective-permute-done.9.refs_5_
  31.4 0.2 collective-permute-start.6
  31.6 4.4 %messages.3.refs_9_ = f32[2,1024,128]{2,1,0:T(8,128)S(1)} custom-call(s32[7,2]{1,0:T(8,128)S(1)} %copy-done.13, f32[8,128]{1,0:T(8,128)S(1)} %copy-done.11, f32[128,128]{1,0:T(8,128)S(1)} %copy-done.9, f32[4,136,128]{2,1,0:T(8,128)S(1)} %pack.1.block_ref.refs_0_.refs_8_, f32[4,136,128]{2,1,0:T(8,128)S(1)} %collective-permute-done.7.refs_1_, ...), custom_call_target="tpu_custom_call" | custom-call | flops 2415919104 | bytes 1048576 | tf_op jit(solution)/shard_map/messages/pallas_call | solution.py:453
  36.0 0.0 collective-permute-done.4.refs_1_
  36.0 0.3 collective-permute-done.5.refs_2_
  36.3 1.3 %collective-permute-done.6.refs_3_ = f32[128,128]{1,0:T(8,128)S(1)} collective-permute-done((f32[128,128]{1,0:T(8,128)S(1)}, f32[128,128]{1,0:T(8,128)S(1)}, u32[]{:S(2)}, u32[]{:S(2)}) %collective-permute-start.6) | collective-permute-done | bytes 65568 | tf_op jit(solution)/shard_map/ppermute | solution.py:32
  37.5 0.2 filter.1
  37.7 0.8 %collective-permute-start.10 = (f32[128,128]{1,0:T(8,128)S(1)}, f32[128,128]{1,0:T(8,128)S(1)}, u32[]{:S(2)}, u32[]{:S(2)}) collective-permute-start(f32[128,128]{1,0:T(8,128)S(1)} %filter.1), channel_id=1, source_target_pairs={{0,1},{1,0},{2,3},{3,2},{4,5},{5,4},{6,7},{7,6},{8,9},{9,8},{10,11... | collective-permute-start | bytes 196616 | tf_op jit(solution)/shard_map/ppermute | solution.py:32
  38.5 1.9 %collective-permute-start.11 = (f32[128,128]{1,0:T(8,128)S(1)}, f32[128,128]{1,0:T(8,128)S(1)}, u32[]{:S(2)}, u32[]{:S(2)}) collective-permute-start(f32[128,128]{1,0:T(8,128)S(1)} %filter.1), channel_id=1, source_target_pairs={{0,2},{1,3},{2,0},{3,1},{4,6},{5,7},{6,4},{7,5},{8,10},{9,11},{10,... | collective-permute-start | bytes 196616 | tf_op jit(solution)/shard_map/ppermute | solution.py:32
  40.5 1.7 %collective-permute-start.12 = (f32[128,128]{1,0:T(8,128)S(1)}, f32[128,128]{1,0:T(8,128)S(1)}, u32[]{:S(2)}, u32[]{:S(2)}) collective-permute-start(f32[128,128]{1,0:T(8,128)S(1)} %filter.1), channel_id=1, source_target_pairs={{0,3},{1,2},{2,1},{3,0},{4,7},{5,6},{6,5},{7,4},{8,11},{9,10},{10,... | collective-permute-start | bytes 196616 | tf_op jit(solution)/shard_map/ppermute | solution.py:32
  42.2 4.6 %messages.4.refs_10_ = f32[2,1024,128]{2,1,0:T(8,128)S(1)} custom-call(s32[7,2]{1,0:T(8,128)S(1)} %copy-done.13, f32[8,128]{1,0:T(8,128)S(1)} %copy-done.11, f32[128,128]{1,0:T(8,128)S(1)} %copy-done.9, f32[4,136,128]{2,1,0:T(8,128)S(1)} %pack.1.block_ref.refs_0_.refs_8_, f32[4,136,128]{2,1,0:T(8,128)S(1)} %collective-permute-done.7.refs_1_, ...), custom_call_target="tpu_custom_call" | custom-call | flops 2415919104 | bytes 1048576 | tf_op jit(solution)/shard_map/messages/pallas_call | solution.py:453
  46.8 0.0 collective-permute-done.11
  46.8 0.0 collective-permute-done.12
  46.8 0.1 collective-permute-start.17
  46.9 0.5 collective-permute-start.18
  47.4 0.1 collective-permute-start.19
  47.5 0.4 collective-permute-start.20
  47.9 0.1 collective-permute-start.21
  48.0 0.4 collective-permute-done.17.refs_1_
  48.4 1.9 %potentials.1 = (f32[4,128,128]{2,1,0:T(8,128)S(1)}, f32[4,128,128]{2,1,0:T(8,128)S(1)}, f32[4,128,128]{2,1,0:T(8,128)S(1)}, f32[4,128,128]{2,1,0:T(8,128)S(1)}) custom-call(f32[512,128]{1,0:T(8,128)S(1)} %pad_maximum_fusion.2.refs_0_, f32[512,128]{1,0:T(8,128)S(1)} %collective-permute-done.17.refs_1_, bf16[1024,1024]{1,0:T(8,128)(2,1)S(1)} %get-tuple-element.58.refs_2_, ...), custom_call_target="tpu_custom_call" | custom-call | flops 1610612736 | bytes 8388608 | tf_op jit(solution)/shard_map/potentials/pallas_call | solution.py:287
  50.3 0.0 copy-start.2
  50.3 0.0 copy-start.3
  50.4 0.0 copy-start.4
  50.4 0.0 copy-start.8
  50.4 1.1 %collective-permute-start.22 = (f32[4,128,128]{2,1,0:T(8,128)S(1)}, f32[4,128,128]{2,1,0:T(8,128)S(1)}, u32[]{:S(2)}, u32[]{:S(2)}) collective-permute-start(f32[4,128,128]{2,1,0:T(8,128)S(1)} %get-tuple-element.72), channel_id=1, source_target_pairs={{0,4},{4,0},{8,12},{12,8},{1,5},{5,1},{9,13},{13,9},{2,6},{6,2},{1... | collective-permute-start | bytes 786440 | tf_op jit(solution)/shard_map/ppermute | solution.py:32
  51.5 0.0 collective-permute-done.18.refs_1_
  51.5 1.5 %collective-permute-start.23 = (f32[4,128,128]{2,1,0:T(8,128)S(1)}, f32[4,128,128]{2,1,0:T(8,128)S(1)}, u32[]{:S(2)}, u32[]{:S(2)}) collective-permute-start(f32[4,128,128]{2,1,0:T(8,128)S(1)} %get-tuple-element.73), channel_id=1, source_target_pairs={{0,8},{4,12},{8,0},{12,4},{1,9},{5,13},{9,1},{13,5},{2,10},{6,14},... | collective-permute-start | bytes 786440 | tf_op jit(solution)/shard_map/ppermute | solution.py:32
  53.0 1.0 %collective-permute-start.24 = (f32[4,128,128]{2,1,0:T(8,128)S(1)}, f32[4,128,128]{2,1,0:T(8,128)S(1)}, u32[]{:S(2)}, u32[]{:S(2)}) collective-permute-start(f32[4,128,128]{2,1,0:T(8,128)S(1)} %get-tuple-element.74), channel_id=1, source_target_pairs={{0,12},{4,8},{8,4},{12,0},{1,13},{5,9},{9,5},{13,1},{2,14},{6,10},... | collective-permute-start | bytes 786440 | tf_op jit(solution)/shard_map/ppermute | solution.py:32
  53.9 0.0 collective-permute-done.20.refs_5_
  53.9 0.0 collective-permute-done.21.refs_7_
  53.9 14.0 %messages.5.refs_2_ = f32[4,128,128]{2,1,0:T(8,128)S(1)} custom-call(s32[7,8]{1,0:T(8,128)S(1)} %copy-done.12, f32[8,128]{1,0:T(8,128)S(1)} %copy-done.11, f32[128,128]{1,0:T(8,128)S(1)} %copy-done.9, f32[4,136,128]{2,1,0:T(8,128)S(1)} %collective-permute-done.13.refs_0_, f32[4,136,128]{2,1,0:T(8,128)S(1)} %collective-permute-done.18.refs_1_, ...), custom_call_target="tpu_custom_call" | custom-call | flops 9663676416 | bytes 1048576 | tf_op jit(solution)/shard_map/messages/pallas_call | solution.py:453
  68.0 2.0 %atom_mlp.1 = f32[4,128,128]{2,1,0:T(8,128)} custom-call(s32[2,1,2]{2,1,0:T(1,128)S(1)} %bitcast.13, f32[4,128,128]{2,1,0:T(8,128)S(1)} %bitcast.10, f32[4,128,128]{2,1,0:T(8,128)S(1)} %messages.5.refs_2_, f32[4,128,128]{2,1,0:T(8,128)S(1)} %get-tuple-element.71.refs_3_, f32[4,128,128]{2,1,0:T(8,128)S(1)} %collective-permute-done.22.refs_4_, ...), custom_call_target="tpu_custom_call" | custom-call | tf_op jit(solution)/shard_map/atom_mlp/pallas_call | solution.py:526
  (31 shorter events, 0.2 us)
Async XLA Ops:
  0.0 0.9 %copy-start.1 = (f32[2,2,1,128,128]{4,3,2,1,0:T(8,128)S(1)}, f32[2,2,1,128,128]{4,3,2,1,0:T(8,128)}, u32[]{:S(2)}) copy-start(f32[2,2,1,128,128]{4,3,2,1,0:T(8,128)} %param.13) | copy-start | bytes 786436
  1.0 0.7 copy-start.6
  1.6 0.7 copy-start.7
  2.9 9.7 %collective-permute-start = (f32[4,136,128]{2,1,0:T(8,128)S(1)}, f32[4,136,128]{2,1,0:T(8,128)S(1)}, u32[]{:S(2)}, u32[]{:S(2)}) collective-permute-start(f32[4,136,128]{2,1,0:T(8,128)S(1)} %pack.1.block_ref.refs_0_.refs_8_), channel_id=1, source_target_pairs={{0,4},{4,0},{8,12},{12,8},{1,5},{5,1},{9,13},{13,9},{2,6},{6,2},{1... | collective-permute-start | bytes 835592 | tf_op jit(solution)/shard_map/ppermute | solution.py:32
  5.9 13.5 %collective-permute-start.2 = (f32[4,136,128]{2,1,0:T(8,128)S(1)}, f32[4,136,128]{2,1,0:T(8,128)S(1)}, u32[]{:S(2)}, u32[]{:S(2)}) collective-permute-start(f32[4,136,128]{2,1,0:T(8,128)S(1)} %pack.1.block_ref.refs_0_.refs_8_), channel_id=1, source_target_pairs={{0,8},{4,12},{8,0},{12,4},{1,9},{5,13},{9,1},{13,5},{2,10},{6,14},... | collective-permute-start | bytes 835592 | tf_op jit(solution)/shard_map/ppermute | solution.py:32
  7.5 14.2 %collective-permute-start.13 = (f32[4,136,128]{2,1,0:T(8,128)S(1)}, f32[4,136,128]{2,1,0:T(8,128)S(1)}, u32[]{:S(2)}, u32[]{:S(2)}) collective-permute-start(f32[4,136,128]{2,1,0:T(8,128)S(1)} %pack.1.block_ref.refs_0_.refs_8_), channel_id=1, source_target_pairs={{0,1},{1,0},{2,3},{3,2},{4,5},{5,4},{6,7},{7,6},{8,9},{9,8},{10,11... | collective-permute-start | bytes 835592 | tf_op jit(solution)/shard_map/ppermute | solution.py:54
  9.0 18.1 %collective-permute-start.7 = (f32[4,136,128]{2,1,0:T(8,128)S(1)}, f32[4,136,128]{2,1,0:T(8,128)S(1)}, u32[]{:S(2)}, u32[]{:S(2)}) collective-permute-start(f32[4,136,128]{2,1,0:T(8,128)S(1)} %pack.1.block_ref.refs_0_.refs_8_), channel_id=1, source_target_pairs={{0,16},{16,0},{1,17},{17,1},{2,18},{18,2},{3,19},{19,3},{4,20},{20... | collective-permute-start | bytes 835592 | tf_op jit(solution)/shard_map/ppermute | solution.py:32
  9.0 15.5 %collective-permute-start.14 = (f32[4,136,128]{2,1,0:T(8,128)S(1)}, f32[4,136,128]{2,1,0:T(8,128)S(1)}, u32[]{:S(2)}, u32[]{:S(2)}) collective-permute-start(f32[4,136,128]{2,1,0:T(8,128)S(1)} %pack.1.block_ref.refs_0_.refs_8_), channel_id=1, source_target_pairs={{0,3},{1,2},{2,1},{3,0},{4,7},{5,6},{6,5},{7,4},{8,11},{9,10},{10,... | collective-permute-start | bytes 835592 | tf_op jit(solution)/shard_map/ppermute | solution.py:54
  12.6 9.1 %collective-permute-start.1 = (f32[4,136,128]{2,1,0:T(8,128)S(1)}, f32[4,136,128]{2,1,0:T(8,128)S(1)}, u32[]{:S(2)}, u32[]{:S(2)}) collective-permute-start(f32[4,136,128]{2,1,0:T(8,128)S(1)} %collective-permute-done.block_ref.refs_2_), channel_id=1, source_target_pairs={{0,8},{4,12},{8,0},{12,4},{1,9},{5,13},{9,1},{13,5},{2,10},{6,14},... | collective-permute-start | bytes 835592 | tf_op jit(solution)/shard_map/ppermute | solution.py:32
  14.4 0.8 %copy-start.10 = (s32[3,2048]{1,0:T(4,128)S(1)}, s32[3,2048]{1,0:T(4,128)}, u32[]{:S(2)}) copy-start(s32[3,2048]{1,0:T(4,128)} %column_ref) | copy-start | bytes 73732
  19.5 9.3 %collective-permute-start.8 = (f32[4,136,128]{2,1,0:T(8,128)S(1)}, f32[4,136,128]{2,1,0:T(8,128)S(1)}, u32[]{:S(2)}, u32[]{:S(2)}) collective-permute-start(f32[4,136,128]{2,1,0:T(8,128)S(1)} %collective-permute-done.block_ref.refs_2_), channel_id=1, source_target_pairs={{0,16},{16,0},{1,17},{17,1},{2,18},{18,2},{3,19},{19,3},{4,20},{20... | collective-permute-start | bytes 835592 | tf_op jit(solution)/shard_map/ppermute | solution.py:32
  21.7 9.9 %copy-start.9 = (f32[128,128]{1,0:T(8,128)S(1)}, f32[128,128]{1,0:T(8,128)}, u32[]{:S(2)}) copy-start(f32[128,128]{1,0:T(8,128)} %value_ref.2) | copy-start | bytes 196612
  21.7 9.9 %copy-start.11 = (f32[8,128]{1,0:T(8,128)S(1)}, f32[8,128]{1,0:T(8,128)}, u32[]{:S(2)}) copy-start(f32[8,128]{1,0:T(8,128)} %mix_ref.5) | copy-start | bytes 12292
  21.7 9.8 %copy-start.13 = (s32[7,2]{1,0:T(8,128)S(1)}, s32[7,2]{1,0:T(8,128)}, u32[]{:S(2)}) copy-start(s32[7,2]{1,0:T(8,128)} %constant.47.clone.step_ref) | copy-start | bytes 172
  23.9 2.3 %collective-permute-start.3 = (f32[512,128]{1,0:T(8,128)S(1)}, f32[512,128]{1,0:T(8,128)S(1)}, u32[]{:S(2)}, u32[]{:S(2)}) collective-permute-start(f32[512,128]{1,0:T(8,128)S(1)} %get-tuple-element.50), channel_id=1, source_target_pairs={{0,16},{16,0},{1,17},{17,1},{2,18},{18,2},{3,19},{19,3},{4,20},{20... | collective-permute-start | bytes 786440 | tf_op jit(solution)/shard_map/ppermute | solution.py:32
  24.4 7.0 %collective-permute-start.9 = (f32[4,136,128]{2,1,0:T(8,128)S(1)}, f32[4,136,128]{2,1,0:T(8,128)S(1)}, u32[]{:S(2)}, u32[]{:S(2)}) collective-permute-start(f32[4,136,128]{2,1,0:T(8,128)S(1)} %collective-permute-done.1.block_ref.refs_4_), channel_id=1, source_target_pairs={{0,16},{16,0},{1,17},{17,1},{2,18},{18,2},{3,19},{19,3},{4,20},{20... | collective-permute-start | bytes 835592 | tf_op jit(solution)/shard_map/ppermute | solution.py:32
  24.6 22.2 %collective-permute-start.15 = (f32[4,136,128]{2,1,0:T(8,128)S(1)}, f32[4,136,128]{2,1,0:T(8,128)S(1)}, u32[]{:S(2)}, u32[]{:S(2)}) collective-permute-start(f32[4,136,128]{2,1,0:T(8,128)S(1)} %get-tuple-element.76), channel_id=1, source_target_pairs={{0,4},{4,0},{8,12},{12,8},{1,5},{5,1},{9,13},{13,9},{2,6},{6,2},{1... | collective-permute-start | bytes 835592 | tf_op jit(solution)/shard_map/ppermute | solution.py:54
  26.2 20.7 %collective-permute-start.16 = (f32[4,136,128]{2,1,0:T(8,128)S(1)}, f32[4,136,128]{2,1,0:T(8,128)S(1)}, u32[]{:S(2)}, u32[]{:S(2)}) collective-permute-start(f32[4,136,128]{2,1,0:T(8,128)S(1)} %get-tuple-element.75), channel_id=1, source_target_pairs={{0,12},{4,8},{8,4},{12,0},{1,13},{5,9},{9,5},{13,1},{2,14},{6,10},... | collective-permute-start | bytes 835592 | tf_op jit(solution)/shard_map/ppermute | solution.py:54
  27.1 8.9 %collective-permute-start.4 = (f32[128,128]{1,0:T(8,128)S(1)}, f32[128,128]{1,0:T(8,128)S(1)}, u32[]{:S(2)}, u32[]{:S(2)}) collective-permute-start(f32[128,128]{1,0:T(8,128)S(1)} %get-tuple-element.87), channel_id=1, source_target_pairs={{0,1},{1,0},{2,3},{3,2},{4,5},{5,4},{6,7},{7,6},{8,9},{9,8},{10,11... | collective-permute-start | bytes 196616 | tf_op jit(solution)/shard_map/ppermute | solution.py:32
  28.8 7.5 %collective-permute-start.5 = (f32[128,128]{1,0:T(8,128)S(1)}, f32[128,128]{1,0:T(8,128)S(1)}, u32[]{:S(2)}, u32[]{:S(2)}) collective-permute-start(f32[128,128]{1,0:T(8,128)S(1)} %get-tuple-element.86), channel_id=1, source_target_pairs={{0,2},{1,3},{2,0},{3,1},{4,6},{5,7},{6,4},{7,5},{8,10},{9,11},{10,... | collective-permute-start | bytes 196616 | tf_op jit(solution)/shard_map/ppermute | solution.py:32
  31.4 6.2 %copy-start = (f32[2048,128]{1,0:T(8,128)S(1)}, f32[2048,128]{1,0:T(8,128)}, u32[]{:S(2)}) copy-start(f32[2048,128]{1,0:T(8,128)} %refs_5_.1) | copy-start | bytes 3145732
  31.4 6.2 %copy-start.5 = (f32[128,128]{1,0:T(8,128)S(1)}, f32[128,128]{1,0:T(8,128)}, u32[]{:S(2)}) copy-start(f32[128,128]{1,0:T(8,128)} %refs_4_) | copy-start | bytes 196612
  31.4 6.2 %collective-permute-start.6 = (f32[128,128]{1,0:T(8,128)S(1)}, f32[128,128]{1,0:T(8,128)S(1)}, u32[]{:S(2)}, u32[]{:S(2)}) collective-permute-start(f32[128,128]{1,0:T(8,128)S(1)} %get-tuple-element.85), channel_id=1, source_target_pairs={{0,3},{1,2},{2,1},{3,0},{4,7},{5,6},{6,5},{7,4},{8,11},{9,10},{10,... | collective-permute-start | bytes 196616 | tf_op jit(solution)/shard_map/ppermute | solution.py:32
  37.7 9.0 %collective-permute-start.10 = (f32[128,128]{1,0:T(8,128)S(1)}, f32[128,128]{1,0:T(8,128)S(1)}, u32[]{:S(2)}, u32[]{:S(2)}) collective-permute-start(f32[128,128]{1,0:T(8,128)S(1)} %filter.1), channel_id=1, source_target_pairs={{0,1},{1,0},{2,3},{3,2},{4,5},{5,4},{6,7},{7,6},{8,9},{9,8},{10,11... | collective-permute-start | bytes 196616 | tf_op jit(solution)/shard_map/ppermute | solution.py:32
  38.5 8.2 %collective-permute-start.11 = (f32[128,128]{1,0:T(8,128)S(1)}, f32[128,128]{1,0:T(8,128)S(1)}, u32[]{:S(2)}, u32[]{:S(2)}) collective-permute-start(f32[128,128]{1,0:T(8,128)S(1)} %filter.1), channel_id=1, source_target_pairs={{0,2},{1,3},{2,0},{3,1},{4,6},{5,7},{6,4},{7,5},{8,10},{9,11},{10,... | collective-permute-start | bytes 196616 | tf_op jit(solution)/shard_map/ppermute | solution.py:32
  40.5 6.3 %collective-permute-start.12 = (f32[128,128]{1,0:T(8,128)S(1)}, f32[128,128]{1,0:T(8,128)S(1)}, u32[]{:S(2)}, u32[]{:S(2)}) collective-permute-start(f32[128,128]{1,0:T(8,128)S(1)} %filter.1), channel_id=1, source_target_pairs={{0,3},{1,2},{2,1},{3,0},{4,7},{5,6},{6,5},{7,4},{8,11},{9,10},{10,... | collective-permute-start | bytes 196616 | tf_op jit(solution)/shard_map/ppermute | solution.py:32
  46.8 1.6 %collective-permute-start.17 = (f32[512,128]{1,0:T(8,128)S(1)}, f32[512,128]{1,0:T(8,128)S(1)}, u32[]{:S(2)}, u32[]{:S(2)}) collective-permute-start(f32[512,128]{1,0:T(8,128)S(1)} %pad_maximum_fusion.2.refs_0_), channel_id=1, source_target_pairs={{0,16},{16,0},{1,17},{17,1},{2,18},{18,2},{3,19},{19,3},{4,20},{20... | collective-permute-start | bytes 786440 | tf_op jit(solution)/shard_map/ppermute | solution.py:32
  46.9 4.6 %collective-permute-start.18 = (f32[4,136,128]{2,1,0:T(8,128)S(1)}, f32[4,136,128]{2,1,0:T(8,128)S(1)}, u32[]{:S(2)}, u32[]{:S(2)}) collective-permute-start(f32[4,136,128]{2,1,0:T(8,128)S(1)} %collective-permute-done.13.refs_0_), channel_id=1, source_target_pairs={{0,16},{16,0},{1,17},{17,1},{2,18},{18,2},{3,19},{19,3},{4,20},{20... | collective-permute-start | bytes 835592 | tf_op jit(solution)/shard_map/ppermute | solution.py:32
  47.4 5.6 %collective-permute-start.19 = (f32[4,136,128]{2,1,0:T(8,128)S(1)}, f32[4,136,128]{2,1,0:T(8,128)S(1)}, u32[]{:S(2)}, u32[]{:S(2)}) collective-permute-start(f32[4,136,128]{2,1,0:T(8,128)S(1)} %collective-permute-done.14.refs_2_), channel_id=1, source_target_pairs={{0,16},{16,0},{1,17},{17,1},{2,18},{18,2},{3,19},{19,3},{4,20},{20... | collective-permute-start | bytes 835592 | tf_op jit(solution)/shard_map/ppermute | solution.py:32
  47.5 6.5 %collective-permute-start.20 = (f32[4,136,128]{2,1,0:T(8,128)S(1)}, f32[4,136,128]{2,1,0:T(8,128)S(1)}, u32[]{:S(2)}, u32[]{:S(2)}) collective-permute-start(f32[4,136,128]{2,1,0:T(8,128)S(1)} %collective-permute-done.15.refs_4_), channel_id=1, source_target_pairs={{0,16},{16,0},{1,17},{17,1},{2,18},{18,2},{3,19},{19,3},{4,20},{20... | collective-permute-start | bytes 835592 | tf_op jit(solution)/shard_map/ppermute | solution.py:32
  47.9 6.0 %collective-permute-start.21 = (f32[4,136,128]{2,1,0:T(8,128)S(1)}, f32[4,136,128]{2,1,0:T(8,128)S(1)}, u32[]{:S(2)}, u32[]{:S(2)}) collective-permute-start(f32[4,136,128]{2,1,0:T(8,128)S(1)} %collective-permute-done.16.refs_6_), channel_id=1, source_target_pairs={{0,16},{16,0},{1,17},{17,1},{2,18},{18,2},{3,19},{19,3},{4,20},{20... | collective-permute-start | bytes 835592 | tf_op jit(solution)/shard_map/ppermute | solution.py:32
  48.4 5.5 %copy-start.12 = (s32[7,8]{1,0:T(8,128)S(1)}, s32[7,8]{1,0:T(8,128)}, u32[]{:S(2)}) copy-start(s32[7,8]{1,0:T(8,128)} %constant.48.clone.step_ref) | copy-start | bytes 676
  50.3 17.7 %copy-start.2 = (f32[2,2,1,128,128]{4,3,2,1,0:T(8,128)S(1)}, f32[2,2,1,128,128]{4,3,2,1,0:T(8,128)}, u32[]{:S(2)}) copy-start(f32[2,2,1,128,128]{4,3,2,1,0:T(8,128)} %param.13) | copy-start | bytes 786436
  50.3 17.7 %copy-start.3 = (f32[128,256]{1,0:T(8,128)S(1)}, f32[128,256]{1,0:T(8,128)}, u32[]{:S(2)}) copy-start(f32[128,256]{1,0:T(8,128)} %refs_7_.1) | copy-start | bytes 393220
  50.4 17.7 %copy-start.4 = (f32[256,128]{1,0:T(8,128)S(1)}, f32[256,128]{1,0:T(8,128)}, u32[]{:S(2)}) copy-start(f32[256,128]{1,0:T(8,128)} %refs_8_.1) | copy-start | bytes 393220
  50.4 17.7 %copy-start.8 = (s32[2,2,1]{1,2,0:T(1,128)S(1)}, s32[2,2,1]{1,2,0:T(1,128)}, u32[]{:S(2)}) copy-start(s32[2,2,1]{1,2,0:T(1,128)} %param.15) | copy-start | bytes 52
  50.4 17.6 %collective-permute-start.22 = (f32[4,128,128]{2,1,0:T(8,128)S(1)}, f32[4,128,128]{2,1,0:T(8,128)S(1)}, u32[]{:S(2)}, u32[]{:S(2)}) collective-permute-start(f32[4,128,128]{2,1,0:T(8,128)S(1)} %get-tuple-element.72), channel_id=1, source_target_pairs={{0,4},{4,0},{8,12},{12,8},{1,5},{5,1},{9,13},{13,9},{2,6},{6,2},{1... | collective-permute-start | bytes 786440 | tf_op jit(solution)/shard_map/ppermute | solution.py:32
  51.5 16.5 %collective-permute-start.23 = (f32[4,128,128]{2,1,0:T(8,128)S(1)}, f32[4,128,128]{2,1,0:T(8,128)S(1)}, u32[]{:S(2)}, u32[]{:S(2)}) collective-permute-start(f32[4,128,128]{2,1,0:T(8,128)S(1)} %get-tuple-element.73), channel_id=1, source_target_pairs={{0,8},{4,12},{8,0},{12,4},{1,9},{5,13},{9,1},{13,5},{2,10},{6,14},... | collective-permute-start | bytes 786440 | tf_op jit(solution)/shard_map/ppermute | solution.py:32
  53.0 15.0 %collective-permute-start.24 = (f32[4,128,128]{2,1,0:T(8,128)S(1)}, f32[4,128,128]{2,1,0:T(8,128)S(1)}, u32[]{:S(2)}, u32[]{:S(2)}) collective-permute-start(f32[4,128,128]{2,1,0:T(8,128)S(1)} %get-tuple-element.74), channel_id=1, source_target_pairs={{0,12},{4,8},{8,4},{12,0},{1,13},{5,9},{9,5},{13,1},{2,14},{6,10},... | collective-permute-start | bytes 786440 | tf_op jit(solution)/shard_map/ppermute | solution.py:32

commit v9 on v8

--- a/solution.py
+++ b/solution.py
@@ -351,7 +351,7 @@
             number = (place_x * along + place_y + n) * planes + plane
             at = at_ref[number]
             near.append((at[0:1] + float(move - 1), at[1:2] + float(n - 1), at[2:3] + shift_z))
-        tile = 16
+        tile = 32
         for m in range(slots // tile):
             at = m * tile
             own_x = own_col_ref[own, 0, at : at + tile, :]
@@ -597,8 +597,8 @@
     piece = half // size_z
     chunk = min(piece, share // size_x)
     first = min(1, size_y - 1)
-    waves, gathered[first] = lax.optimization_barrier((waves, gathered[first]))
-    *parts, table, columns = partial_factors(waves, share, chunk, own, (), size_x)
+    late, gathered[first] = lax.optimization_barrier((own, gathered[first]))
+    *parts, table, columns = partial_factors(waves, share, chunk, late, (), size_x)
     tables = [table]
     for block in gathered[1:]:
         *parts, table = partial_factors(columns, share, chunk, block, parts, size_x)

time: 70.3 us -> 70.3 us (level)
  no operation moved by 1% of the time
where the time goes in v9:
time: 70.3 us; the launch traced here: 70 us
  Pallas kernels  36.1 us (51%)
  starting transfers between devices  27.1 us (39%)
  local copies, waits for them, and re-layouts  3.2 us (5%)
  waiting for transfers between devices  3.13 us (4%)
    pallas_call x3, Pallas kernels, pair_messages(): pl.pallas_call(functools.partial(message_kernel, basis, len(blocks), tabl...  22.9 us
    ppermute x21, starting transfers between devices, exchange(): return lax.ppermute(block, axis, pairs)  20.6 us
    pallas_call x4, Pallas kernels, partial_factors(): pl.pallas_call(functools.partial(factor_kernel, parts, chunk, not before)...  8.52 us
    ppermute x4, starting transfers between devices, neighbours(): return (lax.ppermute(first, axis, one), lax.ppermute(second, axis, two))  6.5 us
    unnamed x28, local copies, waits for them, and re-layouts  3.13 us
    ppermute x21, waiting for transfers between devices, exchange(): return lax.ppermute(block, axis, pairs)  3.12 us
    pallas_call x1, Pallas kernels, atom_mlp(): pl.pallas_call(functools.partial(mlp_kernel, len(potentials), shape), in_...  2 us
    pallas_call x1, Pallas kernels, potentials_of(): pl.pallas_call(functools.partial(potential_kernel, len(held), pieces, len...  1.88 us
  transfers between devices with their start and end apart: 25, of which 4 were waited for; matrix products, arithmetic and copies ran while one was open for 0% of the time, Pallas kernels for 48%

profile of v9, /device:TPU:0, one launch (start us, length us, event | category | flops | bytes accessed | tf_op | source)
XLA Modules:
  0.0 70.0 jit_solution(15346780551248673853)
XLA Ops:
  0.0 0.9 %copy-done.1 = f32[2,2,1,128,128]{4,3,2,1,0:T(8,128)S(1)} copy-done((f32[2,2,1,128,128]{4,3,2,1,0:T(8,128)S(1)}, f32[2,2,1,128,128]{4,3,2,1,0:T(8,128)}, u32[]{:S(2)}) %copy-start.1) | copy-done | bytes 262168
  1.0 0.7 copy-done.6
  1.6 0.7 copy-done.7
  2.3 0.6 pack.1.block_ref.refs_0_.refs_8_
  2.9 3.0 %collective-permute-start = (f32[4,136,128]{2,1,0:T(8,128)S(1)}, f32[4,136,128]{2,1,0:T(8,128)S(1)}, u32[]{:S(2)}, u32[]{:S(2)}) collective-permute-start(f32[4,136,128]{2,1,0:T(8,128)S(1)} %pack.1.block_ref.refs_0_.refs_8_), channel_id=1, source_target_pairs={{0,4},{4,0},{8,12},{12,8},{1,5},{5,1},{9,13},{13,9},{2,6},{6,2},{1... | collective-permute-start | bytes 835592 | tf_op jit(solution)/shard_map/ppermute | solution.py:32
  5.9 1.5 %collective-permute-start.2 = (f32[4,136,128]{2,1,0:T(8,128)S(1)}, f32[4,136,128]{2,1,0:T(8,128)S(1)}, u32[]{:S(2)}, u32[]{:S(2)}) collective-permute-start(f32[4,136,128]{2,1,0:T(8,128)S(1)} %pack.1.block_ref.refs_0_.refs_8_), channel_id=1, source_target_pairs={{0,8},{4,12},{8,0},{12,4},{1,9},{5,13},{9,1},{13,5},{2,10},{6,14},... | collective-permute-start | bytes 835592 | tf_op jit(solution)/shard_map/ppermute | solution.py:32
  7.5 1.6 %collective-permute-start.13 = (f32[4,136,128]{2,1,0:T(8,128)S(1)}, f32[4,136,128]{2,1,0:T(8,128)S(1)}, u32[]{:S(2)}, u32[]{:S(2)}) collective-permute-start(f32[4,136,128]{2,1,0:T(8,128)S(1)} %pack.1.block_ref.refs_0_.refs_8_), channel_id=1, source_target_pairs={{0,1},{1,0},{2,3},{3,2},{4,5},{5,4},{6,7},{7,6},{8,9},{9,8},{10,11... | collective-permute-start | bytes 835592 | tf_op jit(solution)/shard_map/ppermute | solution.py:54
  9.0 0.0 collective-permute-start.7
  9.0 2.5 %collective-permute-start.14 = (f32[4,136,128]{2,1,0:T(8,128)S(1)}, f32[4,136,128]{2,1,0:T(8,128)S(1)}, u32[]{:S(2)}, u32[]{:S(2)}) collective-permute-start(f32[4,136,128]{2,1,0:T(8,128)S(1)} %pack.1.block_ref.refs_0_.refs_8_), channel_id=1, source_target_pairs={{0,3},{1,2},{2,1},{3,0},{4,7},{5,6},{6,5},{7,4},{8,11},{9,10},{10,... | collective-permute-start | bytes 835592 | tf_op jit(solution)/shard_map/ppermute | solution.py:54
  11.5 1.1 %collective-permute-done.block_ref.refs_2_ = f32[4,136,128]{2,1,0:T(8,128)S(1)} collective-permute-done((f32[4,136,128]{2,1,0:T(8,128)S(1)}, f32[4,136,128]{2,1,0:T(8,128)S(1)}, u32[]{:S(2)}, u32[]{:S(2)}) %collective-permute-start) | collective-permute-done | bytes 278560 | tf_op jit(solution)/shard_map/ppermute | solution.py:32
  12.6 1.8 %collective-permute-start.1 = (f32[4,136,128]{2,1,0:T(8,128)S(1)}, f32[4,136,128]{2,1,0:T(8,128)S(1)}, u32[]{:S(2)}, u32[]{:S(2)}) collective-permute-start(f32[4,136,128]{2,1,0:T(8,128)S(1)} %collective-permute-done.block_ref.refs_2_), channel_id=1, source_target_pairs={{0,8},{4,12},{8,0},{12,4},{1,9},{5,13},{9,1},{13,5},{2,10},{6,14},... | collective-permute-start | bytes 835592 | tf_op jit(solution)/shard_map/ppermute | solution.py:32
  14.4 0.8 %copy-done.10 = s32[3,2048]{1,0:T(4,128)S(1)} copy-done((s32[3,2048]{1,0:T(4,128)S(1)}, s32[3,2048]{1,0:T(4,128)}, u32[]{:S(2)}) %copy-start.10) | copy-done | bytes 24600
  15.1 2.3 %factors.4 = (f32[512,128]{1,0:T(8,128)S(1)}, f32[512,128]{1,0:T(8,128)S(1)}, bf16[1024,1024]{1,0:T(8,128)(2,1)S(1)}, f32[512,8]{1,0:T(8,128)S(1)}) custom-call(s32[3,2048]{1,0:T(4,128)S(1)} %copy-done.10, f32[4,136,128]{2,1,0:T(8,128)S(1)} %pack.1.block_ref.refs_0_.refs_8_), custom_call_target="tpu_custom_call" | custom-call | flops 268435456 | bytes 2097152 | tf_op jit(solution)/shard_map/factors/pallas_call | solution.py:211
  17.4 2.1 %factors.5 = (f32[512,128]{1,0:T(8,128)S(1)}, f32[512,128]{1,0:T(8,128)S(1)}, bf16[1024,1024]{1,0:T(8,128)(2,1)S(1)}) custom-call(f32[512,8]{1,0:T(8,128)S(1)} %get-tuple-element.41.column_ref, f32[4,136,128]{2,1,0:T(8,128)S(1)} %collective-permute-done.block_ref.refs_2_, ...), custom_call_target="tpu_custom_call", output_to_operand_aliasing={{0}: (2, {}), {1}: (3, {})} | custom-call | flops 268435456 | bytes 2097152 | tf_op jit(solution)/shard_map/factors/pallas_call | solution.py:211
  19.5 0.1 collective-permute-start.8
  19.6 2.1 %factors.6 = (f32[512,128]{1,0:T(8,128)S(1)}, f32[512,128]{1,0:T(8,128)S(1)}, bf16[1024,1024]{1,0:T(8,128)(2,1)S(1)}) custom-call(f32[512,8]{1,0:T(8,128)S(1)} %get-tuple-element.41.column_ref, f32[4,136,128]{2,1,0:T(8,128)S(1)} %collective-permute-done.2.block_ref, ...), custom_call_target="tpu_custom_call", output_to_operand_aliasing={{0}: (2, {}), {1}: (3, {})} | custom-call | flops 268435456 | bytes 2097152 | tf_op jit(solution)/shard_map/factors/pallas_call | solution.py:211
  21.7 0.0 collective-permute-done.13.refs_0_
  21.7 0.0 copy-start.9
  21.7 0.0 copy-start.11
  21.7 0.0 copy-start.13
  21.7 0.0 collective-permute-done.1.block_ref.refs_4_
  21.8 2.1 %factors.7 = (f32[512,128]{1,0:T(8,128)S(1)}, f32[512,128]{1,0:T(8,128)S(1)}, bf16[1024,1024]{1,0:T(8,128)(2,1)S(1)}) custom-call(f32[512,8]{1,0:T(8,128)S(1)} %get-tuple-element.41.column_ref, f32[4,136,128]{2,1,0:T(8,128)S(1)} %collective-permute-done.1.block_ref.refs_4_, ...), custom_call_target="tpu_custom_call", output_to_operand_aliasing={{0}: (2, {}), {1}: (3, {})} | custom-call | flops 268435456 | bytes 2097152 | tf_op jit(solution)/shard_map/factors/pallas_call | solution.py:211
  23.9 0.6 collective-permute-start.3
  24.4 0.1 collective-permute-start.9
  24.5 0.0 collective-permute-done.14.refs_2_
  24.6 1.6 %collective-permute-start.15 = (f32[4,136,128]{2,1,0:T(8,128)S(1)}, f32[4,136,128]{2,1,0:T(8,128)S(1)}, u32[]{:S(2)}, u32[]{:S(2)}) collective-permute-start(f32[4,136,128]{2,1,0:T(8,128)S(1)} %get-tuple-element.76), channel_id=1, source_target_pairs={{0,4},{4,0},{8,12},{12,8},{1,5},{5,1},{9,13},{13,9},{2,6},{6,2},{1... | collective-permute-start | bytes 835592 | tf_op jit(solution)/shard_map/ppermute | solution.py:54
  26.2 0.0 collective-permute-done.3
  26.2 0.9 %collective-permute-start.16 = (f32[4,136,128]{2,1,0:T(8,128)S(1)}, f32[4,136,128]{2,1,0:T(8,128)S(1)}, u32[]{:S(2)}, u32[]{:S(2)}) collective-permute-start(f32[4,136,128]{2,1,0:T(8,128)S(1)} %get-tuple-element.75), channel_id=1, source_target_pairs={{0,12},{4,8},{8,4},{12,0},{1,13},{5,9},{9,5},{13,1},{2,14},{6,10},... | collective-permute-start | bytes 835592 | tf_op jit(solution)/shard_map/ppermute | solution.py:54
  27.1 0.0 collective-permute-done.7.refs_1_
  27.1 1.6 %collective-permute-start.4 = (f32[128,128]{1,0:T(8,128)S(1)}, f32[128,128]{1,0:T(8,128)S(1)}, u32[]{:S(2)}, u32[]{:S(2)}) collective-permute-start(f32[128,128]{1,0:T(8,128)S(1)} %get-tuple-element.87), channel_id=1, source_target_pairs={{0,1},{1,0},{2,3},{3,2},{4,5},{5,4},{6,7},{7,6},{8,9},{9,8},{10,11... | collective-permute-start | bytes 196616 | tf_op jit(solution)/shard_map/ppermute | solution.py:32
  28.8 2.6 %collective-permute-start.5 = (f32[128,128]{1,0:T(8,128)S(1)}, f32[128,128]{1,0:T(8,128)S(1)}, u32[]{:S(2)}, u32[]{:S(2)}) collective-permute-start(f32[128,128]{1,0:T(8,128)S(1)} %get-tuple-element.86), channel_id=1, source_target_pairs={{0,2},{1,3},{2,0},{3,1},{4,6},{5,7},{6,4},{7,5},{8,10},{9,11},{10,... | collective-permute-start | bytes 196616 | tf_op jit(solution)/shard_map/ppermute | solution.py:32
  31.4 0.0 collective-permute-done.9.refs_5_
  31.4 0.2 collective-permute-start.6
  31.6 4.4 %messages.3.refs_9_ = f32[2,1024,128]{2,1,0:T(8,128)S(1)} custom-call(s32[7,2]{1,0:T(8,128)S(1)} %copy-done.13, f32[8,128]{1,0:T(8,128)S(1)} %copy-done.11, f32[128,128]{1,0:T(8,128)S(1)} %copy-done.9, f32[4,136,128]{2,1,0:T(8,128)S(1)} %pack.1.block_ref.refs_0_.refs_8_, f32[4,136,128]{2,1,0:T(8,128)S(1)} %collective-permute-done.7.refs_1_, ...), custom_call_target="tpu_custom_call" | custom-call | flops 2415919104 | bytes 1048576 | tf_op jit(solution)/shard_map/messages/pallas_call | solution.py:453
  36.0 0.3 collective-permute-done.5.refs_2_
  36.3 1.3 %collective-permute-done.6.refs_3_ = f32[128,128]{1,0:T(8,128)S(1)} collective-permute-done((f32[128,128]{1,0:T(8,128)S(1)}, f32[128,128]{1,0:T(8,128)S(1)}, u32[]{:S(2)}, u32[]{:S(2)}) %collective-permute-start.6) | collective-permute-done | bytes 65568 | tf_op jit(solution)/shard_map/ppermute | solution.py:32
  37.5 0.2 filter.1
  37.7 0.8 %collective-permute-start.10 = (f32[128,128]{1,0:T(8,128)S(1)}, f32[128,128]{1,0:T(8,128)S(1)}, u32[]{:S(2)}, u32[]{:S(2)}) collective-permute-start(f32[128,128]{1,0:T(8,128)S(1)} %filter.1), channel_id=1, source_target_pairs={{0,1},{1,0},{2,3},{3,2},{4,5},{5,4},{6,7},{7,6},{8,9},{9,8},{10,11... | collective-permute-start | bytes 196616 | tf_op jit(solution)/shard_map/ppermute | solution.py:32
  38.5 1.9 %collective-permute-start.11 = (f32[128,128]{1,0:T(8,128)S(1)}, f32[128,128]{1,0:T(8,128)S(1)}, u32[]{:S(2)}, u32[]{:S(2)}) collective-permute-start(f32[128,128]{1,0:T(8,128)S(1)} %filter.1), channel_id=1, source_target_pairs={{0,2},{1,3},{2,0},{3,1},{4,6},{5,7},{6,4},{7,5},{8,10},{9,11},{10,... | collective-permute-start | bytes 196616 | tf_op jit(solution)/shard_map/ppermute | solution.py:32
  40.5 1.7 %collective-permute-start.12 = (f32[128,128]{1,0:T(8,128)S(1)}, f32[128,128]{1,0:T(8,128)S(1)}, u32[]{:S(2)}, u32[]{:S(2)}) collective-permute-start(f32[128,128]{1,0:T(8,128)S(1)} %filter.1), channel_id=1, source_target_pairs={{0,3},{1,2},{2,1},{3,0},{4,7},{5,6},{6,5},{7,4},{8,11},{9,10},{10,... | collective-permute-start | bytes 196616 | tf_op jit(solution)/shard_map/ppermute | solution.py:32
  42.2 4.6 %messages.4.refs_10_ = f32[2,1024,128]{2,1,0:T(8,128)S(1)} custom-call(s32[7,2]{1,0:T(8,128)S(1)} %copy-done.13, f32[8,128]{1,0:T(8,128)S(1)} %copy-done.11, f32[128,128]{1,0:T(8,128)S(1)} %copy-done.9, f32[4,136,128]{2,1,0:T(8,128)S(1)} %pack.1.block_ref.refs_0_.refs_8_, f32[4,136,128]{2,1,0:T(8,128)S(1)} %collective-permute-done.7.refs_1_, ...), custom_call_target="tpu_custom_call" | custom-call | flops 2415919104 | bytes 1048576 | tf_op jit(solution)/shard_map/messages/pallas_call | solution.py:453
  46.7 0.0 collective-permute-done.10
  46.8 0.0 collective-permute-done.11
  46.8 0.0 collective-permute-done.16.refs_6_
  46.8 0.1 collective-permute-start.17
  46.9 0.5 collective-permute-start.18
  47.4 0.1 collective-permute-start.19
  47.5 0.4 collective-permute-start.20
  47.9 0.1 collective-permute-start.21
  48.0 0.4 collective-permute-done.17.refs_1_
  48.4 1.9 %potentials.1 = (f32[4,128,128]{2,1,0:T(8,128)S(1)}, f32[4,128,128]{2,1,0:T(8,128)S(1)}, f32[4,128,128]{2,1,0:T(8,128)S(1)}, f32[4,128,128]{2,1,0:T(8,128)S(1)}) custom-call(f32[512,128]{1,0:T(8,128)S(1)} %pad_maximum_fusion.2.refs_0_, f32[512,128]{1,0:T(8,128)S(1)} %collective-permute-done.17.refs_1_, bf16[1024,1024]{1,0:T(8,128)(2,1)S(1)} %get-tuple-element.58.refs_2_, ...), custom_call_target="tpu_custom_call" | custom-call | flops 1610612736 | bytes 8388608 | tf_op jit(solution)/shard_map/potentials/pallas_call | solution.py:287
  50.3 0.0 copy-start.2
  50.3 0.0 copy-start.3
  50.3 0.0 copy-start.4
  50.4 0.0 copy-start.8
  50.4 1.1 %collective-permute-start.22 = (f32[4,128,128]{2,1,0:T(8,128)S(1)}, f32[4,128,128]{2,1,0:T(8,128)S(1)}, u32[]{:S(2)}, u32[]{:S(2)}) collective-permute-start(f32[4,128,128]{2,1,0:T(8,128)S(1)} %get-tuple-element.72), channel_id=1, source_target_pairs={{0,4},{4,0},{8,12},{12,8},{1,5},{5,1},{9,13},{13,9},{2,6},{6,2},{1... | collective-permute-start | bytes 786440 | tf_op jit(solution)/shard_map/ppermute | solution.py:32
  51.5 0.0 collective-permute-done.18.refs_1_
  51.5 1.5 %collective-permute-start.23 = (f32[4,128,128]{2,1,0:T(8,128)S(1)}, f32[4,128,128]{2,1,0:T(8,128)S(1)}, u32[]{:S(2)}, u32[]{:S(2)}) collective-permute-start(f32[4,128,128]{2,1,0:T(8,128)S(1)} %get-tuple-element.73), channel_id=1, source_target_pairs={{0,8},{4,12},{8,0},{12,4},{1,9},{5,13},{9,1},{13,5},{2,10},{6,14},... | collective-permute-start | bytes 786440 | tf_op jit(solution)/shard_map/ppermute | solution.py:32
  53.0 0.9 %collective-permute-start.24 = (f32[4,128,128]{2,1,0:T(8,128)S(1)}, f32[4,128,128]{2,1,0:T(8,128)S(1)}, u32[]{:S(2)}, u32[]{:S(2)}) collective-permute-start(f32[4,128,128]{2,1,0:T(8,128)S(1)} %get-tuple-element.74), channel_id=1, source_target_pairs={{0,12},{4,8},{8,4},{12,0},{1,13},{5,9},{9,5},{13,1},{2,14},{6,10},... | collective-permute-start | bytes 786440 | tf_op jit(solution)/shard_map/ppermute | solution.py:32
  53.9 0.0 collective-permute-done.20.refs_5_
  53.9 0.0 collective-permute-done.21.refs_7_
  53.9 14.0 %messages.5.refs_2_ = f32[4,128,128]{2,1,0:T(8,128)S(1)} custom-call(s32[7,8]{1,0:T(8,128)S(1)} %copy-done.12, f32[8,128]{1,0:T(8,128)S(1)} %copy-done.11, f32[128,128]{1,0:T(8,128)S(1)} %copy-done.9, f32[4,136,128]{2,1,0:T(8,128)S(1)} %collective-permute-done.13.refs_0_, f32[4,136,128]{2,1,0:T(8,128)S(1)} %collective-permute-done.18.refs_1_, ...), custom_call_target="tpu_custom_call" | custom-call | flops 9663676416 | bytes 1048576 | tf_op jit(solution)/shard_map/messages/pallas_call | solution.py:453
  67.9 0.0 collective-permute-done.22.refs_4_
  68.0 2.0 %atom_mlp.1 = f32[4,128,128]{2,1,0:T(8,128)} custom-call(s32[2,1,2]{2,1,0:T(1,128)S(1)} %bitcast.13, f32[4,128,128]{2,1,0:T(8,128)S(1)} %bitcast.10, f32[4,128,128]{2,1,0:T(8,128)S(1)} %messages.5.refs_2_, f32[4,128,128]{2,1,0:T(8,128)S(1)} %get-tuple-element.71.refs_3_, f32[4,128,128]{2,1,0:T(8,128)S(1)} %collective-permute-done.22.refs_4_, ...), custom_call_target="tpu_custom_call" | custom-call | tf_op jit(solution)/shard_map/atom_mlp/pallas_call | solution.py:526
  (31 shorter events, 0.2 us)
Async XLA Ops:
  0.0 0.9 %copy-start.1 = (f32[2,2,1,128,128]{4,3,2,1,0:T(8,128)S(1)}, f32[2,2,1,128,128]{4,3,2,1,0:T(8,128)}, u32[]{:S(2)}) copy-start(f32[2,2,1,128,128]{4,3,2,1,0:T(8,128)} %param.13) | copy-start | bytes 786436
  1.0 0.7 copy-start.6
  1.6 0.7 copy-start.7
  2.9 9.7 %collective-permute-start = (f32[4,136,128]{2,1,0:T(8,128)S(1)}, f32[4,136,128]{2,1,0:T(8,128)S(1)}, u32[]{:S(2)}, u32[]{:S(2)}) collective-permute-start(f32[4,136,128]{2,1,0:T(8,128)S(1)} %pack.1.block_ref.refs_0_.refs_8_), channel_id=1, source_target_pairs={{0,4},{4,0},{8,12},{12,8},{1,5},{5,1},{9,13},{13,9},{2,6},{6,2},{1... | collective-permute-start | bytes 835592 | tf_op jit(solution)/shard_map/ppermute | solution.py:32
  5.9 13.5 %collective-permute-start.2 = (f32[4,136,128]{2,1,0:T(8,128)S(1)}, f32[4,136,128]{2,1,0:T(8,128)S(1)}, u32[]{:S(2)}, u32[]{:S(2)}) collective-permute-start(f32[4,136,128]{2,1,0:T(8,128)S(1)} %pack.1.block_ref.refs_0_.refs_8_), channel_id=1, source_target_pairs={{0,8},{4,12},{8,0},{12,4},{1,9},{5,13},{9,1},{13,5},{2,10},{6,14},... | collective-permute-start | bytes 835592 | tf_op jit(solution)/shard_map/ppermute | solution.py:32
  7.5 14.2 %collective-permute-start.13 = (f32[4,136,128]{2,1,0:T(8,128)S(1)}, f32[4,136,128]{2,1,0:T(8,128)S(1)}, u32[]{:S(2)}, u32[]{:S(2)}) collective-permute-start(f32[4,136,128]{2,1,0:T(8,128)S(1)} %pack.1.block_ref.refs_0_.refs_8_), channel_id=1, source_target_pairs={{0,1},{1,0},{2,3},{3,2},{4,5},{5,4},{6,7},{7,6},{8,9},{9,8},{10,11... | collective-permute-start | bytes 835592 | tf_op jit(solution)/shard_map/ppermute | solution.py:54
  9.0 18.1 %collective-permute-start.7 = (f32[4,136,128]{2,1,0:T(8,128)S(1)}, f32[4,136,128]{2,1,0:T(8,128)S(1)}, u32[]{:S(2)}, u32[]{:S(2)}) collective-permute-start(f32[4,136,128]{2,1,0:T(8,128)S(1)} %pack.1.block_ref.refs_0_.refs_8_), channel_id=1, source_target_pairs={{0,16},{16,0},{1,17},{17,1},{2,18},{18,2},{3,19},{19,3},{4,20},{20... | collective-permute-start | bytes 835592 | tf_op jit(solution)/shard_map/ppermute | solution.py:32
  9.0 15.5 %collective-permute-start.14 = (f32[4,136,128]{2,1,0:T(8,128)S(1)}, f32[4,136,128]{2,1,0:T(8,128)S(1)}, u32[]{:S(2)}, u32[]{:S(2)}) collective-permute-start(f32[4,136,128]{2,1,0:T(8,128)S(1)} %pack.1.block_ref.refs_0_.refs_8_), channel_id=1, source_target_pairs={{0,3},{1,2},{2,1},{3,0},{4,7},{5,6},{6,5},{7,4},{8,11},{9,10},{10,... | collective-permute-start | bytes 835592 | tf_op jit(solution)/shard_map/ppermute | solution.py:54
  12.6 9.1 %collective-permute-start.1 = (f32[4,136,128]{2,1,0:T(8,128)S(1)}, f32[4,136,128]{2,1,0:T(8,128)S(1)}, u32[]{:S(2)}, u32[]{:S(2)}) collective-permute-start(f32[4,136,128]{2,1,0:T(8,128)S(1)} %collective-permute-done.block_ref.refs_2_), channel_id=1, source_target_pairs={{0,8},{4,12},{8,0},{12,4},{1,9},{5,13},{9,1},{13,5},{2,10},{6,14},... | collective-permute-start | bytes 835592 | tf_op jit(solution)/shard_map/ppermute | solution.py:32
  14.4 0.8 %copy-start.10 = (s32[3,2048]{1,0:T(4,128)S(1)}, s32[3,2048]{1,0:T(4,128)}, u32[]{:S(2)}) copy-start(s32[3,2048]{1,0:T(4,128)} %column_ref.1) | copy-start | bytes 73732
  19.5 9.3 %collective-permute-start.8 = (f32[4,136,128]{2,1,0:T(8,128)S(1)}, f32[4,136,128]{2,1,0:T(8,128)S(1)}, u32[]{:S(2)}, u32[]{:S(2)}) collective-permute-start(f32[4,136,128]{2,1,0:T(8,128)S(1)} %collective-permute-done.block_ref.refs_2_), channel_id=1, source_target_pairs={{0,16},{16,0},{1,17},{17,1},{2,18},{18,2},{3,19},{19,3},{4,20},{20... | collective-permute-start | bytes 835592 | tf_op jit(solution)/shard_map/ppermute | solution.py:32
  21.7 9.9 %copy-start.9 = (f32[128,128]{1,0:T(8,128)S(1)}, f32[128,128]{1,0:T(8,128)}, u32[]{:S(2)}) copy-start(f32[128,128]{1,0:T(8,128)} %value_ref.2) | copy-start | bytes 196612
  21.7 9.9 %copy-start.11 = (f32[8,128]{1,0:T(8,128)S(1)}, f32[8,128]{1,0:T(8,128)}, u32[]{:S(2)}) copy-start(f32[8,128]{1,0:T(8,128)} %mix_ref.5) | copy-start | bytes 12292
  21.7 9.8 %copy-start.13 = (s32[7,2]{1,0:T(8,128)S(1)}, s32[7,2]{1,0:T(8,128)}, u32[]{:S(2)}) copy-start(s32[7,2]{1,0:T(8,128)} %constant.47.clone.step_ref) | copy-start | bytes 172
  23.9 2.3 %collective-permute-start.3 = (f32[512,128]{1,0:T(8,128)S(1)}, f32[512,128]{1,0:T(8,128)S(1)}, u32[]{:S(2)}, u32[]{:S(2)}) collective-permute-start(f32[512,128]{1,0:T(8,128)S(1)} %get-tuple-element.50), channel_id=1, source_target_pairs={{0,16},{16,0},{1,17},{17,1},{2,18},{18,2},{3,19},{19,3},{4,20},{20... | collective-permute-start | bytes 786440 | tf_op jit(solution)/shard_map/ppermute | solution.py:32
  24.4 7.0 %collective-permute-start.9 = (f32[4,136,128]{2,1,0:T(8,128)S(1)}, f32[4,136,128]{2,1,0:T(8,128)S(1)}, u32[]{:S(2)}, u32[]{:S(2)}) collective-permute-start(f32[4,136,128]{2,1,0:T(8,128)S(1)} %collective-permute-done.1.block_ref.refs_4_), channel_id=1, source_target_pairs={{0,16},{16,0},{1,17},{17,1},{2,18},{18,2},{3,19},{19,3},{4,20},{20... | collective-permute-start | bytes 835592 | tf_op jit(solution)/shard_map/ppermute | solution.py:32
  24.6 22.2 %collective-permute-start.15 = (f32[4,136,128]{2,1,0:T(8,128)S(1)}, f32[4,136,128]{2,1,0:T(8,128)S(1)}, u32[]{:S(2)}, u32[]{:S(2)}) collective-permute-start(f32[4,136,128]{2,1,0:T(8,128)S(1)} %get-tuple-element.76), channel_id=1, source_target_pairs={{0,4},{4,0},{8,12},{12,8},{1,5},{5,1},{9,13},{13,9},{2,6},{6,2},{1... | collective-permute-start | bytes 835592 | tf_op jit(solution)/shard_map/ppermute | solution.py:54
  26.2 20.7 %collective-permute-start.16 = (f32[4,136,128]{2,1,0:T(8,128)S(1)}, f32[4,136,128]{2,1,0:T(8,128)S(1)}, u32[]{:S(2)}, u32[]{:S(2)}) collective-permute-start(f32[4,136,128]{2,1,0:T(8,128)S(1)} %get-tuple-element.75), channel_id=1, source_target_pairs={{0,12},{4,8},{8,4},{12,0},{1,13},{5,9},{9,5},{13,1},{2,14},{6,10},... | collective-permute-start | bytes 835592 | tf_op jit(solution)/shard_map/ppermute | solution.py:54
  27.1 8.9 %collective-permute-start.4 = (f32[128,128]{1,0:T(8,128)S(1)}, f32[128,128]{1,0:T(8,128)S(1)}, u32[]{:S(2)}, u32[]{:S(2)}) collective-permute-start(f32[128,128]{1,0:T(8,128)S(1)} %get-tuple-element.87), channel_id=1, source_target_pairs={{0,1},{1,0},{2,3},{3,2},{4,5},{5,4},{6,7},{7,6},{8,9},{9,8},{10,11... | collective-permute-start | bytes 196616 | tf_op jit(solution)/shard_map/ppermute | solution.py:32
  28.8 7.5 %collective-permute-start.5 = (f32[128,128]{1,0:T(8,128)S(1)}, f32[128,128]{1,0:T(8,128)S(1)}, u32[]{:S(2)}, u32[]{:S(2)}) collective-permute-start(f32[128,128]{1,0:T(8,128)S(1)} %get-tuple-element.86), channel_id=1, source_target_pairs={{0,2},{1,3},{2,0},{3,1},{4,6},{5,7},{6,4},{7,5},{8,10},{9,11},{10,... | collective-permute-start | bytes 196616 | tf_op jit(solution)/shard_map/ppermute | solution.py:32
  31.4 6.2 %copy-start = (f32[2048,128]{1,0:T(8,128)S(1)}, f32[2048,128]{1,0:T(8,128)}, u32[]{:S(2)}) copy-start(f32[2048,128]{1,0:T(8,128)} %refs_5_.1) | copy-start | bytes 3145732
  31.4 6.2 %copy-start.5 = (f32[128,128]{1,0:T(8,128)S(1)}, f32[128,128]{1,0:T(8,128)}, u32[]{:S(2)}) copy-start(f32[128,128]{1,0:T(8,128)} %refs_4_) | copy-start | bytes 196612
  31.4 6.2 %collective-permute-start.6 = (f32[128,128]{1,0:T(8,128)S(1)}, f32[128,128]{1,0:T(8,128)S(1)}, u32[]{:S(2)}, u32[]{:S(2)}) collective-permute-start(f32[128,128]{1,0:T(8,128)S(1)} %get-tuple-element.85), channel_id=1, source_target_pairs={{0,3},{1,2},{2,1},{3,0},{4,7},{5,6},{6,5},{7,4},{8,11},{9,10},{10,... | collective-permute-start | bytes 196616 | tf_op jit(solution)/shard_map/ppermute | solution.py:32
  37.7 9.0 %collective-permute-start.10 = (f32[128,128]{1,0:T(8,128)S(1)}, f32[128,128]{1,0:T(8,128)S(1)}, u32[]{:S(2)}, u32[]{:S(2)}) collective-permute-start(f32[128,128]{1,0:T(8,128)S(1)} %filter.1), channel_id=1, source_target_pairs={{0,1},{1,0},{2,3},{3,2},{4,5},{5,4},{6,7},{7,6},{8,9},{9,8},{10,11... | collective-permute-start | bytes 196616 | tf_op jit(solution)/shard_map/ppermute | solution.py:32
  38.5 8.2 %collective-permute-start.11 = (f32[128,128]{1,0:T(8,128)S(1)}, f32[128,128]{1,0:T(8,128)S(1)}, u32[]{:S(2)}, u32[]{:S(2)}) collective-permute-start(f32[128,128]{1,0:T(8,128)S(1)} %filter.1), channel_id=1, source_target_pairs={{0,2},{1,3},{2,0},{3,1},{4,6},{5,7},{6,4},{7,5},{8,10},{9,11},{10,... | collective-permute-start | bytes 196616 | tf_op jit(solution)/shard_map/ppermute | solution.py:32
  40.5 6.3 %collective-permute-start.12 = (f32[128,128]{1,0:T(8,128)S(1)}, f32[128,128]{1,0:T(8,128)S(1)}, u32[]{:S(2)}, u32[]{:S(2)}) collective-permute-start(f32[128,128]{1,0:T(8,128)S(1)} %filter.1), channel_id=1, source_target_pairs={{0,3},{1,2},{2,1},{3,0},{4,7},{5,6},{6,5},{7,4},{8,11},{9,10},{10,... | collective-permute-start | bytes 196616 | tf_op jit(solution)/shard_map/ppermute | solution.py:32
  46.8 1.6 %collective-permute-start.17 = (f32[512,128]{1,0:T(8,128)S(1)}, f32[512,128]{1,0:T(8,128)S(1)}, u32[]{:S(2)}, u32[]{:S(2)}) collective-permute-start(f32[512,128]{1,0:T(8,128)S(1)} %pad_maximum_fusion.2.refs_0_), channel_id=1, source_target_pairs={{0,16},{16,0},{1,17},{17,1},{2,18},{18,2},{3,19},{19,3},{4,20},{20... | collective-permute-start | bytes 786440 | tf_op jit(solution)/shard_map/ppermute | solution.py:32
  46.9 4.6 %collective-permute-start.18 = (f32[4,136,128]{2,1,0:T(8,128)S(1)}, f32[4,136,128]{2,1,0:T(8,128)S(1)}, u32[]{:S(2)}, u32[]{:S(2)}) collective-permute-start(f32[4,136,128]{2,1,0:T(8,128)S(1)} %collective-permute-done.13.refs_0_), channel_id=1, source_target_pairs={{0,16},{16,0},{1,17},{17,1},{2,18},{18,2},{3,19},{19,3},{4,20},{20... | collective-permute-start | bytes 835592 | tf_op jit(solution)/shard_map/ppermute | solution.py:32
  47.4 5.6 %collective-permute-start.19 = (f32[4,136,128]{2,1,0:T(8,128)S(1)}, f32[4,136,128]{2,1,0:T(8,128)S(1)}, u32[]{:S(2)}, u32[]{:S(2)}) collective-permute-start(f32[4,136,128]{2,1,0:T(8,128)S(1)} %collective-permute-done.14.refs_2_), channel_id=1, source_target_pairs={{0,16},{16,0},{1,17},{17,1},{2,18},{18,2},{3,19},{19,3},{4,20},{20... | collective-permute-start | bytes 835592 | tf_op jit(solution)/shard_map/ppermute | solution.py:32
  47.5 6.5 %collective-permute-start.20 = (f32[4,136,128]{2,1,0:T(8,128)S(1)}, f32[4,136,128]{2,1,0:T(8,128)S(1)}, u32[]{:S(2)}, u32[]{:S(2)}) collective-permute-start(f32[4,136,128]{2,1,0:T(8,128)S(1)} %collective-permute-done.15.refs_4_), channel_id=1, source_target_pairs={{0,16},{16,0},{1,17},{17,1},{2,18},{18,2},{3,19},{19,3},{4,20},{20... | collective-permute-start | bytes 835592 | tf_op jit(solution)/shard_map/ppermute | solution.py:32
  47.9 6.0 %collective-permute-start.21 = (f32[4,136,128]{2,1,0:T(8,128)S(1)}, f32[4,136,128]{2,1,0:T(8,128)S(1)}, u32[]{:S(2)}, u32[]{:S(2)}) collective-permute-start(f32[4,136,128]{2,1,0:T(8,128)S(1)} %collective-permute-done.16.refs_6_), channel_id=1, source_target_pairs={{0,16},{16,0},{1,17},{17,1},{2,18},{18,2},{3,19},{19,3},{4,20},{20... | collective-permute-start | bytes 835592 | tf_op jit(solution)/shard_map/ppermute | solution.py:32
  48.4 5.5 %copy-start.12 = (s32[7,8]{1,0:T(8,128)S(1)}, s32[7,8]{1,0:T(8,128)}, u32[]{:S(2)}) copy-start(s32[7,8]{1,0:T(8,128)} %constant.48.clone.step_ref) | copy-start | bytes 676
  50.3 17.7 %copy-start.2 = (f32[2,2,1,128,128]{4,3,2,1,0:T(8,128)S(1)}, f32[2,2,1,128,128]{4,3,2,1,0:T(8,128)}, u32[]{:S(2)}) copy-start(f32[2,2,1,128,128]{4,3,2,1,0:T(8,128)} %param.13) | copy-start | bytes 786436
  50.3 17.7 %copy-start.3 = (f32[128,256]{1,0:T(8,128)S(1)}, f32[128,256]{1,0:T(8,128)}, u32[]{:S(2)}) copy-start(f32[128,256]{1,0:T(8,128)} %refs_7_.1) | copy-start | bytes 393220
  50.3 17.7 %copy-start.4 = (f32[256,128]{1,0:T(8,128)S(1)}, f32[256,128]{1,0:T(8,128)}, u32[]{:S(2)}) copy-start(f32[256,128]{1,0:T(8,128)} %refs_8_.1) | copy-start | bytes 393220
  50.4 17.7 %copy-start.8 = (s32[2,2,1]{1,2,0:T(1,128)S(1)}, s32[2,2,1]{1,2,0:T(1,128)}, u32[]{:S(2)}) copy-start(s32[2,2,1]{1,2,0:T(1,128)} %param.15) | copy-start | bytes 52
  50.4 17.6 %collective-permute-start.22 = (f32[4,128,128]{2,1,0:T(8,128)S(1)}, f32[4,128,128]{2,1,0:T(8,128)S(1)}, u32[]{:S(2)}, u32[]{:S(2)}) collective-permute-start(f32[4,128,128]{2,1,0:T(8,128)S(1)} %get-tuple-element.72), channel_id=1, source_target_pairs={{0,4},{4,0},{8,12},{12,8},{1,5},{5,1},{9,13},{13,9},{2,6},{6,2},{1... | collective-permute-start | bytes 786440 | tf_op jit(solution)/shard_map/ppermute | solution.py:32
  51.5 16.5 %collective-permute-start.23 = (f32[4,128,128]{2,1,0:T(8,128)S(1)}, f32[4,128,128]{2,1,0:T(8,128)S(1)}, u32[]{:S(2)}, u32[]{:S(2)}) collective-permute-start(f32[4,128,128]{2,1,0:T(8,128)S(1)} %get-tuple-element.73), channel_id=1, source_target_pairs={{0,8},{4,12},{8,0},{12,4},{1,9},{5,13},{9,1},{13,5},{2,10},{6,14},... | collective-permute-start | bytes 786440 | tf_op jit(solution)/shard_map/ppermute | solution.py:32
  53.0 15.0 %collective-permute-start.24 = (f32[4,128,128]{2,1,0:T(8,128)S(1)}, f32[4,128,128]{2,1,0:T(8,128)S(1)}, u32[]{:S(2)}, u32[]{:S(2)}) collective-permute-start(f32[4,128,128]{2,1,0:T(8,128)S(1)} %get-tuple-element.74), channel_id=1, source_target_pairs={{0,12},{4,8},{8,4},{12,0},{1,13},{5,9},{9,5},{13,1},{2,14},{6,10},... | collective-permute-start | bytes 786440 | tf_op jit(solution)/shard_map/ppermute | solution.py:32

commit v10 on v9

--- a/solution.py
+++ b/solution.py
@@ -148,12 +148,13 @@
     return 1.0 - sine * sine, sine * cosine
 
 
-def factor_kernel(parts, chunk, first, column_ref, block_ref, *refs):
+def factor_kernel(parts, chunk, first, count, column_ref, *refs):
+    blocks, refs = refs[:count], refs[count:]
     before = refs[: 0 if first else parts]
     refs = refs[len(before) :]
     after, wave_ref, refs = refs[:parts], refs[parts], refs[parts + 1 :]
     weight_ref = refs[-1]
-    cells, _, slots = block_ref.shape
+    cells, _, slots = blocks[0].shape
     channels = after[0].shape[-1]
     span = cells * slots
     total = wave_ref.shape[0] // 2
@@ -163,9 +164,14 @@
         rows = column_ref[:, pl.ds(begin, total)].astype(f32)
         column_ref = refs[0]
         column_ref[...] = jnp.concatenate([rows, jnp.zeros((5, total), f32)], axis=0).T
-    for cell in range(cells):
+    places = [
+        (block_ref, cell, 2 * span * n + cell * slots)
+        for n, block_ref in enumerate(blocks)
+        for cell in range(cells)
+    ]
+    for block_ref, cell, here in places:
         high, low = split(block_ref[cell, :channels, :])
-        for at in (cell * slots, span + cell * slots):
+        for at in (here, span + here):
             weight_ref[:channels, at : at + slots] = high
             weight_ref[channels:, at : at + slots] = low
 
@@ -175,8 +181,7 @@
         wave_y = column_ref[pl.ds(here, chunk), 1:2]
         wave_z = column_ref[pl.ds(here, chunk), 2:3]
         row = pl.multiple_of(j * 2 * chunk, 2 * chunk)
-        for cell in range(cells):
-            at = cell * slots
+        for block_ref, cell, at in places:
             frac = block_ref[cell, channels + 3 : channels + 6, :]
             u = wave_x * frac[0:1] + wave_y * frac[1:2] + wave_z * frac[2:3]
             cosine, sine = turns(u)
@@ -200,27 +205,27 @@
         after[n][...] = both if first else before[n][...] + both
 
 
-def partial_factors(columns, total, chunk, block, before, parts):
-    cells, rows, slots = block.shape
+def partial_factors(columns, total, chunk, blocks, before, parts):
+    cells, rows, slots = blocks[0].shape
     channels = rows - 8
-    span = cells * slots
+    span = len(blocks) * cells * slots
     out = [jax.ShapeDtypeStruct((2 * total // parts, channels), f32)] * parts
     out.append(jax.ShapeDtypeStruct((2 * total, 2 * span), bf16))
     if not before:
         out.append(jax.ShapeDtypeStruct((total, 8), f32))
     return pl.pallas_call(
-        functools.partial(factor_kernel, parts, chunk, not before),
-        in_specs=[whole()] * (2 + len(before)),
+        functools.partial(factor_kernel, parts, chunk, not before, len(blocks)),
+        in_specs=[whole()] * (1 + len(blocks) + len(before)),
         out_specs=[whole()] * len(out),
         out_shape=out,
-        input_output_aliases={2 + n: n for n in range(len(before))},
+        input_output_aliases={1 + len(blocks) + n: n for n in range(len(before))},
         scratch_shapes=[pltpu.VMEM((2 * channels, 2 * span), bf16)],
         compiler_params=params(),
         cost_estimate=pl.CostEstimate(
             flops=8 * total * span * channels, bytes_accessed=8 * total * span, transcendentals=0
         ),
         name="factors",
-    )(columns, block, *before)
+    )(columns, *blocks, *before)
 
 
 def filter_kernel(scale, block_ref, *refs):
@@ -271,11 +276,14 @@
     high, low = split(ordered_ref[...].T)
     turned_ref[:channels, :] = high
     turned_ref[channels:, :] = low
-    for wave_ref, out in zip(waves, outs):
-        cells, _, slots = out.shape
-        span = cells * slots
-        both = jnp.dot(turned_ref[...], wave_ref[:, :span], preferred_element_type=f32)
-        third = jnp.dot(turned_ref[:channels, :], wave_ref[:, span:], preferred_element_type=f32)
+    cells, _, slots = outs[0].shape
+    span = cells * slots
+    places = [(wave_ref, at) for wave_ref in waves for at in range(0, wave_ref.shape[1], 2 * span)]
+    for (wave_ref, at), out in zip(places, outs):
+        both = jnp.dot(turned_ref[...], wave_ref[:, at : at + span], preferred_element_type=f32)
+        third = jnp.dot(
+            turned_ref[:channels, :], wave_ref[:, at + span : at + 2 * span], preferred_element_type=f32
+        )
         potential = both[:channels] + both[channels:] + third
         for cell in range(cells):
             out[cell] = potential[:, cell * slots : (cell + 1) * slots]
@@ -284,19 +292,20 @@
 def potentials_of(held, pieces, waves, cells, slots):
     rows = waves[0].shape[0]
     channels = held[0].shape[-1]
+    count = sum(table.shape[1] for table in waves) // (2 * cells * slots)
     return pl.pallas_call(
         functools.partial(potential_kernel, len(held), pieces, len(waves)),
         in_specs=[whole()] * (len(held) + len(waves)),
-        out_specs=[whole()] * len(waves),
+        out_specs=[whole()] * count,
         scratch_shapes=[
             pltpu.VMEM((rows, channels), f32),
             pltpu.VMEM((2 * channels, rows), bf16),
         ],
-        out_shape=[jax.ShapeDtypeStruct((cells, channels, slots), f32)] * len(waves),
+        out_shape=[jax.ShapeDtypeStruct((cells, channels, slots), f32)] * count,
         compiler_params=params(),
         cost_estimate=pl.CostEstimate(
-            flops=6 * rows * len(waves) * cells * slots * channels,
-            bytes_accessed=4 * rows * len(waves) * cells * slots, transcendentals=0,
+            flops=6 * rows * count * cells * slots * channels,
+            bytes_accessed=4 * rows * count * cells * slots, transcendentals=0,
         ),
         name="potentials",
     )(*held, *waves)
@@ -596,12 +605,11 @@
     half = 2 * share // size_x
     piece = half // size_z
     chunk = min(piece, share // size_x)
-    first = min(1, size_y - 1)
-    late, gathered[first] = lax.optimization_barrier((own, gathered[first]))
-    *parts, table, columns = partial_factors(waves, share, chunk, late, (), size_x)
+    most = min(2, size_y)
+    *parts, table, columns = partial_factors(waves, share, chunk, gathered[:most], (), size_x)
     tables = [table]
-    for block in gathered[1:]:
-        *parts, table = partial_factors(columns, share, chunk, block, parts, size_x)
+    for block in gathered[most:]:
+        *parts, table = partial_factors(columns, share, chunk, [block], parts, size_x)
         tables.append(table)
 
     summed = parts[0]

time: 70.3 us -> 70.1 us (level)
    pallas_call x4 -> x3, Pallas kernels: 8.52 us -> 8.34 us  [partial_factors(): pl.pallas_call(functools.partial(factor_kernel, parts, chunk, not before,...]
where the time goes in v10:
time: 70.1 us; the launch traced here: 69.8 us
  Pallas kernels  35.9 us (51%)
  starting transfers between devices  27.1 us (39%)
  local copies, waits for them, and re-layouts  3.2 us (5%)
  waiting for transfers between devices  3.11 us (4%)
    pallas_call x3, Pallas kernels, pair_messages(): pl.pallas_call(functools.partial(message_kernel, basis, len(blocks), tabl...  22.9 us
    ppermute x21, starting transfers between devices, exchange(): return lax.ppermute(block, axis, pairs)  20.6 us
    pallas_call x3, Pallas kernels, partial_factors(): pl.pallas_call(functools.partial(factor_kernel, parts, chunk, not before,...  8.34 us
    ppermute x4, starting transfers between devices, neighbours(): return (lax.ppermute(first, axis, one), lax.ppermute(second, axis, two))  6.5 us
    unnamed x28, local copies, waits for them, and re-layouts  3.13 us
    ppermute x21, waiting for transfers between devices, exchange(): return lax.ppermute(block, axis, pairs)  3.1 us
    pallas_call x1, Pallas kernels, atom_mlp(): pl.pallas_call(functools.partial(mlp_kernel, len(potentials), shape), in_...  2 us
    pallas_call x1, Pallas kernels, potentials_of(): pl.pallas_call(functools.partial(potential_kernel, len(held), pieces, len...  1.88 us
  transfers between devices with their start and end apart: 25, of which 4 were waited for; matrix products, arithmetic and copies ran while one was open for 0% of the time, Pallas kernels for 48%

profile of v10, /device:TPU:0, one launch (start us, length us, event | category | flops | bytes accessed | tf_op | source)
XLA Modules:
  0.0 69.8 jit_solution(11536592698423925079)
XLA Ops:
  0.0 0.9 %copy-done.1 = f32[2,2,1,128,128]{4,3,2,1,0:T(8,128)S(1)} copy-done((f32[2,2,1,128,128]{4,3,2,1,0:T(8,128)S(1)}, f32[2,2,1,128,128]{4,3,2,1,0:T(8,128)}, u32[]{:S(2)}) %copy-start.1) | copy-done | bytes 262168
  1.0 0.7 copy-done.6
  1.6 0.7 copy-done.7
  2.3 0.6 pack.1.refs_0_.refs_8_
  2.9 3.0 %collective-permute-start = (f32[4,136,128]{2,1,0:T(8,128)S(1)}, f32[4,136,128]{2,1,0:T(8,128)S(1)}, u32[]{:S(2)}, u32[]{:S(2)}) collective-permute-start(f32[4,136,128]{2,1,0:T(8,128)S(1)} %pack.1.refs_0_.refs_8_), channel_id=1, source_target_pairs={{0,4},{4,0},{8,12},{12,8},{1,5},{5,1},{9,13},{13,9},{2,6},{6,2},{1... | collective-permute-start | bytes 835592 | tf_op jit(solution)/shard_map/ppermute | solution.py:32
  5.9 1.5 %collective-permute-start.2 = (f32[4,136,128]{2,1,0:T(8,128)S(1)}, f32[4,136,128]{2,1,0:T(8,128)S(1)}, u32[]{:S(2)}, u32[]{:S(2)}) collective-permute-start(f32[4,136,128]{2,1,0:T(8,128)S(1)} %pack.1.refs_0_.refs_8_), channel_id=1, source_target_pairs={{0,8},{4,12},{8,0},{12,4},{1,9},{5,13},{9,1},{13,5},{2,10},{6,14},... | collective-permute-start | bytes 835592 | tf_op jit(solution)/shard_map/ppermute | solution.py:32
  7.5 1.6 %collective-permute-start.13 = (f32[4,136,128]{2,1,0:T(8,128)S(1)}, f32[4,136,128]{2,1,0:T(8,128)S(1)}, u32[]{:S(2)}, u32[]{:S(2)}) collective-permute-start(f32[4,136,128]{2,1,0:T(8,128)S(1)} %pack.1.refs_0_.refs_8_), channel_id=1, source_target_pairs={{0,1},{1,0},{2,3},{3,2},{4,5},{5,4},{6,7},{7,6},{8,9},{9,8},{10,11... | collective-permute-start | bytes 835592 | tf_op jit(solution)/shard_map/ppermute | solution.py:54
  9.0 0.0 collective-permute-start.7
  9.0 2.5 %collective-permute-start.14 = (f32[4,136,128]{2,1,0:T(8,128)S(1)}, f32[4,136,128]{2,1,0:T(8,128)S(1)}, u32[]{:S(2)}, u32[]{:S(2)}) collective-permute-start(f32[4,136,128]{2,1,0:T(8,128)S(1)} %pack.1.refs_0_.refs_8_), channel_id=1, source_target_pairs={{0,3},{1,2},{2,1},{3,0},{4,7},{5,6},{6,5},{7,4},{8,11},{9,10},{10,... | collective-permute-start | bytes 835592 | tf_op jit(solution)/shard_map/ppermute | solution.py:54
  11.5 1.1 %collective-permute-done.refs_1_.refs_2_ = f32[4,136,128]{2,1,0:T(8,128)S(1)} collective-permute-done((f32[4,136,128]{2,1,0:T(8,128)S(1)}, f32[4,136,128]{2,1,0:T(8,128)S(1)}, u32[]{:S(2)}, u32[]{:S(2)}) %collective-permute-start) | collective-permute-done | bytes 278560 | tf_op jit(solution)/shard_map/ppermute | solution.py:32
  12.6 1.8 %collective-permute-start.1 = (f32[4,136,128]{2,1,0:T(8,128)S(1)}, f32[4,136,128]{2,1,0:T(8,128)S(1)}, u32[]{:S(2)}, u32[]{:S(2)}) collective-permute-start(f32[4,136,128]{2,1,0:T(8,128)S(1)} %collective-permute-done.refs_1_.refs_2_), channel_id=1, source_target_pairs={{0,8},{4,12},{8,0},{12,4},{1,9},{5,13},{9,1},{13,5},{2,10},{6,14},... | collective-permute-start | bytes 835592 | tf_op jit(solution)/shard_map/ppermute | solution.py:32
  14.4 0.8 %copy-done.10 = s32[3,2048]{1,0:T(4,128)S(1)} copy-done((s32[3,2048]{1,0:T(4,128)S(1)}, s32[3,2048]{1,0:T(4,128)}, u32[]{:S(2)}) %copy-start.10) | copy-done | bytes 24600
  15.1 4.2 %factors.3 = (f32[512,128]{1,0:T(8,128)S(1)}, f32[512,128]{1,0:T(8,128)S(1)}, bf16[1024,2048]{1,0:T(8,128)(2,1)S(1)}, f32[512,8]{1,0:T(8,128)S(1)}) custom-call(s32[3,2048]{1,0:T(4,128)S(1)} %copy-done.10, f32[4,136,128]{2,1,0:T(8,128)S(1)} %pack.1.refs_0_.refs_8_, f32[4,136,128]{2,1,0:T(8,128)S(1)} %collective-permute-done.refs_1_.refs_2_), custom_call_target="tpu_custom_call" | custom-call | flops 536870912 | bytes 4194304 | tf_op jit(solution)/shard_map/factors/pallas_call | solution.py:216
  19.3 0.0 collective-permute-done.2.refs_0_
  19.3 0.1 collective-permute-start.8
  19.4 2.1 %factors.4 = (f32[512,128]{1,0:T(8,128)S(1)}, f32[512,128]{1,0:T(8,128)S(1)}, bf16[1024,1024]{1,0:T(8,128)(2,1)S(1)}) custom-call(f32[512,8]{1,0:T(8,128)S(1)} %get-tuple-element.35.column_ref, f32[4,136,128]{2,1,0:T(8,128)S(1)} %collective-permute-done.2.refs_0_, ...), custom_call_target="tpu_custom_call", output_to_operand_aliasing={{0}: (2, {}), {1}: (3, {})} | custom-call | flops 268435456 | bytes 2097152 | tf_op jit(solution)/shard_map/factors/pallas_call | solution.py:216
  21.5 0.0 collective-permute-done.13.refs_0_
  21.5 0.0 copy-start.9
  21.5 0.0 copy-start.11
  21.5 0.0 copy-start.13
  21.6 0.0 collective-permute-done.1.refs_0_.refs_4_
  21.6 2.1 %factors.5 = (f32[512,128]{1,0:T(8,128)S(1)}, f32[512,128]{1,0:T(8,128)S(1)}, bf16[1024,1024]{1,0:T(8,128)(2,1)S(1)}) custom-call(f32[512,8]{1,0:T(8,128)S(1)} %get-tuple-element.35.column_ref, f32[4,136,128]{2,1,0:T(8,128)S(1)} %collective-permute-done.1.refs_0_.refs_4_, ...), custom_call_target="tpu_custom_call", output_to_operand_aliasing={{0}: (2, {}), {1}: (3, {})} | custom-call | flops 268435456 | bytes 2097152 | tf_op jit(solution)/shard_map/factors/pallas_call | solution.py:216
  23.7 0.6 collective-permute-start.3
  24.2 0.1 collective-permute-start.9
  24.3 0.0 collective-permute-done.14.refs_2_
  24.3 0.1 fusion
  24.4 1.6 %collective-permute-start.15 = (f32[4,136,128]{2,1,0:T(8,128)S(1)}, f32[4,136,128]{2,1,0:T(8,128)S(1)}, u32[]{:S(2)}, u32[]{:S(2)}) collective-permute-start(f32[4,136,128]{2,1,0:T(8,128)S(1)} %get-tuple-element.66), channel_id=1, source_target_pairs={{0,4},{4,0},{8,12},{12,8},{1,5},{5,1},{9,13},{13,9},{2,6},{6,2},{1... | collective-permute-start | bytes 835592 | tf_op jit(solution)/shard_map/ppermute | solution.py:54
  26.0 0.0 collective-permute-done.3
  26.0 0.9 %collective-permute-start.16 = (f32[4,136,128]{2,1,0:T(8,128)S(1)}, f32[4,136,128]{2,1,0:T(8,128)S(1)}, u32[]{:S(2)}, u32[]{:S(2)}) collective-permute-start(f32[4,136,128]{2,1,0:T(8,128)S(1)} %get-tuple-element.65), channel_id=1, source_target_pairs={{0,12},{4,8},{8,4},{12,0},{1,13},{5,9},{9,5},{13,1},{2,14},{6,10},... | collective-permute-start | bytes 835592 | tf_op jit(solution)/shard_map/ppermute | solution.py:54
  26.9 0.0 collective-permute-done.7.refs_1_
  26.9 1.6 %collective-permute-start.4 = (f32[128,128]{1,0:T(8,128)S(1)}, f32[128,128]{1,0:T(8,128)S(1)}, u32[]{:S(2)}, u32[]{:S(2)}) collective-permute-start(f32[128,128]{1,0:T(8,128)S(1)} %get-tuple-element.77), channel_id=1, source_target_pairs={{0,1},{1,0},{2,3},{3,2},{4,5},{5,4},{6,7},{7,6},{8,9},{9,8},{10,11... | collective-permute-start | bytes 196616 | tf_op jit(solution)/shard_map/ppermute | solution.py:32
  28.6 0.0 collective-permute-done.8.refs_3_
  28.6 2.6 %collective-permute-start.5 = (f32[128,128]{1,0:T(8,128)S(1)}, f32[128,128]{1,0:T(8,128)S(1)}, u32[]{:S(2)}, u32[]{:S(2)}) collective-permute-start(f32[128,128]{1,0:T(8,128)S(1)} %get-tuple-element.76), channel_id=1, source_target_pairs={{0,2},{1,3},{2,0},{3,1},{4,6},{5,7},{6,4},{7,5},{8,10},{9,11},{10,... | collective-permute-start | bytes 196616 | tf_op jit(solution)/shard_map/ppermute | solution.py:32
  31.2 0.2 collective-permute-start.6
  31.4 4.4 %messages.3.refs_9_ = f32[2,1024,128]{2,1,0:T(8,128)S(1)} custom-call(s32[7,2]{1,0:T(8,128)S(1)} %copy-done.13, f32[8,128]{1,0:T(8,128)S(1)} %copy-done.11, f32[128,128]{1,0:T(8,128)S(1)} %copy-done.9, f32[4,136,128]{2,1,0:T(8,128)S(1)} %pack.1.refs_0_.refs_8_, f32[4,136,128]{2,1,0:T(8,128)S(1)} %collective-permute-done.7.refs_1_, ...), custom_call_target="tpu_custom_call" | custom-call | flops 2415919104 | bytes 1048576 | tf_op jit(solution)/shard_map/messages/pallas_call | solution.py:462
  35.8 0.3 collective-permute-done.5.refs_2_
  36.1 1.3 %collective-permute-done.6.refs_3_ = f32[128,128]{1,0:T(8,128)S(1)} collective-permute-done((f32[128,128]{1,0:T(8,128)S(1)}, f32[128,128]{1,0:T(8,128)S(1)}, u32[]{:S(2)}, u32[]{:S(2)}) %collective-permute-start.6) | collective-permute-done | bytes 65568 | tf_op jit(solution)/shard_map/ppermute | solution.py:32
  37.3 0.2 filter.1
  37.5 0.8 %collective-permute-start.10 = (f32[128,128]{1,0:T(8,128)S(1)}, f32[128,128]{1,0:T(8,128)S(1)}, u32[]{:S(2)}, u32[]{:S(2)}) collective-permute-start(f32[128,128]{1,0:T(8,128)S(1)} %filter.1), channel_id=1, source_target_pairs={{0,1},{1,0},{2,3},{3,2},{4,5},{5,4},{6,7},{7,6},{8,9},{9,8},{10,11... | collective-permute-start | bytes 196616 | tf_op jit(solution)/shard_map/ppermute | solution.py:32
  38.3 1.9 %collective-permute-start.11 = (f32[128,128]{1,0:T(8,128)S(1)}, f32[128,128]{1,0:T(8,128)S(1)}, u32[]{:S(2)}, u32[]{:S(2)}) collective-permute-start(f32[128,128]{1,0:T(8,128)S(1)} %filter.1), channel_id=1, source_target_pairs={{0,2},{1,3},{2,0},{3,1},{4,6},{5,7},{6,4},{7,5},{8,10},{9,11},{10,... | collective-permute-start | bytes 196616 | tf_op jit(solution)/shard_map/ppermute | solution.py:32
  40.2 1.7 %collective-permute-start.12 = (f32[128,128]{1,0:T(8,128)S(1)}, f32[128,128]{1,0:T(8,128)S(1)}, u32[]{:S(2)}, u32[]{:S(2)}) collective-permute-start(f32[128,128]{1,0:T(8,128)S(1)} %filter.1), channel_id=1, source_target_pairs={{0,3},{1,2},{2,1},{3,0},{4,7},{5,6},{6,5},{7,4},{8,11},{9,10},{10,... | collective-permute-start | bytes 196616 | tf_op jit(solution)/shard_map/ppermute | solution.py:32
  42.0 4.6 %messages.4.refs_10_ = f32[2,1024,128]{2,1,0:T(8,128)S(1)} custom-call(s32[7,2]{1,0:T(8,128)S(1)} %copy-done.13, f32[8,128]{1,0:T(8,128)S(1)} %copy-done.11, f32[128,128]{1,0:T(8,128)S(1)} %copy-done.9, f32[4,136,128]{2,1,0:T(8,128)S(1)} %pack.1.refs_0_.refs_8_, f32[4,136,128]{2,1,0:T(8,128)S(1)} %collective-permute-done.7.refs_1_, ...), custom_call_target="tpu_custom_call" | custom-call | flops 2415919104 | bytes 1048576 | tf_op jit(solution)/shard_map/messages/pallas_call | solution.py:462
  46.5 0.0 collective-permute-done.10
  46.6 0.0 collective-permute-done.15.refs_4_
  46.6 0.0 collective-permute-done.16.refs_6_
  46.6 0.1 collective-permute-start.17
  46.7 0.5 collective-permute-start.18
  47.2 0.1 collective-permute-start.19
  47.3 0.4 collective-permute-start.20
  47.7 0.1 collective-permute-start.21
  47.8 0.4 collective-permute-done.17.refs_1_
  48.2 1.9 %potentials.1 = (f32[4,128,128]{2,1,0:T(8,128)S(1)}, f32[4,128,128]{2,1,0:T(8,128)S(1)}, f32[4,128,128]{2,1,0:T(8,128)S(1)}, f32[4,128,128]{2,1,0:T(8,128)S(1)}) custom-call(f32[512,128]{1,0:T(8,128)S(1)} %pad_maximum_fusion.2.refs_0_, f32[512,128]{1,0:T(8,128)S(1)} %collective-permute-done.17.refs_1_, bf16[1024,2048]{1,0:T(8,128)(2,1)S(1)} %get-tuple-element.49.refs_2_, ...), custom_call_target="tpu_custom_call" | custom-call | flops 1610612736 | bytes 8388608 | tf_op jit(solution)/shard_map/potentials/pallas_call | solution.py:296
  50.1 0.0 copy-start.2
  50.1 0.0 copy-start.3
  50.1 0.0 copy-start.4
  50.1 0.0 copy-start.8
  50.2 1.1 %collective-permute-start.22 = (f32[4,128,128]{2,1,0:T(8,128)S(1)}, f32[4,128,128]{2,1,0:T(8,128)S(1)}, u32[]{:S(2)}, u32[]{:S(2)}) collective-permute-start(f32[4,128,128]{2,1,0:T(8,128)S(1)} %get-tuple-element.62), channel_id=1, source_target_pairs={{0,4},{4,0},{8,12},{12,8},{1,5},{5,1},{9,13},{13,9},{2,6},{6,2},{1... | collective-permute-start | bytes 786440 | tf_op jit(solution)/shard_map/ppermute | solution.py:32
  51.3 1.5 %collective-permute-start.23 = (f32[4,128,128]{2,1,0:T(8,128)S(1)}, f32[4,128,128]{2,1,0:T(8,128)S(1)}, u32[]{:S(2)}, u32[]{:S(2)}) collective-permute-start(f32[4,128,128]{2,1,0:T(8,128)S(1)} %get-tuple-element.63), channel_id=1, source_target_pairs={{0,8},{4,12},{8,0},{12,4},{1,9},{5,13},{9,1},{13,5},{2,10},{6,14},... | collective-permute-start | bytes 786440 | tf_op jit(solution)/shard_map/ppermute | solution.py:32
  52.8 0.0 collective-permute-done.19.refs_3_
  52.8 0.9 %collective-permute-start.24 = (f32[4,128,128]{2,1,0:T(8,128)S(1)}, f32[4,128,128]{2,1,0:T(8,128)S(1)}, u32[]{:S(2)}, u32[]{:S(2)}) collective-permute-start(f32[4,128,128]{2,1,0:T(8,128)S(1)} %get-tuple-element.64), channel_id=1, source_target_pairs={{0,12},{4,8},{8,4},{12,0},{1,13},{5,9},{9,5},{13,1},{2,14},{6,10},... | collective-permute-start | bytes 786440 | tf_op jit(solution)/shard_map/ppermute | solution.py:32
  53.7 0.0 collective-permute-done.20.refs_5_
  53.7 0.0 collective-permute-done.21.refs_7_
  53.7 14.0 %messages.5.refs_2_ = f32[4,128,128]{2,1,0:T(8,128)S(1)} custom-call(s32[7,8]{1,0:T(8,128)S(1)} %copy-done.12, f32[8,128]{1,0:T(8,128)S(1)} %copy-done.11, f32[128,128]{1,0:T(8,128)S(1)} %copy-done.9, f32[4,136,128]{2,1,0:T(8,128)S(1)} %collective-permute-done.13.refs_0_, f32[4,136,128]{2,1,0:T(8,128)S(1)} %collective-permute-done.18.refs_1_, ...), custom_call_target="tpu_custom_call" | custom-call | flops 9663676416 | bytes 1048576 | tf_op jit(solution)/shard_map/messages/pallas_call | solution.py:462
  67.8 2.0 %atom_mlp.1 = f32[4,128,128]{2,1,0:T(8,128)} custom-call(s32[2,1,2]{2,1,0:T(1,128)S(1)} %bitcast.13, f32[4,128,128]{2,1,0:T(8,128)S(1)} %bitcast.10, f32[4,128,128]{2,1,0:T(8,128)S(1)} %messages.5.refs_2_, f32[4,128,128]{2,1,0:T(8,128)S(1)} %get-tuple-element.61.refs_3_, f32[4,128,128]{2,1,0:T(8,128)S(1)} %collective-permute-done.22.refs_4_, ...), custom_call_target="tpu_custom_call" | custom-call | tf_op jit(solution)/shard_map/atom_mlp/pallas_call | solution.py:535
  (30 shorter events, 0.2 us)
Async XLA Ops:
  0.0 0.9 %copy-start.1 = (f32[2,2,1,128,128]{4,3,2,1,0:T(8,128)S(1)}, f32[2,2,1,128,128]{4,3,2,1,0:T(8,128)}, u32[]{:S(2)}) copy-start(f32[2,2,1,128,128]{4,3,2,1,0:T(8,128)} %param.13) | copy-start | bytes 786436
  1.0 0.7 copy-start.6
  1.6 0.7 copy-start.7
  2.9 9.7 %collective-permute-start = (f32[4,136,128]{2,1,0:T(8,128)S(1)}, f32[4,136,128]{2,1,0:T(8,128)S(1)}, u32[]{:S(2)}, u32[]{:S(2)}) collective-permute-start(f32[4,136,128]{2,1,0:T(8,128)S(1)} %pack.1.refs_0_.refs_8_), channel_id=1, source_target_pairs={{0,4},{4,0},{8,12},{12,8},{1,5},{5,1},{9,13},{13,9},{2,6},{6,2},{1... | collective-permute-start | bytes 835592 | tf_op jit(solution)/shard_map/ppermute | solution.py:32
  5.9 13.4 %collective-permute-start.2 = (f32[4,136,128]{2,1,0:T(8,128)S(1)}, f32[4,136,128]{2,1,0:T(8,128)S(1)}, u32[]{:S(2)}, u32[]{:S(2)}) collective-permute-start(f32[4,136,128]{2,1,0:T(8,128)S(1)} %pack.1.refs_0_.refs_8_), channel_id=1, source_target_pairs={{0,8},{4,12},{8,0},{12,4},{1,9},{5,13},{9,1},{13,5},{2,10},{6,14},... | collective-permute-start | bytes 835592 | tf_op jit(solution)/shard_map/ppermute | solution.py:32
  7.5 14.0 %collective-permute-start.13 = (f32[4,136,128]{2,1,0:T(8,128)S(1)}, f32[4,136,128]{2,1,0:T(8,128)S(1)}, u32[]{:S(2)}, u32[]{:S(2)}) collective-permute-start(f32[4,136,128]{2,1,0:T(8,128)S(1)} %pack.1.refs_0_.refs_8_), channel_id=1, source_target_pairs={{0,1},{1,0},{2,3},{3,2},{4,5},{5,4},{6,7},{7,6},{8,9},{9,8},{10,11... | collective-permute-start | bytes 835592 | tf_op jit(solution)/shard_map/ppermute | solution.py:54
  9.0 17.9 %collective-permute-start.7 = (f32[4,136,128]{2,1,0:T(8,128)S(1)}, f32[4,136,128]{2,1,0:T(8,128)S(1)}, u32[]{:S(2)}, u32[]{:S(2)}) collective-permute-start(f32[4,136,128]{2,1,0:T(8,128)S(1)} %pack.1.refs_0_.refs_8_), channel_id=1, source_target_pairs={{0,16},{16,0},{1,17},{17,1},{2,18},{18,2},{3,19},{19,3},{4,20},{20... | collective-permute-start | bytes 835592 | tf_op jit(solution)/shard_map/ppermute | solution.py:32
  9.0 15.3 %collective-permute-start.14 = (f32[4,136,128]{2,1,0:T(8,128)S(1)}, f32[4,136,128]{2,1,0:T(8,128)S(1)}, u32[]{:S(2)}, u32[]{:S(2)}) collective-permute-start(f32[4,136,128]{2,1,0:T(8,128)S(1)} %pack.1.refs_0_.refs_8_), channel_id=1, source_target_pairs={{0,3},{1,2},{2,1},{3,0},{4,7},{5,6},{6,5},{7,4},{8,11},{9,10},{10,... | collective-permute-start | bytes 835592 | tf_op jit(solution)/shard_map/ppermute | solution.py:54
  12.6 9.0 %collective-permute-start.1 = (f32[4,136,128]{2,1,0:T(8,128)S(1)}, f32[4,136,128]{2,1,0:T(8,128)S(1)}, u32[]{:S(2)}, u32[]{:S(2)}) collective-permute-start(f32[4,136,128]{2,1,0:T(8,128)S(1)} %collective-permute-done.refs_1_.refs_2_), channel_id=1, source_target_pairs={{0,8},{4,12},{8,0},{12,4},{1,9},{5,13},{9,1},{13,5},{2,10},{6,14},... | collective-permute-start | bytes 835592 | tf_op jit(solution)/shard_map/ppermute | solution.py:32
  14.4 0.8 %copy-start.10 = (s32[3,2048]{1,0:T(4,128)S(1)}, s32[3,2048]{1,0:T(4,128)}, u32[]{:S(2)}) copy-start(s32[3,2048]{1,0:T(4,128)} %column_ref.1) | copy-start | bytes 73732
  19.3 9.3 %collective-permute-start.8 = (f32[4,136,128]{2,1,0:T(8,128)S(1)}, f32[4,136,128]{2,1,0:T(8,128)S(1)}, u32[]{:S(2)}, u32[]{:S(2)}) collective-permute-start(f32[4,136,128]{2,1,0:T(8,128)S(1)} %collective-permute-done.refs_1_.refs_2_), channel_id=1, source_target_pairs={{0,16},{16,0},{1,17},{17,1},{2,18},{18,2},{3,19},{19,3},{4,20},{20... | collective-permute-start | bytes 835592 | tf_op jit(solution)/shard_map/ppermute | solution.py:32
  21.5 9.9 %copy-start.9 = (f32[128,128]{1,0:T(8,128)S(1)}, f32[128,128]{1,0:T(8,128)}, u32[]{:S(2)}) copy-start(f32[128,128]{1,0:T(8,128)} %value_ref.2) | copy-start | bytes 196612
  21.5 9.9 %copy-start.11 = (f32[8,128]{1,0:T(8,128)S(1)}, f32[8,128]{1,0:T(8,128)}, u32[]{:S(2)}) copy-start(f32[8,128]{1,0:T(8,128)} %mix_ref.5) | copy-start | bytes 12292
  21.5 9.8 %copy-start.13 = (s32[7,2]{1,0:T(8,128)S(1)}, s32[7,2]{1,0:T(8,128)}, u32[]{:S(2)}) copy-start(s32[7,2]{1,0:T(8,128)} %constant.47.clone.step_ref) | copy-start | bytes 172
  23.7 2.3 %collective-permute-start.3 = (f32[512,128]{1,0:T(8,128)S(1)}, f32[512,128]{1,0:T(8,128)S(1)}, u32[]{:S(2)}, u32[]{:S(2)}) collective-permute-start(f32[512,128]{1,0:T(8,128)S(1)} %get-tuple-element.41), channel_id=1, source_target_pairs={{0,16},{16,0},{1,17},{17,1},{2,18},{18,2},{3,19},{19,3},{4,20},{20... | collective-permute-start | bytes 786440 | tf_op jit(solution)/shard_map/ppermute | solution.py:32
  24.2 6.9 %collective-permute-start.9 = (f32[4,136,128]{2,1,0:T(8,128)S(1)}, f32[4,136,128]{2,1,0:T(8,128)S(1)}, u32[]{:S(2)}, u32[]{:S(2)}) collective-permute-start(f32[4,136,128]{2,1,0:T(8,128)S(1)} %collective-permute-done.1.refs_0_.refs_4_), channel_id=1, source_target_pairs={{0,16},{16,0},{1,17},{17,1},{2,18},{18,2},{3,19},{19,3},{4,20},{20... | collective-permute-start | bytes 835592 | tf_op jit(solution)/shard_map/ppermute | solution.py:32
  24.4 22.2 %collective-permute-start.15 = (f32[4,136,128]{2,1,0:T(8,128)S(1)}, f32[4,136,128]{2,1,0:T(8,128)S(1)}, u32[]{:S(2)}, u32[]{:S(2)}) collective-permute-start(f32[4,136,128]{2,1,0:T(8,128)S(1)} %get-tuple-element.66), channel_id=1, source_target_pairs={{0,4},{4,0},{8,12},{12,8},{1,5},{5,1},{9,13},{13,9},{2,6},{6,2},{1... | collective-permute-start | bytes 835592 | tf_op jit(solution)/shard_map/ppermute | solution.py:54
  26.0 20.6 %collective-permute-start.16 = (f32[4,136,128]{2,1,0:T(8,128)S(1)}, f32[4,136,128]{2,1,0:T(8,128)S(1)}, u32[]{:S(2)}, u32[]{:S(2)}) collective-permute-start(f32[4,136,128]{2,1,0:T(8,128)S(1)} %get-tuple-element.65), channel_id=1, source_target_pairs={{0,12},{4,8},{8,4},{12,0},{1,13},{5,9},{9,5},{13,1},{2,14},{6,10},... | collective-permute-start | bytes 835592 | tf_op jit(solution)/shard_map/ppermute | solution.py:54
  26.9 8.9 %collective-permute-start.4 = (f32[128,128]{1,0:T(8,128)S(1)}, f32[128,128]{1,0:T(8,128)S(1)}, u32[]{:S(2)}, u32[]{:S(2)}) collective-permute-start(f32[128,128]{1,0:T(8,128)S(1)} %get-tuple-element.77), channel_id=1, source_target_pairs={{0,1},{1,0},{2,3},{3,2},{4,5},{5,4},{6,7},{7,6},{8,9},{9,8},{10,11... | collective-permute-start | bytes 196616 | tf_op jit(solution)/shard_map/ppermute | solution.py:32
  28.6 7.5 %collective-permute-start.5 = (f32[128,128]{1,0:T(8,128)S(1)}, f32[128,128]{1,0:T(8,128)S(1)}, u32[]{:S(2)}, u32[]{:S(2)}) collective-permute-start(f32[128,128]{1,0:T(8,128)S(1)} %get-tuple-element.76), channel_id=1, source_target_pairs={{0,2},{1,3},{2,0},{3,1},{4,6},{5,7},{6,4},{7,5},{8,10},{9,11},{10,... | collective-permute-start | bytes 196616 | tf_op jit(solution)/shard_map/ppermute | solution.py:32
  31.2 6.2 %copy-start = (f32[2048,128]{1,0:T(8,128)S(1)}, f32[2048,128]{1,0:T(8,128)}, u32[]{:S(2)}) copy-start(f32[2048,128]{1,0:T(8,128)} %refs_5_.1) | copy-start | bytes 3145732
  31.2 6.2 %copy-start.5 = (f32[128,128]{1,0:T(8,128)S(1)}, f32[128,128]{1,0:T(8,128)}, u32[]{:S(2)}) copy-start(f32[128,128]{1,0:T(8,128)} %refs_4_) | copy-start | bytes 196612
  31.2 6.2 %collective-permute-start.6 = (f32[128,128]{1,0:T(8,128)S(1)}, f32[128,128]{1,0:T(8,128)S(1)}, u32[]{:S(2)}, u32[]{:S(2)}) collective-permute-start(f32[128,128]{1,0:T(8,128)S(1)} %get-tuple-element.75), channel_id=1, source_target_pairs={{0,3},{1,2},{2,1},{3,0},{4,7},{5,6},{6,5},{7,4},{8,11},{9,10},{10,... | collective-permute-start | bytes 196616 | tf_op jit(solution)/shard_map/ppermute | solution.py:32
  37.5 9.0 %collective-permute-start.10 = (f32[128,128]{1,0:T(8,128)S(1)}, f32[128,128]{1,0:T(8,128)S(1)}, u32[]{:S(2)}, u32[]{:S(2)}) collective-permute-start(f32[128,128]{1,0:T(8,128)S(1)} %filter.1), channel_id=1, source_target_pairs={{0,1},{1,0},{2,3},{3,2},{4,5},{5,4},{6,7},{7,6},{8,9},{9,8},{10,11... | collective-permute-start | bytes 196616 | tf_op jit(solution)/shard_map/ppermute | solution.py:32
  38.3 8.2 %collective-permute-start.11 = (f32[128,128]{1,0:T(8,128)S(1)}, f32[128,128]{1,0:T(8,128)S(1)}, u32[]{:S(2)}, u32[]{:S(2)}) collective-permute-start(f32[128,128]{1,0:T(8,128)S(1)} %filter.1), channel_id=1, source_target_pairs={{0,2},{1,3},{2,0},{3,1},{4,6},{5,7},{6,4},{7,5},{8,10},{9,11},{10,... | collective-permute-start | bytes 196616 | tf_op jit(solution)/shard_map/ppermute | solution.py:32
  40.2 6.3 %collective-permute-start.12 = (f32[128,128]{1,0:T(8,128)S(1)}, f32[128,128]{1,0:T(8,128)S(1)}, u32[]{:S(2)}, u32[]{:S(2)}) collective-permute-start(f32[128,128]{1,0:T(8,128)S(1)} %filter.1), channel_id=1, source_target_pairs={{0,3},{1,2},{2,1},{3,0},{4,7},{5,6},{6,5},{7,4},{8,11},{9,10},{10,... | collective-permute-start | bytes 196616 | tf_op jit(solution)/shard_map/ppermute | solution.py:32
  46.6 1.6 %collective-permute-start.17 = (f32[512,128]{1,0:T(8,128)S(1)}, f32[512,128]{1,0:T(8,128)S(1)}, u32[]{:S(2)}, u32[]{:S(2)}) collective-permute-start(f32[512,128]{1,0:T(8,128)S(1)} %pad_maximum_fusion.2.refs_0_), channel_id=1, source_target_pairs={{0,16},{16,0},{1,17},{17,1},{2,18},{18,2},{3,19},{19,3},{4,20},{20... | collective-permute-start | bytes 786440 | tf_op jit(solution)/shard_map/ppermute | solution.py:32
  46.7 4.6 %collective-permute-start.18 = (f32[4,136,128]{2,1,0:T(8,128)S(1)}, f32[4,136,128]{2,1,0:T(8,128)S(1)}, u32[]{:S(2)}, u32[]{:S(2)}) collective-permute-start(f32[4,136,128]{2,1,0:T(8,128)S(1)} %collective-permute-done.13.refs_0_), channel_id=1, source_target_pairs={{0,16},{16,0},{1,17},{17,1},{2,18},{18,2},{3,19},{19,3},{4,20},{20... | collective-permute-start | bytes 835592 | tf_op jit(solution)/shard_map/ppermute | solution.py:32
  47.2 5.6 %collective-permute-start.19 = (f32[4,136,128]{2,1,0:T(8,128)S(1)}, f32[4,136,128]{2,1,0:T(8,128)S(1)}, u32[]{:S(2)}, u32[]{:S(2)}) collective-permute-start(f32[4,136,128]{2,1,0:T(8,128)S(1)} %collective-permute-done.14.refs_2_), channel_id=1, source_target_pairs={{0,16},{16,0},{1,17},{17,1},{2,18},{18,2},{3,19},{19,3},{4,20},{20... | collective-permute-start | bytes 835592 | tf_op jit(solution)/shard_map/ppermute | solution.py:32
  47.3 6.5 %collective-permute-start.20 = (f32[4,136,128]{2,1,0:T(8,128)S(1)}, f32[4,136,128]{2,1,0:T(8,128)S(1)}, u32[]{:S(2)}, u32[]{:S(2)}) collective-permute-start(f32[4,136,128]{2,1,0:T(8,128)S(1)} %collective-permute-done.15.refs_4_), channel_id=1, source_target_pairs={{0,16},{16,0},{1,17},{17,1},{2,18},{18,2},{3,19},{19,3},{4,20},{20... | collective-permute-start | bytes 835592 | tf_op jit(solution)/shard_map/ppermute | solution.py:32
  47.7 6.0 %collective-permute-start.21 = (f32[4,136,128]{2,1,0:T(8,128)S(1)}, f32[4,136,128]{2,1,0:T(8,128)S(1)}, u32[]{:S(2)}, u32[]{:S(2)}) collective-permute-start(f32[4,136,128]{2,1,0:T(8,128)S(1)} %collective-permute-done.16.refs_6_), channel_id=1, source_target_pairs={{0,16},{16,0},{1,17},{17,1},{2,18},{18,2},{3,19},{19,3},{4,20},{20... | collective-permute-start | bytes 835592 | tf_op jit(solution)/shard_map/ppermute | solution.py:32
  48.2 5.5 %copy-start.12 = (s32[7,8]{1,0:T(8,128)S(1)}, s32[7,8]{1,0:T(8,128)}, u32[]{:S(2)}) copy-start(s32[7,8]{1,0:T(8,128)} %constant.48.clone.step_ref) | copy-start | bytes 676
  50.1 17.7 %copy-start.2 = (f32[2,2,1,128,128]{4,3,2,1,0:T(8,128)S(1)}, f32[2,2,1,128,128]{4,3,2,1,0:T(8,128)}, u32[]{:S(2)}) copy-start(f32[2,2,1,128,128]{4,3,2,1,0:T(8,128)} %param.13) | copy-start | bytes 786436
  50.1 17.7 %copy-start.3 = (f32[128,256]{1,0:T(8,128)S(1)}, f32[128,256]{1,0:T(8,128)}, u32[]{:S(2)}) copy-start(f32[128,256]{1,0:T(8,128)} %refs_7_.1) | copy-start | bytes 393220
  50.1 17.7 %copy-start.4 = (f32[256,128]{1,0:T(8,128)S(1)}, f32[256,128]{1,0:T(8,128)}, u32[]{:S(2)}) copy-start(f32[256,128]{1,0:T(8,128)} %refs_8_.1) | copy-start | bytes 393220
  50.1 17.7 %copy-start.8 = (s32[2,2,1]{1,2,0:T(1,128)S(1)}, s32[2,2,1]{1,2,0:T(1,128)}, u32[]{:S(2)}) copy-start(s32[2,2,1]{1,2,0:T(1,128)} %param.15) | copy-start | bytes 52
  50.2 17.6 %collective-permute-start.22 = (f32[4,128,128]{2,1,0:T(8,128)S(1)}, f32[4,128,128]{2,1,0:T(8,128)S(1)}, u32[]{:S(2)}, u32[]{:S(2)}) collective-permute-start(f32[4,128,128]{2,1,0:T(8,128)S(1)} %get-tuple-element.62), channel_id=1, source_target_pairs={{0,4},{4,0},{8,12},{12,8},{1,5},{5,1},{9,13},{13,9},{2,6},{6,2},{1... | collective-permute-start | bytes 786440 | tf_op jit(solution)/shard_map/ppermute | solution.py:32
  51.3 16.5 %collective-permute-start.23 = (f32[4,128,128]{2,1,0:T(8,128)S(1)}, f32[4,128,128]{2,1,0:T(8,128)S(1)}, u32[]{:S(2)}, u32[]{:S(2)}) collective-permute-start(f32[4,128,128]{2,1,0:T(8,128)S(1)} %get-tuple-element.63), channel_id=1, source_target_pairs={{0,8},{4,12},{8,0},{12,4},{1,9},{5,13},{9,1},{13,5},{2,10},{6,14},... | collective-permute-start | bytes 786440 | tf_op jit(solution)/shard_map/ppermute | solution.py:32
  52.8 15.0 %collective-permute-start.24 = (f32[4,128,128]{2,1,0:T(8,128)S(1)}, f32[4,128,128]{2,1,0:T(8,128)S(1)}, u32[]{:S(2)}, u32[]{:S(2)}) collective-permute-start(f32[4,128,128]{2,1,0:T(8,128)S(1)} %get-tuple-element.64), channel_id=1, source_target_pairs={{0,12},{4,8},{8,4},{12,0},{1,13},{5,9},{9,5},{13,1},{2,14},{6,10},... | collective-permute-start | bytes 786440 | tf_op jit(solution)/shard_map/ppermute | solution.py:32
